TPU v7x, 32 devices: a whole 2x2x4 slice. The times are simulated.
32 devices in a mesh: group: 2 (over x), tensor: 16 (over z, y, core).
Axes of the slice: x: 2, y: 2, z: 4, core: 2. Of those that a mesh axis runs over, the one named last changes fastest.
Arguments:
- hidden: bfloat16 [192, 8192], P(('group', 'tensor')), parts along dimension 0, may hold values from -6 to 6
- input_norm_scale: bfloat16 [8192], replicated, may hold values from 0.099609375 to 1.8984375
- query_key_value_weight: bfloat16 [8192, 10240], P(None, 'tensor'), may hold values from -0.0625 to 0.0625
- projection_bias: bfloat16 [10240], P('tensor'), may hold values from -4 to 4
- rotated_key_cache: bfloat16 [192, 384, 1024], P(('group', 'tensor')), parts along dimension 0, may hold values from -3000 to 3000, as said below
- past_value_cache: bfloat16 [192, 384, 1024], P(('group', 'tensor')), parts along dimension 0, may hold values from -6 to 6
- lengths: int32 [192], P(('group', 'tensor')), parts along dimension 0, may hold values from 96 to 384, as said below
- row_adapter_index: int32 [192], P(('group', 'tensor')), parts along dimension 0, may hold values from 0 to 31
- output_weight: bfloat16 [8192, 8192], P(None, 'tensor'), may hold values from -0.25 to 0.25
- adapter_down_weight: bfloat16 [32, 8192, 16], P('tensor'), may hold values from -0.0625 to 0.0625
- adapter_up_weight: bfloat16 [32, 16, 8192], P(None, None, 'tensor'), may hold values from -3 to 3
Outputs:
- projected: bfloat16 [192, 8192], P(('group', 'tensor')), parts along dimension 0
There are 2 independent parts, one for each index of `group`. A program takes and returns all parts, laid end to end along the dimension named above; an argument that names none is the same for every part. Nothing has to cross between parts.
Inputs may be any that keep to these rules, and one draw needn't show every extreme that they name: `lengths`: every row has at least 96 cached positions, and in every draw some row's cache is full. `rotated_key_cache`: keys are finite and of moderate size in most positions.
All inputs are finite; a program needn't handle non-finite values.
Results may differ from a plain program's by a relative error of at most 0.028.
Values may be sent and summed in bfloat16 or wider, within the bound.
No kernel may reach another device: no remote copies, remote signals or barrier semaphores. Data moves between devices by JAX's collectives and lax.ppermute only.
A program may use at most 128 MiB of HBM per device.

v0:
```python
import jax
import jax.numpy as jnp
from jax import lax
from jax.sharding import PartitionSpec as P

QUERY_HEADS = 64
KVH = 8
HEAD_SIZE = 128
ADAPTER_RANK = 16


EPS = 1e-06
ROPE_BASE = 1000000.0


def rope_tables(lengths):
    half = HEAD_SIZE // 2
    inv = ROPE_BASE ** (-(jnp.arange(half, dtype=jnp.float32) * 2.0 / HEAD_SIZE))
    angle = lengths.astype(jnp.float32)[:, None] * inv[None, :]
    return (jnp.cos(angle), jnp.sin(angle))


def rotate(heads, cosine, sine):
    half = HEAD_SIZE // 2
    first = heads[..., :half]
    second = heads[..., half:]
    cosine = cosine[:, None, :]
    sine = sine[:, None, :]
    return jnp.concatenate(
        [first * cosine - second * sine, second * cosine + first * sine], axis=-1
    )


def per_device(
    hidden,
    input_norm_scale,
    query_key_value_weight,
    projection_bias,
    rotated_key_cache,
    past_value_cache,
    lengths,
    row_adapter_index,
    output_weight,
    adapter_down_weight,
    adapter_up_weight,
):
    row_dev = hidden.shape[0]
    capacity = rotated_key_cache.shape[1]
    groups = QUERY_HEADS // KVH
    gain = input_norm_scale.astype(jnp.float32)
    bias = projection_bias.astype(jnp.float32)
    rows_f = hidden.astype(jnp.float32)
    factor = lax.rsqrt(jnp.mean(rows_f * rows_f, axis=-1, keepdims=True) + EPS)
    normed = (rows_f * factor * gain).astype(jnp.bfloat16)
    qkv_cols = (
        jnp.dot(
            lax.all_gather(normed, "tensor", axis=0, tiled=True),
            query_key_value_weight,
            preferred_element_type=jnp.float32,
        )
        + bias
    ).astype(jnp.bfloat16)
    qkv = lax.all_to_all(qkv_cols, "tensor", split_axis=0, concat_axis=1, tiled=True)
    query = (
        qkv[:, : QUERY_HEADS * HEAD_SIZE]
        .astype(jnp.float32)
        .reshape(row_dev, QUERY_HEADS, HEAD_SIZE)
    )
    new_key = (
        qkv[:, QUERY_HEADS * HEAD_SIZE : (QUERY_HEADS + KVH) * HEAD_SIZE]
        .astype(jnp.float32)
        .reshape(row_dev, KVH, HEAD_SIZE)
    )
    new_value = qkv[:, (QUERY_HEADS + KVH) * HEAD_SIZE :].reshape(row_dev, KVH, HEAD_SIZE)
    cosine, sine = rope_tables(lengths)
    q_rot = (
        rotate(query, cosine, sine).astype(jnp.bfloat16).reshape(row_dev, KVH, groups, HEAD_SIZE)
    )
    k_rot = rotate(new_key, cosine, sine).astype(jnp.bfloat16)
    scale = 1.0 / HEAD_SIZE**0.5
    keys = rotated_key_cache.reshape(row_dev, capacity, KVH, HEAD_SIZE)
    values = past_value_cache.reshape(row_dev, capacity, KVH, HEAD_SIZE)
    scores = jnp.einsum("rkgd,rtkd->rkgt", q_rot, keys, preferred_element_type=jnp.float32) * scale
    own = jnp.einsum("rkgd,rkd->rkg", q_rot, k_rot, preferred_element_type=jnp.float32) * scale
    valid = (jnp.arange(capacity)[None, :] < lengths[:, None])[:, None, None, :]
    top = jnp.maximum(jnp.max(jnp.where(valid, scores, -1e30), axis=-1), own)
    expo = jnp.where(valid, jnp.exp(scores - top[..., None]), 0.0)
    expo_own = jnp.exp(own - top)
    total = jnp.sum(expo, axis=-1) + expo_own
    weights = (expo / total[..., None]).astype(jnp.bfloat16)
    weight_own = (expo_own / total).astype(jnp.bfloat16)
    mixed = jnp.einsum("rkgt,rtkd->rkgd", weights, values, preferred_element_type=jnp.float32)
    mixed = (
        mixed
        + weight_own.astype(jnp.float32)[..., None] * new_value.astype(jnp.float32)[:, :, None, :]
    )
    attn = mixed.reshape(row_dev, QUERY_HEADS * HEAD_SIZE).astype(jnp.bfloat16)
    picked_weights, every_adapter_index = (
        lax.all_gather(attn, "tensor", axis=0, tiled=True),
        lax.all_gather(row_adapter_index, "tensor", axis=0, tiled=True),
    )
    base = jnp.dot(picked_weights, output_weight, preferred_element_type=jnp.float32)
    stored_value = adapter_down_weight.shape[0]
    first_owned = lax.axis_index("tensor") * stored_value
    partial_coords = jnp.zeros((picked_weights.shape[0], ADAPTER_RANK), jnp.float32)
    for row_number in range(stored_value):
        owned = every_adapter_index == first_owned + row_number
        row_positions = jnp.dot(
            picked_weights, adapter_down_weight[row_number], preferred_element_type=jnp.float32
        )
        partial_coords = partial_coords + jnp.where(owned[:, None], row_positions, 0.0)
    shrunk = lax.psum(partial_coords, "tensor").astype(jnp.bfloat16)
    expanded_rows = jnp.take(adapter_up_weight, every_adapter_index, axis=0)
    delta = jnp.einsum("rk,rkc->rc", shrunk, expanded_rows, preferred_element_type=jnp.float32)
    proj_cols = (base + delta).astype(jnp.bfloat16)
    return lax.all_to_all(proj_cols, "tensor", split_axis=0, concat_axis=1, tiled=True)


def solution(mesh):
    in_specs = (
        P(("group", "tensor"), None),
        P(),
        P(None, "tensor"),
        P("tensor"),
        P(("group", "tensor"), None, None),
        P(("group", "tensor"), None, None),
        P(("group", "tensor")),
        P(("group", "tensor")),
        P(None, "tensor"),
        P("tensor", None, None),
        P(None, None, "tensor"),
    )
    out_specs = P(("group", "tensor"), None)
    return jax.shard_map(
        per_device, mesh=mesh, in_specs=in_specs, out_specs=out_specs, check_vma=False
    )
```

profile of v0, /device:TPU:0, one launch (start us, length us, event | category | flops | bytes accessed | tf_op | source)
XLA Modules:
  0.0 183.1 jit_solution(12021590516771213637)
XLA Ops:
  6.5 0.0 copy-start
  6.5 0.0 all-gather.5.cloned.1.call-start
  6.5 0.8 convert_element_type.55
  7.3 1.1 fusion.27
  8.4 1.7 fusion.34
  10.1 0.0 all-gather.5.cloned.1.call-update
  10.1 0.7 convert_element_type.57
  10.8 0.7 iota_compare_fusion
  11.5 42.8 %all-gather.5.cloned.1.call-done = bf16[16,6,8192]{2,1,0:T(8,128)(2,1)} async-done(((bf16[1,6,8192]{2,1,0:T(8,128)(2,1)}), bf16[16,6,8192]{2,1,0:T(8,128)(2,1)}) %all-gather.5.cloned.1.call-update) | async-done | bytes 1572880 | tf_op jit(solution)/shard_map/all_gather | solution.py:57
  54.3 1.8 %reshape.151 = bf16[96,8192]{1,0:T(8,128)(2,1)S(1)} reshape(bf16[16,6,8192]{2,1,0:T(8,128)(2,1)} %all-gather.5.cloned.1.call-done) | data formatting | bytes 3145728
  56.2 0.0 copy-start.2
  56.2 5.8 %fusion.12 = bf16[96,640]{1,0:T(8,128)(2,1)S(1)} fusion(bf16[96,8192]{1,0:T(8,128)(2,1)S(1)} %reshape.151, bf16[8192,640]{1,0:T(8,128)(2,1)} %param.13, f32[640]{0:T(1024)S(1)} %convert_element_type.57), kind=kOutput, calls=%fused_computation.12 | convolution fusion | flops 1006755840 | bytes 12184064 | tf_op jit(solution)/shard_map/dot_general | solution.py:56
  62.0 0.7 all_to_all.28
  62.7 3.5 %all-to-all-start = ((bf16[16,6,640]{2,1,0:T(8,128)(2,1)}), bf16[16,6,640]{2,1,0:T(8,128)(2,1)S(1)}, u32[]{:S(2)}, u32[]{:S(2)}) async-start(bf16[16,6,640]{2,1,0:T(8,128)(2,1)} %all_to_all.28), calls=%async_computation | async-start | bytes 327680 | tf_op jit(solution)/shard_map/all_to_all | solution.py:63
  66.3 0.0 all-gather.7.cloned.1.call-start
  66.3 0.0 copy-done.2
  66.3 0.1 multiply_cosine_fusion
  66.5 8.2 %all-to-all-done = bf16[16,6,640]{2,1,0:T(8,128)(2,1)S(1)} async-done(((bf16[16,6,640]{2,1,0:T(8,128)(2,1)}), bf16[16,6,640]{2,1,0:T(8,128)(2,1)S(1)}, u32[]{:S(2)}, u32[]{:S(2)}) %all-to-all-start) | async-done | bytes 122912 | tf_op jit(solution)/shard_map/all_to_all | solution.py:63
  74.8 0.1 subtract_convert_fusion.1
  74.9 0.1 fusion.35
  75.0 0.1 maximum_bitcast_fusion
  75.1 0.2 fusion.37
  75.3 4.2 %select_reduce_fusion = (f32[6,8,8]{2,1,0:T(8,128)S(1)}, f32[6,8,8,384]{3,2,1,0:T(8,128)S(1)}) fusion(pred[6,384]{1,0:T(8,128)(4,1)S(1)} %iota_compare_fusion, bf16[6,8,8,64]{3,2,1,0:T(8,128)(2,1)S(1)} %get-tuple-element.6, bf16[6,8,8,64]{3,2,1,0:T(8,128)(2,1)S(1)} %get-tuple-element.5, bf16[6,384,1024]{2,1,0:T(8,128)(2,1)} %param.15), kind=kOutput, calls=%fused_computation.23 | convolution fusion | flops 38387328 | bytes 5410560 | tf_op jit(solution)/shard_map/rkgd,rtkd->rkgt/dot_general | solution.py:83
  79.5 0.3 fusion.22
  79.8 0.0 copy-start.4
  79.9 0.0 copy-start.3
  79.9 3.4 %fusion.17 = bf16[6,8,8,128]{3,2,1,0:T(8,128)(2,1)S(1)} fusion(f32[6,8,8,384]{3,2,1,0:T(8,128)S(1)} %get-tuple-element.19, f32[6,8,8]{2,1,0:T(8,128)S(1)} %get-tuple-element.10, f32[6,8,8]{2,1,0:T(8,128)S(1)} %multiply_maximum_fusion, pred[6,384]{1,0:T(8,128)(4,1)S(1)} %iota_compare_fusion, f32[6,8,128]{2,1,0:T(8,128)S(1)} %get-tuple-element.20, ...), kind=kOutput, calls=%fused_computation.16 | convolution fusion | flops 38486016 | bytes 5438208 | tf_op jit(solution)/shard_map/rkgt,rtkd->rkgd/dot_general | solution.py:92
  83.3 0.8 reshape.152
  84.1 0.0 all-gather.7.cloned.1.call-update
  84.1 0.0 copy-done.4
  84.1 0.7 dynamic-slice
  85.4 0.0 copy-done.3
  85.5 0.2 dynamic-update-slice
  85.7 8.8 %all-reduce = s32[96]{0:T(128)S(1)} all-reduce(s32[96]{0:T(128)S(1)} %dynamic-update-slice), channel_id=1, replica_groups=mesh['group'=2,'tensor'=16] {'tensor'}, use_global_device_ids=true, to_apply=%add | all-reduce | flops 96 | bytes 768
  94.5 0.0 copy-done
  94.5 1.9 %gather_fusion = bf16[96,16,512]{2,1,0:T(8,128)(2,1)} fusion(bf16[32,16,512]{2,1,0:T(8,128)(2,1)S(1)} %copy-done, s32[1024]{0:T(1024)S(1)} %pad_clamp_fusion), kind=kCustom, calls=%fused_computation | custom fusion | bytes 3146112 | tf_op jit(solution)/shard_map/jit(_take)/gather | solution.py:113
  96.5 0.0 copy-start.1
  96.5 26.9 %all-gather.7.cloned.1.call-done = bf16[16,6,8192]{2,1,0:T(8,128)(2,1)} async-done(((bf16[1,6,8192]{2,1,0:T(8,128)(2,1)}), bf16[16,6,8192]{2,1,0:T(8,128)(2,1)}) %all-gather.7.cloned.1.call-update) | async-done | bytes 1572880 | tf_op jit(solution)/shard_map/all_gather | solution.py:99
  123.4 1.8 %reshape.153 = bf16[96,8192]{1,0:T(8,128)(2,1)S(1)} reshape(bf16[16,6,8192]{2,1,0:T(8,128)(2,1)} %all-gather.7.cloned.1.call-done) | data formatting | bytes 3145728
  125.2 0.0 copy-done.1
  125.2 0.5 convolution_select_fusion.1
  125.8 0.5 fusion.20
  126.3 31.9 %psum.7 = bf16[96,16]{0,1:T(8,128)(2,1)S(1)} all-reduce(f32[96,16]{0,1:T(8,128)S(1)} %fusion.20), channel_id=1, replica_groups=mesh['group'=2,'tensor'=16] {'tensor'}, use_global_device_ids=true, to_apply=%region_3.4 | all-reduce | flops 1536 | bytes 9216 | tf_op jit(solution)/shard_map/psum | solution.py:112
  158.2 0.1 copy.20
  158.3 1.8 %fusion.6 = f32[96,1,512]{2,1,0:T(1,128)S(1)} fusion(bf16[96,16,1]{1,2,0:T(2,128)(2,1)S(1)} %copy.20, bf16[96,16,512]{2,1,0:T(8,128)(2,1)} %gather_fusion, pred[96]{0:T(512)(128)(4,1)S(1)} %get-tuple-element.15), kind=kOutput, calls=%fused_computation.7 | convolution fusion | flops 2359296 | bytes 1772640 | tf_op jit(solution)/shard_map/rk,rkc->rc/dot_general | solution.py:114
  160.2 4.8 %fusion.16 = bf16[96,512]{1,0:T(8,128)(2,1)S(1)} fusion(bf16[96,8192]{1,0:T(8,128)(2,1)S(1)} %reshape.153, bf16[8192,512]{1,0:T(8,128)(2,1)} %param.19, f32[96,1,512]{2,1,0:T(1,128)S(1)} %fusion.6), kind=kOutput, calls=%fused_computation.15 | convolution fusion | flops 805404672 | bytes 10256384 | tf_op jit(solution)/shard_map/dot_general | solution.py:102
  165.1 10.5 %all_to_all.38 = bf16[16,6,512]{2,1,0:T(8,128)(2,1)S(1)} all-to-all(bf16[16,6,512]{2,1,0:T(8,128)(2,1)S(1)} %all_to_all.32), channel_id=1, replica_groups=mesh['group'=2,'tensor'=16] {'tensor'}, dimensions={0} | all-to-all | bytes 196608 | tf_op jit(solution)/shard_map/all_to_all | solution.py:116
  175.6 0.7 copy.52
  (14 shorter events, 0.2 us)
Async XLA Ops:
  6.5 88.0 %copy-start = (bf16[32,16,512]{2,1,0:T(8,128)(2,1)S(1)}, bf16[32,16,512]{2,1,0:T(8,128)(2,1)}, u32[]{:S(2)}) copy-start(bf16[32,16,512]{2,1,0:T(8,128)(2,1)} %param.21) | copy-start | bytes 1572868
  6.5 47.8 %all-gather.5.cloned.1.call-start = ((), (), s32[]{:S(2)}) async-start(), calls=%async_computation.2 | async-start | bytes 2228224 | tf_op jit(solution)/shard_map/all_gather | solution.py:57
  56.2 10.1 %copy-start.2 = (s32[6]{0:T(128)S(1)}, s32[6]{0:T(128)}, u32[]{:S(2)}) copy-start(s32[6]{0:T(128)} %param.17) | copy-start | bytes 76
  62.7 11.9 %all-to-all-start = ((bf16[16,6,640]{2,1,0:T(8,128)(2,1)}), bf16[16,6,640]{2,1,0:T(8,128)(2,1)S(1)}, u32[]{:S(2)}, u32[]{:S(2)}) async-start(bf16[16,6,640]{2,1,0:T(8,128)(2,1)} %all_to_all.28), calls=%async_computation | async-start | bytes 327680 | tf_op jit(solution)/shard_map/all_to_all | solution.py:63
  66.3 57.1 %all-gather.7.cloned.1.call-start = ((), (), s32[]{:S(2)}) async-start(), calls=%async_computation.3 | async-start | bytes 2228224 | tf_op jit(solution)/shard_map/all_gather | solution.py:99
  79.8 4.2 %copy-start.4 = (u32[32]{0:T(128)S(1)}, u32[32]{0:T(128)}, u32[]{:S(2)}) copy-start(u32[32]{0:T(128)} %constant.53) | copy-start | bytes 388
  79.9 5.6 %copy-start.3 = (s32[6]{0:T(128)S(1)}, s32[6]{0:T(128)}, u32[]{:S(2)}) copy-start(s32[6]{0:T(128)} %param.18) | copy-start | bytes 76
  96.5 28.8 %copy-start.1 = (bf16[2,8192,16]{1,2,0:T(8,128)(2,1)S(1)}, bf16[2,8192,16]{1,2,0:T(8,128)(2,1)}, u32[]{:S(2)}) copy-start(bf16[2,8192,16]{1,2,0:T(8,128)(2,1)} %param.20) | copy-start | bytes 1572868
Sparse Core Ops, SparseCore 0:
  10.2 44.0 all-gather.4
  84.2 39.1 all-gather.6
where the time goes:
time: 184 us; the launch traced here: 183 us
  waiting for transfers between devices  78 us (42%)
  blocking collectives  51.3 us (28%)
  matrix products  21.3 us (12%)
  between operations  14.3 us (8%)
  local copies, waits for them, and re-layouts  8.89 us (5%)
  other arithmetic  5.71 us (3%)
  starting transfers between devices  3.56 us (2%)
    all_gather x1, waiting for transfers between devices, per_device(): lax.all_gather(normed, 'tensor', axis=0, tiled=True)  42.8 us
    psum x1, blocking collectives, per_device(): shrunk = lax.psum(partial_coords, 'tensor').astype(jnp.bfloat16)  31.9 us
    all_gather x1, waiting for transfers between devices, per_device(): lax.all_gather(attn, 'tensor', axis=0, tiled=True)  26.9 us
    all_to_all x1, blocking collectives, per_device(): lax.all_to_all(proj_cols, 'tensor', split_axis=0, concat_axis=1, tiled=True)  10.5 us
    unnamed x1, blocking collectives  8.83 us
    all_to_all x1, waiting for transfers between devices, per_device(): lax.all_to_all(qkv_cols, 'tensor', split_axis=0, concat_axis=1, tiled=True)  8.23 us
    unnamed x18, local copies, waits for them, and re-layouts  6.1 us
    dot_general x1, matrix products, per_device(): jnp.dot(lax.all_gather(normed, 'tensor', axis=0, tiled=True), query_key_v...  5.81 us
  transfers between devices with their start and end apart: 3, of which 3 were waited for; matrix products, arithmetic and copies ran while one was open for 2% of the time, Pallas kernels for 0%

commit v1 on v0

v1 whole, which is shorter than its diff:
```python
import functools

import jax
import jax.numpy as jnp
from jax import lax
from jax.experimental import pallas as pl
from jax.experimental.pallas import tpu as pltpu
from jax.sharding import PartitionSpec as P

QUERY_HEADS = 64
KVH = 8
HEAD_SIZE = 128
ADAPTER_RANK = 16
GROUPS = QUERY_HEADS // KVH

EPS = 1e-06
ROPE_BASE = 1000000.0

BLOCKS = 8
LANES = 128
MIB = 1 << 20

VMEM = pl.BlockSpec(memory_space=pltpu.VMEM)
ANY = pl.BlockSpec(memory_space=pl.ANY)
SMEM = pl.BlockSpec(memory_space=pltpu.SMEM)


def params(mib):
    return pltpu.CompilerParams(vmem_limit_bytes=mib * MIB)


def factors(chips):
    inner = 1
    while inner * inner * 4 <= chips and chips % (inner * 2) == 0:
        inner *= 2
    return chips // inner, inner


def ring_order(chips):
    outer, inner = factors(chips)
    if inner < 2 or outer % 2:
        return list(range(chips))
    order = [a * inner for a in range(outer)]
    for turn, a in enumerate(reversed(range(outer))):
        steps = range(1, inner) if turn % 2 == 0 else range(inner - 1, 0, -1)
        order += [a * inner + b for b in steps]
    return order


def lookup(table, index):
    value = jnp.int32(table[0])
    for at in range(1, len(table)):
        value = jnp.where(index == at, jnp.int32(table[at]), value)
    return value


def slot_chips(devices, me):
    chips = devices // 2
    order = ring_order(chips)
    place_of = [order.index(chip) for chip in range(chips)]
    place = lookup(place_of, lax.div(me, 2))
    ahead = chips // 2
    shifts = [0] + [-j for j in range(1, ahead + 1)] + [j for j in range(1, chips - ahead)]
    return [lookup(order, lax.rem(place + shift + chips, chips)) for shift in shifts]


def gather_chunks(chunk, devices):
    chips = devices // 2
    order = ring_order(chips)
    ahead = chips // 2

    def ring(step):
        return [
            (2 * order[p] + core, 2 * order[(p + step) % chips] + core)
            for p in range(chips)
            for core in range(2)
        ]

    across = [(d, d ^ 1) for d in range(devices)]
    up, down = ring(1), ring(-1)
    from_behind, from_front = [chunk], [chunk]
    other = {("up", 0): lax.ppermute(chunk, "tensor", across)}
    for j in range(1, ahead + 1):
        from_behind.append(lax.ppermute(from_behind[-1], "tensor", up))
        if j < chips - ahead:
            from_front.append(lax.ppermute(from_front[-1], "tensor", down))
        other["up", j] = lax.ppermute(from_behind[j], "tensor", across)
        if j < chips - ahead:
            other["down", j] = lax.ppermute(from_front[j], "tensor", across)
    mine = from_behind + from_front[1:]
    theirs = [other["up", j] for j in range(ahead + 1)]
    theirs += [other["down", j] for j in range(1, chips - ahead)]
    return mine + theirs


def write_chunk(stage, ids_ref, rows, out_ref):
    width = stage.shape[1]
    for g in range(BLOCKS * rows // 8):
        out_ref[:, g * width : (g + 1) * width] = stage[8 * g : 8 * g + 8, :].astype(jnp.bfloat16)
    sub = lax.broadcasted_iota(jnp.int32, (8, LANES), 0)
    ids = jnp.zeros((8, LANES), jnp.float32)
    for r in range(rows):
        ids = jnp.where(sub == r, ids_ref[r].astype(jnp.float32), ids)
    out_ref[:, BLOCKS * rows // 8 * width :] = ids.astype(jnp.bfloat16)


def norm_kernel(ids_ref, x_ref, gain_ref, out_ref, stage):
    rows, width = x_ref.shape
    block = width // BLOCKS
    total = jnp.zeros((rows, LANES), jnp.float32)
    for c in range(width // LANES):
        x = x_ref[:, c * LANES : (c + 1) * LANES].astype(jnp.float32)
        total = total + x * x
    factor = lax.rsqrt(jnp.sum(total, axis=-1, keepdims=True) / width + EPS)
    for j in range(BLOCKS):
        cols = slice(j * block, (j + 1) * block)
        x = x_ref[:, cols].astype(jnp.float32)
        stage[j * rows : (j + 1) * rows, :] = x * factor * gain_ref[:, cols].astype(jnp.float32)
    write_chunk(stage, ids_ref, rows, out_ref)


def norm_chunk(hidden, gain, ids):
    rows, width = hidden.shape
    return pl.pallas_call(
        norm_kernel,
        out_shape=jax.ShapeDtypeStruct((8, rows * width // 8 + LANES), jnp.bfloat16),
        in_specs=[SMEM, VMEM, VMEM],
        out_specs=VMEM,
        scratch_shapes=[pltpu.VMEM((BLOCKS * rows, width // BLOCKS), jnp.float32)],
        compiler_params=params(16),
        name="norm_chunk",
    )(ids, hidden, gain.reshape(1, width))


def unpack(chunks, me, rows, stage, left):
    pairs = len(chunks) // 2
    block = stage.shape[-1]
    core = lax.rem(me, 2)
    for slot, chip in enumerate(slot_chips(2 * pairs, me)):
        turn = slot % stage.shape[0]
        for chunk, place in ((chunks[slot], core), (chunks[pairs + slot], 1 - core)):
            for g in range(BLOCKS * rows // 8):
                stage[turn, place, 8 * g : 8 * g + 8, :] = chunk[
                    :, g * block : (g + 1) * block
                ].astype(jnp.float32)
        at = pl.multiple_of(chip * 16, 16)
        for j in range(BLOCKS):
            both = [stage[turn, place, j * rows : j * rows + 8, :] for place in range(2)]
            left[j, pl.ds(at, 16), :] = jnp.concatenate(both, axis=0).astype(jnp.bfloat16)


def unpack_scratch(rows, block):
    return pltpu.VMEM((4, 2, BLOCKS * rows + 8, block), jnp.float32)


def fetch(weight, held, sems):
    block = held.shape[1]
    copies = [
        pltpu.make_async_copy(weight.at[pl.ds(j * block, block), :], held.at[j], sems.at[j])
        for j in range(BLOCKS)
    ]
    for copy in copies:
        copy.start()
    return copies


def qkv_kernel(devices, rows, *refs):
    me_ref, bias_ref, weight = refs[:3]
    chunks = refs[3 : 3 + devices]
    out_ref, held, sems, stage, left, acc = refs[3 + devices :]
    copies = fetch(weight, held, sems)
    unpack(chunks, me_ref[0], rows, stage, left)
    for j in range(BLOCKS):
        copies[j].wait()
        part = jnp.dot(left[j], held[j], preferred_element_type=jnp.float32)
        if j == 0:
            acc[...] = part + bias_ref[...].astype(jnp.float32)
        else:
            acc[...] += part
    for d in range(devices):
        out_ref[d] = acc[8 * d : 8 * d + rows, :].astype(jnp.bfloat16)


def qkv_project(me, chunks, weight, bias, rows):
    devices = len(chunks)
    width, cols = weight.shape
    block = width // BLOCKS
    return pl.pallas_call(
        functools.partial(qkv_kernel, devices, rows),
        out_shape=jax.ShapeDtypeStruct((devices, rows, cols), jnp.bfloat16),
        in_specs=[SMEM, VMEM, ANY] + [VMEM] * devices,
        out_specs=VMEM,
        scratch_shapes=[
            pltpu.VMEM((BLOCKS, block, cols), jnp.bfloat16),
            pltpu.SemaphoreType.DMA((BLOCKS,)),
            unpack_scratch(rows, block),
            pltpu.VMEM((BLOCKS, devices * 8, block), jnp.bfloat16),
            pltpu.VMEM((devices * 8, cols), jnp.float32),
        ],
        compiler_params=params(56 if devices > 16 else 32),
        cost_estimate=pl.CostEstimate(
            flops=2 * devices * rows * width * cols,
            bytes_accessed=width * cols * 2,
            transcendentals=0,
        ),
        name="qkv_project",
    )(me, bias.reshape(1, cols), weight, *chunks)


def attend_kernel(rows, len_ref, ids_ref, qkv_ref, cos_ref, sin_ref, k_ref, v_ref, out_ref, heads, mixed, stage):
    r = pl.program_id(0)
    total_heads = QUERY_HEADS + 2 * KVH
    half = HEAD_SIZE // 2

    @pl.when(r == 0)
    def _():
        for h in range(total_heads):
            tile = qkv_ref[:, h * HEAD_SIZE : (h + 1) * HEAD_SIZE].astype(jnp.float32)
            heads[pl.ds(h, rows, stride=total_heads), :] = tile

    base = pl.multiple_of(r * total_heads, 8)
    turned = heads[pl.ds(base, QUERY_HEADS + KVH), :]
    cosine = cos_ref[pl.ds(r, 1), :]
    sine = sin_ref[pl.ds(r, 1), :]
    turned = (turned * cosine + pltpu.roll(turned, half, 1) * sine).astype(jnp.bfloat16)
    query = turned[:QUERY_HEADS]
    query_f = query.astype(jnp.float32)
    new_key = turned[QUERY_HEADS:].astype(jnp.float32)
    new_value = heads[pl.ds(base + QUERY_HEADS + KVH, KVH), :]
    scale = 1.0 / HEAD_SIZE**0.5
    scores = []
    own = []
    for k in range(KVH):
        mine = slice(k * GROUPS, (k + 1) * GROUPS)
        keys = k_ref[0, :, k * HEAD_SIZE : (k + 1) * HEAD_SIZE]
        scores.append(
            lax.dot_general(
                query[mine], keys, (((1,), (1,)), ((), ())), preferred_element_type=jnp.float32
            )
        )
        own.append(jnp.sum(query_f[mine] * new_key[k : k + 1], axis=-1, keepdims=True))
    score = jnp.concatenate(scores, axis=0) * scale
    own = jnp.concatenate(own, axis=0) * scale
    valid = lax.broadcasted_iota(jnp.int32, score.shape, 1) < len_ref[r]
    top = jnp.maximum(jnp.max(jnp.where(valid, score, -1e30), axis=-1, keepdims=True), own)
    expo = jnp.where(valid, jnp.exp(score - top), 0.0)
    expo_own = jnp.exp(own - top)
    total = jnp.sum(expo, axis=-1, keepdims=True) + expo_own
    weight = (expo / total).astype(jnp.bfloat16)
    weight_own = (expo_own / total).astype(jnp.bfloat16).astype(jnp.float32)
    for k in range(KVH):
        mine = slice(k * GROUPS, (k + 1) * GROUPS)
        values = v_ref[0, :, k * HEAD_SIZE : (k + 1) * HEAD_SIZE]
        part = jnp.dot(weight[mine], values, preferred_element_type=jnp.float32)
        part = part + weight_own[mine] * new_value[k : k + 1]
        at = pl.multiple_of(r * QUERY_HEADS + k * GROUPS, 8)
        mixed[pl.ds(at, GROUPS), :] = part

    @pl.when(r == rows - 1)
    def _():
        per_block = QUERY_HEADS // BLOCKS
        for h in range(QUERY_HEADS):
            j, lane = h // per_block, h % per_block
            stage[j * rows : (j + 1) * rows, lane * HEAD_SIZE : (lane + 1) * HEAD_SIZE] = mixed[
                pl.ds(h, rows, stride=QUERY_HEADS), :
            ]
        write_chunk(stage, ids_ref, rows, out_ref)


def attend(lengths, ids, qkv, cosine, sine, keys, values):
    rows, capacity, width = keys.shape
    total_heads = QUERY_HEADS + 2 * KVH
    features = QUERY_HEADS * HEAD_SIZE
    cache = pl.BlockSpec((1, capacity, width), lambda r: (r, 0, 0))
    return pl.pallas_call(
        functools.partial(attend_kernel, rows),
        grid=(rows,),
        out_shape=jax.ShapeDtypeStruct((8, rows * features // 8 + LANES), jnp.bfloat16),
        in_specs=[SMEM, SMEM, VMEM, VMEM, VMEM, cache, cache],
        out_specs=VMEM,
        scratch_shapes=[
            pltpu.VMEM((rows * total_heads, HEAD_SIZE), jnp.float32),
            pltpu.VMEM((rows * QUERY_HEADS, HEAD_SIZE), jnp.float32),
            pltpu.VMEM((BLOCKS * rows, features // BLOCKS), jnp.float32),
        ],
        compiler_params=params(24),
        name="attend",
    )(lengths, ids, qkv, cosine, sine, keys, values)


def shrink_kernel(devices, rows, *refs):
    me_ref, down_ref = refs[:2]
    chunks = refs[2 : 2 + devices]
    left, coords_ref, stage, ids, total = refs[2 + devices :]
    me = me_ref[0]
    stored, rank, features = down_ref.shape
    block = features // BLOCKS
    unpack(chunks, me, rows, stage, left)
    for s in range(stored):
        for j in range(BLOCKS):
            part = lax.dot_general(
                down_ref[s, :, j * block : (j + 1) * block],
                left[j],
                (((1,), (1,)), ((), ())),
                preferred_element_type=jnp.float32,
            )
            if j == 0:
                total[s * rank : (s + 1) * rank, :] = part
            else:
                total[s * rank : (s + 1) * rank, :] += part
    core = lax.rem(me, 2)
    pairs = devices // 2
    for slot, chip in enumerate(slot_chips(devices, me)):
        for chunk, place in ((chunks[slot], core), (chunks[pairs + slot], 1 - core)):
            at = pl.multiple_of((2 * chip + place) * 8, 8)
            ids[pl.ds(at, 8), :] = chunk[:, features * rows // 8 :].astype(jnp.float32)
    row_ids = jnp.transpose(ids[...])[: stored * rank, :].astype(jnp.int32)
    adapter = lax.broadcasted_iota(jnp.int32, total.shape, 0) // rank + me * stored
    coords = jnp.where(row_ids == adapter, total[...], 0.0).astype(jnp.bfloat16)
    for d in range(devices):
        coords_ref[d] = coords


def shrink(me, chunks, down, rows):
    devices = len(chunks)
    stored, rank, features = down.shape
    block = features // BLOCKS
    return pl.pallas_call(
        functools.partial(shrink_kernel, devices, rows),
        out_shape=(
            jax.ShapeDtypeStruct((BLOCKS, devices * 8, block), jnp.bfloat16),
            jax.ShapeDtypeStruct((devices, stored * rank, devices * 8), jnp.bfloat16),
        ),
        in_specs=[SMEM, VMEM] + [VMEM] * devices,
        out_specs=(VMEM, VMEM),
        scratch_shapes=[
            unpack_scratch(rows, block),
            pltpu.VMEM((devices * 8, LANES), jnp.float32),
            pltpu.VMEM((stored * rank, devices * 8), jnp.float32),
        ],
        compiler_params=params(56 if devices > 16 else 24),
        name="shrink",
    )(me, down, *chunks)


def base_kernel(left, weight, out_ref, held, sems):
    copies = fetch(weight, held, sems)
    for j in range(BLOCKS):
        copies[j].wait()
        part = jnp.dot(left[j], held[j], preferred_element_type=jnp.float32)
        if j == 0:
            out_ref[...] = part
        else:
            out_ref[...] += part


def base_project(left, weight):
    width, cols = weight.shape
    block = width // BLOCKS
    rows = left.shape[1]
    return pl.pallas_call(
        base_kernel,
        out_shape=jax.ShapeDtypeStruct((rows, cols), jnp.float32),
        in_specs=[VMEM, ANY],
        out_specs=VMEM,
        scratch_shapes=[
            pltpu.VMEM((BLOCKS, block, cols), jnp.bfloat16),
            pltpu.SemaphoreType.DMA((BLOCKS,)),
        ],
        compiler_params=params(32),
        cost_estimate=pl.CostEstimate(
            flops=2 * rows * width * cols, bytes_accessed=width * cols * 2, transcendentals=0
        ),
        name="base_project",
    )(left, weight)


def add_kernel(rows, base_ref, coords_ref, up_ref, out_ref):
    delta = lax.dot_general(
        coords_ref[...], up_ref[...], (((0,), (0,)), ((), ())), preferred_element_type=jnp.float32
    )
    projected = base_ref[...] + delta
    for d in range(out_ref.shape[0]):
        out_ref[d] = projected[8 * d : 8 * d + rows, :].astype(jnp.bfloat16)


def add_delta(base, coords, up, rows):
    return pl.pallas_call(
        functools.partial(add_kernel, rows),
        out_shape=jax.ShapeDtypeStruct((base.shape[0] // 8, rows, base.shape[1]), jnp.bfloat16),
        in_specs=[VMEM, VMEM, VMEM],
        out_specs=VMEM,
        compiler_params=params(40),
        name="add_delta",
    )(base, coords, up)


def exchange(parts):
    return lax.all_to_all(parts, "tensor", split_axis=0, concat_axis=0, tiled=True)


def per_row(parts):
    devices, rows, cols = parts.shape
    return jnp.transpose(parts, (1, 0, 2)).reshape(rows, devices * cols)


def per_device(
    devices,
    hidden,
    input_norm_scale,
    query_key_value_weight,
    projection_bias,
    rotated_key_cache,
    past_value_cache,
    lengths,
    row_adapter_index,
    output_weight,
    adapter_down_weight,
    adapter_up_weight,
):
    rows = hidden.shape[0]
    me = lax.axis_index("tensor").astype(jnp.int32).reshape(1)
    half = HEAD_SIZE // 2
    inv = ROPE_BASE ** (-(jnp.arange(half, dtype=jnp.float32) * 2.0 / HEAD_SIZE))
    angle = lengths.astype(jnp.float32)[:, None] * inv[None, :]
    cosine, sine = jnp.cos(angle), jnp.sin(angle)
    cosine = jnp.concatenate([cosine, cosine], axis=1)
    sine = jnp.concatenate([-sine, sine], axis=1)
    down = jnp.transpose(adapter_down_weight, (0, 2, 1))
    up = adapter_up_weight.reshape(-1, adapter_up_weight.shape[2])

    chunk = norm_chunk(hidden, input_norm_scale, row_adapter_index)
    chunks = gather_chunks(chunk, devices)
    qkv = qkv_project(me, chunks, query_key_value_weight, projection_bias, rows)
    qkv = per_row(exchange(qkv))
    chunk = attend(
        lengths, row_adapter_index, qkv, cosine, sine, rotated_key_cache, past_value_cache
    )
    chunks = gather_chunks(chunk, devices)
    left, coords = shrink(me, chunks, down, rows)
    coords = exchange(coords)
    base = base_project(left, output_weight)
    coords = coords.reshape(-1, coords.shape[2])
    return per_row(exchange(add_delta(base, coords, up, rows)))


def solution(mesh):
    in_specs = (
        P(("group", "tensor"), None),
        P(),
        P(None, "tensor"),
        P("tensor"),
        P(("group", "tensor"), None, None),
        P(("group", "tensor"), None, None),
        P(("group", "tensor")),
        P(("group", "tensor")),
        P(None, "tensor"),
        P("tensor", None, None),
        P(None, None, "tensor"),
    )
    out_specs = P(("group", "tensor"), None)
    return jax.shard_map(
        functools.partial(per_device, mesh.shape["tensor"]),
        mesh=mesh,
        in_specs=in_specs,
        out_specs=out_specs,
        check_vma=False,
    )
```

time: 184 us -> 107 us (0.58)
  waiting for transfers between devices: 78 us -> 32.6 us
  blocking collectives: 51.3 us -> 11.6 us
  starting transfers between devices: 3.56 us -> 27.5 us
  matrix products: 21.3 us -> 0 us
  Pallas kernels: 0 us -> 17.6 us
  between operations: 14.3 us -> 0.18 us
  local copies, waits for them, and re-layouts: 8.89 us -> 15.7 us
  other arithmetic: 5.71 us -> 0.85 us
    all_gather x2 -> x0, waiting for transfers between devices: 69.7 us -> none  [the longest x1 42.8 us: per_device(): lax.all_gather(normed, 'tensor', axis=0, tiled=True)]
    psum x1 -> x0, blocking collectives: 31.9 us -> none  [per_device(): shrunk = lax.psum(partial_coords, 'tensor').astype(jnp.bfloat16)]
    ppermute x0 -> x30, waiting for transfers between devices: none -> 22.2 us  [the longest x8 19.1 us: gather_chunks(): from_behind.append(lax.ppermute(from_behind[-1], 'tensor', up))]
    dot_general x8 -> x0, matrix products: 21.3 us -> none  [the longest x1 5.81 us: per_device(): jnp.dot(lax.all_gather(normed, 'tensor', axis=0, tiled=True), query_key_v...]
    ppermute x0 -> x30, starting transfers between devices: none -> 17.7 us  [the longest x8 8.96 us: gather_chunks(): from_behind.append(lax.ppermute(from_behind[-1], 'tensor', up))]
    pallas_call x0 -> x6, Pallas kernels: none -> 17.6 us  [the longest x1 6.16 us: attend(): pl.pallas_call(functools.partial(attend_kernel, rows), grid=(rows,), out_...]
    unnamed x1 -> x0, blocking collectives: 8.83 us -> none
    unnamed x18 -> x21, local copies, waits for them, and re-layouts: 6.1 us -> 14.3 us
  transfers between devices with their start and end apart: 3 -> 32, of which waited for: 3 -> 14; matrix products, arithmetic and copies ran while one was open for 2% -> 1% of each run, Pallas kernels for 0% -> 2%
where the time goes in v1:
time: 107 us; the launch traced here: 106 us
  waiting for transfers between devices  32.6 us (30%)
  starting transfers between devices  27.5 us (26%)
  Pallas kernels  17.6 us (16%)
  local copies, waits for them, and re-layouts  15.7 us (15%)
  blocking collectives  11.6 us (11%)
    ppermute x8, waiting for transfers between devices, gather_chunks(): from_behind.append(lax.ppermute(from_behind[-1], 'tensor', up))  19.1 us
    unnamed x21, local copies, waits for them, and re-layouts  14.3 us
    all_to_all x1, blocking collectives, exchange(): lax.all_to_all(parts, 'tensor', split_axis=0, concat_axis=0, tiled=True)  11.6 us
    all_to_all x2, waiting for transfers between devices, exchange(): lax.all_to_all(parts, 'tensor', split_axis=0, concat_axis=0, tiled=True)  10.4 us
    all_to_all x2, starting transfers between devices, exchange(): lax.all_to_all(parts, 'tensor', split_axis=0, concat_axis=0, tiled=True)  9.75 us
    ppermute x8, starting transfers between devices, gather_chunks(): from_behind.append(lax.ppermute(from_behind[-1], 'tensor', up))  8.96 us
    ppermute x6, starting transfers between devices, gather_chunks(): from_front.append(lax.ppermute(from_front[-1], 'tensor', down))  6.16 us
    pallas_call x1, Pallas kernels, attend(): pl.pallas_call(functools.partial(attend_kernel, rows), grid=(rows,), out_...  6.16 us
  transfers between devices with their start and end apart: 32, of which 14 were waited for; matrix products, arithmetic and copies ran while one was open for 1% of the time, Pallas kernels for 2%

profile of v1, /device:TPU:0, one launch (start us, length us, event | category | flops | bytes accessed | tf_op | source)
XLA Modules:
  0.0 106.0 jit_solution(10237015219666367823)
XLA Ops:
  0.0 0.7 reshape.30.gain_ref
  0.7 0.0 copy-start.6
  0.8 0.9 copy-done.6
  1.6 0.7 copy-done.7
  2.3 0.7 norm_chunk.1.refs_3_
  3.0 3.1 %collective-permute-start = (bf16[8,6272]{1,0:T(8,128)(2,1)S(1)}, bf16[8,6272]{1,0:T(8,128)(2,1)S(1)}, u32[]{:S(2)}, u32[]{:S(2)}) collective-permute-start(bf16[8,6272]{1,0:T(8,128)(2,1)S(1)} %norm_chunk.1.refs_3_), channel_id=1, source_target_pairs={{0,4},{1,5},{4,8},{5,9},{8,12},{9,13},{12,14},{13,15},{14,10},{15,... | collective-permute-start | bytes 301064 | tf_op jit(solution)/shard_map/ppermute | solution.py:84
  6.1 0.0 collective-permute-start.4
  6.1 2.8 %collective-permute-done.refs_4_ = bf16[8,6272]{1,0:T(8,128)(2,1)S(1)} collective-permute-done((bf16[8,6272]{1,0:T(8,128)(2,1)S(1)}, bf16[8,6272]{1,0:T(8,128)(2,1)S(1)}, u32[]{:S(2)}, u32[]{:S(2)}) %collective-permute-start) | collective-permute-done | bytes 100384 | tf_op jit(solution)/shard_map/ppermute | solution.py:84
  8.9 1.9 %collective-permute-start.1 = (bf16[8,6272]{1,0:T(8,128)(2,1)S(1)}, bf16[8,6272]{1,0:T(8,128)(2,1)S(1)}, u32[]{:S(2)}, u32[]{:S(2)}) collective-permute-start(bf16[8,6272]{1,0:T(8,128)(2,1)S(1)} %collective-permute-done.refs_4_), channel_id=1, source_target_pairs={{0,4},{1,5},{4,8},{5,9},{8,12},{9,13},{12,14},{13,15},{14,10},{15,... | collective-permute-start | bytes 301064 | tf_op jit(solution)/shard_map/ppermute | solution.py:84
  10.8 0.0 collective-permute-done.4.refs_8_
  10.8 0.2 collective-permute-start.5
  10.9 2.6 %collective-permute-done.1.refs_5_ = bf16[8,6272]{1,0:T(8,128)(2,1)S(1)} collective-permute-done((bf16[8,6272]{1,0:T(8,128)(2,1)S(1)}, bf16[8,6272]{1,0:T(8,128)(2,1)S(1)}, u32[]{:S(2)}, u32[]{:S(2)}) %collective-permute-start.1) | collective-permute-done | bytes 100384 | tf_op jit(solution)/shard_map/ppermute | solution.py:84
  13.5 1.9 %collective-permute-start.2 = (bf16[8,6272]{1,0:T(8,128)(2,1)S(1)}, bf16[8,6272]{1,0:T(8,128)(2,1)S(1)}, u32[]{:S(2)}, u32[]{:S(2)}) collective-permute-start(bf16[8,6272]{1,0:T(8,128)(2,1)S(1)} %collective-permute-done.1.refs_5_), channel_id=1, source_target_pairs={{0,4},{1,5},{4,8},{5,9},{8,12},{9,13},{12,14},{13,15},{14,10},{15,... | collective-permute-start | bytes 301064 | tf_op jit(solution)/shard_map/ppermute | solution.py:84
  15.4 0.5 collective-permute-start.12
  15.9 0.0 collective-permute-start.8
  15.9 0.0 collective-permute-done.5.refs_9_
  15.9 0.2 collective-permute-start.6
  16.1 2.1 %collective-permute-done.2.refs_6_ = bf16[8,6272]{1,0:T(8,128)(2,1)S(1)} collective-permute-done((bf16[8,6272]{1,0:T(8,128)(2,1)S(1)}, bf16[8,6272]{1,0:T(8,128)(2,1)S(1)}, u32[]{:S(2)}, u32[]{:S(2)}) %collective-permute-start.2) | collective-permute-done | bytes 100384 | tf_op jit(solution)/shard_map/ppermute | solution.py:84
  18.2 1.9 %collective-permute-start.3 = (bf16[8,6272]{1,0:T(8,128)(2,1)S(1)}, bf16[8,6272]{1,0:T(8,128)(2,1)S(1)}, u32[]{:S(2)}, u32[]{:S(2)}) collective-permute-start(bf16[8,6272]{1,0:T(8,128)(2,1)S(1)} %collective-permute-done.2.refs_6_), channel_id=1, source_target_pairs={{0,4},{1,5},{4,8},{5,9},{8,12},{9,13},{12,14},{13,15},{14,10},{15,... | collective-permute-start | bytes 301064 | tf_op jit(solution)/shard_map/ppermute | solution.py:84
  20.0 0.7 convert_element_type.3
  20.7 0.7 reshape.29.refs_1_
  21.4 0.0 collective-permute-done.12.refs_16_
  21.4 0.5 collective-permute-start.9
  21.9 0.1 collective-permute-start.10
  22.0 0.0 collective-permute-done.6.refs_10_
  22.0 0.4 collective-permute-start.14
  22.4 0.4 collective-permute-done.3.refs_7_
  22.8 0.0 collective-permute-start.11
  22.8 0.5 collective-permute-done.14.refs_18_
  23.4 0.8 collective-permute-done.11.refs_15_
  24.1 4.0 %copy-done = bf16[8192,640]{1,0:T(8,128)(2,1)S(1)} copy-done((bf16[8192,640]{1,0:T(8,128)(2,1)S(1)}, bf16[8192,640]{1,0:T(8,128)(2,1)}, u32[]{:S(2)}) %copy-start) | copy-done | bytes 10485784
  28.1 5.5 %qkv_project.1 = bf16[16,6,640]{2,1,0:T(8,128)(2,1)} custom-call(s32[1]{0:T(128)} %bitcast.refs_0_, bf16[1,640]{1,0:T(2,128)(2,1)S(1)} %reshape.29.refs_1_, bf16[8192,640]{1,0:T(8,128)(2,1)S(1)} %copy-done, bf16[8,6272]{1,0:T(8,128)(2,1)S(1)} %norm_chunk.1.refs_3_, bf16[8,6272]{1,0:T(8,128)(2,1)S(1)} %collective-permute-done.refs_4_, ...), custom_call_target="tpu_custom_call" | custom-call | flops 1006632960 | bytes 10485760 | tf_op jit(solution)/shard_map/qkv_project/pallas_call | solution.py:188
  33.6 6.2 %all-to-all-start = ((bf16[16,6,640]{2,1,0:T(8,128)(2,1)}), bf16[16,6,640]{2,1,0:T(8,128)(2,1)S(1)}, u32[]{:S(2)}, u32[]{:S(2)}) async-start(bf16[16,6,640]{2,1,0:T(8,128)(2,1)} %qkv_project.1), calls=%async_computation | async-start | bytes 327680 | tf_op jit(solution)/shard_map/all_to_all | solution.py:399
  39.9 0.1 fusion
  40.0 0.1 pad_maximum_fusion
  40.1 8.3 %all-to-all-done = bf16[16,6,640]{2,1,0:T(8,128)(2,1)S(1)} async-done(((bf16[16,6,640]{2,1,0:T(8,128)(2,1)}), bf16[16,6,640]{2,1,0:T(8,128)(2,1)S(1)}, u32[]{:S(2)}, u32[]{:S(2)}) %all-to-all-start) | async-done | bytes 122912 | tf_op jit(solution)/shard_map/all_to_all | solution.py:399
  48.3 2.3 %copy-done.2 = bf16[6,384,1024]{2,1,0:T(8,128)(2,1)S(1)} copy-done((bf16[6,384,1024]{2,1,0:T(8,128)(2,1)S(1)}, bf16[6,384,1024]{2,1,0:T(8,128)(2,1)}, u32[]{:S(2)}) %copy-start.2) | copy-done | bytes 4718616
  50.7 2.3 %copy-done.3 = bf16[6,384,1024]{2,1,0:T(8,128)(2,1)S(1)} copy-done((bf16[6,384,1024]{2,1,0:T(8,128)(2,1)S(1)}, bf16[6,384,1024]{2,1,0:T(8,128)(2,1)}, u32[]{:S(2)}) %copy-start.3) | copy-done | bytes 4718616
  53.0 6.2 %attend.1.refs_2_ = bf16[8,6272]{1,0:T(8,128)(2,1)S(1)} custom-call(s32[6]{0:T(128)S(1)} %copy-done.9, s32[6]{0:T(128)S(1)} %copy-done.8, bf16[6,10240]{1,0:T(8,128)(2,1)S(1)} %bitcast.10, f32[6,128]{1,0:T(8,128)S(1)} %get-tuple-element.12.cos_ref, f32[6,128]{1,0:T(8,128)S(1)} %get-tuple-element.13.sin_ref, bf16[6,384,1024]{2,1,0:T(8,128)(2,1)S(1)} %copy-done.2, ...), custom_call_target="tpu_custom_call" | custom-call | tf_op jit(solution)/shard_map/attend/pallas_call | solution.py:275
  59.2 0.1 collective-permute-start.15
  59.3 2.0 %collective-permute-start.19 = (bf16[8,6272]{1,0:T(8,128)(2,1)S(1)}, bf16[8,6272]{1,0:T(8,128)(2,1)S(1)}, u32[]{:S(2)}, u32[]{:S(2)}) collective-permute-start(bf16[8,6272]{1,0:T(8,128)(2,1)S(1)} %attend.1.refs_2_), channel_id=1, source_target_pairs={{0,2},{1,3},{4,0},{5,1},{8,4},{9,5},{12,8},{13,9},{14,12},{15,13},... | collective-permute-start | bytes 301064 | tf_op jit(solution)/shard_map/ppermute | solution.py:86
  61.3 2.6 %collective-permute-done.15.refs_3_ = bf16[8,6272]{1,0:T(8,128)(2,1)S(1)} collective-permute-done((bf16[8,6272]{1,0:T(8,128)(2,1)S(1)}, bf16[8,6272]{1,0:T(8,128)(2,1)S(1)}, u32[]{:S(2)}, u32[]{:S(2)}) %collective-permute-start.15) | collective-permute-done | bytes 100384 | tf_op jit(solution)/shard_map/ppermute | solution.py:84
  63.9 0.2 collective-permute-start.16
  64.1 1.8 %collective-permute-start.20 = (bf16[8,6272]{1,0:T(8,128)(2,1)S(1)}, bf16[8,6272]{1,0:T(8,128)(2,1)S(1)}, u32[]{:S(2)}, u32[]{:S(2)}) collective-permute-start(bf16[8,6272]{1,0:T(8,128)(2,1)S(1)} %collective-permute-done.19.refs_7_), channel_id=1, source_target_pairs={{0,2},{1,3},{4,0},{5,1},{8,4},{9,5},{12,8},{13,9},{14,12},{15,13},... | collective-permute-start | bytes 301064 | tf_op jit(solution)/shard_map/ppermute | solution.py:86
  65.9 3.0 %collective-permute-done.16.refs_4_ = bf16[8,6272]{1,0:T(8,128)(2,1)S(1)} collective-permute-done((bf16[8,6272]{1,0:T(8,128)(2,1)S(1)}, bf16[8,6272]{1,0:T(8,128)(2,1)S(1)}, u32[]{:S(2)}, u32[]{:S(2)}) %collective-permute-start.16) | collective-permute-done | bytes 100384 | tf_op jit(solution)/shard_map/ppermute | solution.py:84
  68.9 0.5 collective-permute-start.27
  69.4 0.0 collective-permute-start.23
  69.4 2.0 %collective-permute-start.21 = (bf16[8,6272]{1,0:T(8,128)(2,1)S(1)}, bf16[8,6272]{1,0:T(8,128)(2,1)S(1)}, u32[]{:S(2)}, u32[]{:S(2)}) collective-permute-start(bf16[8,6272]{1,0:T(8,128)(2,1)S(1)} %collective-permute-done.20.refs_8_), channel_id=1, source_target_pairs={{0,2},{1,3},{4,0},{5,1},{8,4},{9,5},{12,8},{13,9},{14,12},{15,13},... | collective-permute-start | bytes 301064 | tf_op jit(solution)/shard_map/ppermute | solution.py:86
  71.5 2.1 %collective-permute-done.17.refs_5_ = bf16[8,6272]{1,0:T(8,128)(2,1)S(1)} collective-permute-done((bf16[8,6272]{1,0:T(8,128)(2,1)S(1)}, bf16[8,6272]{1,0:T(8,128)(2,1)S(1)}, u32[]{:S(2)}, u32[]{:S(2)}) %collective-permute-start.17) | collective-permute-done | bytes 100384 | tf_op jit(solution)/shard_map/ppermute | solution.py:84
  73.6 0.0 collective-permute-start.18
  73.6 0.5 collective-permute-start.24
  74.1 0.1 collective-permute-start.25
  74.2 0.5 collective-permute-done.21.refs_9_
  74.7 3.5 %collective-permute-done.18.refs_6_ = bf16[8,6272]{1,0:T(8,128)(2,1)S(1)} collective-permute-done((bf16[8,6272]{1,0:T(8,128)(2,1)S(1)}, bf16[8,6272]{1,0:T(8,128)(2,1)S(1)}, u32[]{:S(2)}, u32[]{:S(2)}) %collective-permute-start.18) | collective-permute-done | bytes 100384 | tf_op jit(solution)/shard_map/ppermute | solution.py:84
  78.2 1.3 %collective-permute-done.26.refs_14_ = bf16[8,6272]{1,0:T(8,128)(2,1)S(1)} collective-permute-done((bf16[8,6272]{1,0:T(8,128)(2,1)S(1)}, bf16[8,6272]{1,0:T(8,128)(2,1)S(1)}, u32[]{:S(2)}, u32[]{:S(2)}) %collective-permute-start.26) | collective-permute-done | bytes 100384 | tf_op jit(solution)/shard_map/ppermute | solution.py:87
  79.5 2.6 %shrink.1 = (bf16[8,128,1024]{2,1,0:T(8,128)(2,1)S(1)}, bf16[16,32,128]{2,1,0:T(8,128)(2,1)}) custom-call(s32[1]{0:T(128)} %bitcast.refs_0_, bf16[2,16,8192]{2,1,0:T(8,128)(2,1)S(1)} %bitcast.11, bf16[8,6272]{1,0:T(8,128)(2,1)S(1)} %attend.1.refs_2_, bf16[8,6272]{1,0:T(8,128)(2,1)S(1)} %collective-permute-done.15.refs_3_, ...), custom_call_target="tpu_custom_call" | custom-call | tf_op jit(solution)/shard_map/shrink/pallas_call | solution.py:328
  82.1 3.5 %all-to-all-start.1 = ((bf16[16,32,128]{2,1,0:T(8,128)(2,1)}), bf16[16,32,128]{2,1,0:T(8,128)(2,1)S(1)}, u32[]{:S(2)}, u32[]{:S(2)}) async-start(bf16[16,32,128]{2,1,0:T(8,128)(2,1)} %get-tuple-element.8), calls=%async_computation.1 | async-start | bytes 262144 | tf_op jit(solution)/shard_map/all_to_all | solution.py:399
  85.6 0.0 copy-start.1
  85.6 3.4 %copy-done.1 = bf16[8192,512]{1,0:T(8,128)(2,1)S(1)} copy-done((bf16[8192,512]{1,0:T(8,128)(2,1)S(1)}, bf16[8192,512]{1,0:T(8,128)(2,1)}, u32[]{:S(2)}) %copy-start.1) | copy-done | bytes 8388632
  89.0 2.4 %base_project.1.base_ref = f32[128,512]{1,0:T(8,128)S(1)} custom-call(bf16[8,128,1024]{2,1,0:T(8,128)(2,1)S(1)} %get-tuple-element.7.left, bf16[8192,512]{1,0:T(8,128)(2,1)S(1)} %copy-done.1), custom_call_target="tpu_custom_call" | custom-call | flops 1073741824 | bytes 8388608 | tf_op jit(solution)/shard_map/base_project/pallas_call | solution.py:361
  91.4 2.1 %all-to-all-done.1 = bf16[16,32,128]{2,1,0:T(8,128)(2,1)S(1)} async-done(((bf16[16,32,128]{2,1,0:T(8,128)(2,1)}), bf16[16,32,128]{2,1,0:T(8,128)(2,1)S(1)}, u32[]{:S(2)}, u32[]{:S(2)}) %all-to-all-start.1) | async-done | bytes 131104 | tf_op jit(solution)/shard_map/all_to_all | solution.py:399
  93.5 0.3 add_delta.1
  93.8 11.6 %all_to_all.15 = bf16[16,6,512]{2,1,0:T(8,128)(2,1)S(1)} all-to-all(bf16[16,6,512]{2,1,0:T(8,128)(2,1)S(1)} %add_delta.1), channel_id=1, replica_groups=mesh['group'=2,'tensor'=16] {'tensor'}, dimensions={0} | all-to-all | bytes 196608 | tf_op jit(solution)/shard_map/all_to_all | solution.py:399
  105.4 0.7 copy.13
  (34 shorter events, 0.1 us)
Async XLA Ops:
  0.7 0.9 copy-start.6
  1.6 0.7 copy-start.7
  3.0 5.9 %collective-permute-start = (bf16[8,6272]{1,0:T(8,128)(2,1)S(1)}, bf16[8,6272]{1,0:T(8,128)(2,1)S(1)}, u32[]{:S(2)}, u32[]{:S(2)}) collective-permute-start(bf16[8,6272]{1,0:T(8,128)(2,1)S(1)} %norm_chunk.1.refs_3_), channel_id=1, source_target_pairs={{0,4},{1,5},{4,8},{5,9},{8,12},{9,13},{12,14},{13,15},{14,10},{15,... | collective-permute-start | bytes 301064 | tf_op jit(solution)/shard_map/ppermute | solution.py:84
  6.1 4.6 %collective-permute-start.4 = (bf16[8,6272]{1,0:T(8,128)(2,1)S(1)}, bf16[8,6272]{1,0:T(8,128)(2,1)S(1)}, u32[]{:S(2)}, u32[]{:S(2)}) collective-permute-start(bf16[8,6272]{1,0:T(8,128)(2,1)S(1)} %norm_chunk.1.refs_3_), channel_id=1, source_target_pairs={{0,2},{1,3},{4,0},{5,1},{8,4},{9,5},{12,8},{13,9},{14,12},{15,13},... | collective-permute-start | bytes 301064 | tf_op jit(solution)/shard_map/ppermute | solution.py:86
  8.9 4.6 %collective-permute-start.1 = (bf16[8,6272]{1,0:T(8,128)(2,1)S(1)}, bf16[8,6272]{1,0:T(8,128)(2,1)S(1)}, u32[]{:S(2)}, u32[]{:S(2)}) collective-permute-start(bf16[8,6272]{1,0:T(8,128)(2,1)S(1)} %collective-permute-done.refs_4_), channel_id=1, source_target_pairs={{0,4},{1,5},{4,8},{5,9},{8,12},{9,13},{12,14},{13,15},{14,10},{15,... | collective-permute-start | bytes 301064 | tf_op jit(solution)/shard_map/ppermute | solution.py:84
  10.8 5.2 %collective-permute-start.5 = (bf16[8,6272]{1,0:T(8,128)(2,1)S(1)}, bf16[8,6272]{1,0:T(8,128)(2,1)S(1)}, u32[]{:S(2)}, u32[]{:S(2)}) collective-permute-start(bf16[8,6272]{1,0:T(8,128)(2,1)S(1)} %collective-permute-done.4.refs_8_), channel_id=1, source_target_pairs={{0,2},{1,3},{4,0},{5,1},{8,4},{9,5},{12,8},{13,9},{14,12},{15,13},... | collective-permute-start | bytes 301064 | tf_op jit(solution)/shard_map/ppermute | solution.py:86
  13.5 4.6 %collective-permute-start.2 = (bf16[8,6272]{1,0:T(8,128)(2,1)S(1)}, bf16[8,6272]{1,0:T(8,128)(2,1)S(1)}, u32[]{:S(2)}, u32[]{:S(2)}) collective-permute-start(bf16[8,6272]{1,0:T(8,128)(2,1)S(1)} %collective-permute-done.1.refs_5_), channel_id=1, source_target_pairs={{0,4},{1,5},{4,8},{5,9},{8,12},{9,13},{12,14},{13,15},{14,10},{15,... | collective-permute-start | bytes 301064 | tf_op jit(solution)/shard_map/ppermute | solution.py:84
  15.4 6.0 %collective-permute-start.7 = (bf16[8,6272]{1,0:T(8,128)(2,1)S(1)}, bf16[8,6272]{1,0:T(8,128)(2,1)S(1)}, u32[]{:S(2)}, u32[]{:S(2)}) collective-permute-start(bf16[8,6272]{1,0:T(8,128)(2,1)S(1)} %norm_chunk.1.refs_3_), channel_id=1, source_target_pairs={{0,1},{1,0},{2,3},{3,2},{4,5},{5,4},{6,7},{7,6},{8,9},{9,8},{10,11... | collective-permute-start | bytes 301064 | tf_op jit(solution)/shard_map/ppermute | solution.py:82
  15.4 6.0 %collective-permute-start.12 = (bf16[8,6272]{1,0:T(8,128)(2,1)S(1)}, bf16[8,6272]{1,0:T(8,128)(2,1)S(1)}, u32[]{:S(2)}, u32[]{:S(2)}) collective-permute-start(bf16[8,6272]{1,0:T(8,128)(2,1)S(1)} %collective-permute-done.4.refs_8_), channel_id=1, source_target_pairs={{0,1},{1,0},{2,3},{3,2},{4,5},{5,4},{6,7},{7,6},{8,9},{9,8},{10,11... | collective-permute-start | bytes 301064 | tf_op jit(solution)/shard_map/ppermute | solution.py:89
  15.9 6.0 %collective-permute-start.8 = (bf16[8,6272]{1,0:T(8,128)(2,1)S(1)}, bf16[8,6272]{1,0:T(8,128)(2,1)S(1)}, u32[]{:S(2)}, u32[]{:S(2)}) collective-permute-start(bf16[8,6272]{1,0:T(8,128)(2,1)S(1)} %collective-permute-done.refs_4_), channel_id=1, source_target_pairs={{0,1},{1,0},{2,3},{3,2},{4,5},{5,4},{6,7},{7,6},{8,9},{9,8},{10,11... | collective-permute-start | bytes 301064 | tf_op jit(solution)/shard_map/ppermute | solution.py:87
  15.9 6.1 %collective-permute-start.6 = (bf16[8,6272]{1,0:T(8,128)(2,1)S(1)}, bf16[8,6272]{1,0:T(8,128)(2,1)S(1)}, u32[]{:S(2)}, u32[]{:S(2)}) collective-permute-start(bf16[8,6272]{1,0:T(8,128)(2,1)S(1)} %collective-permute-done.5.refs_9_), channel_id=1, source_target_pairs={{0,2},{1,3},{4,0},{5,1},{8,4},{9,5},{12,8},{13,9},{14,12},{15,13},... | collective-permute-start | bytes 301064 | tf_op jit(solution)/shard_map/ppermute | solution.py:86
  18.2 4.6 %collective-permute-start.3 = (bf16[8,6272]{1,0:T(8,128)(2,1)S(1)}, bf16[8,6272]{1,0:T(8,128)(2,1)S(1)}, u32[]{:S(2)}, u32[]{:S(2)}) collective-permute-start(bf16[8,6272]{1,0:T(8,128)(2,1)S(1)} %collective-permute-done.2.refs_6_), channel_id=1, source_target_pairs={{0,4},{1,5},{4,8},{5,9},{8,12},{9,13},{12,14},{13,15},{14,10},{15,... | collective-permute-start | bytes 301064 | tf_op jit(solution)/shard_map/ppermute | solution.py:84
  21.4 1.5 %collective-permute-start.13 = (bf16[8,6272]{1,0:T(8,128)(2,1)S(1)}, bf16[8,6272]{1,0:T(8,128)(2,1)S(1)}, u32[]{:S(2)}, u32[]{:S(2)}) collective-permute-start(bf16[8,6272]{1,0:T(8,128)(2,1)S(1)} %collective-permute-done.5.refs_9_), channel_id=1, source_target_pairs={{0,1},{1,0},{2,3},{3,2},{4,5},{5,4},{6,7},{7,6},{8,9},{9,8},{10,11... | collective-permute-start | bytes 301064 | tf_op jit(solution)/shard_map/ppermute | solution.py:89
  21.4 1.4 %collective-permute-start.9 = (bf16[8,6272]{1,0:T(8,128)(2,1)S(1)}, bf16[8,6272]{1,0:T(8,128)(2,1)S(1)}, u32[]{:S(2)}, u32[]{:S(2)}) collective-permute-start(bf16[8,6272]{1,0:T(8,128)(2,1)S(1)} %collective-permute-done.1.refs_5_), channel_id=1, source_target_pairs={{0,1},{1,0},{2,3},{3,2},{4,5},{5,4},{6,7},{7,6},{8,9},{9,8},{10,11... | collective-permute-start | bytes 301064 | tf_op jit(solution)/shard_map/ppermute | solution.py:87
  21.9 1.5 %collective-permute-start.10 = (bf16[8,6272]{1,0:T(8,128)(2,1)S(1)}, bf16[8,6272]{1,0:T(8,128)(2,1)S(1)}, u32[]{:S(2)}, u32[]{:S(2)}) collective-permute-start(bf16[8,6272]{1,0:T(8,128)(2,1)S(1)} %collective-permute-done.2.refs_6_), channel_id=1, source_target_pairs={{0,1},{1,0},{2,3},{3,2},{4,5},{5,4},{6,7},{7,6},{8,9},{9,8},{10,11... | collective-permute-start | bytes 301064 | tf_op jit(solution)/shard_map/ppermute | solution.py:87
  22.0 1.4 %collective-permute-start.14 = (bf16[8,6272]{1,0:T(8,128)(2,1)S(1)}, bf16[8,6272]{1,0:T(8,128)(2,1)S(1)}, u32[]{:S(2)}, u32[]{:S(2)}) collective-permute-start(bf16[8,6272]{1,0:T(8,128)(2,1)S(1)} %collective-permute-done.6.refs_10_), channel_id=1, source_target_pairs={{0,1},{1,0},{2,3},{3,2},{4,5},{5,4},{6,7},{7,6},{8,9},{9,8},{10,11... | collective-permute-start | bytes 301064 | tf_op jit(solution)/shard_map/ppermute | solution.py:89
  22.8 1.3 %collective-permute-start.11 = (bf16[8,6272]{1,0:T(8,128)(2,1)S(1)}, bf16[8,6272]{1,0:T(8,128)(2,1)S(1)}, u32[]{:S(2)}, u32[]{:S(2)}) collective-permute-start(bf16[8,6272]{1,0:T(8,128)(2,1)S(1)} %collective-permute-done.3.refs_7_), channel_id=1, source_target_pairs={{0,1},{1,0},{2,3},{3,2},{4,5},{5,4},{6,7},{7,6},{8,9},{9,8},{10,11... | collective-permute-start | bytes 301064 | tf_op jit(solution)/shard_map/ppermute | solution.py:87
  24.1 4.0 %copy-start = (bf16[8192,640]{1,0:T(8,128)(2,1)S(1)}, bf16[8192,640]{1,0:T(8,128)(2,1)}, u32[]{:S(2)}) copy-start(bf16[8192,640]{1,0:T(8,128)(2,1)} %refs_2_.1) | copy-start | bytes 31457284
  28.1 20.2 %copy-start.8 = (s32[6]{0:T(128)S(1)}, s32[6]{0:T(128)}, u32[]{:S(2)}) copy-start(s32[6]{0:T(128)} %ids_ref.3) | copy-start | bytes 76
  28.1 20.2 %copy-start.9 = (s32[6]{0:T(128)S(1)}, s32[6]{0:T(128)}, u32[]{:S(2)}) copy-start(s32[6]{0:T(128)} %len_ref.1) | copy-start | bytes 76
  33.6 14.7 %all-to-all-start = ((bf16[16,6,640]{2,1,0:T(8,128)(2,1)}), bf16[16,6,640]{2,1,0:T(8,128)(2,1)S(1)}, u32[]{:S(2)}, u32[]{:S(2)}) async-start(bf16[16,6,640]{2,1,0:T(8,128)(2,1)} %qkv_project.1), calls=%async_computation | async-start | bytes 327680 | tf_op jit(solution)/shard_map/all_to_all | solution.py:399
  48.3 2.3 %copy-start.2 = (bf16[6,384,1024]{2,1,0:T(8,128)(2,1)S(1)}, bf16[6,384,1024]{2,1,0:T(8,128)(2,1)}, u32[]{:S(2)}) copy-start(bf16[6,384,1024]{2,1,0:T(8,128)(2,1)} %k_ref.1) | copy-start | bytes 14155780
  50.7 2.3 %copy-start.3 = (bf16[6,384,1024]{2,1,0:T(8,128)(2,1)S(1)}, bf16[6,384,1024]{2,1,0:T(8,128)(2,1)}, u32[]{:S(2)}) copy-start(bf16[6,384,1024]{2,1,0:T(8,128)(2,1)} %v_ref.1) | copy-start | bytes 14155780
  53.0 26.5 %copy-start.4 = (bf16[2,8192,16]{1,2,0:T(8,128)(2,1)S(1)}, bf16[2,8192,16]{1,2,0:T(8,128)(2,1)}, u32[]{:S(2)}) copy-start(bf16[2,8192,16]{1,2,0:T(8,128)(2,1)} %param.20) | copy-start | bytes 1572868
  59.2 4.7 %collective-permute-start.15 = (bf16[8,6272]{1,0:T(8,128)(2,1)S(1)}, bf16[8,6272]{1,0:T(8,128)(2,1)S(1)}, u32[]{:S(2)}, u32[]{:S(2)}) collective-permute-start(bf16[8,6272]{1,0:T(8,128)(2,1)S(1)} %attend.1.refs_2_), channel_id=1, source_target_pairs={{0,4},{1,5},{4,8},{5,9},{8,12},{9,13},{12,14},{13,15},{14,10},{15,... | collective-permute-start | bytes 301064 | tf_op jit(solution)/shard_map/ppermute | solution.py:84
  59.3 4.9 %collective-permute-start.19 = (bf16[8,6272]{1,0:T(8,128)(2,1)S(1)}, bf16[8,6272]{1,0:T(8,128)(2,1)S(1)}, u32[]{:S(2)}, u32[]{:S(2)}) collective-permute-start(bf16[8,6272]{1,0:T(8,128)(2,1)S(1)} %attend.1.refs_2_), channel_id=1, source_target_pairs={{0,2},{1,3},{4,0},{5,1},{8,4},{9,5},{12,8},{13,9},{14,12},{15,13},... | collective-permute-start | bytes 301064 | tf_op jit(solution)/shard_map/ppermute | solution.py:86
  63.9 5.0 %collective-permute-start.16 = (bf16[8,6272]{1,0:T(8,128)(2,1)S(1)}, bf16[8,6272]{1,0:T(8,128)(2,1)S(1)}, u32[]{:S(2)}, u32[]{:S(2)}) collective-permute-start(bf16[8,6272]{1,0:T(8,128)(2,1)S(1)} %collective-permute-done.15.refs_3_), channel_id=1, source_target_pairs={{0,4},{1,5},{4,8},{5,9},{8,12},{9,13},{12,14},{13,15},{14,10},{15,... | collective-permute-start | bytes 301064 | tf_op jit(solution)/shard_map/ppermute | solution.py:84
  64.1 5.3 %collective-permute-start.20 = (bf16[8,6272]{1,0:T(8,128)(2,1)S(1)}, bf16[8,6272]{1,0:T(8,128)(2,1)S(1)}, u32[]{:S(2)}, u32[]{:S(2)}) collective-permute-start(bf16[8,6272]{1,0:T(8,128)(2,1)S(1)} %collective-permute-done.19.refs_7_), channel_id=1, source_target_pairs={{0,2},{1,3},{4,0},{5,1},{8,4},{9,5},{12,8},{13,9},{14,12},{15,13},... | collective-permute-start | bytes 301064 | tf_op jit(solution)/shard_map/ppermute | solution.py:86
  68.9 4.6 %collective-permute-start.17 = (bf16[8,6272]{1,0:T(8,128)(2,1)S(1)}, bf16[8,6272]{1,0:T(8,128)(2,1)S(1)}, u32[]{:S(2)}, u32[]{:S(2)}) collective-permute-start(bf16[8,6272]{1,0:T(8,128)(2,1)S(1)} %collective-permute-done.16.refs_4_), channel_id=1, source_target_pairs={{0,4},{1,5},{4,8},{5,9},{8,12},{9,13},{12,14},{13,15},{14,10},{15,... | collective-permute-start | bytes 301064 | tf_op jit(solution)/shard_map/ppermute | solution.py:84
  68.9 4.6 %collective-permute-start.22 = (bf16[8,6272]{1,0:T(8,128)(2,1)S(1)}, bf16[8,6272]{1,0:T(8,128)(2,1)S(1)}, u32[]{:S(2)}, u32[]{:S(2)}) collective-permute-start(bf16[8,6272]{1,0:T(8,128)(2,1)S(1)} %attend.1.refs_2_), channel_id=1, source_target_pairs={{0,1},{1,0},{2,3},{3,2},{4,5},{5,4},{6,7},{7,6},{8,9},{9,8},{10,11... | collective-permute-start | bytes 301064 | tf_op jit(solution)/shard_map/ppermute | solution.py:82
  68.9 4.7 %collective-permute-start.27 = (bf16[8,6272]{1,0:T(8,128)(2,1)S(1)}, bf16[8,6272]{1,0:T(8,128)(2,1)S(1)}, u32[]{:S(2)}, u32[]{:S(2)}) collective-permute-start(bf16[8,6272]{1,0:T(8,128)(2,1)S(1)} %collective-permute-done.19.refs_7_), channel_id=1, source_target_pairs={{0,1},{1,0},{2,3},{3,2},{4,5},{5,4},{6,7},{7,6},{8,9},{9,8},{10,11... | collective-permute-start | bytes 301064 | tf_op jit(solution)/shard_map/ppermute | solution.py:89
  69.4 4.6 %collective-permute-start.23 = (bf16[8,6272]{1,0:T(8,128)(2,1)S(1)}, bf16[8,6272]{1,0:T(8,128)(2,1)S(1)}, u32[]{:S(2)}, u32[]{:S(2)}) collective-permute-start(bf16[8,6272]{1,0:T(8,128)(2,1)S(1)} %collective-permute-done.15.refs_3_), channel_id=1, source_target_pairs={{0,1},{1,0},{2,3},{3,2},{4,5},{5,4},{6,7},{7,6},{8,9},{9,8},{10,11... | collective-permute-start | bytes 301064 | tf_op jit(solution)/shard_map/ppermute | solution.py:87
  69.4 5.3 %collective-permute-start.21 = (bf16[8,6272]{1,0:T(8,128)(2,1)S(1)}, bf16[8,6272]{1,0:T(8,128)(2,1)S(1)}, u32[]{:S(2)}, u32[]{:S(2)}) collective-permute-start(bf16[8,6272]{1,0:T(8,128)(2,1)S(1)} %collective-permute-done.20.refs_8_), channel_id=1, source_target_pairs={{0,2},{1,3},{4,0},{5,1},{8,4},{9,5},{12,8},{13,9},{14,12},{15,13},... | collective-permute-start | bytes 301064 | tf_op jit(solution)/shard_map/ppermute | solution.py:86
  73.6 4.6 %collective-permute-start.18 = (bf16[8,6272]{1,0:T(8,128)(2,1)S(1)}, bf16[8,6272]{1,0:T(8,128)(2,1)S(1)}, u32[]{:S(2)}, u32[]{:S(2)}) collective-permute-start(bf16[8,6272]{1,0:T(8,128)(2,1)S(1)} %collective-permute-done.17.refs_5_), channel_id=1, source_target_pairs={{0,4},{1,5},{4,8},{5,9},{8,12},{9,13},{12,14},{13,15},{14,10},{15,... | collective-permute-start | bytes 301064 | tf_op jit(solution)/shard_map/ppermute | solution.py:84
  73.6 4.6 %collective-permute-start.28 = (bf16[8,6272]{1,0:T(8,128)(2,1)S(1)}, bf16[8,6272]{1,0:T(8,128)(2,1)S(1)}, u32[]{:S(2)}, u32[]{:S(2)}) collective-permute-start(bf16[8,6272]{1,0:T(8,128)(2,1)S(1)} %collective-permute-done.20.refs_8_), channel_id=1, source_target_pairs={{0,1},{1,0},{2,3},{3,2},{4,5},{5,4},{6,7},{7,6},{8,9},{9,8},{10,11... | collective-permute-start | bytes 301064 | tf_op jit(solution)/shard_map/ppermute | solution.py:89
  73.6 4.6 %collective-permute-start.24 = (bf16[8,6272]{1,0:T(8,128)(2,1)S(1)}, bf16[8,6272]{1,0:T(8,128)(2,1)S(1)}, u32[]{:S(2)}, u32[]{:S(2)}) collective-permute-start(bf16[8,6272]{1,0:T(8,128)(2,1)S(1)} %collective-permute-done.16.refs_4_), channel_id=1, source_target_pairs={{0,1},{1,0},{2,3},{3,2},{4,5},{5,4},{6,7},{7,6},{8,9},{9,8},{10,11... | collective-permute-start | bytes 301064 | tf_op jit(solution)/shard_map/ppermute | solution.py:87
  74.1 4.1 %collective-permute-start.25 = (bf16[8,6272]{1,0:T(8,128)(2,1)S(1)}, bf16[8,6272]{1,0:T(8,128)(2,1)S(1)}, u32[]{:S(2)}, u32[]{:S(2)}) collective-permute-start(bf16[8,6272]{1,0:T(8,128)(2,1)S(1)} %collective-permute-done.17.refs_5_), channel_id=1, source_target_pairs={{0,1},{1,0},{2,3},{3,2},{4,5},{5,4},{6,7},{7,6},{8,9},{9,8},{10,11... | collective-permute-start | bytes 301064 | tf_op jit(solution)/shard_map/ppermute | solution.py:87
  74.7 3.5 %collective-permute-start.29 = (bf16[8,6272]{1,0:T(8,128)(2,1)S(1)}, bf16[8,6272]{1,0:T(8,128)(2,1)S(1)}, u32[]{:S(2)}, u32[]{:S(2)}) collective-permute-start(bf16[8,6272]{1,0:T(8,128)(2,1)S(1)} %collective-permute-done.21.refs_9_), channel_id=1, source_target_pairs={{0,1},{1,0},{2,3},{3,2},{4,5},{5,4},{6,7},{7,6},{8,9},{9,8},{10,11... | collective-permute-start | bytes 301064 | tf_op jit(solution)/shard_map/ppermute | solution.py:89
  78.2 1.3 %collective-permute-start.26 = (bf16[8,6272]{1,0:T(8,128)(2,1)S(1)}, bf16[8,6272]{1,0:T(8,128)(2,1)S(1)}, u32[]{:S(2)}, u32[]{:S(2)}) collective-permute-start(bf16[8,6272]{1,0:T(8,128)(2,1)S(1)} %collective-permute-done.18.refs_6_), channel_id=1, source_target_pairs={{0,1},{1,0},{2,3},{3,2},{4,5},{5,4},{6,7},{7,6},{8,9},{9,8},{10,11... | collective-permute-start | bytes 301064 | tf_op jit(solution)/shard_map/ppermute | solution.py:87
  82.1 11.4 %all-to-all-start.1 = ((bf16[16,32,128]{2,1,0:T(8,128)(2,1)}), bf16[16,32,128]{2,1,0:T(8,128)(2,1)S(1)}, u32[]{:S(2)}, u32[]{:S(2)}) async-start(bf16[16,32,128]{2,1,0:T(8,128)(2,1)} %get-tuple-element.8), calls=%async_computation.1 | async-start | bytes 262144 | tf_op jit(solution)/shard_map/all_to_all | solution.py:399
  85.6 3.4 %copy-start.1 = (bf16[8192,512]{1,0:T(8,128)(2,1)S(1)}, bf16[8192,512]{1,0:T(8,128)(2,1)}, u32[]{:S(2)}) copy-start(bf16[8192,512]{1,0:T(8,128)(2,1)} %weight.1) | copy-start | bytes 25165828
  89.0 4.5 %copy-start.5 = (bf16[32,16,512]{2,1,0:T(8,128)(2,1)S(1)}, bf16[32,16,512]{2,1,0:T(8,128)(2,1)}, u32[]{:S(2)}) copy-start(bf16[32,16,512]{2,1,0:T(8,128)(2,1)} %param.21) | copy-start | bytes 1572868

commit v2 on v1

v2 whole, which is shorter than its diff:
```python
import functools

import jax
import jax.numpy as jnp
from jax import lax
from jax.experimental import pallas as pl
from jax.experimental.pallas import tpu as pltpu
from jax.sharding import PartitionSpec as P

QUERY_HEADS = 64
KVH = 8
HEAD_SIZE = 128
ADAPTER_RANK = 16
GROUPS = QUERY_HEADS // KVH

EPS = 1e-06
ROPE_BASE = 1000000.0

BLOCKS = 8
HALF = BLOCKS // 2
LANES = 128
MIB = 1 << 20

VMEM = pl.BlockSpec(memory_space=pltpu.VMEM)
HBM = pl.BlockSpec(memory_space=pltpu.HBM)
SMEM = pl.BlockSpec(memory_space=pltpu.SMEM)


def params(mib):
    return pltpu.CompilerParams(vmem_limit_bytes=mib * MIB)


def factors(chips):
    inner = 1
    while inner * inner * 4 <= chips and chips % (inner * 2) == 0:
        inner *= 2
    return chips // inner, inner


def ring_order(chips):
    outer, inner = factors(chips)
    if inner < 2 or outer % 2:
        return list(range(chips))
    order = [a * inner for a in range(outer)]
    for turn, a in enumerate(reversed(range(outer))):
        steps = range(1, inner) if turn % 2 == 0 else range(inner - 1, 0, -1)
        order += [a * inner + b for b in steps]
    return order


def lookup(table, index):
    value = jnp.int32(table[0])
    for at in range(1, len(table)):
        value = jnp.where(index == at, jnp.int32(table[at]), value)
    return value


def slot_chips(devices, me):
    chips = devices // 2
    order = ring_order(chips)
    place_of = [order.index(chip) for chip in range(chips)]
    place = lookup(place_of, lax.div(me, 2))
    ahead = chips // 2
    shifts = [-j for j in range(ahead)] + [j for j in range(1, chips - ahead + 1)]
    return [lookup(order, lax.rem(place + shift + chips, chips)) for shift in shifts]


def steps(count, unrolled, body):
    if unrolled:
        for i in range(count):
            body(i)
    else:
        lax.fori_loop(0, count, lambda i, _: (body(i), 0)[1], 0)


def gather_chunks(halves, devices):
    chips = devices // 2
    order = ring_order(chips)
    ahead = chips // 2

    def ring(step):
        return [
            (2 * order[p] + core, 2 * order[(p + step) % chips] + core)
            for p in range(chips)
            for core in range(2)
        ]

    up, down = ring(1), ring(-1)
    far = [ahead, chips - ahead - 1], [ahead - 1, chips - ahead]
    behind, front = [[half] for half in halves], [[half] for half in halves]
    for j in range(1, max(ahead, chips - ahead) + 1):
        for h in (0, 1):
            if j <= far[h][0]:
                behind[h].append(lax.ppermute(behind[h][-1], "tensor", up))
            if j <= far[h][1]:
                front[h].append(lax.ppermute(front[h][-1], "tensor", down))
    slots = []
    for h in (0, 1):
        near = behind[h][:ahead] + front[h][1 : chips - ahead]
        slots.append(near + [behind[h][ahead] if h == 0 else front[h][chips - ahead]])
    return slots


def across(x, devices):
    return lax.ppermute(x, "tensor", [(d, d ^ 1) for d in range(devices)])


def write_half(stage, h, rows, out_ref):
    block = stage.shape[1]
    for g in range(HALF * rows // 8):
        at = h * HALF * rows + 8 * g
        out_ref[:, g * block : (g + 1) * block] = stage[at : at + 8, :].astype(jnp.bfloat16)


def write_ids(ids_ref, rows, out_ref):
    sub = lax.broadcasted_iota(jnp.int32, (8, LANES), 0)
    ids = jnp.full((8, LANES), -1.0, jnp.float32)
    for r in range(rows):
        ids = jnp.where(sub == r, ids_ref[r].astype(jnp.float32), ids)
    out_ref[:, out_ref.shape[1] - LANES :] = ids.astype(jnp.bfloat16)


def norm_kernel(x_hbm, gain_hbm, first_ref, second_ref, x_ref, gain_ref, sems, stage):
    copies = [
        pltpu.make_async_copy(x_hbm, x_ref, sems.at[0]),
        pltpu.make_async_copy(gain_hbm, gain_ref, sems.at[1]),
    ]
    for copy in copies:
        copy.start()
    for copy in copies:
        copy.wait()
    rows, width = x_ref.shape
    block = width // BLOCKS
    total = jnp.zeros((rows, LANES), jnp.float32)
    for c in range(width // LANES):
        x = x_ref[:, c * LANES : (c + 1) * LANES].astype(jnp.float32)
        total = total + x * x
    factor = lax.rsqrt(jnp.sum(total, axis=-1, keepdims=True) / width + EPS)
    for c in range(width // LANES):
        x = x_ref[:, c * LANES : (c + 1) * LANES].astype(jnp.float32)
        gain = gain_ref[c : c + 1, :].astype(jnp.float32)
        j, lane = c * LANES // block, c * LANES % block
        stage[j * rows : (j + 1) * rows, lane : lane + LANES] = x * factor * gain
    write_half(stage, 0, rows, first_ref)
    write_half(stage, 1, rows, second_ref)


def norm_chunk(hidden, gain):
    rows, width = hidden.shape
    half = jax.ShapeDtypeStruct((8, rows * width // 16), jnp.bfloat16)
    return pl.pallas_call(
        norm_kernel,
        out_shape=(half, half),
        in_specs=[HBM, HBM],
        out_specs=(VMEM, VMEM),
        scratch_shapes=[
            pltpu.VMEM((rows, width), jnp.bfloat16),
            pltpu.VMEM((width // LANES, LANES), jnp.bfloat16),
            pltpu.SemaphoreType.DMA((2,)),
            pltpu.VMEM((BLOCKS * rows, width // BLOCKS), jnp.float32),
        ],
        compiler_params=params(16),
        name="norm_chunk",
    )(hidden, gain.reshape(width // LANES, LANES))


def unpack_kernel(chips, rows, with_ids, *refs):
    firsts, seconds = refs[:chips], refs[chips : 2 * chips]
    left, stage = refs[2 * chips :]
    block = stage.shape[-1]
    per_half = HALF * rows
    small = chips <= 8
    for pair in range(chips // 2):
        turn = pair % 2
        for place in range(2):
            for h, halves in ((0, firsts), (1, seconds)):
                chunk = halves[2 * pair + place]

                def widen(g, chunk=chunk, place=place, h=h):
                    lane = g * block if small else pl.multiple_of(g * block, block)
                    at = h * per_half + 8 * g
                    at = at if small else pl.multiple_of(at, 8)
                    stage[turn, place, pl.ds(at, 8), :] = chunk[:, pl.ds(lane, block)].astype(
                        jnp.float32
                    )

                steps(per_half // 8, small, widen)

        for j in range(BLOCKS):
            both = [stage[turn, place, j * rows : j * rows + 8, :] for place in range(2)]
            left[j, 16 * pair : 16 * pair + 16, :] = jnp.concatenate(both, axis=0).astype(
                jnp.bfloat16
            )
        if with_ids:
            both = [firsts[2 * pair + place][:, per_half // 8 * block :] for place in range(2)]
            both = jnp.concatenate([ids.astype(jnp.float32) for ids in both], axis=0)
            left[BLOCKS, 16 * pair : 16 * pair + 16, :LANES] = both.astype(jnp.bfloat16)


def unpack(halves, rows, width, with_ids):
    firsts, seconds = halves
    chips = len(firsts)
    block = width // BLOCKS
    return pl.pallas_call(
        functools.partial(unpack_kernel, chips, rows, with_ids),
        out_shape=jax.ShapeDtypeStruct((BLOCKS + with_ids, chips * 8, block), jnp.bfloat16),
        in_specs=[VMEM] * (2 * chips),
        out_specs=VMEM,
        scratch_shapes=[pltpu.VMEM((2, 2, BLOCKS * rows + 8, block), jnp.float32)],
        compiler_params=params(32),
        name="unpack",
    )(*firsts, *seconds)


def fetch(weight, held, sems):
    block = held.shape[1]
    copies = [
        pltpu.make_async_copy(weight.at[pl.ds(j * block, block), :], held.at[j], sems.at[j])
        for j in range(BLOCKS)
    ]
    for copy in copies:
        copy.start()
    return copies


def multiply(left, held, acc, copies=None):
    acc[...] = jnp.zeros_like(acc)
    for j in range(BLOCKS):
        if copies is not None:
            copies[j].wait()
        acc[...] += jnp.dot(left[j], held[j], preferred_element_type=jnp.float32)


def own_kernel(left, weight, held, acc, sems):
    multiply(left, held, acc, fetch(weight, held, sems))


def own_rows(left, weight, name):
    width, cols = weight.shape
    rows = left.shape[1]
    return pl.pallas_call(
        own_kernel,
        out_shape=(
            jax.ShapeDtypeStruct((BLOCKS, width // BLOCKS, cols), jnp.bfloat16),
            jax.ShapeDtypeStruct((rows, cols), jnp.float32),
        ),
        in_specs=[VMEM, HBM],
        out_specs=(VMEM, VMEM),
        scratch_shapes=[pltpu.SemaphoreType.DMA((BLOCKS,))],
        compiler_params=params(24),
        cost_estimate=pl.CostEstimate(
            flops=2 * rows * width * cols, bytes_accessed=width * cols * 2, transcendentals=0
        ),
        name=name,
    )(left, weight)


def qkv_kernel(devices, rows, me_ref, bias_ref, own_ref, left, held, out_ref, acc):
    multiply(left, held, acc)
    bias = bias_ref[...].astype(jnp.float32)
    core = lax.rem(me_ref[0], 2)
    for slot, chip in enumerate(slot_chips(devices, me_ref[0])):
        mine = slice(8 * slot, 8 * slot + rows)
        out_ref[2 * chip + core] = (own_ref[mine, :] + bias).astype(jnp.bfloat16)
        out_ref[2 * chip + 1 - core] = (acc[mine, :] + bias).astype(jnp.bfloat16)


def qkv_project(me, own, left, held, bias, devices, rows):
    cols = own.shape[1]
    return pl.pallas_call(
        functools.partial(qkv_kernel, devices, rows),
        out_shape=jax.ShapeDtypeStruct((devices, rows, cols), jnp.bfloat16),
        in_specs=[SMEM, VMEM, VMEM, VMEM, VMEM],
        out_specs=VMEM,
        scratch_shapes=[pltpu.VMEM(own.shape, jnp.float32)],
        compiler_params=params(40),
        name="qkv_project",
    )(me, bias.reshape(1, cols), own, left, held)


def attend_kernel(
    rows,
    len_ref,
    ids_ref,
    qkv_ref,
    cos_ref,
    sin_ref,
    k_hbm,
    v_hbm,
    first_ref,
    second_ref,
    keys,
    values,
    sems,
    heads,
    mixed,
    stage,
):
    total_heads = QUERY_HEADS + 2 * KVH
    half = HEAD_SIZE // 2
    for r in range(rows):
        pltpu.make_async_copy(k_hbm.at[r], keys.at[r], sems.at[0, r]).start()
        pltpu.make_async_copy(v_hbm.at[r], values.at[r], sems.at[1, r]).start()
    for h in range(total_heads):
        tile = qkv_ref[:, h * HEAD_SIZE : (h + 1) * HEAD_SIZE].astype(jnp.float32)
        heads[pl.ds(h, rows, stride=total_heads), :] = tile
    scale = 1.0 / HEAD_SIZE**0.5

    def one_row(r, carry):
        base = pl.multiple_of(r * total_heads, 8)
        turned = heads[pl.ds(base, QUERY_HEADS + KVH), :]
        cosine = cos_ref[pl.ds(r, 1), :]
        sine = sin_ref[pl.ds(r, 1), :]
        turned = (turned * cosine + pltpu.roll(turned, half, 1) * sine).astype(jnp.bfloat16)
        query = turned[:QUERY_HEADS]
        query_f = query.astype(jnp.float32)
        new_key = turned[QUERY_HEADS:].astype(jnp.float32)
        new_value = heads[pl.ds(base + QUERY_HEADS + KVH, KVH), :]
        pltpu.make_async_copy(k_hbm.at[r], keys.at[r], sems.at[0, r]).wait()
        scores = []
        own = []
        for k in range(KVH):
            mine = slice(k * GROUPS, (k + 1) * GROUPS)
            key = keys[r, :, k * HEAD_SIZE : (k + 1) * HEAD_SIZE]
            scores.append(
                lax.dot_general(
                    query[mine], key, (((1,), (1,)), ((), ())), preferred_element_type=jnp.float32
                )
            )
            own.append(jnp.sum(query_f[mine] * new_key[k : k + 1], axis=-1, keepdims=True))
        score = jnp.concatenate(scores, axis=0) * scale
        own = jnp.concatenate(own, axis=0) * scale
        valid = lax.broadcasted_iota(jnp.int32, score.shape, 1) < len_ref[r]
        top = jnp.maximum(jnp.max(jnp.where(valid, score, -1e30), axis=-1, keepdims=True), own)
        expo = jnp.where(valid, jnp.exp(score - top), 0.0)
        expo_own = jnp.exp(own - top)
        total = jnp.sum(expo, axis=-1, keepdims=True) + expo_own
        weight = (expo / total).astype(jnp.bfloat16)
        weight_own = (expo_own / total).astype(jnp.bfloat16).astype(jnp.float32)
        pltpu.make_async_copy(v_hbm.at[r], values.at[r], sems.at[1, r]).wait()
        for k in range(KVH):
            mine = slice(k * GROUPS, (k + 1) * GROUPS)
            value = values[r, :, k * HEAD_SIZE : (k + 1) * HEAD_SIZE]
            part = jnp.dot(weight[mine], value, preferred_element_type=jnp.float32)
            part = part + weight_own[mine] * new_value[k : k + 1]
            at = pl.multiple_of(r * QUERY_HEADS + k * GROUPS, 8)
            mixed[pl.ds(at, GROUPS), :] = part
        return carry

    lax.fori_loop(0, rows, one_row, 0)
    per_block = QUERY_HEADS // BLOCKS
    for h in range(QUERY_HEADS):
        j, lane = h // per_block, h % per_block
        stage[j * rows : (j + 1) * rows, lane * HEAD_SIZE : (lane + 1) * HEAD_SIZE] = mixed[
            pl.ds(h, rows, stride=QUERY_HEADS), :
        ]
    write_half(stage, 0, rows, first_ref)
    write_half(stage, 1, rows, second_ref)
    write_ids(ids_ref, rows, first_ref)


def attend(lengths, ids, qkv, cosine, sine, keys, values):
    rows, capacity, width = keys.shape
    total_heads = QUERY_HEADS + 2 * KVH
    features = QUERY_HEADS * HEAD_SIZE
    size = rows * features // 16
    return pl.pallas_call(
        functools.partial(attend_kernel, rows),
        out_shape=(
            jax.ShapeDtypeStruct((8, size + LANES), jnp.bfloat16),
            jax.ShapeDtypeStruct((8, size), jnp.bfloat16),
        ),
        in_specs=[SMEM, SMEM, VMEM, VMEM, VMEM, HBM, HBM],
        out_specs=(VMEM, VMEM),
        scratch_shapes=[
            pltpu.VMEM(keys.shape, jnp.bfloat16),
            pltpu.VMEM(keys.shape, jnp.bfloat16),
            pltpu.SemaphoreType.DMA((2, rows)),
            pltpu.VMEM((rows * total_heads, HEAD_SIZE), jnp.float32),
            pltpu.VMEM((rows * QUERY_HEADS, HEAD_SIZE), jnp.float32),
            pltpu.VMEM((BLOCKS * rows, features // BLOCKS), jnp.float32),
        ],
        compiler_params=params(24),
        name="attend",
    )(lengths, ids, qkv, cosine, sine, keys, values)


def shrink_kernel(devices, me_ref, down_ref, own, other, coords_ref, ids, place_of, total):
    me = me_ref[0]
    stored, rank, features = down_ref.shape
    block = features // BLOCKS
    rows = own.shape[1]
    for c, left in enumerate((own, other)):
        mine = slice(c * rows, (c + 1) * rows)
        for s in range(stored):
            part = jnp.zeros((rank, rows), jnp.float32)
            for j in range(BLOCKS):
                part += lax.dot_general(
                    down_ref[s, :, j * block : (j + 1) * block],
                    left[j],
                    (((1,), (1,)), ((), ())),
                    preferred_element_type=jnp.float32,
                )
            total[s * rank : (s + 1) * rank, mine] = part
        ids[mine, :] = left[BLOCKS, :, :LANES].astype(jnp.float32)
    row_ids = jnp.transpose(ids[...])[: stored * rank, :].astype(jnp.int32)
    adapter = lax.broadcasted_iota(jnp.int32, total.shape, 0) // rank + me * stored
    coords = jnp.where(row_ids == adapter, total[...], 0.0).astype(jnp.bfloat16)
    core = lax.rem(me, 2)
    sub = lax.broadcasted_iota(jnp.int32, (8, LANES), 0)
    for slot, chip in enumerate(slot_chips(devices, me)):
        for c, place in ((0, core), (1, 1 - core)):
            at = c * rows + 8 * slot
            place_of[at : at + 8, :] = sub + (2 * chip + place) * 8
    target = lax.broadcasted_iota(jnp.int32, (2 * rows, 2 * rows), 1)
    move = jnp.where(place_of[:, :1] == target, 1.0, 0.0).astype(jnp.bfloat16)
    coords = jnp.dot(coords, move, preferred_element_type=jnp.float32).astype(jnp.bfloat16)
    for d in range(devices):
        coords_ref[d] = coords


def shrink(me, own, other, down, devices):
    stored, rank, features = down.shape
    rows = devices * 8
    return pl.pallas_call(
        functools.partial(shrink_kernel, devices),
        out_shape=jax.ShapeDtypeStruct((devices, stored * rank, rows), jnp.bfloat16),
        in_specs=[SMEM, VMEM, VMEM, VMEM],
        out_specs=VMEM,
        scratch_shapes=[
            pltpu.VMEM((rows, LANES), jnp.float32),
            pltpu.VMEM((rows, LANES), jnp.int32),
            pltpu.VMEM((stored * rank, rows), jnp.float32),
        ],
        compiler_params=params(48),
        name="shrink",
    )(me, down, own, other)


def base_kernel(devices, me_ref, own_ref, left, held, out_ref, acc):
    multiply(left, held, acc)
    core = lax.rem(me_ref[0], 2)
    for slot, chip in enumerate(slot_chips(devices, me_ref[0])):
        mine = slice(8 * slot, 8 * slot + 8)
        at = pl.multiple_of((2 * chip + core) * 8, 8)
        out_ref[pl.ds(at, 8), :] = own_ref[mine, :]
        at = pl.multiple_of((2 * chip + 1 - core) * 8, 8)
        out_ref[pl.ds(at, 8), :] = acc[mine, :]


def base_project(me, own, left, held, devices):
    rows, cols = own.shape
    return pl.pallas_call(
        functools.partial(base_kernel, devices),
        out_shape=jax.ShapeDtypeStruct((2 * rows, cols), jnp.float32),
        in_specs=[SMEM, VMEM, VMEM, VMEM],
        out_specs=VMEM,
        scratch_shapes=[pltpu.VMEM(own.shape, jnp.float32)],
        compiler_params=params(40),
        cost_estimate=pl.CostEstimate(
            flops=2 * rows * held.size, bytes_accessed=2 * held.size, transcendentals=0
        ),
        name="base_project",
    )(me, own, left, held)


def add_kernel(rows, base_ref, coords_ref, up_ref, out_ref):
    delta = lax.dot_general(
        coords_ref[...], up_ref[...], (((0,), (0,)), ((), ())), preferred_element_type=jnp.float32
    )
    projected = base_ref[...] + delta
    for d in range(out_ref.shape[0]):
        out_ref[d] = projected[8 * d : 8 * d + rows, :].astype(jnp.bfloat16)


def add_delta(base, coords, up, rows):
    return pl.pallas_call(
        functools.partial(add_kernel, rows),
        out_shape=jax.ShapeDtypeStruct((base.shape[0] // 8, rows, base.shape[1]), jnp.bfloat16),
        in_specs=[VMEM, VMEM, VMEM],
        out_specs=VMEM,
        compiler_params=params(40),
        name="add_delta",
    )(base, coords, up)


def exchange(parts):
    return lax.all_to_all(parts, "tensor", split_axis=0, concat_axis=0, tiled=True)


def per_row(parts):
    devices, rows, cols = parts.shape
    return jnp.transpose(parts, (1, 0, 2)).reshape(rows, devices * cols)


def per_device(
    devices,
    hidden,
    input_norm_scale,
    query_key_value_weight,
    projection_bias,
    rotated_key_cache,
    past_value_cache,
    lengths,
    row_adapter_index,
    output_weight,
    adapter_down_weight,
    adapter_up_weight,
):
    rows = hidden.shape[0]
    me = lax.axis_index("tensor").astype(jnp.int32).reshape(1)
    half = HEAD_SIZE // 2
    inv = ROPE_BASE ** (-(jnp.arange(half, dtype=jnp.float32) * 2.0 / HEAD_SIZE))
    angle = lengths.astype(jnp.float32)[:, None] * inv[None, :]
    cosine, sine = jnp.cos(angle), jnp.sin(angle)
    cosine = jnp.concatenate([cosine, cosine], axis=1)
    sine = jnp.concatenate([-sine, sine], axis=1)
    down = jnp.transpose(adapter_down_weight, (0, 2, 1))
    up = adapter_up_weight.reshape(-1, adapter_up_weight.shape[2])

    halves = gather_chunks(norm_chunk(hidden, input_norm_scale), devices)
    mine = unpack(halves, rows, hidden.shape[1], False)
    theirs = across(mine, devices)
    held, own = own_rows(mine, query_key_value_weight, "qkv_own")
    qkv = qkv_project(me, own, theirs, held, projection_bias, devices, rows)
    qkv = per_row(exchange(qkv))
    halves = attend(
        lengths, row_adapter_index, qkv, cosine, sine, rotated_key_cache, past_value_cache
    )
    mine = unpack(gather_chunks(halves, devices), rows, QUERY_HEADS * HEAD_SIZE, True)
    theirs = across(mine, devices)
    held, own = own_rows(mine, output_weight, "base_own")
    coords = exchange(shrink(me, mine, theirs, down, devices))
    base = base_project(me, own, theirs, held, devices)
    coords = coords.reshape(-1, coords.shape[2])
    return per_row(exchange(add_delta(base, coords, up, rows)))


def solution(mesh):
    in_specs = (
        P(("group", "tensor"), None),
        P(),
        P(None, "tensor"),
        P("tensor"),
        P(("group", "tensor"), None, None),
        P(("group", "tensor"), None, None),
        P(("group", "tensor")),
        P(("group", "tensor")),
        P(None, "tensor"),
        P("tensor", None, None),
        P(None, None, "tensor"),
    )
    out_specs = P(("group", "tensor"), None)
    return jax.shard_map(
        functools.partial(per_device, mesh.shape["tensor"]),
        mesh=mesh,
        in_specs=in_specs,
        out_specs=out_specs,
        check_vma=False,
    )
```

time: 107 us -> 110 us (1.028)
  waiting for transfers between devices: 32.6 us -> 23.2 us
  starting transfers between devices: 27.5 us -> 36.3 us
  Pallas kernels: 17.6 us -> 21.2 us
  blocking collectives: 11.6 us -> 13.2 us
    ppermute x30, starting transfers between devices: 17.7 us -> 27.3 us  [the longest x14 24.4 us: gather_chunks(): front[h].append(lax.ppermute(front[h][-1], 'tensor', down))]
    ppermute x30, waiting for transfers between devices: 22.2 us -> 14.3 us  [the longest x14 10.4 us: gather_chunks(): behind[h].append(lax.ppermute(behind[h][-1], 'tensor', up))]
    pallas_call x4 -> x8, Pallas kernels: 11.9 us -> 18.4 us  [the longest x1 7.79 us: attend(): pl.pallas_call(functools.partial(attend_kernel, rows), out_shape=(jax.Sha...]
    pallas_call x1, Pallas kernels: 5.52 us -> 2.61 us  [qkv_project(): pl.pallas_call(functools.partial(qkv_kernel, devices, rows), out_shape=ja...]
    all_to_all x1, blocking collectives: 11.6 us -> 13.2 us  [exchange(): lax.all_to_all(parts, 'tensor', split_axis=0, concat_axis=0, tiled=True)]
    all_to_all x2, waiting for transfers between devices: 10.4 us -> 8.88 us  [exchange(): lax.all_to_all(parts, 'tensor', split_axis=0, concat_axis=0, tiled=True)]
  transfers between devices with their start and end apart: 32 -> 32, of which waited for: 14 -> 17; matrix products, arithmetic and copies ran while one was open for 1% -> 1% of each run, Pallas kernels for 2% -> 7%
where the time goes in v2:
time: 110 us
  starting transfers between devices  36.3 us (33%)
  waiting for transfers between devices  23.2 us (21%)
  Pallas kernels  21.2 us (19%)
  local copies, waits for them, and re-layouts  15 us (14%)
  blocking collectives  13.2 us (12%)
    ppermute x14, starting transfers between devices, gather_chunks(): front[h].append(lax.ppermute(front[h][-1], 'tensor', down))  24.4 us
    unnamed x21, local copies, waits for them, and re-layouts  14.3 us
    all_to_all x1, blocking collectives, exchange(): lax.all_to_all(parts, 'tensor', split_axis=0, concat_axis=0, tiled=True)  13.2 us
    ppermute x14, waiting for transfers between devices, gather_chunks(): behind[h].append(lax.ppermute(behind[h][-1], 'tensor', up))  10.4 us
    all_to_all x2, starting transfers between devices, exchange(): lax.all_to_all(parts, 'tensor', split_axis=0, concat_axis=0, tiled=True)  8.94 us
    all_to_all x2, waiting for transfers between devices, exchange(): lax.all_to_all(parts, 'tensor', split_axis=0, concat_axis=0, tiled=True)  8.88 us
    pallas_call x1, Pallas kernels, attend(): pl.pallas_call(functools.partial(attend_kernel, rows), out_shape=(jax.Sha...  7.79 us
    pallas_call x2, Pallas kernels, own_rows(): pl.pallas_call(own_kernel, out_shape=(jax.ShapeDtypeStruct((BLOCKS, width...  5.93 us
  transfers between devices with their start and end apart: 32, of which 17 were waited for; matrix products, arithmetic and copies ran while one was open for 1% of the time, Pallas kernels for 7%

profile of v2, /device:TPU:0, one launch (start us, length us, event | category | flops | bytes accessed | tf_op | source)
XLA Modules:
  0.0 109.9 jit_solution(15852337060996356432)
XLA Ops:
  0.0 0.9 copy-done.6
  0.9 0.7 copy-done.7
  1.6 0.4 norm_chunk.1
  2.0 3.0 %collective-permute-start.10 = (bf16[8,3072]{1,0:T(8,128)(2,1)S(1)}, bf16[8,3072]{1,0:T(8,128)(2,1)S(1)}, u32[]{:S(2)}, u32[]{:S(2)}) collective-permute-start(bf16[8,3072]{1,0:T(8,128)(2,1)S(1)} %get-tuple-element.14.refs_8_), channel_id=1, source_target_pairs={{0,2},{1,3},{4,0},{5,1},{8,4},{9,5},{12,8},{13,9},{14,12},{15,13},... | collective-permute-start | bytes 147464 | tf_op jit(solution)/shard_map/ppermute | solution.py:96
  5.0 0.1 collective-permute-start
  5.1 1.9 %collective-permute-start.3 = (bf16[8,3072]{1,0:T(8,128)(2,1)S(1)}, bf16[8,3072]{1,0:T(8,128)(2,1)S(1)}, u32[]{:S(2)}, u32[]{:S(2)}) collective-permute-start(bf16[8,3072]{1,0:T(8,128)(2,1)S(1)} %get-tuple-element.13.refs_0_), channel_id=1, source_target_pairs={{0,2},{1,3},{4,0},{5,1},{8,4},{9,5},{12,8},{13,9},{14,12},{15,13},... | collective-permute-start | bytes 147464 | tf_op jit(solution)/shard_map/ppermute | solution.py:96
  7.1 0.1 collective-permute-start.7
  7.2 2.1 %collective-permute-start.11 = (bf16[8,3072]{1,0:T(8,128)(2,1)S(1)}, bf16[8,3072]{1,0:T(8,128)(2,1)S(1)}, u32[]{:S(2)}, u32[]{:S(2)}) collective-permute-start(bf16[8,3072]{1,0:T(8,128)(2,1)S(1)} %collective-permute-done.10.refs_12_), channel_id=1, source_target_pairs={{0,2},{1,3},{4,0},{5,1},{8,4},{9,5},{12,8},{13,9},{14,12},{15,13},... | collective-permute-start | bytes 147464 | tf_op jit(solution)/shard_map/ppermute | solution.py:96
  9.3 0.3 collective-permute-done.refs_1_
  9.6 0.1 collective-permute-done.3.refs_4_
  9.7 1.9 %collective-permute-start.4 = (bf16[8,3072]{1,0:T(8,128)(2,1)S(1)}, bf16[8,3072]{1,0:T(8,128)(2,1)S(1)}, u32[]{:S(2)}, u32[]{:S(2)}) collective-permute-start(bf16[8,3072]{1,0:T(8,128)(2,1)S(1)} %collective-permute-done.3.refs_4_), channel_id=1, source_target_pairs={{0,2},{1,3},{4,0},{5,1},{8,4},{9,5},{12,8},{13,9},{14,12},{15,13},... | collective-permute-start | bytes 147464 | tf_op jit(solution)/shard_map/ppermute | solution.py:96
  11.6 0.1 collective-permute-start.8
  11.7 1.9 %collective-permute-start.12 = (bf16[8,3072]{1,0:T(8,128)(2,1)S(1)}, bf16[8,3072]{1,0:T(8,128)(2,1)S(1)}, u32[]{:S(2)}, u32[]{:S(2)}) collective-permute-start(bf16[8,3072]{1,0:T(8,128)(2,1)S(1)} %collective-permute-done.11.refs_13_), channel_id=1, source_target_pairs={{0,2},{1,3},{4,0},{5,1},{8,4},{9,5},{12,8},{13,9},{14,12},{15,13},... | collective-permute-start | bytes 147464 | tf_op jit(solution)/shard_map/ppermute | solution.py:96
  13.7 0.1 collective-permute-start.2
  13.8 2.1 %collective-permute-start.5 = (bf16[8,3072]{1,0:T(8,128)(2,1)S(1)}, bf16[8,3072]{1,0:T(8,128)(2,1)S(1)}, u32[]{:S(2)}, u32[]{:S(2)}) collective-permute-start(bf16[8,3072]{1,0:T(8,128)(2,1)S(1)} %collective-permute-done.4.refs_5_), channel_id=1, source_target_pairs={{0,2},{1,3},{4,0},{5,1},{8,4},{9,5},{12,8},{13,9},{14,12},{15,13},... | collective-permute-start | bytes 147464 | tf_op jit(solution)/shard_map/ppermute | solution.py:96
  15.9 0.2 collective-permute-done.8.refs_10_
  16.1 2.0 %collective-permute-start.13 = (bf16[8,3072]{1,0:T(8,128)(2,1)S(1)}, bf16[8,3072]{1,0:T(8,128)(2,1)S(1)}, u32[]{:S(2)}, u32[]{:S(2)}) collective-permute-start(bf16[8,3072]{1,0:T(8,128)(2,1)S(1)} %collective-permute-done.12.refs_14_), channel_id=1, source_target_pairs={{0,2},{1,3},{4,0},{5,1},{8,4},{9,5},{12,8},{13,9},{14,12},{15,13},... | collective-permute-start | bytes 147464 | tf_op jit(solution)/shard_map/ppermute | solution.py:96
  18.2 0.1 collective-permute-start.6
  18.3 1.9 %collective-permute-done.9.refs_11_ = bf16[8,3072]{1,0:T(8,128)(2,1)S(1)} collective-permute-done((bf16[8,3072]{1,0:T(8,128)(2,1)S(1)}, bf16[8,3072]{1,0:T(8,128)(2,1)S(1)}, u32[]{:S(2)}, u32[]{:S(2)}) %collective-permute-start.9) | collective-permute-done | bytes 49184 | tf_op jit(solution)/shard_map/ppermute | solution.py:94
  20.2 0.1 collective-permute-done.13.refs_15_
  20.3 1.9 %collective-permute-done.6.refs_7_ = bf16[8,3072]{1,0:T(8,128)(2,1)S(1)} collective-permute-done((bf16[8,3072]{1,0:T(8,128)(2,1)S(1)}, bf16[8,3072]{1,0:T(8,128)(2,1)S(1)}, u32[]{:S(2)}, u32[]{:S(2)}) %collective-permute-start.6) | collective-permute-done | bytes 49184 | tf_op jit(solution)/shard_map/ppermute | solution.py:94
  22.3 0.3 unpack.2.left
  22.6 0.1 collective-permute-start.14
  22.6 0.7 reshape.29.bias_ref
  23.3 0.7 convert_element_type.3
  24.0 4.0 %copy-done = bf16[8192,640]{1,0:T(8,128)(2,1)S(1)} copy-done((bf16[8192,640]{1,0:T(8,128)(2,1)S(1)}, bf16[8192,640]{1,0:T(8,128)(2,1)}, u32[]{:S(2)}) %copy-start) | copy-done | bytes 10485784
  28.0 3.6 %qkv_own.1 = (bf16[8,1024,640]{2,1,0:T(8,128)(2,1)S(1)}, f32[64,640]{1,0:T(8,128)S(1)}) custom-call(bf16[8,64,1024]{2,1,0:T(8,128)(2,1)S(1)} %unpack.2.left, bf16[8192,640]{1,0:T(8,128)(2,1)S(1)} %copy-done), custom_call_target="tpu_custom_call" | custom-call | flops 671088640 | bytes 10485760 | tf_op jit(solution)/shard_map/qkv_own/pallas_call | solution.py:241
  31.6 2.6 %qkv_project.1 = bf16[16,6,640]{2,1,0:T(8,128)(2,1)} custom-call(s32[1]{0:T(128)} %bitcast.me_ref, bf16[1,640]{1,0:T(2,128)(2,1)S(1)} %reshape.29.bias_ref, f32[64,640]{1,0:T(8,128)S(1)} %get-tuple-element.15.own_ref, bf16[8,64,1024]{2,1,0:T(8,128)(2,1)S(1)} %collective-permute-done.14.left, bf16[8,1024,640]{2,1,0:T(8,128)(2,1)S(1)} %get-tuple-element.16.held), custom_call_target="tpu_custom_call" | custom-call | tf_op jit(solution)/shard_map/qkv_project/pallas_call | solution.py:270
  34.2 5.2 %all-to-all-start = ((bf16[16,6,640]{2,1,0:T(8,128)(2,1)}), bf16[16,6,640]{2,1,0:T(8,128)(2,1)S(1)}, u32[]{:S(2)}, u32[]{:S(2)}) async-start(bf16[16,6,640]{2,1,0:T(8,128)(2,1)} %qkv_project.1), calls=%async_computation | async-start | bytes 327680 | tf_op jit(solution)/shard_map/all_to_all | solution.py:488
  39.4 0.1 fusion
  39.5 0.1 pad_maximum_fusion
  39.6 8.3 %all-to-all-done = bf16[16,6,640]{2,1,0:T(8,128)(2,1)S(1)} async-done(((bf16[16,6,640]{2,1,0:T(8,128)(2,1)}), bf16[16,6,640]{2,1,0:T(8,128)(2,1)S(1)}, u32[]{:S(2)}, u32[]{:S(2)}) %all-to-all-start) | async-done | bytes 122912 | tf_op jit(solution)/shard_map/all_to_all | solution.py:488
  47.9 2.3 %copy-done.2 = bf16[6,384,1024]{2,1,0:T(8,128)(2,1)S(1)} copy-done((bf16[6,384,1024]{2,1,0:T(8,128)(2,1)S(1)}, bf16[6,384,1024]{2,1,0:T(8,128)(2,1)}, u32[]{:S(2)}) %copy-start.2) | copy-done | bytes 4718616
  50.2 2.3 %copy-done.3 = bf16[6,384,1024]{2,1,0:T(8,128)(2,1)S(1)} copy-done((bf16[6,384,1024]{2,1,0:T(8,128)(2,1)S(1)}, bf16[6,384,1024]{2,1,0:T(8,128)(2,1)}, u32[]{:S(2)}) %copy-start.3) | copy-done | bytes 4718616
  52.6 7.8 %attend.1 = (bf16[8,3200]{1,0:T(8,128)(2,1)S(1)}, bf16[8,3072]{1,0:T(8,128)(2,1)S(1)}) custom-call(s32[6]{0:T(128)S(1)} %copy-done.8, s32[6]{0:T(128)S(1)} %copy-done.9, bf16[6,10240]{1,0:T(8,128)(2,1)S(1)} %bitcast.11, f32[6,128]{1,0:T(8,128)S(1)} %get-tuple-element.24.cos_ref, f32[6,128]{1,0:T(8,128)S(1)} %get-tuple-element.25.sin_ref, ...), custom_call_target="tpu_custom_call" | custom-call | tf_op jit(solution)/shard_map/attend/pallas_call | solution.py:367
  60.4 2.0 %collective-permute-start.25 = (bf16[8,3072]{1,0:T(8,128)(2,1)S(1)}, bf16[8,3072]{1,0:T(8,128)(2,1)S(1)}, u32[]{:S(2)}, u32[]{:S(2)}) collective-permute-start(bf16[8,3072]{1,0:T(8,128)(2,1)S(1)} %get-tuple-element.18.refs_8_), channel_id=1, source_target_pairs={{0,2},{1,3},{4,0},{5,1},{8,4},{9,5},{12,8},{13,9},{14,12},{15,13},... | collective-permute-start | bytes 147464 | tf_op jit(solution)/shard_map/ppermute | solution.py:96
  62.5 2.1 %collective-permute-done.15.refs_1_ = bf16[8,3200]{1,0:T(8,128)(2,1)S(1)} collective-permute-done((bf16[8,3200]{1,0:T(8,128)(2,1)S(1)}, bf16[8,3200]{1,0:T(8,128)(2,1)S(1)}, u32[]{:S(2)}, u32[]{:S(2)}) %collective-permute-start.15) | collective-permute-done | bytes 51232 | tf_op jit(solution)/shard_map/ppermute | solution.py:94
  64.5 1.1 collective-permute-start.22
  65.6 1.0 collective-permute-start.26
  66.6 0.3 collective-permute-done.18.refs_4_
  66.9 1.7 %collective-permute-start.19 = (bf16[8,3200]{1,0:T(8,128)(2,1)S(1)}, bf16[8,3200]{1,0:T(8,128)(2,1)S(1)}, u32[]{:S(2)}, u32[]{:S(2)}) collective-permute-start(bf16[8,3200]{1,0:T(8,128)(2,1)S(1)} %collective-permute-done.18.refs_4_), channel_id=1, source_target_pairs={{0,2},{1,3},{4,0},{5,1},{8,4},{9,5},{12,8},{13,9},{14,12},{15,13},... | collective-permute-start | bytes 153608 | tf_op jit(solution)/shard_map/ppermute | solution.py:96
  68.6 0.4 collective-permute-done.16.refs_2_
  69.0 1.1 collective-permute-done.22.refs_9_
  70.1 2.0 %collective-permute-start.27 = (bf16[8,3072]{1,0:T(8,128)(2,1)S(1)}, bf16[8,3072]{1,0:T(8,128)(2,1)S(1)}, u32[]{:S(2)}, u32[]{:S(2)}) collective-permute-start(bf16[8,3072]{1,0:T(8,128)(2,1)S(1)} %collective-permute-done.26.refs_13_), channel_id=1, source_target_pairs={{0,2},{1,3},{4,0},{5,1},{8,4},{9,5},{12,8},{13,9},{14,12},{15,13},... | collective-permute-start | bytes 147464 | tf_op jit(solution)/shard_map/ppermute | solution.py:96
  72.1 1.1 %collective-permute-start.20 = (bf16[8,3200]{1,0:T(8,128)(2,1)S(1)}, bf16[8,3200]{1,0:T(8,128)(2,1)S(1)}, u32[]{:S(2)}, u32[]{:S(2)}) collective-permute-start(bf16[8,3200]{1,0:T(8,128)(2,1)S(1)} %collective-permute-done.19.refs_5_), channel_id=1, source_target_pairs={{0,2},{1,3},{4,0},{5,1},{8,4},{9,5},{12,8},{13,9},{14,12},{15,13},... | collective-permute-start | bytes 153608 | tf_op jit(solution)/shard_map/ppermute | solution.py:96
  73.2 0.4 collective-permute-done.17.refs_3_
  73.6 0.5 collective-permute-start.21
  74.1 0.1 collective-permute-done.23.refs_10_
  74.2 0.4 collective-permute-start.24
  74.7 1.6 %collective-permute-start.28 = (bf16[8,3072]{1,0:T(8,128)(2,1)S(1)}, bf16[8,3072]{1,0:T(8,128)(2,1)S(1)}, u32[]{:S(2)}, u32[]{:S(2)}) collective-permute-start(bf16[8,3072]{1,0:T(8,128)(2,1)S(1)} %collective-permute-done.27.refs_14_), channel_id=1, source_target_pairs={{0,2},{1,3},{4,0},{5,1},{8,4},{9,5},{12,8},{13,9},{14,12},{15,13},... | collective-permute-start | bytes 147464 | tf_op jit(solution)/shard_map/ppermute | solution.py:96
  76.3 2.1 %collective-permute-done.24.refs_11_ = bf16[8,3072]{1,0:T(8,128)(2,1)S(1)} collective-permute-done((bf16[8,3072]{1,0:T(8,128)(2,1)S(1)}, bf16[8,3072]{1,0:T(8,128)(2,1)S(1)}, u32[]{:S(2)}, u32[]{:S(2)}) %collective-permute-start.24) | collective-permute-done | bytes 49184 | tf_op jit(solution)/shard_map/ppermute | solution.py:94
  78.3 0.4 collective-permute-done.28.refs_15_
  78.8 0.3 unpack.3.left.own
  79.1 0.1 collective-permute-start.29
  79.2 2.8 %collective-permute-done.29.left.other = bf16[9,64,1024]{2,1,0:T(8,128)(2,1)S(1)} collective-permute-done((bf16[9,64,1024]{2,1,0:T(8,128)(2,1)S(1)}, bf16[9,64,1024]{2,1,0:T(8,128)(2,1)S(1)}, u32[]{:S(2)}, u32[]{:S(2)}) %collective-permute-start.29) | collective-permute-done | bytes 1179680 | tf_op jit(solution)/shard_map/ppermute | solution.py:105
  82.0 2.1 %shrink.1 = bf16[16,32,128]{2,1,0:T(8,128)(2,1)} custom-call(s32[1]{0:T(128)} %bitcast.me_ref, bf16[2,16,8192]{2,1,0:T(8,128)(2,1)S(1)} %bitcast.12, bf16[9,64,1024]{2,1,0:T(8,128)(2,1)S(1)} %unpack.3.left.own, bf16[9,64,1024]{2,1,0:T(8,128)(2,1)S(1)} %collective-permute-done.29.left.other), custom_call_target="tpu_custom_call" | custom-call | tf_op jit(solution)/shard_map/shrink/pallas_call | solution.py:425
  84.1 3.8 %all-to-all-start.1 = ((bf16[16,32,128]{2,1,0:T(8,128)(2,1)}), bf16[16,32,128]{2,1,0:T(8,128)(2,1)S(1)}, u32[]{:S(2)}, u32[]{:S(2)}) async-start(bf16[16,32,128]{2,1,0:T(8,128)(2,1)} %shrink.1), calls=%async_computation.1 | async-start | bytes 262144 | tf_op jit(solution)/shard_map/all_to_all | solution.py:488
  87.9 3.4 %copy-done.1 = bf16[8192,512]{1,0:T(8,128)(2,1)S(1)} copy-done((bf16[8192,512]{1,0:T(8,128)(2,1)S(1)}, bf16[8192,512]{1,0:T(8,128)(2,1)}, u32[]{:S(2)}) %copy-start.1) | copy-done | bytes 8388632
  91.3 2.3 %base_own.1 = (bf16[8,1024,512]{2,1,0:T(8,128)(2,1)S(1)}, f32[64,512]{1,0:T(8,128)S(1)}) custom-call(bf16[9,64,1024]{2,1,0:T(8,128)(2,1)S(1)} %unpack.3.left.own, bf16[8192,512]{1,0:T(8,128)(2,1)S(1)} %copy-done.1), custom_call_target="tpu_custom_call" | custom-call | flops 536870912 | bytes 8388608 | tf_op jit(solution)/shard_map/base_own/pallas_call | solution.py:241
  93.6 1.6 %base_project.1.base_ref = f32[128,512]{1,0:T(8,128)S(1)} custom-call(s32[1]{0:T(128)} %bitcast.me_ref, f32[64,512]{1,0:T(8,128)S(1)} %get-tuple-element.19.own_ref, bf16[9,64,1024]{2,1,0:T(8,128)(2,1)S(1)} %collective-permute-done.29.left.other, bf16[8,1024,512]{2,1,0:T(8,128)(2,1)S(1)} %get-tuple-element.20.held), custom_call_target="tpu_custom_call" | custom-call | flops 536870912 | bytes 8388608 | tf_op jit(solution)/shard_map/base_project/pallas_call | solution.py:453
  95.2 0.6 all-to-all-done.1
  95.8 0.2 add_delta.1
  96.1 13.2 %all_to_all.15 = bf16[16,6,512]{2,1,0:T(8,128)(2,1)S(1)} all-to-all(bf16[16,6,512]{2,1,0:T(8,128)(2,1)S(1)} %add_delta.1), channel_id=1, replica_groups=mesh['group'=2,'tensor'=16] {'tensor'}, dimensions={0} | all-to-all | bytes 196608 | tf_op jit(solution)/shard_map/all_to_all | solution.py:488
  109.2 0.7 copy.13
  (37 shorter events, 0.3 us)
Async XLA Ops:
  0.0 0.9 copy-start.6
  0.9 0.7 copy-start.7
  2.0 5.2 %collective-permute-start.10 = (bf16[8,3072]{1,0:T(8,128)(2,1)S(1)}, bf16[8,3072]{1,0:T(8,128)(2,1)S(1)}, u32[]{:S(2)}, u32[]{:S(2)}) collective-permute-start(bf16[8,3072]{1,0:T(8,128)(2,1)S(1)} %get-tuple-element.14.refs_8_), channel_id=1, source_target_pairs={{0,2},{1,3},{4,0},{5,1},{8,4},{9,5},{12,8},{13,9},{14,12},{15,13},... | collective-permute-start | bytes 147464 | tf_op jit(solution)/shard_map/ppermute | solution.py:96
  5.0 4.6 %collective-permute-start = (bf16[8,3072]{1,0:T(8,128)(2,1)S(1)}, bf16[8,3072]{1,0:T(8,128)(2,1)S(1)}, u32[]{:S(2)}, u32[]{:S(2)}) collective-permute-start(bf16[8,3072]{1,0:T(8,128)(2,1)S(1)} %get-tuple-element.13.refs_0_), channel_id=1, source_target_pairs={{0,4},{1,5},{4,8},{5,9},{8,12},{9,13},{12,14},{13,15},{14,10},{15,... | collective-permute-start | bytes 147464 | tf_op jit(solution)/shard_map/ppermute | solution.py:94
  5.1 4.6 %collective-permute-start.3 = (bf16[8,3072]{1,0:T(8,128)(2,1)S(1)}, bf16[8,3072]{1,0:T(8,128)(2,1)S(1)}, u32[]{:S(2)}, u32[]{:S(2)}) collective-permute-start(bf16[8,3072]{1,0:T(8,128)(2,1)S(1)} %get-tuple-element.13.refs_0_), channel_id=1, source_target_pairs={{0,2},{1,3},{4,0},{5,1},{8,4},{9,5},{12,8},{13,9},{14,12},{15,13},... | collective-permute-start | bytes 147464 | tf_op jit(solution)/shard_map/ppermute | solution.py:96
  7.1 4.6 %collective-permute-start.7 = (bf16[8,3072]{1,0:T(8,128)(2,1)S(1)}, bf16[8,3072]{1,0:T(8,128)(2,1)S(1)}, u32[]{:S(2)}, u32[]{:S(2)}) collective-permute-start(bf16[8,3072]{1,0:T(8,128)(2,1)S(1)} %get-tuple-element.14.refs_8_), channel_id=1, source_target_pairs={{0,4},{1,5},{4,8},{5,9},{8,12},{9,13},{12,14},{13,15},{14,10},{15,... | collective-permute-start | bytes 147464 | tf_op jit(solution)/shard_map/ppermute | solution.py:94
  7.2 4.6 %collective-permute-start.11 = (bf16[8,3072]{1,0:T(8,128)(2,1)S(1)}, bf16[8,3072]{1,0:T(8,128)(2,1)S(1)}, u32[]{:S(2)}, u32[]{:S(2)}) collective-permute-start(bf16[8,3072]{1,0:T(8,128)(2,1)S(1)} %collective-permute-done.10.refs_12_), channel_id=1, source_target_pairs={{0,2},{1,3},{4,0},{5,1},{8,4},{9,5},{12,8},{13,9},{14,12},{15,13},... | collective-permute-start | bytes 147464 | tf_op jit(solution)/shard_map/ppermute | solution.py:96
  9.6 4.1 %collective-permute-start.1 = (bf16[8,3072]{1,0:T(8,128)(2,1)S(1)}, bf16[8,3072]{1,0:T(8,128)(2,1)S(1)}, u32[]{:S(2)}, u32[]{:S(2)}) collective-permute-start(bf16[8,3072]{1,0:T(8,128)(2,1)S(1)} %collective-permute-done.refs_1_), channel_id=1, source_target_pairs={{0,4},{1,5},{4,8},{5,9},{8,12},{9,13},{12,14},{13,15},{14,10},{15,... | collective-permute-start | bytes 147464 | tf_op jit(solution)/shard_map/ppermute | solution.py:94
  9.7 4.1 %collective-permute-start.4 = (bf16[8,3072]{1,0:T(8,128)(2,1)S(1)}, bf16[8,3072]{1,0:T(8,128)(2,1)S(1)}, u32[]{:S(2)}, u32[]{:S(2)}) collective-permute-start(bf16[8,3072]{1,0:T(8,128)(2,1)S(1)} %collective-permute-done.3.refs_4_), channel_id=1, source_target_pairs={{0,2},{1,3},{4,0},{5,1},{8,4},{9,5},{12,8},{13,9},{14,12},{15,13},... | collective-permute-start | bytes 147464 | tf_op jit(solution)/shard_map/ppermute | solution.py:96
  11.6 4.5 %collective-permute-start.8 = (bf16[8,3072]{1,0:T(8,128)(2,1)S(1)}, bf16[8,3072]{1,0:T(8,128)(2,1)S(1)}, u32[]{:S(2)}, u32[]{:S(2)}) collective-permute-start(bf16[8,3072]{1,0:T(8,128)(2,1)S(1)} %collective-permute-done.7.refs_9_), channel_id=1, source_target_pairs={{0,4},{1,5},{4,8},{5,9},{8,12},{9,13},{12,14},{13,15},{14,10},{15,... | collective-permute-start | bytes 147464 | tf_op jit(solution)/shard_map/ppermute | solution.py:94
  11.7 4.4 %collective-permute-start.12 = (bf16[8,3072]{1,0:T(8,128)(2,1)S(1)}, bf16[8,3072]{1,0:T(8,128)(2,1)S(1)}, u32[]{:S(2)}, u32[]{:S(2)}) collective-permute-start(bf16[8,3072]{1,0:T(8,128)(2,1)S(1)} %collective-permute-done.11.refs_13_), channel_id=1, source_target_pairs={{0,2},{1,3},{4,0},{5,1},{8,4},{9,5},{12,8},{13,9},{14,12},{15,13},... | collective-permute-start | bytes 147464 | tf_op jit(solution)/shard_map/ppermute | solution.py:96
  13.7 4.5 %collective-permute-start.2 = (bf16[8,3072]{1,0:T(8,128)(2,1)S(1)}, bf16[8,3072]{1,0:T(8,128)(2,1)S(1)}, u32[]{:S(2)}, u32[]{:S(2)}) collective-permute-start(bf16[8,3072]{1,0:T(8,128)(2,1)S(1)} %collective-permute-done.1.refs_2_), channel_id=1, source_target_pairs={{0,4},{1,5},{4,8},{5,9},{8,12},{9,13},{12,14},{13,15},{14,10},{15,... | collective-permute-start | bytes 147464 | tf_op jit(solution)/shard_map/ppermute | solution.py:94
  13.8 4.5 %collective-permute-start.5 = (bf16[8,3072]{1,0:T(8,128)(2,1)S(1)}, bf16[8,3072]{1,0:T(8,128)(2,1)S(1)}, u32[]{:S(2)}, u32[]{:S(2)}) collective-permute-start(bf16[8,3072]{1,0:T(8,128)(2,1)S(1)} %collective-permute-done.4.refs_5_), channel_id=1, source_target_pairs={{0,2},{1,3},{4,0},{5,1},{8,4},{9,5},{12,8},{13,9},{14,12},{15,13},... | collective-permute-start | bytes 147464 | tf_op jit(solution)/shard_map/ppermute | solution.py:96
  16.1 4.1 %collective-permute-start.9 = (bf16[8,3072]{1,0:T(8,128)(2,1)S(1)}, bf16[8,3072]{1,0:T(8,128)(2,1)S(1)}, u32[]{:S(2)}, u32[]{:S(2)}) collective-permute-start(bf16[8,3072]{1,0:T(8,128)(2,1)S(1)} %collective-permute-done.8.refs_10_), channel_id=1, source_target_pairs={{0,4},{1,5},{4,8},{5,9},{8,12},{9,13},{12,14},{13,15},{14,10},{15,... | collective-permute-start | bytes 147464 | tf_op jit(solution)/shard_map/ppermute | solution.py:94
  16.1 4.2 %collective-permute-start.13 = (bf16[8,3072]{1,0:T(8,128)(2,1)S(1)}, bf16[8,3072]{1,0:T(8,128)(2,1)S(1)}, u32[]{:S(2)}, u32[]{:S(2)}) collective-permute-start(bf16[8,3072]{1,0:T(8,128)(2,1)S(1)} %collective-permute-done.12.refs_14_), channel_id=1, source_target_pairs={{0,2},{1,3},{4,0},{5,1},{8,4},{9,5},{12,8},{13,9},{14,12},{15,13},... | collective-permute-start | bytes 147464 | tf_op jit(solution)/shard_map/ppermute | solution.py:96
  18.2 4.1 %collective-permute-start.6 = (bf16[8,3072]{1,0:T(8,128)(2,1)S(1)}, bf16[8,3072]{1,0:T(8,128)(2,1)S(1)}, u32[]{:S(2)}, u32[]{:S(2)}) collective-permute-start(bf16[8,3072]{1,0:T(8,128)(2,1)S(1)} %collective-permute-done.2.refs_3_), channel_id=1, source_target_pairs={{0,4},{1,5},{4,8},{5,9},{8,12},{9,13},{12,14},{13,15},{14,10},{15,... | collective-permute-start | bytes 147464 | tf_op jit(solution)/shard_map/ppermute | solution.py:94
  22.6 9.1 %collective-permute-start.14 = (bf16[8,64,1024]{2,1,0:T(8,128)(2,1)S(1)}, bf16[8,64,1024]{2,1,0:T(8,128)(2,1)S(1)}, u32[]{:S(2)}, u32[]{:S(2)}) collective-permute-start(bf16[8,64,1024]{2,1,0:T(8,128)(2,1)S(1)} %unpack.2.left), channel_id=1, source_target_pairs={{0,1},{1,0},{2,3},{3,2},{4,5},{5,4},{6,7},{7,6},{8,9},{9,8},{10,11... | collective-permute-start | bytes 3145736 | tf_op jit(solution)/shard_map/ppermute | solution.py:105
  24.0 4.0 %copy-start = (bf16[8192,640]{1,0:T(8,128)(2,1)S(1)}, bf16[8192,640]{1,0:T(8,128)(2,1)}, u32[]{:S(2)}) copy-start(bf16[8192,640]{1,0:T(8,128)(2,1)} %weight.2) | copy-start | bytes 31457284
  31.6 16.3 %copy-start.8 = (s32[6]{0:T(128)S(1)}, s32[6]{0:T(128)}, u32[]{:S(2)}) copy-start(s32[6]{0:T(128)} %len_ref.1) | copy-start | bytes 76
  31.6 16.3 %copy-start.9 = (s32[6]{0:T(128)S(1)}, s32[6]{0:T(128)}, u32[]{:S(2)}) copy-start(s32[6]{0:T(128)} %ids_ref.1) | copy-start | bytes 76
  31.6 50.4 %copy-start.4 = (bf16[2,8192,16]{1,2,0:T(8,128)(2,1)S(1)}, bf16[2,8192,16]{1,2,0:T(8,128)(2,1)}, u32[]{:S(2)}) copy-start(bf16[2,8192,16]{1,2,0:T(8,128)(2,1)} %param.20) | copy-start | bytes 1572868
  34.2 13.6 %all-to-all-start = ((bf16[16,6,640]{2,1,0:T(8,128)(2,1)}), bf16[16,6,640]{2,1,0:T(8,128)(2,1)S(1)}, u32[]{:S(2)}, u32[]{:S(2)}) async-start(bf16[16,6,640]{2,1,0:T(8,128)(2,1)} %qkv_project.1), calls=%async_computation | async-start | bytes 327680 | tf_op jit(solution)/shard_map/all_to_all | solution.py:488
  47.9 2.3 %copy-start.2 = (bf16[6,384,1024]{2,1,0:T(8,128)(2,1)S(1)}, bf16[6,384,1024]{2,1,0:T(8,128)(2,1)}, u32[]{:S(2)}) copy-start(bf16[6,384,1024]{2,1,0:T(8,128)(2,1)} %k_hbm.1) | copy-start | bytes 14155780
  50.2 2.3 %copy-start.3 = (bf16[6,384,1024]{2,1,0:T(8,128)(2,1)S(1)}, bf16[6,384,1024]{2,1,0:T(8,128)(2,1)}, u32[]{:S(2)}) copy-start(bf16[6,384,1024]{2,1,0:T(8,128)(2,1)} %v_hbm.1) | copy-start | bytes 14155780
  60.4 4.2 %collective-permute-start.15 = (bf16[8,3200]{1,0:T(8,128)(2,1)S(1)}, bf16[8,3200]{1,0:T(8,128)(2,1)S(1)}, u32[]{:S(2)}, u32[]{:S(2)}) collective-permute-start(bf16[8,3200]{1,0:T(8,128)(2,1)S(1)} %get-tuple-element.17.refs_0_), channel_id=1, source_target_pairs={{0,4},{1,5},{4,8},{5,9},{8,12},{9,13},{12,14},{13,15},{14,10},{15,... | collective-permute-start | bytes 153608 | tf_op jit(solution)/shard_map/ppermute | solution.py:94
  60.4 5.2 %collective-permute-start.25 = (bf16[8,3072]{1,0:T(8,128)(2,1)S(1)}, bf16[8,3072]{1,0:T(8,128)(2,1)S(1)}, u32[]{:S(2)}, u32[]{:S(2)}) collective-permute-start(bf16[8,3072]{1,0:T(8,128)(2,1)S(1)} %get-tuple-element.18.refs_8_), channel_id=1, source_target_pairs={{0,2},{1,3},{4,0},{5,1},{8,4},{9,5},{12,8},{13,9},{14,12},{15,13},... | collective-permute-start | bytes 147464 | tf_op jit(solution)/shard_map/ppermute | solution.py:96
  62.4 4.5 %collective-permute-start.18 = (bf16[8,3200]{1,0:T(8,128)(2,1)S(1)}, bf16[8,3200]{1,0:T(8,128)(2,1)S(1)}, u32[]{:S(2)}, u32[]{:S(2)}) collective-permute-start(bf16[8,3200]{1,0:T(8,128)(2,1)S(1)} %get-tuple-element.17.refs_0_), channel_id=1, source_target_pairs={{0,2},{1,3},{4,0},{5,1},{8,4},{9,5},{12,8},{13,9},{14,12},{15,13},... | collective-permute-start | bytes 153608 | tf_op jit(solution)/shard_map/ppermute | solution.py:96
  64.5 4.5 %collective-permute-start.16 = (bf16[8,3200]{1,0:T(8,128)(2,1)S(1)}, bf16[8,3200]{1,0:T(8,128)(2,1)S(1)}, u32[]{:S(2)}, u32[]{:S(2)}) collective-permute-start(bf16[8,3200]{1,0:T(8,128)(2,1)S(1)} %collective-permute-done.15.refs_1_), channel_id=1, source_target_pairs={{0,4},{1,5},{4,8},{5,9},{8,12},{9,13},{12,14},{13,15},{14,10},{15,... | collective-permute-start | bytes 153608 | tf_op jit(solution)/shard_map/ppermute | solution.py:94
  64.5 5.5 %collective-permute-start.22 = (bf16[8,3072]{1,0:T(8,128)(2,1)S(1)}, bf16[8,3072]{1,0:T(8,128)(2,1)S(1)}, u32[]{:S(2)}, u32[]{:S(2)}) collective-permute-start(bf16[8,3072]{1,0:T(8,128)(2,1)S(1)} %get-tuple-element.18.refs_8_), channel_id=1, source_target_pairs={{0,4},{1,5},{4,8},{5,9},{8,12},{9,13},{12,14},{13,15},{14,10},{15,... | collective-permute-start | bytes 147464 | tf_op jit(solution)/shard_map/ppermute | solution.py:94
  65.6 4.5 %collective-permute-start.26 = (bf16[8,3072]{1,0:T(8,128)(2,1)S(1)}, bf16[8,3072]{1,0:T(8,128)(2,1)S(1)}, u32[]{:S(2)}, u32[]{:S(2)}) collective-permute-start(bf16[8,3072]{1,0:T(8,128)(2,1)S(1)} %collective-permute-done.25.refs_12_), channel_id=1, source_target_pairs={{0,2},{1,3},{4,0},{5,1},{8,4},{9,5},{12,8},{13,9},{14,12},{15,13},... | collective-permute-start | bytes 147464 | tf_op jit(solution)/shard_map/ppermute | solution.py:96
  66.9 5.2 %collective-permute-start.19 = (bf16[8,3200]{1,0:T(8,128)(2,1)S(1)}, bf16[8,3200]{1,0:T(8,128)(2,1)S(1)}, u32[]{:S(2)}, u32[]{:S(2)}) collective-permute-start(bf16[8,3200]{1,0:T(8,128)(2,1)S(1)} %collective-permute-done.18.refs_4_), channel_id=1, source_target_pairs={{0,2},{1,3},{4,0},{5,1},{8,4},{9,5},{12,8},{13,9},{14,12},{15,13},... | collective-permute-start | bytes 153608 | tf_op jit(solution)/shard_map/ppermute | solution.py:96
  69.0 4.6 %collective-permute-start.17 = (bf16[8,3200]{1,0:T(8,128)(2,1)S(1)}, bf16[8,3200]{1,0:T(8,128)(2,1)S(1)}, u32[]{:S(2)}, u32[]{:S(2)}) collective-permute-start(bf16[8,3200]{1,0:T(8,128)(2,1)S(1)} %collective-permute-done.16.refs_2_), channel_id=1, source_target_pairs={{0,4},{1,5},{4,8},{5,9},{8,12},{9,13},{12,14},{13,15},{14,10},{15,... | collective-permute-start | bytes 153608 | tf_op jit(solution)/shard_map/ppermute | solution.py:94
  70.1 4.2 %collective-permute-start.23 = (bf16[8,3072]{1,0:T(8,128)(2,1)S(1)}, bf16[8,3072]{1,0:T(8,128)(2,1)S(1)}, u32[]{:S(2)}, u32[]{:S(2)}) collective-permute-start(bf16[8,3072]{1,0:T(8,128)(2,1)S(1)} %collective-permute-done.22.refs_9_), channel_id=1, source_target_pairs={{0,4},{1,5},{4,8},{5,9},{8,12},{9,13},{12,14},{13,15},{14,10},{15,... | collective-permute-start | bytes 147464 | tf_op jit(solution)/shard_map/ppermute | solution.py:94
  70.1 4.6 %collective-permute-start.27 = (bf16[8,3072]{1,0:T(8,128)(2,1)S(1)}, bf16[8,3072]{1,0:T(8,128)(2,1)S(1)}, u32[]{:S(2)}, u32[]{:S(2)}) collective-permute-start(bf16[8,3072]{1,0:T(8,128)(2,1)S(1)} %collective-permute-done.26.refs_13_), channel_id=1, source_target_pairs={{0,2},{1,3},{4,0},{5,1},{8,4},{9,5},{12,8},{13,9},{14,12},{15,13},... | collective-permute-start | bytes 147464 | tf_op jit(solution)/shard_map/ppermute | solution.py:96
  72.1 6.2 %collective-permute-start.20 = (bf16[8,3200]{1,0:T(8,128)(2,1)S(1)}, bf16[8,3200]{1,0:T(8,128)(2,1)S(1)}, u32[]{:S(2)}, u32[]{:S(2)}) collective-permute-start(bf16[8,3200]{1,0:T(8,128)(2,1)S(1)} %collective-permute-done.19.refs_5_), channel_id=1, source_target_pairs={{0,2},{1,3},{4,0},{5,1},{8,4},{9,5},{12,8},{13,9},{14,12},{15,13},... | collective-permute-start | bytes 153608 | tf_op jit(solution)/shard_map/ppermute | solution.py:96
  73.6 5.2 %collective-permute-start.21 = (bf16[8,3200]{1,0:T(8,128)(2,1)S(1)}, bf16[8,3200]{1,0:T(8,128)(2,1)S(1)}, u32[]{:S(2)}, u32[]{:S(2)}) collective-permute-start(bf16[8,3200]{1,0:T(8,128)(2,1)S(1)} %collective-permute-done.17.refs_3_), channel_id=1, source_target_pairs={{0,4},{1,5},{4,8},{5,9},{8,12},{9,13},{12,14},{13,15},{14,10},{15,... | collective-permute-start | bytes 153608 | tf_op jit(solution)/shard_map/ppermute | solution.py:94
  74.2 4.1 %collective-permute-start.24 = (bf16[8,3072]{1,0:T(8,128)(2,1)S(1)}, bf16[8,3072]{1,0:T(8,128)(2,1)S(1)}, u32[]{:S(2)}, u32[]{:S(2)}) collective-permute-start(bf16[8,3072]{1,0:T(8,128)(2,1)S(1)} %collective-permute-done.23.refs_10_), channel_id=1, source_target_pairs={{0,4},{1,5},{4,8},{5,9},{8,12},{9,13},{12,14},{13,15},{14,10},{15,... | collective-permute-start | bytes 147464 | tf_op jit(solution)/shard_map/ppermute | solution.py:94
  74.7 4.1 %collective-permute-start.28 = (bf16[8,3072]{1,0:T(8,128)(2,1)S(1)}, bf16[8,3072]{1,0:T(8,128)(2,1)S(1)}, u32[]{:S(2)}, u32[]{:S(2)}) collective-permute-start(bf16[8,3072]{1,0:T(8,128)(2,1)S(1)} %collective-permute-done.27.refs_14_), channel_id=1, source_target_pairs={{0,2},{1,3},{4,0},{5,1},{8,4},{9,5},{12,8},{13,9},{14,12},{15,13},... | collective-permute-start | bytes 147464 | tf_op jit(solution)/shard_map/ppermute | solution.py:96
  79.1 2.9 %collective-permute-start.29 = (bf16[9,64,1024]{2,1,0:T(8,128)(2,1)S(1)}, bf16[9,64,1024]{2,1,0:T(8,128)(2,1)S(1)}, u32[]{:S(2)}, u32[]{:S(2)}) collective-permute-start(bf16[9,64,1024]{2,1,0:T(8,128)(2,1)S(1)} %unpack.3.left.own), channel_id=1, source_target_pairs={{0,1},{1,0},{2,3},{3,2},{4,5},{5,4},{6,7},{7,6},{8,9},{9,8},{10,11... | collective-permute-start | bytes 3538952 | tf_op jit(solution)/shard_map/ppermute | solution.py:105
  84.1 11.7 %all-to-all-start.1 = ((bf16[16,32,128]{2,1,0:T(8,128)(2,1)}), bf16[16,32,128]{2,1,0:T(8,128)(2,1)S(1)}, u32[]{:S(2)}, u32[]{:S(2)}) async-start(bf16[16,32,128]{2,1,0:T(8,128)(2,1)} %shrink.1), calls=%async_computation.1 | async-start | bytes 262144 | tf_op jit(solution)/shard_map/all_to_all | solution.py:488
  87.9 3.4 %copy-start.1 = (bf16[8192,512]{1,0:T(8,128)(2,1)S(1)}, bf16[8192,512]{1,0:T(8,128)(2,1)}, u32[]{:S(2)}) copy-start(bf16[8192,512]{1,0:T(8,128)(2,1)} %weight.3) | copy-start | bytes 25165828
  91.3 4.6 %copy-start.5 = (bf16[32,16,512]{2,1,0:T(8,128)(2,1)S(1)}, bf16[32,16,512]{2,1,0:T(8,128)(2,1)}, u32[]{:S(2)}) copy-start(bf16[32,16,512]{2,1,0:T(8,128)(2,1)} %param.21) | copy-start | bytes 1572868

commit v3 on v2

--- a/solution.py
+++ b/solution.py
@@ -17,7 +17,6 @@
 ROPE_BASE = 1000000.0
 
 BLOCKS = 8
-HALF = BLOCKS // 2
 LANES = 128
 MIB = 1 << 20
 
@@ -37,32 +36,21 @@
     return chips // inner, inner
 
 
-def ring_order(chips):
-    outer, inner = factors(chips)
-    if inner < 2 or outer % 2:
-        return list(range(chips))
-    order = [a * inner for a in range(outer)]
-    for turn, a in enumerate(reversed(range(outer))):
-        steps = range(1, inner) if turn % 2 == 0 else range(inner - 1, 0, -1)
-        order += [a * inner + b for b in steps]
-    return order
-
-
-def lookup(table, index):
-    value = jnp.int32(table[0])
-    for at in range(1, len(table)):
-        value = jnp.where(index == at, jnp.int32(table[at]), value)
-    return value
-
-
 def slot_chips(devices, me):
-    chips = devices // 2
-    order = ring_order(chips)
-    place_of = [order.index(chip) for chip in range(chips)]
-    place = lookup(place_of, lax.div(me, 2))
-    ahead = chips // 2
-    shifts = [-j for j in range(ahead)] + [j for j in range(1, chips - ahead + 1)]
-    return [lookup(order, lax.rem(place + shift + chips, chips)) for shift in shifts]
+    outer, inner = factors(devices // 2)
+    chip = lax.div(me, 2)
+    a, b = lax.div(chip, inner), lax.rem(chip, inner)
+    return [
+        partner(a, k, outer, -1) * inner + partner(b, m, inner, -1)
+        for m in range(inner)
+        for k in range(outer)
+    ]
+
+
+def partner(at, step, size, sign=1):
+    if size & (size - 1) == 0:
+        return at ^ step
+    return (at + sign * step + size) % size
 
 
 def steps(count, unrolled, body):
@@ -73,43 +61,33 @@
         lax.fori_loop(0, count, lambda i, _: (body(i), 0)[1], 0)
 
 
-def gather_chunks(halves, devices):
-    chips = devices // 2
-    order = ring_order(chips)
-    ahead = chips // 2
-
-    def ring(step):
+def gather_chunks(chunk, devices):
+    outer, inner = factors(devices // 2)
+
+    def pairs(k, m):
         return [
-            (2 * order[p] + core, 2 * order[(p + step) % chips] + core)
-            for p in range(chips)
-            for core in range(2)
+            (d, 2 * (partner(d // 2 // inner, k, outer) * inner + partner(d // 2 % inner, m, inner)) + d % 2)
+            for d in range(devices)
         ]
 
-    up, down = ring(1), ring(-1)
-    far = [ahead, chips - ahead - 1], [ahead - 1, chips - ahead]
-    behind, front = [[half] for half in halves], [[half] for half in halves]
-    for j in range(1, max(ahead, chips - ahead) + 1):
-        for h in (0, 1):
-            if j <= far[h][0]:
-                behind[h].append(lax.ppermute(behind[h][-1], "tensor", up))
-            if j <= far[h][1]:
-                front[h].append(lax.ppermute(front[h][-1], "tensor", down))
-    slots = []
-    for h in (0, 1):
-        near = behind[h][:ahead] + front[h][1 : chips - ahead]
-        slots.append(near + [behind[h][ahead] if h == 0 else front[h][chips - ahead]])
-    return slots
+    line = [chunk] + [lax.ppermute(chunk, "tensor", pairs(k, 0)) for k in range(1, outer)]
+    slots = {}
+    for k in range(outer):
+        for m in range(1, inner):
+            slots[k, m] = lax.ppermute(line[k], "tensor", pairs(0, m))
+    for k in range(outer):
+        slots[k, 0] = line[k]
+    return [slots[k, m] for m in range(inner) for k in range(outer)]
 
 
 def across(x, devices):
     return lax.ppermute(x, "tensor", [(d, d ^ 1) for d in range(devices)])
 
 
-def write_half(stage, h, rows, out_ref):
+def write_chunk(stage, rows, out_ref):
     block = stage.shape[1]
-    for g in range(HALF * rows // 8):
-        at = h * HALF * rows + 8 * g
-        out_ref[:, g * block : (g + 1) * block] = stage[at : at + 8, :].astype(jnp.bfloat16)
+    for g in range(BLOCKS * rows // 8):
+        out_ref[:, g * block : (g + 1) * block] = stage[8 * g : 8 * g + 8, :].astype(jnp.bfloat16)
 
 
 def write_ids(ids_ref, rows, out_ref):
@@ -120,7 +98,7 @@
     out_ref[:, out_ref.shape[1] - LANES :] = ids.astype(jnp.bfloat16)
 
 
-def norm_kernel(x_hbm, gain_hbm, first_ref, second_ref, x_ref, gain_ref, sems, stage):
+def norm_kernel(x_hbm, gain_hbm, out_ref, x_ref, gain_ref, sems, stage):
     copies = [
         pltpu.make_async_copy(x_hbm, x_ref, sems.at[0]),
         pltpu.make_async_copy(gain_hbm, gain_ref, sems.at[1]),
@@ -141,18 +119,16 @@
         gain = gain_ref[c : c + 1, :].astype(jnp.float32)
         j, lane = c * LANES // block, c * LANES % block
         stage[j * rows : (j + 1) * rows, lane : lane + LANES] = x * factor * gain
-    write_half(stage, 0, rows, first_ref)
-    write_half(stage, 1, rows, second_ref)
+    write_chunk(stage, rows, out_ref)
 
 
 def norm_chunk(hidden, gain):
     rows, width = hidden.shape
-    half = jax.ShapeDtypeStruct((8, rows * width // 16), jnp.bfloat16)
     return pl.pallas_call(
         norm_kernel,
-        out_shape=(half, half),
+        out_shape=jax.ShapeDtypeStruct((8, rows * width // 8), jnp.bfloat16),
         in_specs=[HBM, HBM],
-        out_specs=(VMEM, VMEM),
+        out_specs=VMEM,
         scratch_shapes=[
             pltpu.VMEM((rows, width), jnp.bfloat16),
             pltpu.VMEM((width // LANES, LANES), jnp.bfloat16),
@@ -165,51 +141,46 @@
 
 
 def unpack_kernel(chips, rows, with_ids, *refs):
-    firsts, seconds = refs[:chips], refs[chips : 2 * chips]
-    left, stage = refs[2 * chips :]
+    chunks = refs[:chips]
+    left, stage = refs[chips:]
     block = stage.shape[-1]
-    per_half = HALF * rows
     small = chips <= 8
     for pair in range(chips // 2):
         turn = pair % 2
         for place in range(2):
-            for h, halves in ((0, firsts), (1, seconds)):
-                chunk = halves[2 * pair + place]
-
-                def widen(g, chunk=chunk, place=place, h=h):
-                    lane = g * block if small else pl.multiple_of(g * block, block)
-                    at = h * per_half + 8 * g
-                    at = at if small else pl.multiple_of(at, 8)
-                    stage[turn, place, pl.ds(at, 8), :] = chunk[:, pl.ds(lane, block)].astype(
-                        jnp.float32
-                    )
-
-                steps(per_half // 8, small, widen)
-
+            chunk = chunks[2 * pair + place]
+
+            def widen(g, chunk=chunk, turn=turn, place=place):
+                lane = g * block if small else pl.multiple_of(g * block, block)
+                at = 8 * g if small else pl.multiple_of(8 * g, 8)
+                wide = chunk[:, pl.ds(lane, block)].astype(jnp.float32)
+                stage[turn, place, pl.ds(at, 8), :] = wide
+
+            steps(BLOCKS * rows // 8, small, widen)
         for j in range(BLOCKS):
             both = [stage[turn, place, j * rows : j * rows + 8, :] for place in range(2)]
             left[j, 16 * pair : 16 * pair + 16, :] = jnp.concatenate(both, axis=0).astype(
                 jnp.bfloat16
             )
         if with_ids:
-            both = [firsts[2 * pair + place][:, per_half // 8 * block :] for place in range(2)]
+            at = BLOCKS * rows // 8 * block
+            both = [chunks[2 * pair + place][:, at : at + LANES] for place in range(2)]
             both = jnp.concatenate([ids.astype(jnp.float32) for ids in both], axis=0)
             left[BLOCKS, 16 * pair : 16 * pair + 16, :LANES] = both.astype(jnp.bfloat16)
 
 
-def unpack(halves, rows, width, with_ids):
-    firsts, seconds = halves
-    chips = len(firsts)
+def unpack(chunks, rows, width, with_ids):
+    chips = len(chunks)
     block = width // BLOCKS
     return pl.pallas_call(
         functools.partial(unpack_kernel, chips, rows, with_ids),
         out_shape=jax.ShapeDtypeStruct((BLOCKS + with_ids, chips * 8, block), jnp.bfloat16),
-        in_specs=[VMEM] * (2 * chips),
+        in_specs=[VMEM] * chips,
         out_specs=VMEM,
         scratch_shapes=[pltpu.VMEM((2, 2, BLOCKS * rows + 8, block), jnp.float32)],
         compiler_params=params(32),
         name="unpack",
-    )(*firsts, *seconds)
+    )(*chunks)
 
 
 def fetch(weight, held, sems):
@@ -235,7 +206,7 @@
     multiply(left, held, acc, fetch(weight, held, sems))
 
 
-def own_rows(left, weight, name):
+def own_rows(left, weight, mib, name):
     width, cols = weight.shape
     rows = left.shape[1]
     return pl.pallas_call(
@@ -247,7 +218,7 @@
         in_specs=[VMEM, HBM],
         out_specs=(VMEM, VMEM),
         scratch_shapes=[pltpu.SemaphoreType.DMA((BLOCKS,))],
-        compiler_params=params(24),
+        compiler_params=params(mib),
         cost_estimate=pl.CostEstimate(
             flops=2 * rows * width * cols, bytes_accessed=width * cols * 2, transcendentals=0
         ),
@@ -278,6 +249,31 @@
     )(me, bias.reshape(1, cols), own, left, held)
 
 
+def hold_kernel(after, k_hbm, v_hbm, keys, values, sems):
+    copies = [
+        pltpu.make_async_copy(k_hbm, keys, sems.at[0]),
+        pltpu.make_async_copy(v_hbm, values, sems.at[1]),
+    ]
+    for copy in copies:
+        copy.start()
+    for copy in copies:
+        copy.wait()
+
+
+def hold_caches(after, keys, values):
+    cache = jax.ShapeDtypeStruct(keys.shape, keys.dtype)
+    return pl.pallas_call(
+        hold_kernel,
+        out_shape=(cache, cache),
+        in_specs=[HBM, HBM, HBM],
+        out_specs=(VMEM, VMEM),
+        scratch_shapes=[pltpu.SemaphoreType.DMA((2,))],
+        compiler_params=params(43),
+        cost_estimate=pl.CostEstimate(flops=0, bytes_accessed=8 * keys.size, transcendentals=0),
+        name="hold_caches",
+    )(after, keys, values)
+
+
 def attend_kernel(
     rows,
     len_ref,
@@ -285,38 +281,30 @@
     qkv_ref,
     cos_ref,
     sin_ref,
-    k_hbm,
-    v_hbm,
-    first_ref,
-    second_ref,
     keys,
     values,
-    sems,
+    out_ref,
     heads,
     mixed,
     stage,
 ):
     total_heads = QUERY_HEADS + 2 * KVH
     half = HEAD_SIZE // 2
-    for r in range(rows):
-        pltpu.make_async_copy(k_hbm.at[r], keys.at[r], sems.at[0, r]).start()
-        pltpu.make_async_copy(v_hbm.at[r], values.at[r], sems.at[1, r]).start()
     for h in range(total_heads):
         tile = qkv_ref[:, h * HEAD_SIZE : (h + 1) * HEAD_SIZE].astype(jnp.float32)
         heads[pl.ds(h, rows, stride=total_heads), :] = tile
     scale = 1.0 / HEAD_SIZE**0.5
 
-    def one_row(r, carry):
-        base = pl.multiple_of(r * total_heads, 8)
-        turned = heads[pl.ds(base, QUERY_HEADS + KVH), :]
-        cosine = cos_ref[pl.ds(r, 1), :]
-        sine = sin_ref[pl.ds(r, 1), :]
+    for r in range(rows):
+        base = r * total_heads
+        turned = heads[base : base + QUERY_HEADS + KVH, :]
+        cosine = cos_ref[r : r + 1, :]
+        sine = sin_ref[r : r + 1, :]
         turned = (turned * cosine + pltpu.roll(turned, half, 1) * sine).astype(jnp.bfloat16)
         query = turned[:QUERY_HEADS]
         query_f = query.astype(jnp.float32)
         new_key = turned[QUERY_HEADS:].astype(jnp.float32)
-        new_value = heads[pl.ds(base + QUERY_HEADS + KVH, KVH), :]
-        pltpu.make_async_copy(k_hbm.at[r], keys.at[r], sems.at[0, r]).wait()
+        new_value = heads[base + QUERY_HEADS + KVH : base + total_heads, :]
         scores = []
         own = []
         for k in range(KVH):
@@ -337,45 +325,33 @@
         total = jnp.sum(expo, axis=-1, keepdims=True) + expo_own
         weight = (expo / total).astype(jnp.bfloat16)
         weight_own = (expo_own / total).astype(jnp.bfloat16).astype(jnp.float32)
-        pltpu.make_async_copy(v_hbm.at[r], values.at[r], sems.at[1, r]).wait()
         for k in range(KVH):
             mine = slice(k * GROUPS, (k + 1) * GROUPS)
             value = values[r, :, k * HEAD_SIZE : (k + 1) * HEAD_SIZE]
             part = jnp.dot(weight[mine], value, preferred_element_type=jnp.float32)
             part = part + weight_own[mine] * new_value[k : k + 1]
-            at = pl.multiple_of(r * QUERY_HEADS + k * GROUPS, 8)
-            mixed[pl.ds(at, GROUPS), :] = part
-        return carry
-
-    lax.fori_loop(0, rows, one_row, 0)
+            at = r * QUERY_HEADS + k * GROUPS
+            mixed[at : at + GROUPS, :] = part
     per_block = QUERY_HEADS // BLOCKS
     for h in range(QUERY_HEADS):
         j, lane = h // per_block, h % per_block
         stage[j * rows : (j + 1) * rows, lane * HEAD_SIZE : (lane + 1) * HEAD_SIZE] = mixed[
             pl.ds(h, rows, stride=QUERY_HEADS), :
         ]
-    write_half(stage, 0, rows, first_ref)
-    write_half(stage, 1, rows, second_ref)
-    write_ids(ids_ref, rows, first_ref)
+    write_chunk(stage, rows, out_ref)
+    write_ids(ids_ref, rows, out_ref)
 
 
 def attend(lengths, ids, qkv, cosine, sine, keys, values):
     rows, capacity, width = keys.shape
     total_heads = QUERY_HEADS + 2 * KVH
     features = QUERY_HEADS * HEAD_SIZE
-    size = rows * features // 16
     return pl.pallas_call(
         functools.partial(attend_kernel, rows),
-        out_shape=(
-            jax.ShapeDtypeStruct((8, size + LANES), jnp.bfloat16),
-            jax.ShapeDtypeStruct((8, size), jnp.bfloat16),
-        ),
-        in_specs=[SMEM, SMEM, VMEM, VMEM, VMEM, HBM, HBM],
-        out_specs=(VMEM, VMEM),
+        out_shape=jax.ShapeDtypeStruct((8, rows * features // 8 + LANES), jnp.bfloat16),
+        in_specs=[SMEM, SMEM, VMEM, VMEM, VMEM, VMEM, VMEM],
+        out_specs=VMEM,
         scratch_shapes=[
-            pltpu.VMEM(keys.shape, jnp.bfloat16),
-            pltpu.VMEM(keys.shape, jnp.bfloat16),
-            pltpu.SemaphoreType.DMA((2, rows)),
             pltpu.VMEM((rows * total_heads, HEAD_SIZE), jnp.float32),
             pltpu.VMEM((rows * QUERY_HEADS, HEAD_SIZE), jnp.float32),
             pltpu.VMEM((BLOCKS * rows, features // BLOCKS), jnp.float32),
@@ -385,24 +361,57 @@
     )(lengths, ids, qkv, cosine, sine, keys, values)
 
 
-def shrink_kernel(devices, me_ref, down_ref, own, other, coords_ref, ids, place_of, total):
-    me = me_ref[0]
+def times_down(down_ref, left, write):
     stored, rank, features = down_ref.shape
     block = features // BLOCKS
+    for s in range(stored):
+        part = jnp.zeros((rank, left.shape[1]), jnp.float32)
+        for j in range(BLOCKS):
+            part += lax.dot_general(
+                down_ref[s, :, j * block : (j + 1) * block],
+                left[j],
+                (((1,), (1,)), ((), ())),
+                preferred_element_type=jnp.float32,
+            )
+        write(slice(s * rank, (s + 1) * rank), part)
+
+
+def shrink_own_kernel(down_ref, left, out_ref):
+    def write(at, part):
+        out_ref[at, :] = part
+
+    times_down(down_ref, left, write)
+
+
+def shrink_own(left, down):
+    stored, rank, features = down.shape
+    return pl.pallas_call(
+        shrink_own_kernel,
+        out_shape=jax.ShapeDtypeStruct((stored * rank, left.shape[1]), jnp.float32),
+        in_specs=[VMEM, VMEM],
+        out_specs=VMEM,
+        compiler_params=params(48),
+        cost_estimate=pl.CostEstimate(
+            flops=2 * left.size * stored * rank, bytes_accessed=2 * left.size, transcendentals=0
+        ),
+        name="shrink_own",
+    )(down, left)
+
+
+def shrink_kernel(
+    devices, me_ref, down_ref, own_part, own, other, coords_ref, ids, place_of, total
+):
+    me = me_ref[0]
+    stored, rank, _ = down_ref.shape
     rows = own.shape[1]
+    total[:, :rows] = own_part[...]
+
+    def write(at, part):
+        total[at, rows:] = part
+
+    times_down(down_ref, other, write)
     for c, left in enumerate((own, other)):
-        mine = slice(c * rows, (c + 1) * rows)
-        for s in range(stored):
-            part = jnp.zeros((rank, rows), jnp.float32)
-            for j in range(BLOCKS):
-                part += lax.dot_general(
-                    down_ref[s, :, j * block : (j + 1) * block],
-                    left[j],
-                    (((1,), (1,)), ((), ())),
-                    preferred_element_type=jnp.float32,
-                )
-            total[s * rank : (s + 1) * rank, mine] = part
-        ids[mine, :] = left[BLOCKS, :, :LANES].astype(jnp.float32)
+        ids[c * rows : (c + 1) * rows, :] = left[BLOCKS, :, :LANES].astype(jnp.float32)
     row_ids = jnp.transpose(ids[...])[: stored * rank, :].astype(jnp.int32)
     adapter = lax.broadcasted_iota(jnp.int32, total.shape, 0) // rank + me * stored
     coords = jnp.where(row_ids == adapter, total[...], 0.0).astype(jnp.bfloat16)
@@ -419,13 +428,13 @@
         coords_ref[d] = coords
 
 
-def shrink(me, own, other, down, devices):
+def shrink(me, own_part, own, other, down, devices):
     stored, rank, features = down.shape
     rows = devices * 8
     return pl.pallas_call(
         functools.partial(shrink_kernel, devices),
         out_shape=jax.ShapeDtypeStruct((devices, stored * rank, rows), jnp.bfloat16),
-        in_specs=[SMEM, VMEM, VMEM, VMEM],
+        in_specs=[SMEM, VMEM, VMEM, VMEM, VMEM],
         out_specs=VMEM,
         scratch_shapes=[
             pltpu.VMEM((rows, LANES), jnp.float32),
@@ -434,7 +443,7 @@
         ],
         compiler_params=params(48),
         name="shrink",
-    )(me, down, own, other)
+    )(me, down, own_part, own, other)
 
 
 def base_kernel(devices, me_ref, own_ref, left, held, out_ref, acc):
@@ -518,19 +527,20 @@
     down = jnp.transpose(adapter_down_weight, (0, 2, 1))
     up = adapter_up_weight.reshape(-1, adapter_up_weight.shape[2])
 
-    halves = gather_chunks(norm_chunk(hidden, input_norm_scale), devices)
-    mine = unpack(halves, rows, hidden.shape[1], False)
+    chunks = gather_chunks(norm_chunk(hidden, input_norm_scale), devices)
+    mine = unpack(chunks, rows, hidden.shape[1], False)
     theirs = across(mine, devices)
-    held, own = own_rows(mine, query_key_value_weight, "qkv_own")
+    held, own = own_rows(mine, query_key_value_weight, 40, "qkv_own")
     qkv = qkv_project(me, own, theirs, held, projection_bias, devices, rows)
+    keys, values = hold_caches(qkv, rotated_key_cache, past_value_cache)
     qkv = per_row(exchange(qkv))
-    halves = attend(
-        lengths, row_adapter_index, qkv, cosine, sine, rotated_key_cache, past_value_cache
-    )
-    mine = unpack(gather_chunks(halves, devices), rows, QUERY_HEADS * HEAD_SIZE, True)
+    chunk = attend(lengths, row_adapter_index, qkv, cosine, sine, keys, values)
+    chunks = gather_chunks(chunk, devices)
+    mine = unpack(chunks, rows, QUERY_HEADS * HEAD_SIZE, True)
     theirs = across(mine, devices)
-    held, own = own_rows(mine, output_weight, "base_own")
-    coords = exchange(shrink(me, mine, theirs, down, devices))
+    own_part = shrink_own(mine, down)
+    coords = exchange(shrink(me, own_part, mine, theirs, down, devices))
+    held, own = own_rows(mine, output_weight, 43, "base_own")
     base = base_project(me, own, theirs, held, devices)
     coords = coords.reshape(-1, coords.shape[2])
     return per_row(exchange(add_delta(base, coords, up, rows)))

time: 110 us -> 102 us (0.927)
  starting transfers between devices: 36.3 us -> 27.4 us
  Pallas kernels: 21.2 us -> 24.7 us
  local copies, waits for them, and re-layouts: 15 us -> 12 us
  blocking collectives: 13.2 us -> 11.2 us
  waiting for transfers between devices: 23.2 us -> 24.8 us
    ppermute x28 -> x14, starting transfers between devices: 27.2 us -> 18.5 us  [the longest x6 10.1 us: gather_chunks(): lax.ppermute(chunk, 'tensor', pairs(k, 0))]
    ppermute x28 -> x14, waiting for transfers between devices: 11.4 us -> 19.9 us  [the longest x6 11.8 us: gather_chunks(): lax.ppermute(chunk, 'tensor', pairs(k, 0))]
    all_to_all x2, waiting for transfers between devices: 8.88 us -> 2.69 us  [exchange(): lax.all_to_all(parts, 'tensor', split_axis=0, concat_axis=0, tiled=True)]
    unnamed x21, local copies, waits for them, and re-layouts: 14.3 us -> 11.3 us
    pallas_call x2, Pallas kernels: 5.93 us -> 8.22 us  [own_rows(): pl.pallas_call(own_kernel, out_shape=(jax.ShapeDtypeStruct((BLOCKS, width...]
    all_to_all x1, blocking collectives: 13.2 us -> 11.2 us  [exchange(): lax.all_to_all(parts, 'tensor', split_axis=0, concat_axis=0, tiled=True)]
    pallas_call x2 -> x4, Pallas kernels: 8.16 us -> 9.96 us  [the longest x1 5.14 us: attend(): pl.pallas_call(functools.partial(attend_kernel, rows), out_shape=jax.Shap...]
  transfers between devices with their start and end apart: 32 -> 18, of which waited for: 17 -> 9; matrix products, arithmetic and copies ran while one was open for 1% -> 2% of each run, Pallas kernels for 7% -> 14%
where the time goes in v3:
time: 102 us; the launch traced here: 101 us
  starting transfers between devices  27.4 us (27%)
  waiting for transfers between devices  24.8 us (24%)
  Pallas kernels  24.7 us (24%)
  local copies, waits for them, and re-layouts  12 us (12%)
  blocking collectives  11.2 us (11%)
    ppermute x6, waiting for transfers between devices, gather_chunks(): lax.ppermute(chunk, 'tensor', pairs(k, 0))  11.8 us
    unnamed x21, local copies, waits for them, and re-layouts  11.3 us
    all_to_all x1, blocking collectives, exchange(): lax.all_to_all(parts, 'tensor', split_axis=0, concat_axis=0, tiled=True)  11.2 us
    ppermute x6, starting transfers between devices, gather_chunks(): lax.ppermute(chunk, 'tensor', pairs(k, 0))  10.1 us
    all_to_all x2, starting transfers between devices, exchange(): lax.all_to_all(parts, 'tensor', split_axis=0, concat_axis=0, tiled=True)  8.69 us
    ppermute x8, starting transfers between devices, gather_chunks(): slots[k, m] = lax.ppermute(line[k], 'tensor', pairs(0, m))  8.42 us
    pallas_call x2, Pallas kernels, own_rows(): pl.pallas_call(own_kernel, out_shape=(jax.ShapeDtypeStruct((BLOCKS, width...  8.22 us
    ppermute x8, waiting for transfers between devices, gather_chunks(): slots[k, m] = lax.ppermute(line[k], 'tensor', pairs(0, m))  8.18 us
  transfers between devices with their start and end apart: 18, of which 9 were waited for; matrix products, arithmetic and copies ran while one was open for 2% of the time, Pallas kernels for 14%

profile of v3, /device:TPU:0, one launch (start us, length us, event | category | flops | bytes accessed | tf_op | source)
XLA Modules:
  0.0 101.1 jit_solution(13078615971392642845)
XLA Ops:
  0.0 0.9 copy-done.6
  0.9 0.7 copy-done.7
  1.6 0.4 norm_chunk.1.refs_0_
  2.0 3.1 %collective-permute-start = (bf16[8,6144]{1,0:T(8,128)(2,1)S(1)}, bf16[8,6144]{1,0:T(8,128)(2,1)S(1)}, u32[]{:S(2)}, u32[]{:S(2)}) collective-permute-start(bf16[8,6144]{1,0:T(8,128)(2,1)S(1)} %norm_chunk.1.refs_0_), channel_id=1, source_target_pairs={{0,4},{1,5},{2,6},{3,7},{4,0},{5,1},{6,2},{7,3},{8,12},{9,13},{10,... | collective-permute-start | bytes 294920 | tf_op jit(solution)/shard_map/ppermute | solution.py:73
  5.1 2.6 %collective-permute-start.1 = (bf16[8,6144]{1,0:T(8,128)(2,1)S(1)}, bf16[8,6144]{1,0:T(8,128)(2,1)S(1)}, u32[]{:S(2)}, u32[]{:S(2)}) collective-permute-start(bf16[8,6144]{1,0:T(8,128)(2,1)S(1)} %norm_chunk.1.refs_0_), channel_id=1, source_target_pairs={{0,8},{1,9},{2,10},{3,11},{4,12},{5,13},{6,14},{7,15},{8,0},{9,1},... | collective-permute-start | bytes 294920 | tf_op jit(solution)/shard_map/ppermute | solution.py:73
  7.7 0.0 collective-permute-start.2
  7.7 1.7 %collective-permute-start.3 = (bf16[8,6144]{1,0:T(8,128)(2,1)S(1)}, bf16[8,6144]{1,0:T(8,128)(2,1)S(1)}, u32[]{:S(2)}, u32[]{:S(2)}) collective-permute-start(bf16[8,6144]{1,0:T(8,128)(2,1)S(1)} %norm_chunk.1.refs_0_), channel_id=1, source_target_pairs={{0,2},{1,3},{2,0},{3,1},{4,6},{5,7},{6,4},{7,5},{8,10},{9,11},{10,... | collective-permute-start | bytes 294920 | tf_op jit(solution)/shard_map/ppermute | solution.py:77
  9.4 0.0 collective-permute-done.refs_1_
  9.4 0.3 collective-permute-start.4
  9.7 5.8 %collective-permute-done.1.refs_2_ = bf16[8,6144]{1,0:T(8,128)(2,1)S(1)} collective-permute-done((bf16[8,6144]{1,0:T(8,128)(2,1)S(1)}, bf16[8,6144]{1,0:T(8,128)(2,1)S(1)}, u32[]{:S(2)}, u32[]{:S(2)}) %collective-permute-start.1) | collective-permute-done | bytes 98336 | tf_op jit(solution)/shard_map/ppermute | solution.py:73
  15.5 1.5 %collective-permute-start.5 = (bf16[8,6144]{1,0:T(8,128)(2,1)S(1)}, bf16[8,6144]{1,0:T(8,128)(2,1)S(1)}, u32[]{:S(2)}, u32[]{:S(2)}) collective-permute-start(bf16[8,6144]{1,0:T(8,128)(2,1)S(1)} %collective-permute-done.1.refs_2_), channel_id=1, source_target_pairs={{0,2},{1,3},{2,0},{3,1},{4,6},{5,7},{6,4},{7,5},{8,10},{9,11},{10,... | collective-permute-start | bytes 294920 | tf_op jit(solution)/shard_map/ppermute | solution.py:77
  17.0 0.0 collective-permute-done.2.refs_3_
  17.0 0.5 collective-permute-start.6
  17.5 0.0 collective-permute-done.3.refs_4_
  17.6 0.0 collective-permute-done.4.refs_5_
  17.6 2.6 %collective-permute-done.5.refs_6_ = bf16[8,6144]{1,0:T(8,128)(2,1)S(1)} collective-permute-done((bf16[8,6144]{1,0:T(8,128)(2,1)S(1)}, bf16[8,6144]{1,0:T(8,128)(2,1)S(1)}, u32[]{:S(2)}, u32[]{:S(2)}) %collective-permute-start.5) | collective-permute-done | bytes 98336 | tf_op jit(solution)/shard_map/ppermute | solution.py:77
  20.1 1.5 %collective-permute-done.6.refs_7_ = bf16[8,6144]{1,0:T(8,128)(2,1)S(1)} collective-permute-done((bf16[8,6144]{1,0:T(8,128)(2,1)S(1)}, bf16[8,6144]{1,0:T(8,128)(2,1)S(1)}, u32[]{:S(2)}, u32[]{:S(2)}) %collective-permute-start.6) | collective-permute-done | bytes 98336 | tf_op jit(solution)/shard_map/ppermute | solution.py:77
  21.7 0.3 unpack.2.left
  22.0 0.1 collective-permute-start.7
  22.0 0.7 reshape.29.bias_ref
  22.7 0.7 convert_element_type.3
  23.4 4.4 %qkv_own.1 = (bf16[8,1024,640]{2,1,0:T(8,128)(2,1)S(1)}, f32[64,640]{1,0:T(8,128)S(1)}) custom-call(bf16[8,64,1024]{2,1,0:T(8,128)(2,1)S(1)} %unpack.2.left, bf16[8192,640]{1,0:T(8,128)(2,1)} %weight.2), custom_call_target="tpu_custom_call" | custom-call | flops 671088640 | bytes 10485760 | tf_op jit(solution)/shard_map/qkv_own/pallas_call | solution.py:212
  27.9 0.0 collective-permute-done.7.left
  27.9 2.6 %qkv_project.1.after = bf16[16,6,640]{2,1,0:T(8,128)(2,1)} custom-call(s32[1]{0:T(128)} %bitcast.me_ref, bf16[1,640]{1,0:T(2,128)(2,1)S(1)} %reshape.29.bias_ref, f32[64,640]{1,0:T(8,128)S(1)} %get-tuple-element.11.own_ref, bf16[8,64,1024]{2,1,0:T(8,128)(2,1)S(1)} %collective-permute-done.7.left, bf16[8,1024,640]{2,1,0:T(8,128)(2,1)S(1)} %get-tuple-element.12.held), custom_call_target="tpu_custom_call" | custom-call | tf_op jit(solution)/shard_map/qkv_project/pallas_call | solution.py:241
  30.5 4.4 %all-to-all-start = ((bf16[16,6,640]{2,1,0:T(8,128)(2,1)}), bf16[16,6,640]{2,1,0:T(8,128)(2,1)S(1)}, u32[]{:S(2)}, u32[]{:S(2)}) async-start(bf16[16,6,640]{2,1,0:T(8,128)(2,1)} %qkv_project.1.after), calls=%async_computation | async-start | bytes 327680 | tf_op jit(solution)/shard_map/all_to_all | solution.py:497
  34.9 0.1 fusion
  35.0 0.1 pad_maximum_fusion
  35.1 3.8 %hold_caches.1 = (bf16[6,384,1024]{2,1,0:T(8,128)(2,1)S(1)}, bf16[6,384,1024]{2,1,0:T(8,128)(2,1)S(1)}) custom-call(bf16[16,6,640]{2,1,0:T(8,128)(2,1)} %qkv_project.1.after, bf16[6,384,1024]{2,1,0:T(8,128)(2,1)} %k_hbm.1, bf16[6,384,1024]{2,1,0:T(8,128)(2,1)} %v_hbm.1), custom_call_target="tpu_custom_call" | custom-call | bytes 18874368 | tf_op jit(solution)/shard_map/hold_caches/pallas_call | solution.py:265
  38.9 0.0 copy-start
  38.9 2.1 %copy-done = bf16[6,384,1024]{2,1,0:T(8,128)(2,1)} copy-done((bf16[6,384,1024]{2,1,0:T(8,128)(2,1)}, bf16[6,384,1024]{2,1,0:T(8,128)(2,1)S(1)}, u32[]{:S(2)}) %copy-start) | copy-done | bytes 4718616
  41.1 2.2 %copy-done.2 = bf16[6,384,1024]{2,1,0:T(8,128)(2,1)} copy-done((bf16[6,384,1024]{2,1,0:T(8,128)(2,1)}, bf16[6,384,1024]{2,1,0:T(8,128)(2,1)S(1)}, u32[]{:S(2)}) %copy-start.2) | copy-done | bytes 4718616
  43.3 0.1 all-to-all-done
  43.4 0.0 copy-done.9
  43.4 2.3 %copy-done.1 = bf16[6,384,1024]{2,1,0:T(8,128)(2,1)S(1)} copy-done((bf16[6,384,1024]{2,1,0:T(8,128)(2,1)S(1)}, bf16[6,384,1024]{2,1,0:T(8,128)(2,1)}, u32[]{:S(2)}) %copy-start.1) | copy-done | bytes 4718616
  45.7 2.3 %copy-done.3 = bf16[6,384,1024]{2,1,0:T(8,128)(2,1)S(1)} copy-done((bf16[6,384,1024]{2,1,0:T(8,128)(2,1)S(1)}, bf16[6,384,1024]{2,1,0:T(8,128)(2,1)}, u32[]{:S(2)}) %copy-start.3) | copy-done | bytes 4718616
  48.1 5.1 %attend.1.refs_0_ = bf16[8,6272]{1,0:T(8,128)(2,1)S(1)} custom-call(s32[6]{0:T(128)S(1)} %copy-done.8, s32[6]{0:T(128)S(1)} %copy-done.9, bf16[6,10240]{1,0:T(8,128)(2,1)S(1)} %bitcast.13, f32[6,128]{1,0:T(8,128)S(1)} %get-tuple-element.20.cos_ref, f32[6,128]{1,0:T(8,128)S(1)} %get-tuple-element.21.sin_ref, bf16[6,384,1024]{2,1,0:T(8,128)(2,1)S(1)} %copy-done.1, ...), custom_call_target="tpu_custom_call" | custom-call | tf_op jit(solution)/shard_map/attend/pallas_call | solution.py:349
  53.2 1.9 %collective-permute-start.8 = (bf16[8,6272]{1,0:T(8,128)(2,1)S(1)}, bf16[8,6272]{1,0:T(8,128)(2,1)S(1)}, u32[]{:S(2)}, u32[]{:S(2)}) collective-permute-start(bf16[8,6272]{1,0:T(8,128)(2,1)S(1)} %attend.1.refs_0_), channel_id=1, source_target_pairs={{0,4},{1,5},{2,6},{3,7},{4,0},{5,1},{6,2},{7,3},{8,12},{9,13},{10,... | collective-permute-start | bytes 301064 | tf_op jit(solution)/shard_map/ppermute | solution.py:73
  55.1 2.4 %collective-permute-start.9 = (bf16[8,6272]{1,0:T(8,128)(2,1)S(1)}, bf16[8,6272]{1,0:T(8,128)(2,1)S(1)}, u32[]{:S(2)}, u32[]{:S(2)}) collective-permute-start(bf16[8,6272]{1,0:T(8,128)(2,1)S(1)} %attend.1.refs_0_), channel_id=1, source_target_pairs={{0,8},{1,9},{2,10},{3,11},{4,12},{5,13},{6,14},{7,15},{8,0},{9,1},... | collective-permute-start | bytes 301064 | tf_op jit(solution)/shard_map/ppermute | solution.py:73
  57.5 0.2 collective-permute-start.10
  57.7 1.8 %collective-permute-start.11 = (bf16[8,6272]{1,0:T(8,128)(2,1)S(1)}, bf16[8,6272]{1,0:T(8,128)(2,1)S(1)}, u32[]{:S(2)}, u32[]{:S(2)}) collective-permute-start(bf16[8,6272]{1,0:T(8,128)(2,1)S(1)} %attend.1.refs_0_), channel_id=1, source_target_pairs={{0,2},{1,3},{2,0},{3,1},{4,6},{5,7},{6,4},{7,5},{8,10},{9,11},{10,... | collective-permute-start | bytes 301064 | tf_op jit(solution)/shard_map/ppermute | solution.py:77
  59.5 0.0 collective-permute-done.8.refs_1_
  59.5 0.5 collective-permute-start.12
  60.0 6.0 %collective-permute-done.9.refs_2_ = bf16[8,6272]{1,0:T(8,128)(2,1)S(1)} collective-permute-done((bf16[8,6272]{1,0:T(8,128)(2,1)S(1)}, bf16[8,6272]{1,0:T(8,128)(2,1)S(1)}, u32[]{:S(2)}, u32[]{:S(2)}) %collective-permute-start.9) | collective-permute-done | bytes 100384 | tf_op jit(solution)/shard_map/ppermute | solution.py:73
  66.0 1.5 %collective-permute-start.13 = (bf16[8,6272]{1,0:T(8,128)(2,1)S(1)}, bf16[8,6272]{1,0:T(8,128)(2,1)S(1)}, u32[]{:S(2)}, u32[]{:S(2)}) collective-permute-start(bf16[8,6272]{1,0:T(8,128)(2,1)S(1)} %collective-permute-done.9.refs_2_), channel_id=1, source_target_pairs={{0,2},{1,3},{2,0},{3,1},{4,6},{5,7},{6,4},{7,5},{8,10},{9,11},{10,... | collective-permute-start | bytes 301064 | tf_op jit(solution)/shard_map/ppermute | solution.py:77
  67.4 0.0 collective-permute-done.10.refs_3_
  67.4 0.6 collective-permute-start.14
  68.0 0.0 collective-permute-done.11.refs_4_
  68.0 0.0 collective-permute-done.12.refs_5_
  68.0 2.6 %collective-permute-done.13.refs_6_ = bf16[8,6272]{1,0:T(8,128)(2,1)S(1)} collective-permute-done((bf16[8,6272]{1,0:T(8,128)(2,1)S(1)}, bf16[8,6272]{1,0:T(8,128)(2,1)S(1)}, u32[]{:S(2)}, u32[]{:S(2)}) %collective-permute-start.13) | collective-permute-done | bytes 100384 | tf_op jit(solution)/shard_map/ppermute | solution.py:77
  70.6 1.5 %collective-permute-done.14.refs_7_ = bf16[8,6272]{1,0:T(8,128)(2,1)S(1)} collective-permute-done((bf16[8,6272]{1,0:T(8,128)(2,1)S(1)}, bf16[8,6272]{1,0:T(8,128)(2,1)S(1)}, u32[]{:S(2)}, u32[]{:S(2)}) %collective-permute-start.14) | collective-permute-done | bytes 100384 | tf_op jit(solution)/shard_map/ppermute | solution.py:77
  72.1 0.3 unpack.3.left.own
  72.4 0.1 collective-permute-start.15
  72.5 0.6 shrink_own.1.own_part
  73.1 2.2 %collective-permute-done.15.left.other = bf16[9,64,1024]{2,1,0:T(8,128)(2,1)S(1)} collective-permute-done((bf16[9,64,1024]{2,1,0:T(8,128)(2,1)S(1)}, bf16[9,64,1024]{2,1,0:T(8,128)(2,1)S(1)}, u32[]{:S(2)}, u32[]{:S(2)}) %collective-permute-start.15) | collective-permute-done | bytes 1179680 | tf_op jit(solution)/shard_map/ppermute | solution.py:84
  75.3 1.5 %shrink.1 = bf16[16,32,128]{2,1,0:T(8,128)(2,1)} custom-call(s32[1]{0:T(128)} %bitcast.me_ref, bf16[2,16,8192]{2,1,0:T(8,128)(2,1)S(1)} %bitcast.12, f32[32,64]{1,0:T(8,128)S(1)} %shrink_own.1.own_part, bf16[9,64,1024]{2,1,0:T(8,128)(2,1)S(1)} %unpack.3.left.own, bf16[9,64,1024]{2,1,0:T(8,128)(2,1)S(1)} %collective-permute-done.15.left.other), custom_call_target="tpu_custom_call" | custom-call | tf_op jit(solution)/shard_map/shrink/pallas_call | solution.py:434
  76.8 4.3 %all-to-all-start.1 = ((bf16[16,32,128]{2,1,0:T(8,128)(2,1)}), bf16[16,32,128]{2,1,0:T(8,128)(2,1)S(1)}, u32[]{:S(2)}, u32[]{:S(2)}) async-start(bf16[16,32,128]{2,1,0:T(8,128)(2,1)} %shrink.1), calls=%async_computation.1 | async-start | bytes 262144 | tf_op jit(solution)/shard_map/all_to_all | solution.py:497
  81.1 3.8 %base_own.1 = (bf16[8,1024,512]{2,1,0:T(8,128)(2,1)S(1)}, f32[64,512]{1,0:T(8,128)S(1)}) custom-call(bf16[9,64,1024]{2,1,0:T(8,128)(2,1)S(1)} %unpack.3.left.own, bf16[8192,512]{1,0:T(8,128)(2,1)} %weight.3), custom_call_target="tpu_custom_call" | custom-call | flops 536870912 | bytes 8388608 | tf_op jit(solution)/shard_map/base_own/pallas_call | solution.py:212
  84.9 0.0 copy-start.5
  84.9 1.5 %base_project.1.base_ref = f32[128,512]{1,0:T(8,128)S(1)} custom-call(s32[1]{0:T(128)} %bitcast.me_ref, f32[64,512]{1,0:T(8,128)S(1)} %get-tuple-element.15.own_ref, bf16[9,64,1024]{2,1,0:T(8,128)(2,1)S(1)} %collective-permute-done.15.left.other, bf16[8,1024,512]{2,1,0:T(8,128)(2,1)S(1)} %get-tuple-element.16.held), custom_call_target="tpu_custom_call" | custom-call | flops 536870912 | bytes 8388608 | tf_op jit(solution)/shard_map/base_project/pallas_call | solution.py:462
  86.5 2.6 %all-to-all-done.1 = bf16[16,32,128]{2,1,0:T(8,128)(2,1)S(1)} async-done(((bf16[16,32,128]{2,1,0:T(8,128)(2,1)}), bf16[16,32,128]{2,1,0:T(8,128)(2,1)S(1)}, u32[]{:S(2)}, u32[]{:S(2)}) %all-to-all-start.1) | async-done | bytes 131104 | tf_op jit(solution)/shard_map/all_to_all | solution.py:497
  89.0 0.0 copy-done.5
  89.0 0.3 add_delta.1
  89.3 11.2 %all_to_all.15 = bf16[16,6,512]{2,1,0:T(8,128)(2,1)S(1)} all-to-all(bf16[16,6,512]{2,1,0:T(8,128)(2,1)S(1)} %add_delta.1), channel_id=1, replica_groups=mesh['group'=2,'tensor'=16] {'tensor'}, dimensions={0} | all-to-all | bytes 196608 | tf_op jit(solution)/shard_map/all_to_all | solution.py:497
  100.5 0.7 copy.13
  (11 shorter events, 0.0 us)
Async XLA Ops:
  0.0 0.9 copy-start.6
  0.9 0.7 copy-start.7
  2.0 7.4 %collective-permute-start = (bf16[8,6144]{1,0:T(8,128)(2,1)S(1)}, bf16[8,6144]{1,0:T(8,128)(2,1)S(1)}, u32[]{:S(2)}, u32[]{:S(2)}) collective-permute-start(bf16[8,6144]{1,0:T(8,128)(2,1)S(1)} %norm_chunk.1.refs_0_), channel_id=1, source_target_pairs={{0,4},{1,5},{2,6},{3,7},{4,0},{5,1},{6,2},{7,3},{8,12},{9,13},{10,... | collective-permute-start | bytes 294920 | tf_op jit(solution)/shard_map/ppermute | solution.py:73
  5.1 10.4 %collective-permute-start.1 = (bf16[8,6144]{1,0:T(8,128)(2,1)S(1)}, bf16[8,6144]{1,0:T(8,128)(2,1)S(1)}, u32[]{:S(2)}, u32[]{:S(2)}) collective-permute-start(bf16[8,6144]{1,0:T(8,128)(2,1)S(1)} %norm_chunk.1.refs_0_), channel_id=1, source_target_pairs={{0,8},{1,9},{2,10},{3,11},{4,12},{5,13},{6,14},{7,15},{8,0},{9,1},... | collective-permute-start | bytes 294920 | tf_op jit(solution)/shard_map/ppermute | solution.py:73
  7.7 9.4 %collective-permute-start.2 = (bf16[8,6144]{1,0:T(8,128)(2,1)S(1)}, bf16[8,6144]{1,0:T(8,128)(2,1)S(1)}, u32[]{:S(2)}, u32[]{:S(2)}) collective-permute-start(bf16[8,6144]{1,0:T(8,128)(2,1)S(1)} %norm_chunk.1.refs_0_), channel_id=1, source_target_pairs={{0,12},{1,13},{2,14},{3,15},{4,8},{5,9},{6,10},{7,11},{8,4},{9,5},... | collective-permute-start | bytes 294920 | tf_op jit(solution)/shard_map/ppermute | solution.py:73
  7.7 9.9 %collective-permute-start.3 = (bf16[8,6144]{1,0:T(8,128)(2,1)S(1)}, bf16[8,6144]{1,0:T(8,128)(2,1)S(1)}, u32[]{:S(2)}, u32[]{:S(2)}) collective-permute-start(bf16[8,6144]{1,0:T(8,128)(2,1)S(1)} %norm_chunk.1.refs_0_), channel_id=1, source_target_pairs={{0,2},{1,3},{2,0},{3,1},{4,6},{5,7},{6,4},{7,5},{8,10},{9,11},{10,... | collective-permute-start | bytes 294920 | tf_op jit(solution)/shard_map/ppermute | solution.py:77
  9.4 8.1 %collective-permute-start.4 = (bf16[8,6144]{1,0:T(8,128)(2,1)S(1)}, bf16[8,6144]{1,0:T(8,128)(2,1)S(1)}, u32[]{:S(2)}, u32[]{:S(2)}) collective-permute-start(bf16[8,6144]{1,0:T(8,128)(2,1)S(1)} %collective-permute-done.refs_1_), channel_id=1, source_target_pairs={{0,2},{1,3},{2,0},{3,1},{4,6},{5,7},{6,4},{7,5},{8,10},{9,11},{10,... | collective-permute-start | bytes 294920 | tf_op jit(solution)/shard_map/ppermute | solution.py:77
  15.5 4.6 %collective-permute-start.5 = (bf16[8,6144]{1,0:T(8,128)(2,1)S(1)}, bf16[8,6144]{1,0:T(8,128)(2,1)S(1)}, u32[]{:S(2)}, u32[]{:S(2)}) collective-permute-start(bf16[8,6144]{1,0:T(8,128)(2,1)S(1)} %collective-permute-done.1.refs_2_), channel_id=1, source_target_pairs={{0,2},{1,3},{2,0},{3,1},{4,6},{5,7},{6,4},{7,5},{8,10},{9,11},{10,... | collective-permute-start | bytes 294920 | tf_op jit(solution)/shard_map/ppermute | solution.py:77
  17.0 4.6 %collective-permute-start.6 = (bf16[8,6144]{1,0:T(8,128)(2,1)S(1)}, bf16[8,6144]{1,0:T(8,128)(2,1)S(1)}, u32[]{:S(2)}, u32[]{:S(2)}) collective-permute-start(bf16[8,6144]{1,0:T(8,128)(2,1)S(1)} %collective-permute-done.2.refs_3_), channel_id=1, source_target_pairs={{0,2},{1,3},{2,0},{3,1},{4,6},{5,7},{6,4},{7,5},{8,10},{9,11},{10,... | collective-permute-start | bytes 294920 | tf_op jit(solution)/shard_map/ppermute | solution.py:77
  22.0 5.9 %collective-permute-start.7 = (bf16[8,64,1024]{2,1,0:T(8,128)(2,1)S(1)}, bf16[8,64,1024]{2,1,0:T(8,128)(2,1)S(1)}, u32[]{:S(2)}, u32[]{:S(2)}) collective-permute-start(bf16[8,64,1024]{2,1,0:T(8,128)(2,1)S(1)} %unpack.2.left), channel_id=1, source_target_pairs={{0,1},{1,0},{2,3},{3,2},{4,5},{5,4},{6,7},{7,6},{8,9},{9,8},{10,11... | collective-permute-start | bytes 3145736 | tf_op jit(solution)/shard_map/ppermute | solution.py:84
  30.5 12.9 %all-to-all-start = ((bf16[16,6,640]{2,1,0:T(8,128)(2,1)}), bf16[16,6,640]{2,1,0:T(8,128)(2,1)S(1)}, u32[]{:S(2)}, u32[]{:S(2)}) async-start(bf16[16,6,640]{2,1,0:T(8,128)(2,1)} %qkv_project.1.after), calls=%async_computation | async-start | bytes 327680 | tf_op jit(solution)/shard_map/all_to_all | solution.py:497
  35.1 8.3 %copy-start.8 = (s32[6]{0:T(128)S(1)}, s32[6]{0:T(128)}, u32[]{:S(2)}) copy-start(s32[6]{0:T(128)} %len_ref.1) | copy-start | bytes 76
  35.1 8.3 %copy-start.9 = (s32[6]{0:T(128)S(1)}, s32[6]{0:T(128)}, u32[]{:S(2)}) copy-start(s32[6]{0:T(128)} %ids_ref.1) | copy-start | bytes 76
  38.9 2.1 %copy-start = (bf16[6,384,1024]{2,1,0:T(8,128)(2,1)}, bf16[6,384,1024]{2,1,0:T(8,128)(2,1)S(1)}, u32[]{:S(2)}) copy-start(bf16[6,384,1024]{2,1,0:T(8,128)(2,1)S(1)} %get-tuple-element.13.keys) | copy-start | bytes 14155780
  41.1 2.2 %copy-start.2 = (bf16[6,384,1024]{2,1,0:T(8,128)(2,1)}, bf16[6,384,1024]{2,1,0:T(8,128)(2,1)S(1)}, u32[]{:S(2)}) copy-start(bf16[6,384,1024]{2,1,0:T(8,128)(2,1)S(1)} %get-tuple-element.14.values) | copy-start | bytes 14155780
  43.4 2.3 %copy-start.1 = (bf16[6,384,1024]{2,1,0:T(8,128)(2,1)S(1)}, bf16[6,384,1024]{2,1,0:T(8,128)(2,1)}, u32[]{:S(2)}) copy-start(bf16[6,384,1024]{2,1,0:T(8,128)(2,1)} %copy-done) | copy-start | bytes 14155780
  45.7 2.3 %copy-start.3 = (bf16[6,384,1024]{2,1,0:T(8,128)(2,1)S(1)}, bf16[6,384,1024]{2,1,0:T(8,128)(2,1)}, u32[]{:S(2)}) copy-start(bf16[6,384,1024]{2,1,0:T(8,128)(2,1)} %copy-done.2) | copy-start | bytes 14155780
  48.1 24.4 %copy-start.4 = (bf16[2,8192,16]{1,2,0:T(8,128)(2,1)S(1)}, bf16[2,8192,16]{1,2,0:T(8,128)(2,1)}, u32[]{:S(2)}) copy-start(bf16[2,8192,16]{1,2,0:T(8,128)(2,1)} %param.20) | copy-start | bytes 1572868
  53.2 6.3 %collective-permute-start.8 = (bf16[8,6272]{1,0:T(8,128)(2,1)S(1)}, bf16[8,6272]{1,0:T(8,128)(2,1)S(1)}, u32[]{:S(2)}, u32[]{:S(2)}) collective-permute-start(bf16[8,6272]{1,0:T(8,128)(2,1)S(1)} %attend.1.refs_0_), channel_id=1, source_target_pairs={{0,4},{1,5},{2,6},{3,7},{4,0},{5,1},{6,2},{7,3},{8,12},{9,13},{10,... | collective-permute-start | bytes 301064 | tf_op jit(solution)/shard_map/ppermute | solution.py:73
  55.1 10.9 %collective-permute-start.9 = (bf16[8,6272]{1,0:T(8,128)(2,1)S(1)}, bf16[8,6272]{1,0:T(8,128)(2,1)S(1)}, u32[]{:S(2)}, u32[]{:S(2)}) collective-permute-start(bf16[8,6272]{1,0:T(8,128)(2,1)S(1)} %attend.1.refs_0_), channel_id=1, source_target_pairs={{0,8},{1,9},{2,10},{3,11},{4,12},{5,13},{6,14},{7,15},{8,0},{9,1},... | collective-permute-start | bytes 301064 | tf_op jit(solution)/shard_map/ppermute | solution.py:73
  57.5 10.0 %collective-permute-start.10 = (bf16[8,6272]{1,0:T(8,128)(2,1)S(1)}, bf16[8,6272]{1,0:T(8,128)(2,1)S(1)}, u32[]{:S(2)}, u32[]{:S(2)}) collective-permute-start(bf16[8,6272]{1,0:T(8,128)(2,1)S(1)} %attend.1.refs_0_), channel_id=1, source_target_pairs={{0,12},{1,13},{2,14},{3,15},{4,8},{5,9},{6,10},{7,11},{8,4},{9,5},... | collective-permute-start | bytes 301064 | tf_op jit(solution)/shard_map/ppermute | solution.py:73
  57.7 10.3 %collective-permute-start.11 = (bf16[8,6272]{1,0:T(8,128)(2,1)S(1)}, bf16[8,6272]{1,0:T(8,128)(2,1)S(1)}, u32[]{:S(2)}, u32[]{:S(2)}) collective-permute-start(bf16[8,6272]{1,0:T(8,128)(2,1)S(1)} %attend.1.refs_0_), channel_id=1, source_target_pairs={{0,2},{1,3},{2,0},{3,1},{4,6},{5,7},{6,4},{7,5},{8,10},{9,11},{10,... | collective-permute-start | bytes 301064 | tf_op jit(solution)/shard_map/ppermute | solution.py:77
  59.5 8.5 %collective-permute-start.12 = (bf16[8,6272]{1,0:T(8,128)(2,1)S(1)}, bf16[8,6272]{1,0:T(8,128)(2,1)S(1)}, u32[]{:S(2)}, u32[]{:S(2)}) collective-permute-start(bf16[8,6272]{1,0:T(8,128)(2,1)S(1)} %collective-permute-done.8.refs_1_), channel_id=1, source_target_pairs={{0,2},{1,3},{2,0},{3,1},{4,6},{5,7},{6,4},{7,5},{8,10},{9,11},{10,... | collective-permute-start | bytes 301064 | tf_op jit(solution)/shard_map/ppermute | solution.py:77
  66.0 4.6 %collective-permute-start.13 = (bf16[8,6272]{1,0:T(8,128)(2,1)S(1)}, bf16[8,6272]{1,0:T(8,128)(2,1)S(1)}, u32[]{:S(2)}, u32[]{:S(2)}) collective-permute-start(bf16[8,6272]{1,0:T(8,128)(2,1)S(1)} %collective-permute-done.9.refs_2_), channel_id=1, source_target_pairs={{0,2},{1,3},{2,0},{3,1},{4,6},{5,7},{6,4},{7,5},{8,10},{9,11},{10,... | collective-permute-start | bytes 301064 | tf_op jit(solution)/shard_map/ppermute | solution.py:77
  67.4 4.6 %collective-permute-start.14 = (bf16[8,6272]{1,0:T(8,128)(2,1)S(1)}, bf16[8,6272]{1,0:T(8,128)(2,1)S(1)}, u32[]{:S(2)}, u32[]{:S(2)}) collective-permute-start(bf16[8,6272]{1,0:T(8,128)(2,1)S(1)} %collective-permute-done.10.refs_3_), channel_id=1, source_target_pairs={{0,2},{1,3},{2,0},{3,1},{4,6},{5,7},{6,4},{7,5},{8,10},{9,11},{10,... | collective-permute-start | bytes 301064 | tf_op jit(solution)/shard_map/ppermute | solution.py:77
  72.4 2.9 %collective-permute-start.15 = (bf16[9,64,1024]{2,1,0:T(8,128)(2,1)S(1)}, bf16[9,64,1024]{2,1,0:T(8,128)(2,1)S(1)}, u32[]{:S(2)}, u32[]{:S(2)}) collective-permute-start(bf16[9,64,1024]{2,1,0:T(8,128)(2,1)S(1)} %unpack.3.left.own), channel_id=1, source_target_pairs={{0,1},{1,0},{2,3},{3,2},{4,5},{5,4},{6,7},{7,6},{8,9},{9,8},{10,11... | collective-permute-start | bytes 3538952 | tf_op jit(solution)/shard_map/ppermute | solution.py:84
  76.8 12.2 %all-to-all-start.1 = ((bf16[16,32,128]{2,1,0:T(8,128)(2,1)}), bf16[16,32,128]{2,1,0:T(8,128)(2,1)S(1)}, u32[]{:S(2)}, u32[]{:S(2)}) async-start(bf16[16,32,128]{2,1,0:T(8,128)(2,1)} %shrink.1), calls=%async_computation.1 | async-start | bytes 262144 | tf_op jit(solution)/shard_map/all_to_all | solution.py:497
  84.9 4.2 %copy-start.5 = (bf16[32,16,512]{2,1,0:T(8,128)(2,1)S(1)}, bf16[32,16,512]{2,1,0:T(8,128)(2,1)}, u32[]{:S(2)}) copy-start(bf16[32,16,512]{2,1,0:T(8,128)(2,1)} %param.21) | copy-start | bytes 1572868

commit v4 on v3

--- a/solution.py
+++ b/solution.py
@@ -22,6 +22,7 @@
 
 VMEM = pl.BlockSpec(memory_space=pltpu.VMEM)
 HBM = pl.BlockSpec(memory_space=pltpu.HBM)
+ANY = pl.BlockSpec(memory_space=pl.ANY)
 SMEM = pl.BlockSpec(memory_space=pltpu.SMEM)
 
 
@@ -61,7 +62,7 @@
         lax.fori_loop(0, count, lambda i, _: (body(i), 0)[1], 0)
 
 
-def gather_chunks(chunk, devices):
+def gather_chunks(chunk, devices, meanwhile):
     outer, inner = factors(devices // 2)
 
     def pairs(k, m):
@@ -71,13 +72,14 @@
         ]
 
     line = [chunk] + [lax.ppermute(chunk, "tensor", pairs(k, 0)) for k in range(1, outer)]
+    held, line[outer // 4] = meanwhile(line[outer // 4])
     slots = {}
     for k in range(outer):
         for m in range(1, inner):
             slots[k, m] = lax.ppermute(line[k], "tensor", pairs(0, m))
     for k in range(outer):
         slots[k, 0] = line[k]
-    return [slots[k, m] for m in range(inner) for k in range(outer)]
+    return [slots[k, m] for m in range(inner) for k in range(outer)], held
 
 
 def across(x, devices):
@@ -183,47 +185,61 @@
     )(*chunks)
 
 
-def fetch(weight, held, sems):
-    block = held.shape[1]
+def hold_kernel(count, *refs):
+    weight, held, _, sems = refs[count:]
+    block = weight.shape[0] // BLOCKS
     copies = [
-        pltpu.make_async_copy(weight.at[pl.ds(j * block, block), :], held.at[j], sems.at[j])
+        pltpu.make_async_copy(
+            weight.at[pl.ds(j * block, block), :], held.at[pl.ds(j * block, block), :], sems.at[j]
+        )
         for j in range(BLOCKS)
     ]
     for copy in copies:
         copy.start()
-    return copies
-
-
-def multiply(left, held, acc, copies=None):
+    for copy in copies:
+        copy.wait()
+
+
+def hold(weight, chunk, after, mib, name):
+    arrays = (chunk, *after)
+    return pl.pallas_call(
+        functools.partial(hold_kernel, len(arrays)),
+        out_shape=(
+            jax.ShapeDtypeStruct(weight.shape, weight.dtype),
+            jax.ShapeDtypeStruct(chunk.shape, chunk.dtype),
+        ),
+        in_specs=[ANY] * len(arrays) + [HBM],
+        out_specs=(VMEM, ANY),
+        scratch_shapes=[pltpu.SemaphoreType.DMA((BLOCKS,))],
+        input_output_aliases={0: 1},
+        compiler_params=params(mib),
+        cost_estimate=pl.CostEstimate(flops=0, bytes_accessed=4 * weight.size, transcendentals=0),
+        name=name,
+    )(*arrays, weight)
+
+
+def multiply(left, held, acc):
+    block = left.shape[2]
     acc[...] = jnp.zeros_like(acc)
     for j in range(BLOCKS):
-        if copies is not None:
-            copies[j].wait()
-        acc[...] += jnp.dot(left[j], held[j], preferred_element_type=jnp.float32)
-
-
-def own_kernel(left, weight, held, acc, sems):
-    multiply(left, held, acc, fetch(weight, held, sems))
-
-
-def own_rows(left, weight, mib, name):
-    width, cols = weight.shape
-    rows = left.shape[1]
-    return pl.pallas_call(
-        own_kernel,
-        out_shape=(
-            jax.ShapeDtypeStruct((BLOCKS, width // BLOCKS, cols), jnp.bfloat16),
-            jax.ShapeDtypeStruct((rows, cols), jnp.float32),
-        ),
-        in_specs=[VMEM, HBM],
-        out_specs=(VMEM, VMEM),
-        scratch_shapes=[pltpu.SemaphoreType.DMA((BLOCKS,))],
-        compiler_params=params(mib),
+        acc[...] += jnp.dot(
+            left[j], held[j * block : (j + 1) * block, :], preferred_element_type=jnp.float32
+        )
+
+
+def own_rows(left, held, name):
+    rows, cols = left.shape[1], held.shape[1]
+    return pl.pallas_call(
+        multiply,
+        out_shape=jax.ShapeDtypeStruct((rows, cols), jnp.float32),
+        in_specs=[VMEM, VMEM],
+        out_specs=VMEM,
+        compiler_params=params(40),
         cost_estimate=pl.CostEstimate(
-            flops=2 * rows * width * cols, bytes_accessed=width * cols * 2, transcendentals=0
+            flops=2 * rows * held.size, bytes_accessed=2 * held.size, transcendentals=0
         ),
         name=name,
-    )(left, weight)
+    )(left, held)
 
 
 def qkv_kernel(devices, rows, me_ref, bias_ref, own_ref, left, held, out_ref, acc):
@@ -246,32 +262,7 @@
         scratch_shapes=[pltpu.VMEM(own.shape, jnp.float32)],
         compiler_params=params(40),
         name="qkv_project",
-    )(me, bias.reshape(1, cols), own, left, held)
-
-
-def hold_kernel(after, k_hbm, v_hbm, keys, values, sems):
-    copies = [
-        pltpu.make_async_copy(k_hbm, keys, sems.at[0]),
-        pltpu.make_async_copy(v_hbm, values, sems.at[1]),
-    ]
-    for copy in copies:
-        copy.start()
-    for copy in copies:
-        copy.wait()
-
-
-def hold_caches(after, keys, values):
-    cache = jax.ShapeDtypeStruct(keys.shape, keys.dtype)
-    return pl.pallas_call(
-        hold_kernel,
-        out_shape=(cache, cache),
-        in_specs=[HBM, HBM, HBM],
-        out_specs=(VMEM, VMEM),
-        scratch_shapes=[pltpu.SemaphoreType.DMA((2,))],
-        compiler_params=params(43),
-        cost_estimate=pl.CostEstimate(flops=0, bytes_accessed=8 * keys.size, transcendentals=0),
-        name="hold_caches",
-    )(after, keys, values)
+    )(me, bias, own, left, held)
 
 
 def attend_kernel(
@@ -281,13 +272,27 @@
     qkv_ref,
     cos_ref,
     sin_ref,
+    k_hbm,
+    v_hbm,
+    out_ref,
     keys,
     values,
-    out_ref,
+    sems,
     heads,
     mixed,
     stage,
 ):
+    copies = []
+    for r in range(rows):
+        copies.append(
+            (
+                pltpu.make_async_copy(k_hbm.at[r], keys.at[r], sems.at[0, r]),
+                pltpu.make_async_copy(v_hbm.at[r], values.at[r], sems.at[1, r]),
+            )
+        )
+    for of_row in copies:
+        for copy in of_row:
+            copy.start()
     total_heads = QUERY_HEADS + 2 * KVH
     half = HEAD_SIZE // 2
     for h in range(total_heads):
@@ -296,6 +301,9 @@
     scale = 1.0 / HEAD_SIZE**0.5
 
     for r in range(rows):
+        for of_row in {0: copies[:1], 1: copies[1:3], 3: copies[3:]}.get(r, []):
+            for copy in of_row:
+                copy.wait()
         base = r * total_heads
         turned = heads[base : base + QUERY_HEADS + KVH, :]
         cosine = cos_ref[r : r + 1, :]
@@ -349,14 +357,17 @@
     return pl.pallas_call(
         functools.partial(attend_kernel, rows),
         out_shape=jax.ShapeDtypeStruct((8, rows * features // 8 + LANES), jnp.bfloat16),
-        in_specs=[SMEM, SMEM, VMEM, VMEM, VMEM, VMEM, VMEM],
+        in_specs=[SMEM, SMEM, VMEM, VMEM, VMEM, HBM, HBM],
         out_specs=VMEM,
         scratch_shapes=[
+            pltpu.VMEM(keys.shape, jnp.bfloat16),
+            pltpu.VMEM(keys.shape, jnp.bfloat16),
+            pltpu.SemaphoreType.DMA((2, rows)),
             pltpu.VMEM((rows * total_heads, HEAD_SIZE), jnp.float32),
             pltpu.VMEM((rows * QUERY_HEADS, HEAD_SIZE), jnp.float32),
             pltpu.VMEM((BLOCKS * rows, features // BLOCKS), jnp.float32),
         ],
-        compiler_params=params(24),
+        compiler_params=params(50),
         name="attend",
     )(lengths, ids, qkv, cosine, sine, keys, values)
 
@@ -527,20 +538,29 @@
     down = jnp.transpose(adapter_down_weight, (0, 2, 1))
     up = adapter_up_weight.reshape(-1, adapter_up_weight.shape[2])
 
-    chunks = gather_chunks(norm_chunk(hidden, input_norm_scale), devices)
+    bias = projection_bias.reshape(1, -1)
+    tables = (bias, cosine, sine)
+    chunks, held = gather_chunks(
+        norm_chunk(hidden, input_norm_scale),
+        devices,
+        lambda chunk: hold(query_key_value_weight, chunk, tables, 40, "hold_qkv"),
+    )
     mine = unpack(chunks, rows, hidden.shape[1], False)
     theirs = across(mine, devices)
-    held, own = own_rows(mine, query_key_value_weight, 40, "qkv_own")
-    qkv = qkv_project(me, own, theirs, held, projection_bias, devices, rows)
-    keys, values = hold_caches(qkv, rotated_key_cache, past_value_cache)
+    own = own_rows(mine, held, "qkv_own")
+    qkv = qkv_project(me, own, theirs, held, bias, devices, rows)
     qkv = per_row(exchange(qkv))
-    chunk = attend(lengths, row_adapter_index, qkv, cosine, sine, keys, values)
-    chunks = gather_chunks(chunk, devices)
+    chunk = attend(
+        lengths, row_adapter_index, qkv, cosine, sine, rotated_key_cache, past_value_cache
+    )
+    chunks, held = gather_chunks(
+        chunk, devices, lambda chunk: hold(output_weight, chunk, (), 42, "hold_output")
+    )
     mine = unpack(chunks, rows, QUERY_HEADS * HEAD_SIZE, True)
     theirs = across(mine, devices)
     own_part = shrink_own(mine, down)
+    own = own_rows(mine, held, "base_own")
     coords = exchange(shrink(me, own_part, mine, theirs, down, devices))
-    held, own = own_rows(mine, output_weight, 43, "base_own")
     base = base_project(me, own, theirs, held, devices)
     coords = coords.reshape(-1, coords.shape[2])
     return per_row(exchange(add_delta(base, coords, up, rows)))

time: 102 us -> 110 us (1.078)
  blocking collectives: 11.2 us -> 27.2 us
  waiting for transfers between devices: 24.8 us -> 13.4 us
  local copies, waits for them, and re-layouts: 12 us -> 21.4 us
  starting transfers between devices: 27.4 us -> 21.1 us
    all_to_all x1 -> x2, blocking collectives: 11.2 us -> 27.2 us  [exchange(): lax.all_to_all(parts, 'tensor', split_axis=0, concat_axis=0, tiled=True)]
    ppermute x6, waiting for transfers between devices: 11.8 us -> 1.3 us  [gather_chunks(): lax.ppermute(chunk, 'tensor', pairs(k, 0))]
    unnamed x21 -> x25, local copies, waits for them, and re-layouts: 11.3 us -> 20.7 us
    all_to_all x2 -> x1, starting transfers between devices: 8.69 us -> 4.03 us  [exchange(): lax.all_to_all(parts, 'tensor', split_axis=0, concat_axis=0, tiled=True)]
    all_to_all x2 -> x1, waiting for transfers between devices: 2.69 us -> 0.01 us  [exchange(): lax.all_to_all(parts, 'tensor', split_axis=0, concat_axis=0, tiled=True)]
    pallas_call x1, Pallas kernels: 5.14 us -> 6.92 us  [attend(): pl.pallas_call(functools.partial(attend_kernel, rows), out_shape=jax.Shap...]
    ppermute x8, waiting for transfers between devices: 8.18 us -> 9.95 us  [gather_chunks(): slots[k, m] = lax.ppermute(line[k], 'tensor', pairs(0, m))]
    ppermute x8, starting transfers between devices: 8.42 us -> 6.82 us  [gather_chunks(): slots[k, m] = lax.ppermute(line[k], 'tensor', pairs(0, m))]
  transfers between devices with their start and end apart: 18 -> 17, of which waited for: 9 -> 8; matrix products, arithmetic and copies ran while one was open for 2% -> 1% of each run, Pallas kernels for 14% -> 12%
where the time goes in v4:
time: 110 us; the launch traced here: 109 us
  blocking collectives  27.2 us (25%)
  Pallas kernels  24.9 us (23%)
  local copies, waits for them, and re-layouts  21.4 us (19%)
  starting transfers between devices  21.1 us (19%)
  waiting for transfers between devices  13.4 us (12%)
    all_to_all x2, blocking collectives, exchange(): lax.all_to_all(parts, 'tensor', split_axis=0, concat_axis=0, tiled=True)  27.2 us
    unnamed x25, local copies, waits for them, and re-layouts  20.7 us
    ppermute x6, starting transfers between devices, gather_chunks(): lax.ppermute(chunk, 'tensor', pairs(k, 0))  10.1 us
    ppermute x8, waiting for transfers between devices, gather_chunks(): slots[k, m] = lax.ppermute(line[k], 'tensor', pairs(0, m))  9.95 us
    pallas_call x2, Pallas kernels, hold(): pl.pallas_call(functools.partial(hold_kernel, len(arrays)), out_shape=(ja...  7.56 us
    pallas_call x1, Pallas kernels, attend(): pl.pallas_call(functools.partial(attend_kernel, rows), out_shape=jax.Shap...  6.92 us
    ppermute x8, starting transfers between devices, gather_chunks(): slots[k, m] = lax.ppermute(line[k], 'tensor', pairs(0, m))  6.82 us
    all_to_all x1, starting transfers between devices, exchange(): lax.all_to_all(parts, 'tensor', split_axis=0, concat_axis=0, tiled=True)  4.03 us
  transfers between devices with their start and end apart: 17, of which 8 were waited for; matrix products, arithmetic and copies ran while one was open for 1% of the time, Pallas kernels for 12%

profile of v4, /device:TPU:0, one launch (start us, length us, event | category | flops | bytes accessed | tf_op | source)
XLA Modules:
  0.0 109.1 jit_solution(271889837278225459)
XLA Ops:
  0.0 0.9 copy-done.8
  0.9 0.7 copy-done.9
  1.6 0.4 norm_chunk.1.refs_0_
  2.0 3.1 %collective-permute-start = (bf16[8,6144]{1,0:T(8,128)(2,1)S(1)}, bf16[8,6144]{1,0:T(8,128)(2,1)S(1)}, u32[]{:S(2)}, u32[]{:S(2)}) collective-permute-start(bf16[8,6144]{1,0:T(8,128)(2,1)S(1)} %norm_chunk.1.refs_0_), channel_id=1, source_target_pairs={{0,4},{1,5},{2,6},{3,7},{4,0},{5,1},{6,2},{7,3},{8,12},{9,13},{10,... | collective-permute-start | bytes 294920 | tf_op jit(solution)/shard_map/ppermute | solution.py:74
  5.1 2.6 %collective-permute-start.1 = (bf16[8,6144]{1,0:T(8,128)(2,1)S(1)}, bf16[8,6144]{1,0:T(8,128)(2,1)S(1)}, u32[]{:S(2)}, u32[]{:S(2)}) collective-permute-start(bf16[8,6144]{1,0:T(8,128)(2,1)S(1)} %norm_chunk.1.refs_0_), channel_id=1, source_target_pairs={{0,8},{1,9},{2,10},{3,11},{4,12},{5,13},{6,14},{7,15},{8,0},{9,1},... | collective-permute-start | bytes 294920 | tf_op jit(solution)/shard_map/ppermute | solution.py:74
  7.7 0.0 collective-permute-start.2
  7.7 1.7 %collective-permute-start.3 = (bf16[8,6144]{1,0:T(8,128)(2,1)S(1)}, bf16[8,6144]{1,0:T(8,128)(2,1)S(1)}, u32[]{:S(2)}, u32[]{:S(2)}) collective-permute-start(bf16[8,6144]{1,0:T(8,128)(2,1)S(1)} %norm_chunk.1.refs_0_), channel_id=1, source_target_pairs={{0,2},{1,3},{2,0},{3,1},{4,6},{5,7},{6,4},{7,5},{8,10},{9,11},{10,... | collective-permute-start | bytes 294920 | tf_op jit(solution)/shard_map/ppermute | solution.py:79
  9.4 0.7 convert_element_type.3
  10.1 0.7 reshape.29.refs_1_.bias_ref
  10.8 0.1 fusion
  10.9 0.1 pad_maximum_fusion
  11.0 0.0 collective-permute-done.refs_0_
  11.0 4.1 %hold_qkv.1 = (bf16[8192,640]{1,0:T(8,128)(2,1)S(1)}, bf16[8,6144]{1,0:T(8,128)(2,1)S(1)}) custom-call(bf16[8,6144]{1,0:T(8,128)(2,1)S(1)} %collective-permute-done.refs_0_, bf16[1,640]{1,0:T(2,128)(2,1)S(1)} %reshape.29.refs_1_.bias_ref, f32[6,128]{1,0:T(8,128)S(1)} %get-tuple-element.16.refs_2_.cos_ref, ...), custom_call_target="tpu_custom_call", output_to_operand_aliasing={{1}: (0, {})} | custom-call | bytes 20971520 | tf_op jit(solution)/shard_map/hold_qkv/pallas_call | solution.py:205
  15.1 4.0 %copy-done = bf16[8192,640]{1,0:T(8,128)(2,1)} copy-done((bf16[8192,640]{1,0:T(8,128)(2,1)}, bf16[8192,640]{1,0:T(8,128)(2,1)S(1)}, u32[]{:S(2)}) %copy-start) | copy-done | bytes 10485784
  19.1 0.3 collective-permute-start.4
  19.4 0.0 collective-permute-done.1.refs_2_
  19.4 1.7 %collective-permute-start.5 = (bf16[8,6144]{1,0:T(8,128)(2,1)S(1)}, bf16[8,6144]{1,0:T(8,128)(2,1)S(1)}, u32[]{:S(2)}, u32[]{:S(2)}) collective-permute-start(bf16[8,6144]{1,0:T(8,128)(2,1)S(1)} %collective-permute-done.1.refs_2_), channel_id=1, source_target_pairs={{0,2},{1,3},{2,0},{3,1},{4,6},{5,7},{6,4},{7,5},{8,10},{9,11},{10,... | collective-permute-start | bytes 294920 | tf_op jit(solution)/shard_map/ppermute | solution.py:79
  21.1 0.0 collective-permute-done.2.refs_3_
  21.1 0.3 collective-permute-start.6
  21.4 0.0 collective-permute-done.3.refs_4_
  21.4 3.3 %collective-permute-done.4.refs_5_ = bf16[8,6144]{1,0:T(8,128)(2,1)S(1)} collective-permute-done((bf16[8,6144]{1,0:T(8,128)(2,1)S(1)}, bf16[8,6144]{1,0:T(8,128)(2,1)S(1)}, u32[]{:S(2)}, u32[]{:S(2)}) %collective-permute-start.4) | collective-permute-done | bytes 98336 | tf_op jit(solution)/shard_map/ppermute | solution.py:79
  24.7 1.1 collective-permute-done.5.refs_6_
  25.7 1.1 collective-permute-done.6.refs_7_
  26.8 0.3 unpack.2.left
  27.1 0.1 collective-permute-start.7
  27.2 4.0 %copy-done.1 = bf16[8192,640]{1,0:T(8,128)(2,1)S(1)} copy-done((bf16[8192,640]{1,0:T(8,128)(2,1)S(1)}, bf16[8192,640]{1,0:T(8,128)(2,1)}, u32[]{:S(2)}) %copy-start.1) | copy-done | bytes 10485784
  31.1 1.9 %qkv_own.1.own_ref = f32[64,640]{1,0:T(8,128)S(1)} custom-call(bf16[8,64,1024]{2,1,0:T(8,128)(2,1)S(1)} %unpack.2.left, bf16[8192,640]{1,0:T(8,128)(2,1)S(1)} %copy-done.1), custom_call_target="tpu_custom_call" | custom-call | flops 671088640 | bytes 10485760 | tf_op jit(solution)/shard_map/qkv_own/pallas_call | solution.py:232
  33.1 0.0 copy-start.10
  33.1 0.0 copy-start.11
  33.1 0.0 collective-permute-done.7.left
  33.1 2.0 %copy-done.2 = bf16[8192,640]{1,0:T(8,128)(2,1)S(1)} copy-done((bf16[8192,640]{1,0:T(8,128)(2,1)S(1)}, bf16[8192,640]{1,0:T(8,128)(2,1)}, u32[]{:S(2)}) %copy-start.2) | copy-done | bytes 10485784
  35.1 1.9 %qkv_project.1 = bf16[16,6,640]{2,1,0:T(8,128)(2,1)S(1)} custom-call(s32[1]{0:T(128)} %bitcast.me_ref, bf16[1,640]{1,0:T(2,128)(2,1)S(1)} %reshape.29.refs_1_.bias_ref, f32[64,640]{1,0:T(8,128)S(1)} %qkv_own.1.own_ref, bf16[8,64,1024]{2,1,0:T(8,128)(2,1)S(1)} %collective-permute-done.7.left, bf16[8192,640]{1,0:T(8,128)(2,1)S(1)} %copy-done.2), custom_call_target="tpu_custom_call" | custom-call | tf_op jit(solution)/shard_map/qkv_project/pallas_call | solution.py:257
  37.1 13.4 %all_to_all.15 = bf16[16,6,640]{2,1,0:T(8,128)(2,1)S(1)} all-to-all(bf16[16,6,640]{2,1,0:T(8,128)(2,1)S(1)} %qkv_project.1), channel_id=1, replica_groups=mesh['group'=2,'tensor'=16] {'tensor'}, dimensions={0} | all-to-all | bytes 245760 | tf_op jit(solution)/shard_map/all_to_all | solution.py:508
  50.5 6.9 %attend.1.refs_0_ = bf16[8,6272]{1,0:T(8,128)(2,1)S(1)} custom-call(s32[6]{0:T(128)S(1)} %copy-done.10, s32[6]{0:T(128)S(1)} %copy-done.11, bf16[6,10240]{1,0:T(8,128)(2,1)S(1)} %bitcast.13, f32[6,128]{1,0:T(8,128)S(1)} %get-tuple-element.16.refs_2_.cos_ref, f32[6,128]{1,0:T(8,128)S(1)} %get-tuple-element.17.refs_3_.sin_ref, bf16[6,384,1024]{2,1,0:T(8,128)(2,1)} %k_hbm.1, ...), custom_call_target="tpu_custom_call" | custom-call | tf_op jit(solution)/shard_map/attend/pallas_call | solution.py:357
  57.4 0.1 collective-permute-start.8
  57.5 1.3 %collective-permute-start.9 = (bf16[8,6272]{1,0:T(8,128)(2,1)S(1)}, bf16[8,6272]{1,0:T(8,128)(2,1)S(1)}, u32[]{:S(2)}, u32[]{:S(2)}) collective-permute-start(bf16[8,6272]{1,0:T(8,128)(2,1)S(1)} %attend.1.refs_0_), channel_id=1, source_target_pairs={{0,8},{1,9},{2,10},{3,11},{4,12},{5,13},{6,14},{7,15},{8,0},{9,1},... | collective-permute-start | bytes 301064 | tf_op jit(solution)/shard_map/ppermute | solution.py:74
  58.8 3.0 %collective-permute-start.10 = (bf16[8,6272]{1,0:T(8,128)(2,1)S(1)}, bf16[8,6272]{1,0:T(8,128)(2,1)S(1)}, u32[]{:S(2)}, u32[]{:S(2)}) collective-permute-start(bf16[8,6272]{1,0:T(8,128)(2,1)S(1)} %attend.1.refs_0_), channel_id=1, source_target_pairs={{0,12},{1,13},{2,14},{3,15},{4,8},{5,9},{6,10},{7,11},{8,4},{9,5},... | collective-permute-start | bytes 301064 | tf_op jit(solution)/shard_map/ppermute | solution.py:74
  61.9 0.0 collective-permute-start.11
  61.9 1.3 %collective-permute-done.8.refs_0_ = bf16[8,6272]{1,0:T(8,128)(2,1)S(1)} collective-permute-done((bf16[8,6272]{1,0:T(8,128)(2,1)S(1)}, bf16[8,6272]{1,0:T(8,128)(2,1)S(1)}, u32[]{:S(2)}, u32[]{:S(2)}) %collective-permute-start.8) | collective-permute-done | bytes 100384 | tf_op jit(solution)/shard_map/ppermute | solution.py:74
  63.2 3.5 %hold_output.1 = (bf16[8192,512]{1,0:T(8,128)(2,1)S(1)}, bf16[8,6272]{1,0:T(8,128)(2,1)S(1)}) custom-call(bf16[8,6272]{1,0:T(8,128)(2,1)S(1)} %collective-permute-done.8.refs_0_, bf16[8192,512]{1,0:T(8,128)(2,1)} %refs_1_.1), custom_call_target="tpu_custom_call", output_to_operand_aliasing={{1}: (0, {})} | custom-call | bytes 16777216 | tf_op jit(solution)/shard_map/hold_output/pallas_call | solution.py:205
  66.7 3.3 %copy-done.3 = bf16[8192,512]{1,0:T(8,128)(2,1)} copy-done((bf16[8192,512]{1,0:T(8,128)(2,1)}, bf16[8192,512]{1,0:T(8,128)(2,1)S(1)}, u32[]{:S(2)}) %copy-start.3) | copy-done | bytes 8388632
  69.9 0.7 collective-permute-start.12
  70.7 0.0 collective-permute-done.9.refs_2_
  70.7 1.3 %collective-permute-start.13 = (bf16[8,6272]{1,0:T(8,128)(2,1)S(1)}, bf16[8,6272]{1,0:T(8,128)(2,1)S(1)}, u32[]{:S(2)}, u32[]{:S(2)}) collective-permute-start(bf16[8,6272]{1,0:T(8,128)(2,1)S(1)} %collective-permute-done.9.refs_2_), channel_id=1, source_target_pairs={{0,2},{1,3},{2,0},{3,1},{4,6},{5,7},{6,4},{7,5},{8,10},{9,11},{10,... | collective-permute-start | bytes 301064 | tf_op jit(solution)/shard_map/ppermute | solution.py:79
  72.0 0.0 collective-permute-done.10.refs_3_
  72.0 0.7 collective-permute-start.14
  72.7 0.0 collective-permute-done.11.refs_4_
  72.7 2.4 %collective-permute-done.12.refs_5_ = bf16[8,6272]{1,0:T(8,128)(2,1)S(1)} collective-permute-done((bf16[8,6272]{1,0:T(8,128)(2,1)S(1)}, bf16[8,6272]{1,0:T(8,128)(2,1)S(1)}, u32[]{:S(2)}, u32[]{:S(2)}) %collective-permute-start.12) | collective-permute-done | bytes 100384 | tf_op jit(solution)/shard_map/ppermute | solution.py:79
  75.1 1.1 collective-permute-done.13.refs_6_
  76.2 1.1 collective-permute-done.14.refs_7_
  77.3 0.3 unpack.3.left.own
  77.6 0.1 collective-permute-start.15
  77.7 0.6 shrink_own.1.own_part
  78.3 2.2 %collective-permute-done.15.left.other = bf16[9,64,1024]{2,1,0:T(8,128)(2,1)S(1)} collective-permute-done((bf16[9,64,1024]{2,1,0:T(8,128)(2,1)S(1)}, bf16[9,64,1024]{2,1,0:T(8,128)(2,1)S(1)}, u32[]{:S(2)}, u32[]{:S(2)}) %collective-permute-start.15) | collective-permute-done | bytes 1179680 | tf_op jit(solution)/shard_map/ppermute | solution.py:86
  80.5 1.5 %shrink.1 = bf16[16,32,128]{2,1,0:T(8,128)(2,1)} custom-call(s32[1]{0:T(128)} %bitcast.me_ref, bf16[2,16,8192]{2,1,0:T(8,128)(2,1)S(1)} %bitcast.12, f32[32,64]{1,0:T(8,128)S(1)} %shrink_own.1.own_part, bf16[9,64,1024]{2,1,0:T(8,128)(2,1)S(1)} %unpack.3.left.own, bf16[9,64,1024]{2,1,0:T(8,128)(2,1)S(1)} %collective-permute-done.15.left.other), custom_call_target="tpu_custom_call" | custom-call | tf_op jit(solution)/shard_map/shrink/pallas_call | solution.py:445
  82.0 4.0 %all-to-all-start.1 = ((bf16[16,32,128]{2,1,0:T(8,128)(2,1)}), bf16[16,32,128]{2,1,0:T(8,128)(2,1)S(1)}, u32[]{:S(2)}, u32[]{:S(2)}) async-start(bf16[16,32,128]{2,1,0:T(8,128)(2,1)} %shrink.1), calls=%async_computation.1 | async-start | bytes 262144 | tf_op jit(solution)/shard_map/all_to_all | solution.py:508
  86.1 3.4 %copy-done.4 = bf16[8192,512]{1,0:T(8,128)(2,1)S(1)} copy-done((bf16[8192,512]{1,0:T(8,128)(2,1)S(1)}, bf16[8192,512]{1,0:T(8,128)(2,1)}, u32[]{:S(2)}) %copy-start.4) | copy-done | bytes 8388632
  89.5 1.5 %base_own.1.own_ref = f32[64,512]{1,0:T(8,128)S(1)} custom-call(bf16[9,64,1024]{2,1,0:T(8,128)(2,1)S(1)} %unpack.3.left.own, bf16[8192,512]{1,0:T(8,128)(2,1)S(1)} %copy-done.4), custom_call_target="tpu_custom_call" | custom-call | flops 536870912 | bytes 8388608 | tf_op jit(solution)/shard_map/base_own/pallas_call | solution.py:232
  91.0 1.8 %copy-done.5 = bf16[8192,512]{1,0:T(8,128)(2,1)S(1)} copy-done((bf16[8192,512]{1,0:T(8,128)(2,1)S(1)}, bf16[8192,512]{1,0:T(8,128)(2,1)}, u32[]{:S(2)}) %copy-start.5) | copy-done | bytes 8388632
  92.8 1.6 %base_project.1.base_ref = f32[128,512]{1,0:T(8,128)S(1)} custom-call(s32[1]{0:T(128)} %bitcast.me_ref, f32[64,512]{1,0:T(8,128)S(1)} %base_own.1.own_ref, bf16[9,64,1024]{2,1,0:T(8,128)(2,1)S(1)} %collective-permute-done.15.left.other, bf16[8192,512]{1,0:T(8,128)(2,1)S(1)} %copy-done.5), custom_call_target="tpu_custom_call" | custom-call | flops 536870912 | bytes 8388608 | tf_op jit(solution)/shard_map/base_project/pallas_call | solution.py:473
  94.4 0.0 all-to-all-done.1
  94.5 0.3 add_delta.1
  94.7 13.7 %all_to_all.16 = bf16[16,6,512]{2,1,0:T(8,128)(2,1)S(1)} all-to-all(bf16[16,6,512]{2,1,0:T(8,128)(2,1)S(1)} %add_delta.1), channel_id=1, replica_groups=mesh['group'=2,'tensor'=16] {'tensor'}, dimensions={0} | all-to-all | bytes 196608 | tf_op jit(solution)/shard_map/all_to_all | solution.py:508
  108.5 0.7 copy.17
  (15 shorter events, 0.0 us)
Async XLA Ops:
  0.0 0.9 copy-start.8
  0.9 0.7 copy-start.9
  2.0 9.0 %collective-permute-start = (bf16[8,6144]{1,0:T(8,128)(2,1)S(1)}, bf16[8,6144]{1,0:T(8,128)(2,1)S(1)}, u32[]{:S(2)}, u32[]{:S(2)}) collective-permute-start(bf16[8,6144]{1,0:T(8,128)(2,1)S(1)} %norm_chunk.1.refs_0_), channel_id=1, source_target_pairs={{0,4},{1,5},{2,6},{3,7},{4,0},{5,1},{6,2},{7,3},{8,12},{9,13},{10,... | collective-permute-start | bytes 294920 | tf_op jit(solution)/shard_map/ppermute | solution.py:74
  5.1 14.3 %collective-permute-start.1 = (bf16[8,6144]{1,0:T(8,128)(2,1)S(1)}, bf16[8,6144]{1,0:T(8,128)(2,1)S(1)}, u32[]{:S(2)}, u32[]{:S(2)}) collective-permute-start(bf16[8,6144]{1,0:T(8,128)(2,1)S(1)} %norm_chunk.1.refs_0_), channel_id=1, source_target_pairs={{0,8},{1,9},{2,10},{3,11},{4,12},{5,13},{6,14},{7,15},{8,0},{9,1},... | collective-permute-start | bytes 294920 | tf_op jit(solution)/shard_map/ppermute | solution.py:74
  7.7 13.4 %collective-permute-start.2 = (bf16[8,6144]{1,0:T(8,128)(2,1)S(1)}, bf16[8,6144]{1,0:T(8,128)(2,1)S(1)}, u32[]{:S(2)}, u32[]{:S(2)}) collective-permute-start(bf16[8,6144]{1,0:T(8,128)(2,1)S(1)} %norm_chunk.1.refs_0_), channel_id=1, source_target_pairs={{0,12},{1,13},{2,14},{3,15},{4,8},{5,9},{6,10},{7,11},{8,4},{9,5},... | collective-permute-start | bytes 294920 | tf_op jit(solution)/shard_map/ppermute | solution.py:74
  7.7 13.7 %collective-permute-start.3 = (bf16[8,6144]{1,0:T(8,128)(2,1)S(1)}, bf16[8,6144]{1,0:T(8,128)(2,1)S(1)}, u32[]{:S(2)}, u32[]{:S(2)}) collective-permute-start(bf16[8,6144]{1,0:T(8,128)(2,1)S(1)} %norm_chunk.1.refs_0_), channel_id=1, source_target_pairs={{0,2},{1,3},{2,0},{3,1},{4,6},{5,7},{6,4},{7,5},{8,10},{9,11},{10,... | collective-permute-start | bytes 294920 | tf_op jit(solution)/shard_map/ppermute | solution.py:79
  15.1 4.0 %copy-start = (bf16[8192,640]{1,0:T(8,128)(2,1)}, bf16[8192,640]{1,0:T(8,128)(2,1)S(1)}, u32[]{:S(2)}) copy-start(bf16[8192,640]{1,0:T(8,128)(2,1)S(1)} %get-tuple-element.10.held) | copy-start | bytes 31457284
  19.1 5.6 %collective-permute-start.4 = (bf16[8,6144]{1,0:T(8,128)(2,1)S(1)}, bf16[8,6144]{1,0:T(8,128)(2,1)S(1)}, u32[]{:S(2)}, u32[]{:S(2)}) collective-permute-start(bf16[8,6144]{1,0:T(8,128)(2,1)S(1)} %get-tuple-element.9.refs_1_), channel_id=1, source_target_pairs={{0,2},{1,3},{2,0},{3,1},{4,6},{5,7},{6,4},{7,5},{8,10},{9,11},{10,... | collective-permute-start | bytes 294920 | tf_op jit(solution)/shard_map/ppermute | solution.py:79
  19.4 6.3 %collective-permute-start.5 = (bf16[8,6144]{1,0:T(8,128)(2,1)S(1)}, bf16[8,6144]{1,0:T(8,128)(2,1)S(1)}, u32[]{:S(2)}, u32[]{:S(2)}) collective-permute-start(bf16[8,6144]{1,0:T(8,128)(2,1)S(1)} %collective-permute-done.1.refs_2_), channel_id=1, source_target_pairs={{0,2},{1,3},{2,0},{3,1},{4,6},{5,7},{6,4},{7,5},{8,10},{9,11},{10,... | collective-permute-start | bytes 294920 | tf_op jit(solution)/shard_map/ppermute | solution.py:79
  21.1 5.7 %collective-permute-start.6 = (bf16[8,6144]{1,0:T(8,128)(2,1)S(1)}, bf16[8,6144]{1,0:T(8,128)(2,1)S(1)}, u32[]{:S(2)}, u32[]{:S(2)}) collective-permute-start(bf16[8,6144]{1,0:T(8,128)(2,1)S(1)} %collective-permute-done.2.refs_3_), channel_id=1, source_target_pairs={{0,2},{1,3},{2,0},{3,1},{4,6},{5,7},{6,4},{7,5},{8,10},{9,11},{10,... | collective-permute-start | bytes 294920 | tf_op jit(solution)/shard_map/ppermute | solution.py:79
  27.1 6.0 %collective-permute-start.7 = (bf16[8,64,1024]{2,1,0:T(8,128)(2,1)S(1)}, bf16[8,64,1024]{2,1,0:T(8,128)(2,1)S(1)}, u32[]{:S(2)}, u32[]{:S(2)}) collective-permute-start(bf16[8,64,1024]{2,1,0:T(8,128)(2,1)S(1)} %unpack.2.left), channel_id=1, source_target_pairs={{0,1},{1,0},{2,3},{3,2},{4,5},{5,4},{6,7},{7,6},{8,9},{9,8},{10,11... | collective-permute-start | bytes 3145736 | tf_op jit(solution)/shard_map/ppermute | solution.py:86
  27.2 4.0 %copy-start.1 = (bf16[8192,640]{1,0:T(8,128)(2,1)S(1)}, bf16[8192,640]{1,0:T(8,128)(2,1)}, u32[]{:S(2)}) copy-start(bf16[8192,640]{1,0:T(8,128)(2,1)} %copy-done) | copy-start | bytes 31457284
  31.1 4.0 %copy-start.2 = (bf16[8192,640]{1,0:T(8,128)(2,1)S(1)}, bf16[8192,640]{1,0:T(8,128)(2,1)}, u32[]{:S(2)}) copy-start(bf16[8192,640]{1,0:T(8,128)(2,1)} %copy-done) | copy-start | bytes 31457284
  33.1 17.4 %copy-start.10 = (s32[6]{0:T(128)S(1)}, s32[6]{0:T(128)}, u32[]{:S(2)}) copy-start(s32[6]{0:T(128)} %len_ref.1) | copy-start | bytes 76
  33.1 17.4 %copy-start.11 = (s32[6]{0:T(128)S(1)}, s32[6]{0:T(128)}, u32[]{:S(2)}) copy-start(s32[6]{0:T(128)} %ids_ref.1) | copy-start | bytes 76
  50.5 27.2 %copy-start.6 = (bf16[2,8192,16]{1,2,0:T(8,128)(2,1)S(1)}, bf16[2,8192,16]{1,2,0:T(8,128)(2,1)}, u32[]{:S(2)}) copy-start(bf16[2,8192,16]{1,2,0:T(8,128)(2,1)} %param.20) | copy-start | bytes 1572868
  57.4 5.7 %collective-permute-start.8 = (bf16[8,6272]{1,0:T(8,128)(2,1)S(1)}, bf16[8,6272]{1,0:T(8,128)(2,1)S(1)}, u32[]{:S(2)}, u32[]{:S(2)}) collective-permute-start(bf16[8,6272]{1,0:T(8,128)(2,1)S(1)} %attend.1.refs_0_), channel_id=1, source_target_pairs={{0,4},{1,5},{2,6},{3,7},{4,0},{5,1},{6,2},{7,3},{8,12},{9,13},{10,... | collective-permute-start | bytes 301064 | tf_op jit(solution)/shard_map/ppermute | solution.py:74
  57.5 13.2 %collective-permute-start.9 = (bf16[8,6272]{1,0:T(8,128)(2,1)S(1)}, bf16[8,6272]{1,0:T(8,128)(2,1)S(1)}, u32[]{:S(2)}, u32[]{:S(2)}) collective-permute-start(bf16[8,6272]{1,0:T(8,128)(2,1)S(1)} %attend.1.refs_0_), channel_id=1, source_target_pairs={{0,8},{1,9},{2,10},{3,11},{4,12},{5,13},{6,14},{7,15},{8,0},{9,1},... | collective-permute-start | bytes 301064 | tf_op jit(solution)/shard_map/ppermute | solution.py:74
  58.8 13.1 %collective-permute-start.10 = (bf16[8,6272]{1,0:T(8,128)(2,1)S(1)}, bf16[8,6272]{1,0:T(8,128)(2,1)S(1)}, u32[]{:S(2)}, u32[]{:S(2)}) collective-permute-start(bf16[8,6272]{1,0:T(8,128)(2,1)S(1)} %attend.1.refs_0_), channel_id=1, source_target_pairs={{0,12},{1,13},{2,14},{3,15},{4,8},{5,9},{6,10},{7,11},{8,4},{9,5},... | collective-permute-start | bytes 301064 | tf_op jit(solution)/shard_map/ppermute | solution.py:74
  61.9 10.8 %collective-permute-start.11 = (bf16[8,6272]{1,0:T(8,128)(2,1)S(1)}, bf16[8,6272]{1,0:T(8,128)(2,1)S(1)}, u32[]{:S(2)}, u32[]{:S(2)}) collective-permute-start(bf16[8,6272]{1,0:T(8,128)(2,1)S(1)} %attend.1.refs_0_), channel_id=1, source_target_pairs={{0,2},{1,3},{2,0},{3,1},{4,6},{5,7},{6,4},{7,5},{8,10},{9,11},{10,... | collective-permute-start | bytes 301064 | tf_op jit(solution)/shard_map/ppermute | solution.py:79
  66.6 3.3 %copy-start.3 = (bf16[8192,512]{1,0:T(8,128)(2,1)}, bf16[8192,512]{1,0:T(8,128)(2,1)S(1)}, u32[]{:S(2)}) copy-start(bf16[8192,512]{1,0:T(8,128)(2,1)S(1)} %get-tuple-element.12.held) | copy-start | bytes 25165828
  69.9 5.2 %collective-permute-start.12 = (bf16[8,6272]{1,0:T(8,128)(2,1)S(1)}, bf16[8,6272]{1,0:T(8,128)(2,1)S(1)}, u32[]{:S(2)}, u32[]{:S(2)}) collective-permute-start(bf16[8,6272]{1,0:T(8,128)(2,1)S(1)} %get-tuple-element.11.refs_1_), channel_id=1, source_target_pairs={{0,2},{1,3},{2,0},{3,1},{4,6},{5,7},{6,4},{7,5},{8,10},{9,11},{10,... | collective-permute-start | bytes 301064 | tf_op jit(solution)/shard_map/ppermute | solution.py:79
  70.7 5.5 %collective-permute-start.13 = (bf16[8,6272]{1,0:T(8,128)(2,1)S(1)}, bf16[8,6272]{1,0:T(8,128)(2,1)S(1)}, u32[]{:S(2)}, u32[]{:S(2)}) collective-permute-start(bf16[8,6272]{1,0:T(8,128)(2,1)S(1)} %collective-permute-done.9.refs_2_), channel_id=1, source_target_pairs={{0,2},{1,3},{2,0},{3,1},{4,6},{5,7},{6,4},{7,5},{8,10},{9,11},{10,... | collective-permute-start | bytes 301064 | tf_op jit(solution)/shard_map/ppermute | solution.py:79
  72.0 5.3 %collective-permute-start.14 = (bf16[8,6272]{1,0:T(8,128)(2,1)S(1)}, bf16[8,6272]{1,0:T(8,128)(2,1)S(1)}, u32[]{:S(2)}, u32[]{:S(2)}) collective-permute-start(bf16[8,6272]{1,0:T(8,128)(2,1)S(1)} %collective-permute-done.10.refs_3_), channel_id=1, source_target_pairs={{0,2},{1,3},{2,0},{3,1},{4,6},{5,7},{6,4},{7,5},{8,10},{9,11},{10,... | collective-permute-start | bytes 301064 | tf_op jit(solution)/shard_map/ppermute | solution.py:79
  77.6 2.9 %collective-permute-start.15 = (bf16[9,64,1024]{2,1,0:T(8,128)(2,1)S(1)}, bf16[9,64,1024]{2,1,0:T(8,128)(2,1)S(1)}, u32[]{:S(2)}, u32[]{:S(2)}) collective-permute-start(bf16[9,64,1024]{2,1,0:T(8,128)(2,1)S(1)} %unpack.3.left.own), channel_id=1, source_target_pairs={{0,1},{1,0},{2,3},{3,2},{4,5},{5,4},{6,7},{7,6},{8,9},{9,8},{10,11... | collective-permute-start | bytes 3538952 | tf_op jit(solution)/shard_map/ppermute | solution.py:86
  82.0 12.4 %all-to-all-start.1 = ((bf16[16,32,128]{2,1,0:T(8,128)(2,1)}), bf16[16,32,128]{2,1,0:T(8,128)(2,1)S(1)}, u32[]{:S(2)}, u32[]{:S(2)}) async-start(bf16[16,32,128]{2,1,0:T(8,128)(2,1)} %shrink.1), calls=%async_computation.1 | async-start | bytes 262144 | tf_op jit(solution)/shard_map/all_to_all | solution.py:508
  86.1 3.4 %copy-start.4 = (bf16[8192,512]{1,0:T(8,128)(2,1)S(1)}, bf16[8192,512]{1,0:T(8,128)(2,1)}, u32[]{:S(2)}) copy-start(bf16[8192,512]{1,0:T(8,128)(2,1)} %copy-done.3) | copy-start | bytes 25165828
  89.5 3.4 %copy-start.5 = (bf16[8192,512]{1,0:T(8,128)(2,1)S(1)}, bf16[8192,512]{1,0:T(8,128)(2,1)}, u32[]{:S(2)}) copy-start(bf16[8192,512]{1,0:T(8,128)(2,1)} %copy-done.3) | copy-start | bytes 25165828
  89.5 5.0 %copy-start.7 = (bf16[32,16,512]{2,1,0:T(8,128)(2,1)S(1)}, bf16[32,16,512]{2,1,0:T(8,128)(2,1)}, u32[]{:S(2)}) copy-start(bf16[32,16,512]{2,1,0:T(8,128)(2,1)} %param.21) | copy-start | bytes 1572868

commit v5 on v4

--- a/solution.py
+++ b/solution.py
@@ -80,6 +80,65 @@
     for k in range(outer):
         slots[k, 0] = line[k]
     return [slots[k, m] for m in range(inner) for k in range(outer)], held
+
+
+def neighbours(devices):
+    inner = factors(devices // 2)[1]
+    return [(m, c) for m in range(inner) for c in range(2)]
+
+
+def to_neighbour(x, devices, m, c):
+    inner = factors(devices // 2)[1]
+    return lax.ppermute(
+        x,
+        "tensor",
+        [
+            (d, 2 * (d // 2 // inner * inner + partner(d // 2 % inner, m, inner)) + (d % 2 ^ c))
+            for d in range(devices)
+        ],
+    )
+
+
+def along_line(x, devices, k):
+    outer, inner = factors(devices // 2)
+    return lax.ppermute(
+        x,
+        "tensor",
+        [
+            (d, 2 * (partner(d // 2 // inner, k, outer) * inner + d // 2 % inner) + d % 2)
+            for d in range(devices)
+        ],
+    )
+
+
+def source(devices, me, k, m, c):
+    outer, inner = factors(devices // 2)
+    chip = lax.div(me, 2)
+    a, b = lax.div(chip, inner), lax.rem(chip, inner)
+    chip = partner(a, k, outer, -1) * inner + partner(b, m, inner, -1)
+    return 2 * chip + (lax.rem(me, 2) ^ c)
+
+
+def join_kernel(*refs):
+    parts, out_ref = refs[:-1], refs[-1]
+    rows = parts[0].shape[0]
+    for at, part in enumerate(parts):
+        out_ref[at * rows : (at + 1) * rows, :] = part[...]
+
+
+def gather_coords(coords, devices):
+    around = [coords if mc == (0, 0) else to_neighbour(coords, devices, *mc) for mc in neighbours(devices)]
+    rows, cols = coords.shape
+    joined = pl.pallas_call(
+        join_kernel,
+        out_shape=jax.ShapeDtypeStruct((len(around) * rows, cols), coords.dtype),
+        in_specs=[VMEM] * len(around),
+        out_specs=VMEM,
+        compiler_params=params(16),
+        name="join_coords",
+    )(*around)
+    outer = factors(devices // 2)[0]
+    return [joined] + [along_line(joined, devices, k) for k in range(1, outer)]
 
 
 def across(x, devices):
@@ -242,7 +301,46 @@
     )(left, held)
 
 
-def qkv_kernel(devices, rows, me_ref, bias_ref, own_ref, left, held, out_ref, acc):
+def cache_copies(cache, kept, sems):
+    return [
+        pltpu.make_async_copy(cache.at[r], kept.at[r], sems.at[r]) for r in range(cache.shape[0])
+    ]
+
+
+def qkv_own_kernel(left, held, cache, acc, kept, sems):
+    copies = cache_copies(cache, kept, sems)
+    for copy in copies:
+        copy.start()
+    multiply(left, held, acc)
+    for copy in copies:
+        copy.wait()
+
+
+def qkv_own(left, held, cache):
+    rows, cols = left.shape[1], held.shape[1]
+    return pl.pallas_call(
+        qkv_own_kernel,
+        out_shape=(
+            jax.ShapeDtypeStruct((rows, cols), jnp.float32),
+            jax.ShapeDtypeStruct(cache.shape, cache.dtype),
+        ),
+        in_specs=[VMEM, VMEM, HBM],
+        out_specs=(VMEM, VMEM),
+        scratch_shapes=[pltpu.SemaphoreType.DMA((cache.shape[0],))],
+        compiler_params=params(32),
+        cost_estimate=pl.CostEstimate(
+            flops=2 * rows * held.size, bytes_accessed=2 * held.size, transcendentals=0
+        ),
+        name="qkv_own",
+    )(left, held, cache)
+
+
+def qkv_kernel(
+    devices, rows, me_ref, bias_ref, own_ref, left, held, cache, out_ref, kept, acc, sems
+):
+    copies = cache_copies(cache, kept, sems)
+    for copy in copies:
+        copy.start()
     multiply(left, held, acc)
     bias = bias_ref[...].astype(jnp.float32)
     core = lax.rem(me_ref[0], 2)
@@ -250,19 +348,27 @@
         mine = slice(8 * slot, 8 * slot + rows)
         out_ref[2 * chip + core] = (own_ref[mine, :] + bias).astype(jnp.bfloat16)
         out_ref[2 * chip + 1 - core] = (acc[mine, :] + bias).astype(jnp.bfloat16)
-
-
-def qkv_project(me, own, left, held, bias, devices, rows):
+    for copy in copies:
+        copy.wait()
+
+
+def qkv_project(me, own, left, held, bias, cache, devices, rows):
     cols = own.shape[1]
     return pl.pallas_call(
         functools.partial(qkv_kernel, devices, rows),
-        out_shape=jax.ShapeDtypeStruct((devices, rows, cols), jnp.bfloat16),
-        in_specs=[SMEM, VMEM, VMEM, VMEM, VMEM],
-        out_specs=VMEM,
-        scratch_shapes=[pltpu.VMEM(own.shape, jnp.float32)],
-        compiler_params=params(40),
+        out_shape=(
+            jax.ShapeDtypeStruct((devices, rows, cols), jnp.bfloat16),
+            jax.ShapeDtypeStruct(cache.shape, cache.dtype),
+        ),
+        in_specs=[SMEM, VMEM, VMEM, VMEM, VMEM, HBM],
+        out_specs=(VMEM, VMEM),
+        scratch_shapes=[
+            pltpu.VMEM(own.shape, jnp.float32),
+            pltpu.SemaphoreType.DMA((cache.shape[0],)),
+        ],
+        compiler_params=params(28),
         name="qkv_project",
-    )(me, bias, own, left, held)
+    )(me, bias, own, left, held, cache)
 
 
 def attend_kernel(
@@ -272,27 +378,13 @@
     qkv_ref,
     cos_ref,
     sin_ref,
-    k_hbm,
-    v_hbm,
-    out_ref,
     keys,
     values,
-    sems,
+    out_ref,
     heads,
     mixed,
     stage,
 ):
-    copies = []
-    for r in range(rows):
-        copies.append(
-            (
-                pltpu.make_async_copy(k_hbm.at[r], keys.at[r], sems.at[0, r]),
-                pltpu.make_async_copy(v_hbm.at[r], values.at[r], sems.at[1, r]),
-            )
-        )
-    for of_row in copies:
-        for copy in of_row:
-            copy.start()
     total_heads = QUERY_HEADS + 2 * KVH
     half = HEAD_SIZE // 2
     for h in range(total_heads):
@@ -301,9 +393,6 @@
     scale = 1.0 / HEAD_SIZE**0.5
 
     for r in range(rows):
-        for of_row in {0: copies[:1], 1: copies[1:3], 3: copies[3:]}.get(r, []):
-            for copy in of_row:
-                copy.wait()
         base = r * total_heads
         turned = heads[base : base + QUERY_HEADS + KVH, :]
         cosine = cos_ref[r : r + 1, :]
@@ -357,17 +446,14 @@
     return pl.pallas_call(
         functools.partial(attend_kernel, rows),
         out_shape=jax.ShapeDtypeStruct((8, rows * features // 8 + LANES), jnp.bfloat16),
-        in_specs=[SMEM, SMEM, VMEM, VMEM, VMEM, HBM, HBM],
+        in_specs=[SMEM, SMEM, VMEM, VMEM, VMEM, VMEM, VMEM],
         out_specs=VMEM,
         scratch_shapes=[
-            pltpu.VMEM(keys.shape, jnp.bfloat16),
-            pltpu.VMEM(keys.shape, jnp.bfloat16),
-            pltpu.SemaphoreType.DMA((2, rows)),
             pltpu.VMEM((rows * total_heads, HEAD_SIZE), jnp.float32),
             pltpu.VMEM((rows * QUERY_HEADS, HEAD_SIZE), jnp.float32),
             pltpu.VMEM((BLOCKS * rows, features // BLOCKS), jnp.float32),
         ],
-        compiler_params=params(50),
+        compiler_params=params(24),
         name="attend",
     )(lengths, ids, qkv, cosine, sine, keys, values)
 
@@ -435,8 +521,7 @@
     target = lax.broadcasted_iota(jnp.int32, (2 * rows, 2 * rows), 1)
     move = jnp.where(place_of[:, :1] == target, 1.0, 0.0).astype(jnp.bfloat16)
     coords = jnp.dot(coords, move, preferred_element_type=jnp.float32).astype(jnp.bfloat16)
-    for d in range(devices):
-        coords_ref[d] = coords
+    coords_ref[...] = coords
 
 
 def shrink(me, own_part, own, other, down, devices):
@@ -444,7 +529,7 @@
     rows = devices * 8
     return pl.pallas_call(
         functools.partial(shrink_kernel, devices),
-        out_shape=jax.ShapeDtypeStruct((devices, stored * rank, rows), jnp.bfloat16),
+        out_shape=jax.ShapeDtypeStruct((stored * rank, rows), jnp.bfloat16),
         in_specs=[SMEM, VMEM, VMEM, VMEM, VMEM],
         out_specs=VMEM,
         scratch_shapes=[
@@ -484,24 +569,34 @@
     )(me, own, left, held)
 
 
-def add_kernel(rows, base_ref, coords_ref, up_ref, out_ref):
+def add_kernel(devices, rows, me_ref, base_ref, up_ref, *refs):
+    lines, (out_ref, coords) = refs[:-2], refs[-2:]
+    part = coords.shape[1]
+    for k, line in enumerate(lines):
+        for at, (m, c) in enumerate(neighbours(devices)):
+            coords[source(devices, me_ref[0], k, m, c)] = line[at * part : (at + 1) * part, :]
     delta = lax.dot_general(
-        coords_ref[...], up_ref[...], (((0,), (0,)), ((), ())), preferred_element_type=jnp.float32
+        coords[...].reshape(devices * part, coords.shape[2]),
+        up_ref[...],
+        (((0,), (0,)), ((), ())),
+        preferred_element_type=jnp.float32,
     )
     projected = base_ref[...] + delta
-    for d in range(out_ref.shape[0]):
+    for d in range(devices):
         out_ref[d] = projected[8 * d : 8 * d + rows, :].astype(jnp.bfloat16)
 
 
-def add_delta(base, coords, up, rows):
-    return pl.pallas_call(
-        functools.partial(add_kernel, rows),
-        out_shape=jax.ShapeDtypeStruct((base.shape[0] // 8, rows, base.shape[1]), jnp.bfloat16),
-        in_specs=[VMEM, VMEM, VMEM],
-        out_specs=VMEM,
-        compiler_params=params(40),
+def add_delta(me, base, lines, up, devices, rows):
+    part = up.shape[0] // devices
+    return pl.pallas_call(
+        functools.partial(add_kernel, devices, rows),
+        out_shape=jax.ShapeDtypeStruct((devices, rows, base.shape[1]), jnp.bfloat16),
+        in_specs=[SMEM, VMEM, VMEM] + [VMEM] * len(lines),
+        out_specs=VMEM,
+        scratch_shapes=[pltpu.VMEM((devices, part, lines[0].shape[1]), jnp.bfloat16)],
+        compiler_params=params(48),
         name="add_delta",
-    )(base, coords, up)
+    )(me, base, up, *lines)
 
 
 def exchange(parts):
@@ -539,20 +634,19 @@
     up = adapter_up_weight.reshape(-1, adapter_up_weight.shape[2])
 
     bias = projection_bias.reshape(1, -1)
-    tables = (bias, cosine, sine)
     chunks, held = gather_chunks(
         norm_chunk(hidden, input_norm_scale),
         devices,
-        lambda chunk: hold(query_key_value_weight, chunk, tables, 40, "hold_qkv"),
+        lambda chunk: hold(query_key_value_weight, chunk, (me,), 40, "hold_qkv"),
     )
     mine = unpack(chunks, rows, hidden.shape[1], False)
     theirs = across(mine, devices)
-    own = own_rows(mine, held, "qkv_own")
-    qkv = qkv_project(me, own, theirs, held, bias, devices, rows)
+    own, keys = qkv_own(mine, held, rotated_key_cache)
+    qkv, values = qkv_project(
+        me, own, theirs, held, bias, past_value_cache, devices, rows
+    )
     qkv = per_row(exchange(qkv))
-    chunk = attend(
-        lengths, row_adapter_index, qkv, cosine, sine, rotated_key_cache, past_value_cache
-    )
+    chunk = attend(lengths, row_adapter_index, qkv, cosine, sine, keys, values)
     chunks, held = gather_chunks(
         chunk, devices, lambda chunk: hold(output_weight, chunk, (), 42, "hold_output")
     )
@@ -560,10 +654,9 @@
     theirs = across(mine, devices)
     own_part = shrink_own(mine, down)
     own = own_rows(mine, held, "base_own")
-    coords = exchange(shrink(me, own_part, mine, theirs, down, devices))
+    lines = gather_coords(shrink(me, own_part, mine, theirs, down, devices), devices)
     base = base_project(me, own, theirs, held, devices)
-    coords = coords.reshape(-1, coords.shape[2])
-    return per_row(exchange(add_delta(base, coords, up, rows)))
+    return per_row(exchange(add_delta(me, base, lines, up, devices, rows)))
 
 
 def solution(mesh):

time: 110 us -> 101 us (0.918)
  blocking collectives: 27.2 us -> 11.5 us
  waiting for transfers between devices: 13.4 us -> 25.3 us
  local copies, waits for them, and re-layouts: 21.4 us -> 11.3 us
  starting transfers between devices: 21.1 us -> 28.4 us
    all_to_all x2 -> x1, blocking collectives: 27.2 us -> 11.5 us  [exchange(): lax.all_to_all(parts, 'tensor', split_axis=0, concat_axis=0, tiled=True)]
    unnamed x25 -> x31, local copies, waits for them, and re-layouts: 20.7 us -> 11.3 us
    all_to_all x1, waiting for transfers between devices: 0.01 us -> 8.27 us  [exchange(): lax.all_to_all(parts, 'tensor', split_axis=0, concat_axis=0, tiled=True)]
    ppermute x0 -> x6, starting transfers between devices: none -> 6.26 us  [the longest x3 4.38 us: along_line(): lax.ppermute(x, 'tensor', [(d, 2 * (partner(d // 2 // inner, k, outer) *...]
    pallas_call x2 -> x4, Pallas kernels: 2.18 us -> 5.61 us  [the longest x1 3.02 us: qkv_project(): pl.pallas_call(functools.partial(qkv_kernel, devices, rows), out_shape=(j...]
    ppermute x0 -> x6, waiting for transfers between devices: none -> 3.04 us  [the longest x3 1.88 us: along_line(): lax.ppermute(x, 'tensor', [(d, 2 * (partner(d // 2 // inner, k, outer) *...]
    ppermute x6, waiting for transfers between devices: 1.3 us -> 3.52 us  [gather_chunks(): lax.ppermute(chunk, 'tensor', pairs(k, 0))]
    pallas_call x2 -> x1, Pallas kernels: 3.47 us -> 1.54 us  [own_rows(): pl.pallas_call(multiply, out_shape=jax.ShapeDtypeStruct((rows, cols), jnp...]
  transfers between devices with their start and end apart: 17 -> 23, of which waited for: 8 -> 14; matrix products, arithmetic and copies ran while one was open for 1% -> 0% of each run, Pallas kernels for 12% -> 14%
where the time goes in v5:
time: 101 us
  starting transfers between devices  28.4 us (28%)
  waiting for transfers between devices  25.3 us (25%)
  Pallas kernels  24 us (24%)
  blocking collectives  11.5 us (11%)
  local copies, waits for them, and re-layouts  11.3 us (11%)
    all_to_all x1, blocking collectives, exchange(): lax.all_to_all(parts, 'tensor', split_axis=0, concat_axis=0, tiled=True)  11.5 us
    unnamed x31, local copies, waits for them, and re-layouts  11.3 us
    ppermute x6, starting transfers between devices, gather_chunks(): lax.ppermute(chunk, 'tensor', pairs(k, 0))  10.1 us
    all_to_all x1, waiting for transfers between devices, exchange(): lax.all_to_all(parts, 'tensor', split_axis=0, concat_axis=0, tiled=True)  8.27 us
    ppermute x8, waiting for transfers between devices, gather_chunks(): slots[k, m] = lax.ppermute(line[k], 'tensor', pairs(0, m))  8.24 us
    pallas_call x2, Pallas kernels, hold(): pl.pallas_call(functools.partial(hold_kernel, len(arrays)), out_shape=(ja...  7.7 us
    ppermute x8, starting transfers between devices, gather_chunks(): slots[k, m] = lax.ppermute(line[k], 'tensor', pairs(0, m))  6.95 us
    pallas_call x1, Pallas kernels, attend(): pl.pallas_call(functools.partial(attend_kernel, rows), out_shape=jax.Shap...  5.14 us
  transfers between devices with their start and end apart: 23, of which 14 were waited for; matrix products, arithmetic and copies ran while one was open for 0% of the time, Pallas kernels for 14%

profile of v5, /device:TPU:0, one launch (start us, length us, event | category | flops | bytes accessed | tf_op | source)
XLA Modules:
  0.0 101.0 jit_solution(9590519951951513238)
XLA Ops:
  0.0 0.9 copy-done.6
  0.9 0.7 copy-done.7
  1.6 0.4 norm_chunk.1.refs_0_
  2.0 3.1 %collective-permute-start = (bf16[8,6144]{1,0:T(8,128)(2,1)S(1)}, bf16[8,6144]{1,0:T(8,128)(2,1)S(1)}, u32[]{:S(2)}, u32[]{:S(2)}) collective-permute-start(bf16[8,6144]{1,0:T(8,128)(2,1)S(1)} %norm_chunk.1.refs_0_), channel_id=1, source_target_pairs={{0,4},{1,5},{2,6},{3,7},{4,0},{5,1},{6,2},{7,3},{8,12},{9,13},{10,... | collective-permute-start | bytes 294920 | tf_op jit(solution)/shard_map/ppermute | solution.py:74
  5.1 2.6 %collective-permute-start.1 = (bf16[8,6144]{1,0:T(8,128)(2,1)S(1)}, bf16[8,6144]{1,0:T(8,128)(2,1)S(1)}, u32[]{:S(2)}, u32[]{:S(2)}) collective-permute-start(bf16[8,6144]{1,0:T(8,128)(2,1)S(1)} %norm_chunk.1.refs_0_), channel_id=1, source_target_pairs={{0,8},{1,9},{2,10},{3,11},{4,12},{5,13},{6,14},{7,15},{8,0},{9,1},... | collective-permute-start | bytes 294920 | tf_op jit(solution)/shard_map/ppermute | solution.py:74
  7.7 0.0 collective-permute-start.2
  7.7 1.7 %collective-permute-start.3 = (bf16[8,6144]{1,0:T(8,128)(2,1)S(1)}, bf16[8,6144]{1,0:T(8,128)(2,1)S(1)}, u32[]{:S(2)}, u32[]{:S(2)}) collective-permute-start(bf16[8,6144]{1,0:T(8,128)(2,1)S(1)} %norm_chunk.1.refs_0_), channel_id=1, source_target_pairs={{0,2},{1,3},{2,0},{3,1},{4,6},{5,7},{6,4},{7,5},{8,10},{9,11},{10,... | collective-permute-start | bytes 294920 | tf_op jit(solution)/shard_map/ppermute | solution.py:79
  9.5 4.2 %hold_qkv.1 = (bf16[8192,640]{1,0:T(8,128)(2,1)S(1)}, bf16[8,6144]{1,0:T(8,128)(2,1)S(1)}) custom-call(bf16[8,6144]{1,0:T(8,128)(2,1)S(1)} %collective-permute-done.refs_0_, s32[1]{0:T(128)} %bitcast.refs_1_.me_ref, bf16[8192,640]{1,0:T(8,128)(2,1)} %refs_2_.1), custom_call_target="tpu_custom_call", output_to_operand_aliasing={{1}: (0, {})} | custom-call | bytes 20971520 | tf_op jit(solution)/shard_map/hold_qkv/pallas_call | solution.py:264
  13.7 0.4 collective-permute-start.4
  14.0 1.5 %collective-permute-done.1.refs_2_ = bf16[8,6144]{1,0:T(8,128)(2,1)S(1)} collective-permute-done((bf16[8,6144]{1,0:T(8,128)(2,1)S(1)}, bf16[8,6144]{1,0:T(8,128)(2,1)S(1)}, u32[]{:S(2)}, u32[]{:S(2)}) %collective-permute-start.1) | collective-permute-done | bytes 98336 | tf_op jit(solution)/shard_map/ppermute | solution.py:74
  15.5 1.5 %collective-permute-start.5 = (bf16[8,6144]{1,0:T(8,128)(2,1)S(1)}, bf16[8,6144]{1,0:T(8,128)(2,1)S(1)}, u32[]{:S(2)}, u32[]{:S(2)}) collective-permute-start(bf16[8,6144]{1,0:T(8,128)(2,1)S(1)} %collective-permute-done.1.refs_2_), channel_id=1, source_target_pairs={{0,2},{1,3},{2,0},{3,1},{4,6},{5,7},{6,4},{7,5},{8,10},{9,11},{10,... | collective-permute-start | bytes 294920 | tf_op jit(solution)/shard_map/ppermute | solution.py:79
  17.0 0.0 collective-permute-done.2.refs_3_
  17.0 0.5 collective-permute-start.6
  17.6 1.8 %collective-permute-done.4.refs_5_ = bf16[8,6144]{1,0:T(8,128)(2,1)S(1)} collective-permute-done((bf16[8,6144]{1,0:T(8,128)(2,1)S(1)}, bf16[8,6144]{1,0:T(8,128)(2,1)S(1)}, u32[]{:S(2)}, u32[]{:S(2)}) %collective-permute-start.4) | collective-permute-done | bytes 98336 | tf_op jit(solution)/shard_map/ppermute | solution.py:79
  19.3 1.1 %collective-permute-done.5.refs_6_ = bf16[8,6144]{1,0:T(8,128)(2,1)S(1)} collective-permute-done((bf16[8,6144]{1,0:T(8,128)(2,1)S(1)}, bf16[8,6144]{1,0:T(8,128)(2,1)S(1)}, u32[]{:S(2)}, u32[]{:S(2)}) %collective-permute-start.5) | collective-permute-done | bytes 98336 | tf_op jit(solution)/shard_map/ppermute | solution.py:79
  20.4 1.3 %collective-permute-done.6.refs_7_ = bf16[8,6144]{1,0:T(8,128)(2,1)S(1)} collective-permute-done((bf16[8,6144]{1,0:T(8,128)(2,1)S(1)}, bf16[8,6144]{1,0:T(8,128)(2,1)S(1)}, u32[]{:S(2)}, u32[]{:S(2)}) %collective-permute-start.6) | collective-permute-done | bytes 98336 | tf_op jit(solution)/shard_map/ppermute | solution.py:79
  21.7 0.3 unpack.2.left
  22.0 0.1 collective-permute-start.7
  22.1 0.0 slice-start.3
  22.1 2.3 %qkv_own.1 = (f32[64,640]{1,0:T(8,128)S(1)}, bf16[6,384,1024]{2,1,0:T(8,128)(2,1)S(1)}) custom-call(bf16[8,64,1024]{2,1,0:T(8,128)(2,1)S(1)} %unpack.2.left, bf16[8192,640]{1,0:T(8,128)(2,1)S(1)} %get-tuple-element.14.held, bf16[6,384,1024]{2,1,0:T(8,128)(2,1)S(1)} %bitcast.11), custom_call_target="tpu_custom_call" | custom-call | flops 671088640 | bytes 10485760 | tf_op jit(solution)/shard_map/qkv_own/pallas_call | solution.py:321
  24.5 2.1 %copy-done = bf16[6,384,1024]{2,1,0:T(8,128)(2,1)} copy-done((bf16[6,384,1024]{2,1,0:T(8,128)(2,1)}, bf16[6,384,1024]{2,1,0:T(8,128)(2,1)S(1)}, u32[]{:S(2)}) %copy-start) | copy-done | bytes 4718616
  26.6 0.0 collective-permute-done.7.left
  26.6 0.0 copy-start.9
  26.6 3.0 %qkv_project.1 = (bf16[16,6,640]{2,1,0:T(8,128)(2,1)}, bf16[6,384,1024]{2,1,0:T(8,128)(2,1)S(1)}) custom-call(s32[1]{0:T(128)} %bitcast.refs_1_.me_ref, bf16[1,640]{1,0:T(2,128)(2,1)S(1)} %reshape.26.bias_ref, f32[64,640]{1,0:T(8,128)S(1)} %get-tuple-element.15.own_ref, bf16[8,64,1024]{2,1,0:T(8,128)(2,1)S(1)} %collective-permute-done.7.left, ...), custom_call_target="tpu_custom_call" | custom-call | tf_op jit(solution)/shard_map/qkv_project/pallas_call | solution.py:357
  29.7 2.2 %copy-done.2 = bf16[6,384,1024]{2,1,0:T(8,128)(2,1)} copy-done((bf16[6,384,1024]{2,1,0:T(8,128)(2,1)}, bf16[6,384,1024]{2,1,0:T(8,128)(2,1)S(1)}, u32[]{:S(2)}) %copy-start.2) | copy-done | bytes 4718616
  31.8 4.9 %all-to-all-start = ((bf16[16,6,640]{2,1,0:T(8,128)(2,1)}), bf16[16,6,640]{2,1,0:T(8,128)(2,1)S(1)}, u32[]{:S(2)}, u32[]{:S(2)}) async-start(bf16[16,6,640]{2,1,0:T(8,128)(2,1)} %get-tuple-element.16), calls=%async_computation | async-start | bytes 327680 | tf_op jit(solution)/shard_map/all_to_all | solution.py:603
  36.8 0.1 fusion
  36.9 0.1 pad_maximum_fusion
  37.0 8.3 %all-to-all-done = bf16[16,6,640]{2,1,0:T(8,128)(2,1)S(1)} async-done(((bf16[16,6,640]{2,1,0:T(8,128)(2,1)}), bf16[16,6,640]{2,1,0:T(8,128)(2,1)S(1)}, u32[]{:S(2)}, u32[]{:S(2)}) %all-to-all-start) | async-done | bytes 122912 | tf_op jit(solution)/shard_map/all_to_all | solution.py:603
  45.2 2.3 %copy-done.1 = bf16[6,384,1024]{2,1,0:T(8,128)(2,1)S(1)} copy-done((bf16[6,384,1024]{2,1,0:T(8,128)(2,1)S(1)}, bf16[6,384,1024]{2,1,0:T(8,128)(2,1)}, u32[]{:S(2)}) %copy-start.1) | copy-done | bytes 4718616
  47.6 2.3 %copy-done.3 = bf16[6,384,1024]{2,1,0:T(8,128)(2,1)S(1)} copy-done((bf16[6,384,1024]{2,1,0:T(8,128)(2,1)S(1)}, bf16[6,384,1024]{2,1,0:T(8,128)(2,1)}, u32[]{:S(2)}) %copy-start.3) | copy-done | bytes 4718616
  49.9 5.1 %attend.1.refs_0_ = bf16[8,6272]{1,0:T(8,128)(2,1)S(1)} custom-call(s32[6]{0:T(128)S(1)} %copy-done.8, s32[6]{0:T(128)S(1)} %copy-done.9, bf16[6,10240]{1,0:T(8,128)(2,1)S(1)} %bitcast.16, f32[6,128]{1,0:T(8,128)S(1)} %get-tuple-element.24.cos_ref, f32[6,128]{1,0:T(8,128)S(1)} %get-tuple-element.25.sin_ref, bf16[6,384,1024]{2,1,0:T(8,128)(2,1)S(1)} %copy-done.1, ...), custom_call_target="tpu_custom_call" | custom-call | tf_op jit(solution)/shard_map/attend/pallas_call | solution.py:446
  55.1 0.0 copy-start.4
  55.1 0.1 collective-permute-start.8
  55.1 1.3 %collective-permute-start.9 = (bf16[8,6272]{1,0:T(8,128)(2,1)S(1)}, bf16[8,6272]{1,0:T(8,128)(2,1)S(1)}, u32[]{:S(2)}, u32[]{:S(2)}) collective-permute-start(bf16[8,6272]{1,0:T(8,128)(2,1)S(1)} %attend.1.refs_0_), channel_id=1, source_target_pairs={{0,8},{1,9},{2,10},{3,11},{4,12},{5,13},{6,14},{7,15},{8,0},{9,1},... | collective-permute-start | bytes 301064 | tf_op jit(solution)/shard_map/ppermute | solution.py:74
  56.5 3.0 %collective-permute-start.10 = (bf16[8,6272]{1,0:T(8,128)(2,1)S(1)}, bf16[8,6272]{1,0:T(8,128)(2,1)S(1)}, u32[]{:S(2)}, u32[]{:S(2)}) collective-permute-start(bf16[8,6272]{1,0:T(8,128)(2,1)S(1)} %attend.1.refs_0_), channel_id=1, source_target_pairs={{0,12},{1,13},{2,14},{3,15},{4,8},{5,9},{6,10},{7,11},{8,4},{9,5},... | collective-permute-start | bytes 301064 | tf_op jit(solution)/shard_map/ppermute | solution.py:74
  59.5 0.0 collective-permute-start.11
  59.5 1.3 %collective-permute-done.8.refs_0_ = bf16[8,6272]{1,0:T(8,128)(2,1)S(1)} collective-permute-done((bf16[8,6272]{1,0:T(8,128)(2,1)S(1)}, bf16[8,6272]{1,0:T(8,128)(2,1)S(1)}, u32[]{:S(2)}, u32[]{:S(2)}) %collective-permute-start.8) | collective-permute-done | bytes 100384 | tf_op jit(solution)/shard_map/ppermute | solution.py:74
  60.8 3.5 %hold_output.1 = (bf16[8192,512]{1,0:T(8,128)(2,1)S(1)}, bf16[8,6272]{1,0:T(8,128)(2,1)S(1)}) custom-call(bf16[8,6272]{1,0:T(8,128)(2,1)S(1)} %collective-permute-done.8.refs_0_, bf16[8192,512]{1,0:T(8,128)(2,1)} %refs_1_.1), custom_call_target="tpu_custom_call", output_to_operand_aliasing={{1}: (0, {})} | custom-call | bytes 16777216 | tf_op jit(solution)/shard_map/hold_output/pallas_call | solution.py:264
  64.3 0.8 collective-permute-start.12
  65.1 0.8 collective-permute-done.9.refs_2_
  65.9 0.5 collective-permute-start.13
  66.4 1.5 %collective-permute-start.14 = (bf16[8,6272]{1,0:T(8,128)(2,1)S(1)}, bf16[8,6272]{1,0:T(8,128)(2,1)S(1)}, u32[]{:S(2)}, u32[]{:S(2)}) collective-permute-start(bf16[8,6272]{1,0:T(8,128)(2,1)S(1)} %collective-permute-done.10.refs_3_), channel_id=1, source_target_pairs={{0,2},{1,3},{2,0},{3,1},{4,6},{5,7},{6,4},{7,5},{8,10},{9,11},{10,... | collective-permute-start | bytes 301064 | tf_op jit(solution)/shard_map/ppermute | solution.py:79
  67.9 2.0 %collective-permute-done.12.refs_5_ = bf16[8,6272]{1,0:T(8,128)(2,1)S(1)} collective-permute-done((bf16[8,6272]{1,0:T(8,128)(2,1)S(1)}, bf16[8,6272]{1,0:T(8,128)(2,1)S(1)}, u32[]{:S(2)}, u32[]{:S(2)}) %collective-permute-start.12) | collective-permute-done | bytes 100384 | tf_op jit(solution)/shard_map/ppermute | solution.py:79
  69.9 1.1 %collective-permute-done.13.refs_6_ = bf16[8,6272]{1,0:T(8,128)(2,1)S(1)} collective-permute-done((bf16[8,6272]{1,0:T(8,128)(2,1)S(1)}, bf16[8,6272]{1,0:T(8,128)(2,1)S(1)}, u32[]{:S(2)}, u32[]{:S(2)}) %collective-permute-start.13) | collective-permute-done | bytes 100384 | tf_op jit(solution)/shard_map/ppermute | solution.py:79
  70.9 1.1 %collective-permute-done.14.refs_7_ = bf16[8,6272]{1,0:T(8,128)(2,1)S(1)} collective-permute-done((bf16[8,6272]{1,0:T(8,128)(2,1)S(1)}, bf16[8,6272]{1,0:T(8,128)(2,1)S(1)}, u32[]{:S(2)}, u32[]{:S(2)}) %collective-permute-start.14) | collective-permute-done | bytes 100384 | tf_op jit(solution)/shard_map/ppermute | solution.py:79
  72.0 0.3 unpack.3.left.own
  72.3 0.1 collective-permute-start.15
  72.4 0.6 shrink_own.1.own_part
  73.0 2.2 %collective-permute-done.15.left.other = bf16[9,64,1024]{2,1,0:T(8,128)(2,1)S(1)} collective-permute-done((bf16[9,64,1024]{2,1,0:T(8,128)(2,1)S(1)}, bf16[9,64,1024]{2,1,0:T(8,128)(2,1)S(1)}, u32[]{:S(2)}, u32[]{:S(2)}) %collective-permute-start.15) | collective-permute-done | bytes 1179680 | tf_op jit(solution)/shard_map/ppermute | solution.py:145
  75.2 0.9 shrink.1.refs_0_
  76.1 0.2 collective-permute-start.16
  76.2 1.4 %collective-permute-start.17 = (bf16[32,128]{1,0:T(8,128)(2,1)S(1)}, bf16[32,128]{1,0:T(8,128)(2,1)S(1)}, u32[]{:S(2)}, u32[]{:S(2)}) collective-permute-start(bf16[32,128]{1,0:T(8,128)(2,1)S(1)} %shrink.1.refs_0_), channel_id=1, source_target_pairs={{0,2},{1,3},{2,0},{3,1},{4,6},{5,7},{6,4},{7,5},{8,10},{9,11},{10,... | collective-permute-start | bytes 24584 | tf_op jit(solution)/shard_map/ppermute | solution.py:92
  77.6 0.4 collective-permute-start.18
  78.0 1.5 %base_own.1.own_ref = f32[64,512]{1,0:T(8,128)S(1)} custom-call(bf16[9,64,1024]{2,1,0:T(8,128)(2,1)S(1)} %unpack.3.left.own, bf16[8192,512]{1,0:T(8,128)(2,1)S(1)} %get-tuple-element.20.held), custom_call_target="tpu_custom_call" | custom-call | flops 536870912 | bytes 8388608 | tf_op jit(solution)/shard_map/base_own/pallas_call | solution.py:291
  79.5 0.4 collective-permute-done.17.refs_2_
  79.9 0.8 collective-permute-done.18.refs_3_
  80.7 2.1 %collective-permute-start.20 = (bf16[128,128]{1,0:T(8,128)(2,1)S(1)}, bf16[128,128]{1,0:T(8,128)(2,1)S(1)}, u32[]{:S(2)}, u32[]{:S(2)}) collective-permute-start(bf16[128,128]{1,0:T(8,128)(2,1)S(1)} %join_coords.1.refs_0_), channel_id=1, source_target_pairs={{0,8},{1,9},{2,10},{3,11},{4,12},{5,13},{6,14},{7,15},{8,0},{9,1},... | collective-permute-start | bytes 98312 | tf_op jit(solution)/shard_map/ppermute | solution.py:104
  82.8 2.3 %collective-permute-start.21 = (bf16[128,128]{1,0:T(8,128)(2,1)S(1)}, bf16[128,128]{1,0:T(8,128)(2,1)S(1)}, u32[]{:S(2)}, u32[]{:S(2)}) collective-permute-start(bf16[128,128]{1,0:T(8,128)(2,1)S(1)} %join_coords.1.refs_0_), channel_id=1, source_target_pairs={{0,12},{1,13},{2,14},{3,15},{4,8},{5,9},{6,10},{7,11},{8,4},{9,5},... | collective-permute-start | bytes 98312 | tf_op jit(solution)/shard_map/ppermute | solution.py:104
  85.1 1.5 %base_project.1.base_ref = f32[128,512]{1,0:T(8,128)S(1)} custom-call(s32[1]{0:T(128)} %bitcast.refs_1_.me_ref, f32[64,512]{1,0:T(8,128)S(1)} %base_own.1.own_ref, bf16[9,64,1024]{2,1,0:T(8,128)(2,1)S(1)} %collective-permute-done.15.left.other, bf16[8192,512]{1,0:T(8,128)(2,1)S(1)} %get-tuple-element.20.held), custom_call_target="tpu_custom_call" | custom-call | flops 536870912 | bytes 8388608 | tf_op jit(solution)/shard_map/base_project/pallas_call | solution.py:558
  86.7 1.9 %collective-permute-done.21.refs_3_ = bf16[128,128]{1,0:T(8,128)(2,1)S(1)} collective-permute-done((bf16[128,128]{1,0:T(8,128)(2,1)S(1)}, bf16[128,128]{1,0:T(8,128)(2,1)S(1)}, u32[]{:S(2)}, u32[]{:S(2)}) %collective-permute-start.21) | collective-permute-done | bytes 32800 | tf_op jit(solution)/shard_map/ppermute | solution.py:104
  88.5 0.3 add_delta.1
  88.8 11.5 %all_to_all.10 = bf16[16,6,512]{2,1,0:T(8,128)(2,1)S(1)} all-to-all(bf16[16,6,512]{2,1,0:T(8,128)(2,1)S(1)} %add_delta.1), channel_id=1, replica_groups=mesh['group'=2,'tensor'=16] {'tensor'}, dimensions={0} | all-to-all | bytes 196608 | tf_op jit(solution)/shard_map/all_to_all | solution.py:603
  100.3 0.7 copy.17
  (35 shorter events, 0.1 us)
Async XLA Ops:
  0.0 0.9 copy-start.6
  0.9 0.7 copy-start.7
  2.0 7.4 %collective-permute-start = (bf16[8,6144]{1,0:T(8,128)(2,1)S(1)}, bf16[8,6144]{1,0:T(8,128)(2,1)S(1)}, u32[]{:S(2)}, u32[]{:S(2)}) collective-permute-start(bf16[8,6144]{1,0:T(8,128)(2,1)S(1)} %norm_chunk.1.refs_0_), channel_id=1, source_target_pairs={{0,4},{1,5},{2,6},{3,7},{4,0},{5,1},{6,2},{7,3},{8,12},{9,13},{10,... | collective-permute-start | bytes 294920 | tf_op jit(solution)/shard_map/ppermute | solution.py:74
  5.1 10.4 %collective-permute-start.1 = (bf16[8,6144]{1,0:T(8,128)(2,1)S(1)}, bf16[8,6144]{1,0:T(8,128)(2,1)S(1)}, u32[]{:S(2)}, u32[]{:S(2)}) collective-permute-start(bf16[8,6144]{1,0:T(8,128)(2,1)S(1)} %norm_chunk.1.refs_0_), channel_id=1, source_target_pairs={{0,8},{1,9},{2,10},{3,11},{4,12},{5,13},{6,14},{7,15},{8,0},{9,1},... | collective-permute-start | bytes 294920 | tf_op jit(solution)/shard_map/ppermute | solution.py:74
  7.7 9.4 %collective-permute-start.2 = (bf16[8,6144]{1,0:T(8,128)(2,1)S(1)}, bf16[8,6144]{1,0:T(8,128)(2,1)S(1)}, u32[]{:S(2)}, u32[]{:S(2)}) collective-permute-start(bf16[8,6144]{1,0:T(8,128)(2,1)S(1)} %norm_chunk.1.refs_0_), channel_id=1, source_target_pairs={{0,12},{1,13},{2,14},{3,15},{4,8},{5,9},{6,10},{7,11},{8,4},{9,5},... | collective-permute-start | bytes 294920 | tf_op jit(solution)/shard_map/ppermute | solution.py:74
  7.7 9.9 %collective-permute-start.3 = (bf16[8,6144]{1,0:T(8,128)(2,1)S(1)}, bf16[8,6144]{1,0:T(8,128)(2,1)S(1)}, u32[]{:S(2)}, u32[]{:S(2)}) collective-permute-start(bf16[8,6144]{1,0:T(8,128)(2,1)S(1)} %norm_chunk.1.refs_0_), channel_id=1, source_target_pairs={{0,2},{1,3},{2,0},{3,1},{4,6},{5,7},{6,4},{7,5},{8,10},{9,11},{10,... | collective-permute-start | bytes 294920 | tf_op jit(solution)/shard_map/ppermute | solution.py:79
  9.4 12.7 %slice-start = ((s8[4718592]{0:T(1024)(128)(4,1)}), s8[4194304]{0:T(1024)(128)(4,1)S(1)}, s32[]{:S(2)}) async-start(s8[4718592]{0:T(1024)(128)(4,1)} %bitcast.10), calls=%async_computation.2 | async-start | bytes 8388608
  9.4 12.6 %copy-start.10 = (bf16[640]{0:T(1024)(128)(2,1)S(1)}, bf16[640]{0:T(1024)(128)(2,1)}, u32[]{:S(2)}) copy-start(bf16[640]{0:T(1024)(128)(2,1)} %param.14) | copy-start | bytes 3844
  9.4 12.6 %copy-start.8 = (s32[6]{0:T(128)S(1)}, s32[6]{0:T(128)}, u32[]{:S(2)}) copy-start(s32[6]{0:T(128)} %len_ref.1) | copy-start | bytes 76
  9.4 12.7 %slice-start.1 = ((s8[4718592]{0:T(1024)(128)(4,1)}), s8[524288]{0:T(1024)(128)(4,1)S(1)}, s32[]{:S(2)}) async-start(s8[4718592]{0:T(1024)(128)(4,1)} %bitcast.10), calls=%async_computation.3 | async-start | bytes 1048576
  13.7 5.6 %collective-permute-start.4 = (bf16[8,6144]{1,0:T(8,128)(2,1)S(1)}, bf16[8,6144]{1,0:T(8,128)(2,1)S(1)}, u32[]{:S(2)}, u32[]{:S(2)}) collective-permute-start(bf16[8,6144]{1,0:T(8,128)(2,1)S(1)} %get-tuple-element.13.refs_1_), channel_id=1, source_target_pairs={{0,2},{1,3},{2,0},{3,1},{4,6},{5,7},{6,4},{7,5},{8,10},{9,11},{10,... | collective-permute-start | bytes 294920 | tf_op jit(solution)/shard_map/ppermute | solution.py:79
  15.5 4.9 %collective-permute-start.5 = (bf16[8,6144]{1,0:T(8,128)(2,1)S(1)}, bf16[8,6144]{1,0:T(8,128)(2,1)S(1)}, u32[]{:S(2)}, u32[]{:S(2)}) collective-permute-start(bf16[8,6144]{1,0:T(8,128)(2,1)S(1)} %collective-permute-done.1.refs_2_), channel_id=1, source_target_pairs={{0,2},{1,3},{2,0},{3,1},{4,6},{5,7},{6,4},{7,5},{8,10},{9,11},{10,... | collective-permute-start | bytes 294920 | tf_op jit(solution)/shard_map/ppermute | solution.py:79
  17.0 4.6 %collective-permute-start.6 = (bf16[8,6144]{1,0:T(8,128)(2,1)S(1)}, bf16[8,6144]{1,0:T(8,128)(2,1)S(1)}, u32[]{:S(2)}, u32[]{:S(2)}) collective-permute-start(bf16[8,6144]{1,0:T(8,128)(2,1)S(1)} %collective-permute-done.2.refs_3_), channel_id=1, source_target_pairs={{0,2},{1,3},{2,0},{3,1},{4,6},{5,7},{6,4},{7,5},{8,10},{9,11},{10,... | collective-permute-start | bytes 294920 | tf_op jit(solution)/shard_map/ppermute | solution.py:79
  21.7 5.0 %slice-start.2 = ((s8[4718592]{0:T(1024)(128)(4,1)}), s8[524288]{0:T(1024)(128)(4,1)S(1)}, s32[]{:S(2)}) async-start(s8[4718592]{0:T(1024)(128)(4,1)} %bitcast.12), calls=%async_computation.4 | async-start | bytes 1048576
  22.0 4.6 %collective-permute-start.7 = (bf16[8,64,1024]{2,1,0:T(8,128)(2,1)S(1)}, bf16[8,64,1024]{2,1,0:T(8,128)(2,1)S(1)}, u32[]{:S(2)}, u32[]{:S(2)}) collective-permute-start(bf16[8,64,1024]{2,1,0:T(8,128)(2,1)S(1)} %unpack.2.left), channel_id=1, source_target_pairs={{0,1},{1,0},{2,3},{3,2},{4,5},{5,4},{6,7},{7,6},{8,9},{9,8},{10,11... | collective-permute-start | bytes 3145736 | tf_op jit(solution)/shard_map/ppermute | solution.py:145
  22.1 4.5 %slice-start.3 = ((s8[4718592]{0:T(1024)(128)(4,1)}), s8[4194304]{0:T(1024)(128)(4,1)S(1)}, s32[]{:S(2)}) async-start(s8[4718592]{0:T(1024)(128)(4,1)} %bitcast.12), calls=%async_computation.5 | async-start | bytes 8388608
  24.5 2.1 %copy-start = (bf16[6,384,1024]{2,1,0:T(8,128)(2,1)}, bf16[6,384,1024]{2,1,0:T(8,128)(2,1)S(1)}, u32[]{:S(2)}) copy-start(bf16[6,384,1024]{2,1,0:T(8,128)(2,1)S(1)} %get-tuple-element.17.keys) | copy-start | bytes 14155780
  26.6 18.6 %copy-start.9 = (s32[6]{0:T(128)S(1)}, s32[6]{0:T(128)}, u32[]{:S(2)}) copy-start(s32[6]{0:T(128)} %ids_ref.1) | copy-start | bytes 76
  29.7 2.2 %copy-start.2 = (bf16[6,384,1024]{2,1,0:T(8,128)(2,1)}, bf16[6,384,1024]{2,1,0:T(8,128)(2,1)S(1)}, u32[]{:S(2)}) copy-start(bf16[6,384,1024]{2,1,0:T(8,128)(2,1)S(1)} %get-tuple-element.18.values) | copy-start | bytes 14155780
  31.8 13.4 %all-to-all-start = ((bf16[16,6,640]{2,1,0:T(8,128)(2,1)}), bf16[16,6,640]{2,1,0:T(8,128)(2,1)S(1)}, u32[]{:S(2)}, u32[]{:S(2)}) async-start(bf16[16,6,640]{2,1,0:T(8,128)(2,1)} %get-tuple-element.16), calls=%async_computation | async-start | bytes 327680 | tf_op jit(solution)/shard_map/all_to_all | solution.py:603
  45.2 2.3 %copy-start.1 = (bf16[6,384,1024]{2,1,0:T(8,128)(2,1)S(1)}, bf16[6,384,1024]{2,1,0:T(8,128)(2,1)}, u32[]{:S(2)}) copy-start(bf16[6,384,1024]{2,1,0:T(8,128)(2,1)} %copy-done) | copy-start | bytes 14155780
  47.6 2.3 %copy-start.3 = (bf16[6,384,1024]{2,1,0:T(8,128)(2,1)S(1)}, bf16[6,384,1024]{2,1,0:T(8,128)(2,1)}, u32[]{:S(2)}) copy-start(bf16[6,384,1024]{2,1,0:T(8,128)(2,1)} %copy-done.2) | copy-start | bytes 14155780
  55.1 17.4 %copy-start.4 = (bf16[2,8192,16]{1,2,0:T(8,128)(2,1)S(1)}, bf16[2,8192,16]{1,2,0:T(8,128)(2,1)}, u32[]{:S(2)}) copy-start(bf16[2,8192,16]{1,2,0:T(8,128)(2,1)} %param.20) | copy-start | bytes 1572868
  55.1 5.7 %collective-permute-start.8 = (bf16[8,6272]{1,0:T(8,128)(2,1)S(1)}, bf16[8,6272]{1,0:T(8,128)(2,1)S(1)}, u32[]{:S(2)}, u32[]{:S(2)}) collective-permute-start(bf16[8,6272]{1,0:T(8,128)(2,1)S(1)} %attend.1.refs_0_), channel_id=1, source_target_pairs={{0,4},{1,5},{2,6},{3,7},{4,0},{5,1},{6,2},{7,3},{8,12},{9,13},{10,... | collective-permute-start | bytes 301064 | tf_op jit(solution)/shard_map/ppermute | solution.py:74
  55.1 10.7 %collective-permute-start.9 = (bf16[8,6272]{1,0:T(8,128)(2,1)S(1)}, bf16[8,6272]{1,0:T(8,128)(2,1)S(1)}, u32[]{:S(2)}, u32[]{:S(2)}) collective-permute-start(bf16[8,6272]{1,0:T(8,128)(2,1)S(1)} %attend.1.refs_0_), channel_id=1, source_target_pairs={{0,8},{1,9},{2,10},{3,11},{4,12},{5,13},{6,14},{7,15},{8,0},{9,1},... | collective-permute-start | bytes 301064 | tf_op jit(solution)/shard_map/ppermute | solution.py:74
  56.5 9.9 %collective-permute-start.10 = (bf16[8,6272]{1,0:T(8,128)(2,1)S(1)}, bf16[8,6272]{1,0:T(8,128)(2,1)S(1)}, u32[]{:S(2)}, u32[]{:S(2)}) collective-permute-start(bf16[8,6272]{1,0:T(8,128)(2,1)S(1)} %attend.1.refs_0_), channel_id=1, source_target_pairs={{0,12},{1,13},{2,14},{3,15},{4,8},{5,9},{6,10},{7,11},{8,4},{9,5},... | collective-permute-start | bytes 301064 | tf_op jit(solution)/shard_map/ppermute | solution.py:74
  59.5 8.4 %collective-permute-start.11 = (bf16[8,6272]{1,0:T(8,128)(2,1)S(1)}, bf16[8,6272]{1,0:T(8,128)(2,1)S(1)}, u32[]{:S(2)}, u32[]{:S(2)}) collective-permute-start(bf16[8,6272]{1,0:T(8,128)(2,1)S(1)} %attend.1.refs_0_), channel_id=1, source_target_pairs={{0,2},{1,3},{2,0},{3,1},{4,6},{5,7},{6,4},{7,5},{8,10},{9,11},{10,... | collective-permute-start | bytes 301064 | tf_op jit(solution)/shard_map/ppermute | solution.py:79
  64.3 5.6 %collective-permute-start.12 = (bf16[8,6272]{1,0:T(8,128)(2,1)S(1)}, bf16[8,6272]{1,0:T(8,128)(2,1)S(1)}, u32[]{:S(2)}, u32[]{:S(2)}) collective-permute-start(bf16[8,6272]{1,0:T(8,128)(2,1)S(1)} %get-tuple-element.19.refs_1_), channel_id=1, source_target_pairs={{0,2},{1,3},{2,0},{3,1},{4,6},{5,7},{6,4},{7,5},{8,10},{9,11},{10,... | collective-permute-start | bytes 301064 | tf_op jit(solution)/shard_map/ppermute | solution.py:79
  65.9 5.1 %collective-permute-start.13 = (bf16[8,6272]{1,0:T(8,128)(2,1)S(1)}, bf16[8,6272]{1,0:T(8,128)(2,1)S(1)}, u32[]{:S(2)}, u32[]{:S(2)}) collective-permute-start(bf16[8,6272]{1,0:T(8,128)(2,1)S(1)} %collective-permute-done.9.refs_2_), channel_id=1, source_target_pairs={{0,2},{1,3},{2,0},{3,1},{4,6},{5,7},{6,4},{7,5},{8,10},{9,11},{10,... | collective-permute-start | bytes 301064 | tf_op jit(solution)/shard_map/ppermute | solution.py:79
  66.4 5.6 %collective-permute-start.14 = (bf16[8,6272]{1,0:T(8,128)(2,1)S(1)}, bf16[8,6272]{1,0:T(8,128)(2,1)S(1)}, u32[]{:S(2)}, u32[]{:S(2)}) collective-permute-start(bf16[8,6272]{1,0:T(8,128)(2,1)S(1)} %collective-permute-done.10.refs_3_), channel_id=1, source_target_pairs={{0,2},{1,3},{2,0},{3,1},{4,6},{5,7},{6,4},{7,5},{8,10},{9,11},{10,... | collective-permute-start | bytes 301064 | tf_op jit(solution)/shard_map/ppermute | solution.py:79
  72.3 2.9 %collective-permute-start.15 = (bf16[9,64,1024]{2,1,0:T(8,128)(2,1)S(1)}, bf16[9,64,1024]{2,1,0:T(8,128)(2,1)S(1)}, u32[]{:S(2)}, u32[]{:S(2)}) collective-permute-start(bf16[9,64,1024]{2,1,0:T(8,128)(2,1)S(1)} %unpack.3.left.own), channel_id=1, source_target_pairs={{0,1},{1,0},{2,3},{3,2},{4,5},{5,4},{6,7},{7,6},{8,9},{9,8},{10,11... | collective-permute-start | bytes 3538952 | tf_op jit(solution)/shard_map/ppermute | solution.py:145
  76.1 3.4 %collective-permute-start.16 = (bf16[32,128]{1,0:T(8,128)(2,1)S(1)}, bf16[32,128]{1,0:T(8,128)(2,1)S(1)}, u32[]{:S(2)}, u32[]{:S(2)}) collective-permute-start(bf16[32,128]{1,0:T(8,128)(2,1)S(1)} %shrink.1.refs_0_), channel_id=1, source_target_pairs={{0,1},{1,0},{2,3},{3,2},{4,5},{5,4},{6,7},{7,6},{8,9},{9,8},{10,11... | collective-permute-start | bytes 24584 | tf_op jit(solution)/shard_map/ppermute | solution.py:92
  76.2 3.7 %collective-permute-start.17 = (bf16[32,128]{1,0:T(8,128)(2,1)S(1)}, bf16[32,128]{1,0:T(8,128)(2,1)S(1)}, u32[]{:S(2)}, u32[]{:S(2)}) collective-permute-start(bf16[32,128]{1,0:T(8,128)(2,1)S(1)} %shrink.1.refs_0_), channel_id=1, source_target_pairs={{0,2},{1,3},{2,0},{3,1},{4,6},{5,7},{6,4},{7,5},{8,10},{9,11},{10,... | collective-permute-start | bytes 24584 | tf_op jit(solution)/shard_map/ppermute | solution.py:92
  77.6 3.1 %collective-permute-start.18 = (bf16[32,128]{1,0:T(8,128)(2,1)S(1)}, bf16[32,128]{1,0:T(8,128)(2,1)S(1)}, u32[]{:S(2)}, u32[]{:S(2)}) collective-permute-start(bf16[32,128]{1,0:T(8,128)(2,1)S(1)} %shrink.1.refs_0_), channel_id=1, source_target_pairs={{0,3},{1,2},{2,1},{3,0},{4,7},{5,6},{6,5},{7,4},{8,11},{9,10},{10,... | collective-permute-start | bytes 24584 | tf_op jit(solution)/shard_map/ppermute | solution.py:92
  80.7 7.8 %copy-start.5 = (bf16[32,16,512]{2,1,0:T(8,128)(2,1)S(1)}, bf16[32,16,512]{2,1,0:T(8,128)(2,1)}, u32[]{:S(2)}) copy-start(bf16[32,16,512]{2,1,0:T(8,128)(2,1)} %param.21) | copy-start | bytes 1572868
  80.7 5.9 %collective-permute-start.19 = (bf16[128,128]{1,0:T(8,128)(2,1)S(1)}, bf16[128,128]{1,0:T(8,128)(2,1)S(1)}, u32[]{:S(2)}, u32[]{:S(2)}) collective-permute-start(bf16[128,128]{1,0:T(8,128)(2,1)S(1)} %join_coords.1.refs_0_), channel_id=1, source_target_pairs={{0,4},{1,5},{2,6},{3,7},{4,0},{5,1},{6,2},{7,3},{8,12},{9,13},{10,... | collective-permute-start | bytes 98312 | tf_op jit(solution)/shard_map/ppermute | solution.py:104
  80.7 5.9 %collective-permute-start.20 = (bf16[128,128]{1,0:T(8,128)(2,1)S(1)}, bf16[128,128]{1,0:T(8,128)(2,1)S(1)}, u32[]{:S(2)}, u32[]{:S(2)}) collective-permute-start(bf16[128,128]{1,0:T(8,128)(2,1)S(1)} %join_coords.1.refs_0_), channel_id=1, source_target_pairs={{0,8},{1,9},{2,10},{3,11},{4,12},{5,13},{6,14},{7,15},{8,0},{9,1},... | collective-permute-start | bytes 98312 | tf_op jit(solution)/shard_map/ppermute | solution.py:104
  82.8 5.7 %collective-permute-start.21 = (bf16[128,128]{1,0:T(8,128)(2,1)S(1)}, bf16[128,128]{1,0:T(8,128)(2,1)S(1)}, u32[]{:S(2)}, u32[]{:S(2)}) collective-permute-start(bf16[128,128]{1,0:T(8,128)(2,1)S(1)} %join_coords.1.refs_0_), channel_id=1, source_target_pairs={{0,12},{1,13},{2,14},{3,15},{4,8},{5,9},{6,10},{7,11},{8,4},{9,5},... | collective-permute-start | bytes 98312 | tf_op jit(solution)/shard_map/ppermute | solution.py:104

commit v6 on v5

--- a/solution.py
+++ b/solution.py
@@ -39,19 +39,7 @@
 
 def slot_chips(devices, me):
     outer, inner = factors(devices // 2)
-    chip = lax.div(me, 2)
-    a, b = lax.div(chip, inner), lax.rem(chip, inner)
-    return [
-        partner(a, k, outer, -1) * inner + partner(b, m, inner, -1)
-        for m in range(inner)
-        for k in range(outer)
-    ]
-
-
-def partner(at, step, size, sign=1):
-    if size & (size - 1) == 0:
-        return at ^ step
-    return (at + sign * step + size) % size
+    return [lax.div(place(devices, me, k, m, 0), 2) for m in range(inner) for k in range(outer)]
 
 
 def steps(count, unrolled, body):
@@ -65,58 +53,30 @@
 def gather_chunks(chunk, devices, meanwhile):
     outer, inner = factors(devices // 2)
 
-    def pairs(k, m):
-        return [
-            (d, 2 * (partner(d // 2 // inner, k, outer) * inner + partner(d // 2 % inner, m, inner)) + d % 2)
-            for d in range(devices)
-        ]
-
-    line = [chunk] + [lax.ppermute(chunk, "tensor", pairs(k, 0)) for k in range(1, outer)]
+    line = [chunk] + [move(chunk, devices, k, 0, 0) for k in range(1, outer)]
     held, line[outer // 4] = meanwhile(line[outer // 4])
     slots = {}
     for k in range(outer):
         for m in range(1, inner):
-            slots[k, m] = lax.ppermute(line[k], "tensor", pairs(0, m))
+            slots[k, m] = move(line[k], devices, 0, m, 0)
     for k in range(outer):
         slots[k, 0] = line[k]
     return [slots[k, m] for m in range(inner) for k in range(outer)], held
 
 
 def neighbours(devices):
-    inner = factors(devices // 2)[1]
-    return [(m, c) for m in range(inner) for c in range(2)]
-
-
-def to_neighbour(x, devices, m, c):
-    inner = factors(devices // 2)[1]
+    return [(m, c) for m in range(factors(devices // 2)[1]) for c in range(2)]
+
+
+def place(devices, d, k, m, c):
+    outer, inner = factors(devices // 2)
+    return 2 * ((d // 2 // inner ^ k) * inner + (d // 2 % inner ^ m)) + (d % 2 ^ c)
+
+
+def move(x, devices, k, m, c):
     return lax.ppermute(
-        x,
-        "tensor",
-        [
-            (d, 2 * (d // 2 // inner * inner + partner(d // 2 % inner, m, inner)) + (d % 2 ^ c))
-            for d in range(devices)
-        ],
+        x, "tensor", [(d, place(devices, d, k, m, c)) for d in range(devices)]
     )
-
-
-def along_line(x, devices, k):
-    outer, inner = factors(devices // 2)
-    return lax.ppermute(
-        x,
-        "tensor",
-        [
-            (d, 2 * (partner(d // 2 // inner, k, outer) * inner + d // 2 % inner) + d % 2)
-            for d in range(devices)
-        ],
-    )
-
-
-def source(devices, me, k, m, c):
-    outer, inner = factors(devices // 2)
-    chip = lax.div(me, 2)
-    a, b = lax.div(chip, inner), lax.rem(chip, inner)
-    chip = partner(a, k, outer, -1) * inner + partner(b, m, inner, -1)
-    return 2 * chip + (lax.rem(me, 2) ^ c)
 
 
 def join_kernel(*refs):
@@ -127,7 +87,7 @@
 
 
 def gather_coords(coords, devices):
-    around = [coords if mc == (0, 0) else to_neighbour(coords, devices, *mc) for mc in neighbours(devices)]
+    around = [coords if mc == (0, 0) else move(coords, devices, 0, *mc) for mc in neighbours(devices)]
     rows, cols = coords.shape
     joined = pl.pallas_call(
         join_kernel,
@@ -138,7 +98,59 @@
         name="join_coords",
     )(*around)
     outer = factors(devices // 2)[0]
-    return [joined] + [along_line(joined, devices, k) for k in range(1, outer)]
+    return [joined] + [move(joined, devices, k, 0, 0) for k in range(1, outer)]
+
+
+def turn_kernel(devices, me_ref, *refs):
+    outer, _ = factors(devices // 2)
+    parts, outs = refs[:outer], refs[outer:]
+    in_plane = [lax.rem(place(devices, me_ref[0], 0, m, c), len(outs)) for m, c in neighbours(devices)]
+    for out_ref, at in zip(outs, in_plane):
+        for k in range(outer):
+            out_ref[k] = parts[k][at]
+
+
+def exchange(parts, me, devices):
+    outer, _ = factors(devices // 2)
+    around = neighbours(devices)
+    _, rows, cols = parts[0].shape
+    arrived = [parts[0]] + [move(parts[k], devices, k, 0, 0) for k in range(1, outer)]
+    turned = pl.pallas_call(
+        functools.partial(turn_kernel, devices),
+        out_shape=[jax.ShapeDtypeStruct((outer, rows, cols), parts[0].dtype) for _ in around],
+        in_specs=[SMEM] + [VMEM] * outer,
+        out_specs=[VMEM] * len(around),
+        compiler_params=params(16),
+        name="turn",
+    )(me, *arrived)
+    return [x if mc == (0, 0) else move(x, devices, 0, *mc) for x, mc in zip(turned, around)]
+
+
+def in_order(devices, me, parts, ordered):
+    for part, (m, c) in zip(parts, neighbours(devices)):
+        for k in range(part.shape[0]):
+            ordered[place(devices, me, k, m, c)] = part[k]
+
+
+def collect_kernel(devices, me_ref, *refs):
+    parts, (out_ref, ordered) = refs[:-2], refs[-2:]
+    in_order(devices, me_ref[0], parts, ordered)
+    cols = ordered.shape[2]
+    for d in range(devices):
+        out_ref[:, d * cols : (d + 1) * cols] = ordered[d]
+
+
+def collect(me, parts, devices):
+    _, rows, cols = parts[0].shape
+    return pl.pallas_call(
+        functools.partial(collect_kernel, devices),
+        out_shape=jax.ShapeDtypeStruct((rows, devices * cols), parts[0].dtype),
+        in_specs=[SMEM] + [VMEM] * len(parts),
+        out_specs=VMEM,
+        scratch_shapes=[pltpu.VMEM((devices, rows, cols), parts[0].dtype)],
+        compiler_params=params(16),
+        name="collect",
+    )(me, *parts)
 
 
 def across(x, devices):
@@ -335,33 +347,35 @@
     )(left, held, cache)
 
 
-def qkv_kernel(
-    devices, rows, me_ref, bias_ref, own_ref, left, held, cache, out_ref, kept, acc, sems
-):
+def qkv_kernel(devices, rows, me_ref, bias_ref, own_ref, left, held, cache, *refs):
+    outer, inner = factors(devices // 2)
+    outs, (kept, acc, sems) = refs[:outer], refs[outer:]
     copies = cache_copies(cache, kept, sems)
     for copy in copies:
         copy.start()
     multiply(left, held, acc)
     bias = bias_ref[...].astype(jnp.float32)
-    core = lax.rem(me_ref[0], 2)
-    for slot, chip in enumerate(slot_chips(devices, me_ref[0])):
-        mine = slice(8 * slot, 8 * slot + rows)
-        out_ref[2 * chip + core] = (own_ref[mine, :] + bias).astype(jnp.bfloat16)
-        out_ref[2 * chip + 1 - core] = (acc[mine, :] + bias).astype(jnp.bfloat16)
+    me = me_ref[0]
+    for c, product in enumerate((own_ref, acc)):
+        for m in range(inner):
+            at = lax.rem(place(devices, me, 0, m, c), 2 * inner)
+            for k in range(outer):
+                slot = m * outer + k
+                mine = product[8 * slot : 8 * slot + rows, :]
+                outs[k][at] = (mine + bias).astype(jnp.bfloat16)
     for copy in copies:
         copy.wait()
 
 
 def qkv_project(me, own, left, held, bias, cache, devices, rows):
+    outer, inner = factors(devices // 2)
     cols = own.shape[1]
-    return pl.pallas_call(
+    part = jax.ShapeDtypeStruct((2 * inner, rows, cols), jnp.bfloat16)
+    *parts, kept = pl.pallas_call(
         functools.partial(qkv_kernel, devices, rows),
-        out_shape=(
-            jax.ShapeDtypeStruct((devices, rows, cols), jnp.bfloat16),
-            jax.ShapeDtypeStruct(cache.shape, cache.dtype),
-        ),
+        out_shape=[part] * outer + [jax.ShapeDtypeStruct(cache.shape, cache.dtype)],
         in_specs=[SMEM, VMEM, VMEM, VMEM, VMEM, HBM],
-        out_specs=(VMEM, VMEM),
+        out_specs=[VMEM] * (outer + 1),
         scratch_shapes=[
             pltpu.VMEM(own.shape, jnp.float32),
             pltpu.SemaphoreType.DMA((cache.shape[0],)),
@@ -369,27 +383,28 @@
         compiler_params=params(28),
         name="qkv_project",
     )(me, bias, own, left, held, cache)
-
-
-def attend_kernel(
-    rows,
-    len_ref,
-    ids_ref,
-    qkv_ref,
-    cos_ref,
-    sin_ref,
-    keys,
-    values,
-    out_ref,
-    heads,
-    mixed,
-    stage,
-):
+    return parts, kept
+
+
+def head_of(ordered, h):
+    cols = ordered.shape[2]
+    pieces = []
+    at, end = h * HEAD_SIZE, (h + 1) * HEAD_SIZE
+    while at < end:
+        d, lane = at // cols, at % cols
+        width = min(end - at, cols - lane)
+        pieces.append(ordered[d, :, lane : lane + width].astype(jnp.float32))
+        at += width
+    return pieces[0] if len(pieces) == 1 else jnp.concatenate(pieces, axis=1)
+
+
+def attend_kernel(devices, rows, me_ref, len_ref, ids_ref, cos_ref, sin_ref, keys, values, *refs):
+    parts, (out_ref, ordered, heads, mixed, stage) = refs[:-5], refs[-5:]
     total_heads = QUERY_HEADS + 2 * KVH
     half = HEAD_SIZE // 2
+    in_order(devices, me_ref[0], parts, ordered)
     for h in range(total_heads):
-        tile = qkv_ref[:, h * HEAD_SIZE : (h + 1) * HEAD_SIZE].astype(jnp.float32)
-        heads[pl.ds(h, rows, stride=total_heads), :] = tile
+        heads[pl.ds(h, rows, stride=total_heads), :] = head_of(ordered, h)
     scale = 1.0 / HEAD_SIZE**0.5
 
     for r in range(rows):
@@ -439,23 +454,24 @@
     write_ids(ids_ref, rows, out_ref)
 
 
-def attend(lengths, ids, qkv, cosine, sine, keys, values):
+def attend(me, lengths, ids, parts, cosine, sine, keys, values, devices):
     rows, capacity, width = keys.shape
     total_heads = QUERY_HEADS + 2 * KVH
     features = QUERY_HEADS * HEAD_SIZE
     return pl.pallas_call(
-        functools.partial(attend_kernel, rows),
+        functools.partial(attend_kernel, devices, rows),
         out_shape=jax.ShapeDtypeStruct((8, rows * features // 8 + LANES), jnp.bfloat16),
-        in_specs=[SMEM, SMEM, VMEM, VMEM, VMEM, VMEM, VMEM],
+        in_specs=[SMEM] * 3 + [VMEM] * (4 + len(parts)),
         out_specs=VMEM,
         scratch_shapes=[
+            pltpu.VMEM((devices, rows, parts[0].shape[2]), jnp.bfloat16),
             pltpu.VMEM((rows * total_heads, HEAD_SIZE), jnp.float32),
             pltpu.VMEM((rows * QUERY_HEADS, HEAD_SIZE), jnp.float32),
             pltpu.VMEM((BLOCKS * rows, features // BLOCKS), jnp.float32),
         ],
         compiler_params=params(24),
         name="attend",
-    )(lengths, ids, qkv, cosine, sine, keys, values)
+    )(me, lengths, ids, cosine, sine, keys, values, *parts)
 
 
 def times_down(down_ref, left, write):
@@ -570,42 +586,43 @@
 
 
 def add_kernel(devices, rows, me_ref, base_ref, up_ref, *refs):
-    lines, (out_ref, coords) = refs[:-2], refs[-2:]
+    outer, inner = factors(devices // 2)
+    lines, outs, (coords, projected) = refs[:outer], refs[outer : 2 * outer], refs[2 * outer :]
     part = coords.shape[1]
+    me = me_ref[0]
     for k, line in enumerate(lines):
         for at, (m, c) in enumerate(neighbours(devices)):
-            coords[source(devices, me_ref[0], k, m, c)] = line[at * part : (at + 1) * part, :]
+            coords[place(devices, me, k, m, c)] = line[at * part : (at + 1) * part, :]
     delta = lax.dot_general(
         coords[...].reshape(devices * part, coords.shape[2]),
         up_ref[...],
         (((0,), (0,)), ((), ())),
         preferred_element_type=jnp.float32,
     )
-    projected = base_ref[...] + delta
-    for d in range(devices):
-        out_ref[d] = projected[8 * d : 8 * d + rows, :].astype(jnp.bfloat16)
+    projected[...] = base_ref[...] + delta
+    for k, out_ref in enumerate(outs):
+        for m, c in neighbours(devices):
+            d = place(devices, me, k, m, c)
+            row = projected[pl.ds(pl.multiple_of(8 * d, 8), 8), :]
+            out_ref[lax.rem(d, 2 * inner)] = row[:rows].astype(jnp.bfloat16)
 
 
 def add_delta(me, base, lines, up, devices, rows):
+    outer, inner = factors(devices // 2)
     part = up.shape[0] // devices
+    out = jax.ShapeDtypeStruct((2 * inner, rows, base.shape[1]), jnp.bfloat16)
     return pl.pallas_call(
         functools.partial(add_kernel, devices, rows),
-        out_shape=jax.ShapeDtypeStruct((devices, rows, base.shape[1]), jnp.bfloat16),
-        in_specs=[SMEM, VMEM, VMEM] + [VMEM] * len(lines),
-        out_specs=VMEM,
-        scratch_shapes=[pltpu.VMEM((devices, part, lines[0].shape[1]), jnp.bfloat16)],
+        out_shape=[out] * outer,
+        in_specs=[SMEM, VMEM, VMEM] + [VMEM] * outer,
+        out_specs=[VMEM] * outer,
+        scratch_shapes=[
+            pltpu.VMEM((devices, part, lines[0].shape[1]), jnp.bfloat16),
+            pltpu.VMEM(base.shape, jnp.float32),
+        ],
         compiler_params=params(48),
         name="add_delta",
     )(me, base, up, *lines)
-
-
-def exchange(parts):
-    return lax.all_to_all(parts, "tensor", split_axis=0, concat_axis=0, tiled=True)
-
-
-def per_row(parts):
-    devices, rows, cols = parts.shape
-    return jnp.transpose(parts, (1, 0, 2)).reshape(rows, devices * cols)
 
 
 def per_device(
@@ -642,11 +659,11 @@
     mine = unpack(chunks, rows, hidden.shape[1], False)
     theirs = across(mine, devices)
     own, keys = qkv_own(mine, held, rotated_key_cache)
-    qkv, values = qkv_project(
-        me, own, theirs, held, bias, past_value_cache, devices, rows
+    parts, values = qkv_project(me, own, theirs, held, bias, past_value_cache, devices, rows)
+    parts = exchange(parts, me, devices)
+    chunk = attend(
+        me, lengths, row_adapter_index, parts, cosine, sine, keys, values, devices
     )
-    qkv = per_row(exchange(qkv))
-    chunk = attend(lengths, row_adapter_index, qkv, cosine, sine, keys, values)
     chunks, held = gather_chunks(
         chunk, devices, lambda chunk: hold(output_weight, chunk, (), 42, "hold_output")
     )
@@ -656,7 +673,8 @@
     own = own_rows(mine, held, "base_own")
     lines = gather_coords(shrink(me, own_part, mine, theirs, down, devices), devices)
     base = base_project(me, own, theirs, held, devices)
-    return per_row(exchange(add_delta(me, base, lines, up, devices, rows)))
+    parts = exchange(add_delta(me, base, lines, up, devices, rows), me, devices)
+    return collect(me, parts, devices)
 
 
 def solution(mesh):

time: 101 us -> 94.4 us (0.935)
  blocking collectives: 11.5 us -> 0 us
  local copies, waits for them, and re-layouts: 11.3 us -> 1.67 us
  starting transfers between devices: 28.4 us -> 37.5 us
  waiting for transfers between devices: 25.3 us -> 30.1 us
    ppermute x20 -> x32, starting transfers between devices: 23.3 us -> 37.4 us  [move(): lax.ppermute(x, 'tensor', [(d, place(devices, d, k, m, c)) for d in range...]
    ppermute x20 -> x32, waiting for transfers between devices: 14.8 us -> 27.7 us  [move(): lax.ppermute(x, 'tensor', [(d, place(devices, d, k, m, c)) for d in range...]
    all_to_all x1 -> x0, blocking collectives: 11.5 us -> none  [exchange(): lax.all_to_all(parts, 'tensor', split_axis=0, concat_axis=0, tiled=True)]
    unnamed x31 -> x22, local copies, waits for them, and re-layouts: 11.3 us -> 1.66 us
    all_to_all x1 -> x0, waiting for transfers between devices: 8.27 us -> none  [exchange(): lax.all_to_all(parts, 'tensor', split_axis=0, concat_axis=0, tiled=True)]
    all_to_all x1 -> x0, starting transfers between devices: 4.93 us -> none  [exchange(): lax.all_to_all(parts, 'tensor', split_axis=0, concat_axis=0, tiled=True)]
    pallas_call x3 -> x6, Pallas kernels: 8.44 us -> 8.75 us  [the longest x1 5.19 us: attend(): pl.pallas_call(functools.partial(attend_kernel, devices, rows), out_shape...]
  transfers between devices with their start and end apart: 23 -> 34, of which waited for: 14 -> 22; matrix products, arithmetic and copies ran while one was open for 0% -> 0% of each run, Pallas kernels for 14% -> 15%
where the time goes in v6:
time: 94.4 us; the launch traced here: 94.2 us
  starting transfers between devices  37.5 us (40%)
  waiting for transfers between devices  30.1 us (32%)
  Pallas kernels  24.3 us (26%)
  local copies, waits for them, and re-layouts  1.67 us (2%)
    ppermute x32, starting transfers between devices, move(): lax.ppermute(x, 'tensor', [(d, place(devices, d, k, m, c)) for d in range...  37.4 us
    ppermute x32, waiting for transfers between devices, move(): lax.ppermute(x, 'tensor', [(d, place(devices, d, k, m, c)) for d in range...  27.7 us
    pallas_call x2, Pallas kernels, hold(): pl.pallas_call(functools.partial(hold_kernel, len(arrays)), out_shape=(ja...  7.7 us
    pallas_call x1, Pallas kernels, attend(): pl.pallas_call(functools.partial(attend_kernel, devices, rows), out_shape...  5.19 us
    pallas_call x1, Pallas kernels, qkv_project(): pl.pallas_call(functools.partial(qkv_kernel, devices, rows), out_shape=[p...  2.53 us
    ppermute x2, waiting for transfers between devices, across(): return lax.ppermute(x, 'tensor', [(d, d ^ 1) for d in range(devices)])  2.41 us
    pallas_call x1, Pallas kernels, qkv_own(): pl.pallas_call(qkv_own_kernel, out_shape=(jax.ShapeDtypeStruct((rows, col...  2.33 us
  transfers between devices with their start and end apart: 34, of which 22 were waited for; matrix products, arithmetic and copies ran while one was open for 0% of the time, Pallas kernels for 15%

profile of v6, /device:TPU:0, one launch (start us, length us, event | category | flops | bytes accessed | tf_op | source)
XLA Modules:
  0.0 94.2 jit_solution(10836837847585286257)
XLA Ops:
  0.0 0.9 copy-done.2
  0.9 0.7 copy-done.3
  1.6 0.4 norm_chunk.1.refs_0_
  2.0 3.1 %collective-permute-start = (bf16[8,6144]{1,0:T(8,128)(2,1)S(1)}, bf16[8,6144]{1,0:T(8,128)(2,1)S(1)}, u32[]{:S(2)}, u32[]{:S(2)}) collective-permute-start(bf16[8,6144]{1,0:T(8,128)(2,1)S(1)} %norm_chunk.1.refs_0_), channel_id=1, source_target_pairs={{0,4},{1,5},{2,6},{3,7},{4,0},{5,1},{6,2},{7,3},{8,12},{9,13},{10,... | collective-permute-start | bytes 294920 | tf_op jit(solution)/shard_map/ppermute | solution.py:77
  5.1 2.6 %collective-permute-start.1 = (bf16[8,6144]{1,0:T(8,128)(2,1)S(1)}, bf16[8,6144]{1,0:T(8,128)(2,1)S(1)}, u32[]{:S(2)}, u32[]{:S(2)}) collective-permute-start(bf16[8,6144]{1,0:T(8,128)(2,1)S(1)} %norm_chunk.1.refs_0_), channel_id=1, source_target_pairs={{0,8},{1,9},{2,10},{3,11},{4,12},{5,13},{6,14},{7,15},{8,0},{9,1},... | collective-permute-start | bytes 294920 | tf_op jit(solution)/shard_map/ppermute | solution.py:77
  7.7 1.7 %collective-permute-start.3 = (bf16[8,6144]{1,0:T(8,128)(2,1)S(1)}, bf16[8,6144]{1,0:T(8,128)(2,1)S(1)}, u32[]{:S(2)}, u32[]{:S(2)}) collective-permute-start(bf16[8,6144]{1,0:T(8,128)(2,1)S(1)} %norm_chunk.1.refs_0_), channel_id=1, source_target_pairs={{0,2},{1,3},{2,0},{3,1},{4,6},{5,7},{6,4},{7,5},{8,10},{9,11},{10,... | collective-permute-start | bytes 294920 | tf_op jit(solution)/shard_map/ppermute | solution.py:77
  9.5 4.2 %hold_qkv.1 = (bf16[8192,640]{1,0:T(8,128)(2,1)S(1)}, bf16[8,6144]{1,0:T(8,128)(2,1)S(1)}) custom-call(bf16[8,6144]{1,0:T(8,128)(2,1)S(1)} %collective-permute-done.refs_0_, s32[1]{0:T(128)} %bitcast.refs_1_.me_ref, bf16[8192,640]{1,0:T(8,128)(2,1)} %refs_2_.1), custom_call_target="tpu_custom_call", output_to_operand_aliasing={{1}: (0, {})} | custom-call | bytes 20971520 | tf_op jit(solution)/shard_map/hold_qkv/pallas_call | solution.py:276
  13.7 0.4 collective-permute-start.4
  14.0 1.5 %collective-permute-done.1.refs_2_ = bf16[8,6144]{1,0:T(8,128)(2,1)S(1)} collective-permute-done((bf16[8,6144]{1,0:T(8,128)(2,1)S(1)}, bf16[8,6144]{1,0:T(8,128)(2,1)S(1)}, u32[]{:S(2)}, u32[]{:S(2)}) %collective-permute-start.1) | collective-permute-done | bytes 98336 | tf_op jit(solution)/shard_map/ppermute | solution.py:77
  15.5 1.5 %collective-permute-start.5 = (bf16[8,6144]{1,0:T(8,128)(2,1)S(1)}, bf16[8,6144]{1,0:T(8,128)(2,1)S(1)}, u32[]{:S(2)}, u32[]{:S(2)}) collective-permute-start(bf16[8,6144]{1,0:T(8,128)(2,1)S(1)} %collective-permute-done.1.refs_2_), channel_id=1, source_target_pairs={{0,2},{1,3},{2,0},{3,1},{4,6},{5,7},{6,4},{7,5},{8,10},{9,11},{10,... | collective-permute-start | bytes 294920 | tf_op jit(solution)/shard_map/ppermute | solution.py:77
  17.0 0.5 collective-permute-start.6
  17.6 1.8 %collective-permute-done.4.refs_5_ = bf16[8,6144]{1,0:T(8,128)(2,1)S(1)} collective-permute-done((bf16[8,6144]{1,0:T(8,128)(2,1)S(1)}, bf16[8,6144]{1,0:T(8,128)(2,1)S(1)}, u32[]{:S(2)}, u32[]{:S(2)}) %collective-permute-start.4) | collective-permute-done | bytes 98336 | tf_op jit(solution)/shard_map/ppermute | solution.py:77
  19.3 1.1 %collective-permute-done.5.refs_6_ = bf16[8,6144]{1,0:T(8,128)(2,1)S(1)} collective-permute-done((bf16[8,6144]{1,0:T(8,128)(2,1)S(1)}, bf16[8,6144]{1,0:T(8,128)(2,1)S(1)}, u32[]{:S(2)}, u32[]{:S(2)}) %collective-permute-start.5) | collective-permute-done | bytes 98336 | tf_op jit(solution)/shard_map/ppermute | solution.py:77
  20.4 1.3 %collective-permute-done.6.refs_7_ = bf16[8,6144]{1,0:T(8,128)(2,1)S(1)} collective-permute-done((bf16[8,6144]{1,0:T(8,128)(2,1)S(1)}, bf16[8,6144]{1,0:T(8,128)(2,1)S(1)}, u32[]{:S(2)}, u32[]{:S(2)}) %collective-permute-start.6) | collective-permute-done | bytes 98336 | tf_op jit(solution)/shard_map/ppermute | solution.py:77
  21.7 0.3 unpack.2.left
  22.1 2.3 %qkv_own.1 = (f32[64,640]{1,0:T(8,128)S(1)}, bf16[6,384,1024]{2,1,0:T(8,128)(2,1)S(1)}) custom-call(bf16[8,64,1024]{2,1,0:T(8,128)(2,1)S(1)} %unpack.2.left, bf16[8192,640]{1,0:T(8,128)(2,1)S(1)} %get-tuple-element.29.held, bf16[6,384,1024]{2,1,0:T(8,128)(2,1)S(1)} %bitcast.5), custom_call_target="tpu_custom_call" | custom-call | flops 671088640 | bytes 10485760 | tf_op jit(solution)/shard_map/qkv_own/pallas_call | solution.py:333
  24.5 0.2 collective-permute-done.7.left
  24.7 2.5 %qkv_project.1 = (bf16[4,6,640]{2,1,0:T(8,128)(2,1)S(1)}, bf16[4,6,640]{2,1,0:T(8,128)(2,1)S(1)}, bf16[4,6,640]{2,1,0:T(8,128)(2,1)S(1)}, bf16[4,6,640]{2,1,0:T(8,128)(2,1)S(1)}, bf16[6,384,1024]{2,1,0:T(8,128)(2,1)S(1)}) custom-call(s32[1]{0:T(128)} %bitcast.refs_1_.me_ref, bf16[1,640]{1,0:T(2,128)(2,1)S(1)} %reshape.21.bias_ref, ...), custom_call_target="tpu_custom_call" | custom-call | tf_op jit(solution)/shard_map/qkv_project/pallas_call | solution.py:374
  27.2 3.4 %collective-permute-start.10 = (bf16[4,6,640]{2,1,0:T(8,128)(2,1)S(1)}, bf16[4,6,640]{2,1,0:T(8,128)(2,1)S(1)}, u32[]{:S(2)}, u32[]{:S(2)}) collective-permute-start(bf16[4,6,640]{2,1,0:T(8,128)(2,1)S(1)} %get-tuple-element.36), channel_id=1, source_target_pairs={{0,12},{1,13},{2,14},{3,15},{4,8},{5,9},{6,10},{7,11},{8,4},{9,5},... | collective-permute-start | bytes 92168 | tf_op jit(solution)/shard_map/ppermute | solution.py:77
  30.6 1.1 %collective-permute-start.9 = (bf16[4,6,640]{2,1,0:T(8,128)(2,1)S(1)}, bf16[4,6,640]{2,1,0:T(8,128)(2,1)S(1)}, u32[]{:S(2)}, u32[]{:S(2)}) collective-permute-start(bf16[4,6,640]{2,1,0:T(8,128)(2,1)S(1)} %get-tuple-element.35), channel_id=1, source_target_pairs={{0,8},{1,9},{2,10},{3,11},{4,12},{5,13},{6,14},{7,15},{8,0},{9,1},... | collective-permute-start | bytes 92168 | tf_op jit(solution)/shard_map/ppermute | solution.py:77
  31.8 1.5 %collective-permute-done.10.refs_3_ = bf16[4,6,640]{2,1,0:T(8,128)(2,1)S(1)} collective-permute-done((bf16[4,6,640]{2,1,0:T(8,128)(2,1)S(1)}, bf16[4,6,640]{2,1,0:T(8,128)(2,1)S(1)}, u32[]{:S(2)}, u32[]{:S(2)}) %collective-permute-start.10) | collective-permute-done | bytes 30752 | tf_op jit(solution)/shard_map/ppermute | solution.py:77
  33.3 1.7 %collective-permute-done.8.refs_1_ = bf16[4,6,640]{2,1,0:T(8,128)(2,1)S(1)} collective-permute-done((bf16[4,6,640]{2,1,0:T(8,128)(2,1)S(1)}, bf16[4,6,640]{2,1,0:T(8,128)(2,1)S(1)}, u32[]{:S(2)}, u32[]{:S(2)}) %collective-permute-start.8) | collective-permute-done | bytes 30752 | tf_op jit(solution)/shard_map/ppermute | solution.py:77
  35.0 0.9 collective-permute-done.9.refs_2_
  36.1 0.8 collective-permute-start.12
  36.8 1.1 %collective-permute-start.13 = (bf16[4,6,640]{2,1,0:T(8,128)(2,1)S(1)}, bf16[4,6,640]{2,1,0:T(8,128)(2,1)S(1)}, u32[]{:S(2)}, u32[]{:S(2)}) collective-permute-start(bf16[4,6,640]{2,1,0:T(8,128)(2,1)S(1)} %get-tuple-element.40), channel_id=1, source_target_pairs={{0,3},{1,2},{2,1},{3,0},{4,7},{5,6},{6,5},{7,4},{8,11},{9,10},{10,... | collective-permute-start | bytes 92168 | tf_op jit(solution)/shard_map/ppermute | solution.py:77
  38.0 2.4 %collective-permute-done.12.refs_2_ = bf16[4,6,640]{2,1,0:T(8,128)(2,1)S(1)} collective-permute-done((bf16[4,6,640]{2,1,0:T(8,128)(2,1)S(1)}, bf16[4,6,640]{2,1,0:T(8,128)(2,1)S(1)}, u32[]{:S(2)}, u32[]{:S(2)}) %collective-permute-start.12) | collective-permute-done | bytes 30752 | tf_op jit(solution)/shard_map/ppermute | solution.py:77
  40.5 0.3 collective-permute-done.13.refs_3_
  40.7 5.2 %attend.1.refs_0_ = bf16[8,6272]{1,0:T(8,128)(2,1)S(1)} custom-call(s32[1]{0:T(128)} %bitcast.refs_1_.me_ref, s32[6]{0:T(128)S(1)} %copy-done.4, s32[6]{0:T(128)S(1)} %copy-done.5, f32[6,128]{1,0:T(8,128)S(1)} %get-tuple-element.54.cos_ref, f32[6,128]{1,0:T(8,128)S(1)} %get-tuple-element.55.sin_ref, bf16[6,384,1024]{2,1,0:T(8,128)(2,1)S(1)} %get-tuple-element.30.keys, ...), custom_call_target="tpu_custom_call" | custom-call | tf_op jit(solution)/shard_map/attend/pallas_call | solution.py:461
  45.9 1.6 %collective-permute-start.14 = (bf16[8,6272]{1,0:T(8,128)(2,1)S(1)}, bf16[8,6272]{1,0:T(8,128)(2,1)S(1)}, u32[]{:S(2)}, u32[]{:S(2)}) collective-permute-start(bf16[8,6272]{1,0:T(8,128)(2,1)S(1)} %attend.1.refs_0_), channel_id=1, source_target_pairs={{0,4},{1,5},{2,6},{3,7},{4,0},{5,1},{6,2},{7,3},{8,12},{9,13},{10,... | collective-permute-start | bytes 301064 | tf_op jit(solution)/shard_map/ppermute | solution.py:77
  47.6 0.7 collective-permute-start.15
  48.2 2.1 %collective-permute-start.16 = (bf16[8,6272]{1,0:T(8,128)(2,1)S(1)}, bf16[8,6272]{1,0:T(8,128)(2,1)S(1)}, u32[]{:S(2)}, u32[]{:S(2)}) collective-permute-start(bf16[8,6272]{1,0:T(8,128)(2,1)S(1)} %attend.1.refs_0_), channel_id=1, source_target_pairs={{0,12},{1,13},{2,14},{3,15},{4,8},{5,9},{6,10},{7,11},{8,4},{9,5},... | collective-permute-start | bytes 301064 | tf_op jit(solution)/shard_map/ppermute | solution.py:77
  50.4 1.0 %collective-permute-start.17 = (bf16[8,6272]{1,0:T(8,128)(2,1)S(1)}, bf16[8,6272]{1,0:T(8,128)(2,1)S(1)}, u32[]{:S(2)}, u32[]{:S(2)}) collective-permute-start(bf16[8,6272]{1,0:T(8,128)(2,1)S(1)} %attend.1.refs_0_), channel_id=1, source_target_pairs={{0,2},{1,3},{2,0},{3,1},{4,6},{5,7},{6,4},{7,5},{8,10},{9,11},{10,... | collective-permute-start | bytes 301064 | tf_op jit(solution)/shard_map/ppermute | solution.py:77
  51.4 3.5 %hold_output.1 = (bf16[8192,512]{1,0:T(8,128)(2,1)S(1)}, bf16[8,6272]{1,0:T(8,128)(2,1)S(1)}) custom-call(bf16[8,6272]{1,0:T(8,128)(2,1)S(1)} %collective-permute-done.14.refs_0_, bf16[8192,512]{1,0:T(8,128)(2,1)} %refs_1_.1), custom_call_target="tpu_custom_call", output_to_operand_aliasing={{1}: (0, {})} | custom-call | bytes 16777216 | tf_op jit(solution)/shard_map/hold_output/pallas_call | solution.py:276
  54.8 1.1 %collective-permute-start.18 = (bf16[8,6272]{1,0:T(8,128)(2,1)S(1)}, bf16[8,6272]{1,0:T(8,128)(2,1)S(1)}, u32[]{:S(2)}, u32[]{:S(2)}) collective-permute-start(bf16[8,6272]{1,0:T(8,128)(2,1)S(1)} %get-tuple-element.41.refs_1_), channel_id=1, source_target_pairs={{0,2},{1,3},{2,0},{3,1},{4,6},{5,7},{6,4},{7,5},{8,10},{9,11},{10,... | collective-permute-start | bytes 301064 | tf_op jit(solution)/shard_map/ppermute | solution.py:77
  55.9 1.9 %collective-permute-done.15.refs_2_ = bf16[8,6272]{1,0:T(8,128)(2,1)S(1)} collective-permute-done((bf16[8,6272]{1,0:T(8,128)(2,1)S(1)}, bf16[8,6272]{1,0:T(8,128)(2,1)S(1)}, u32[]{:S(2)}, u32[]{:S(2)}) %collective-permute-start.15) | collective-permute-done | bytes 100384 | tf_op jit(solution)/shard_map/ppermute | solution.py:77
  57.9 1.0 %collective-permute-start.19 = (bf16[8,6272]{1,0:T(8,128)(2,1)S(1)}, bf16[8,6272]{1,0:T(8,128)(2,1)S(1)}, u32[]{:S(2)}, u32[]{:S(2)}) collective-permute-start(bf16[8,6272]{1,0:T(8,128)(2,1)S(1)} %collective-permute-done.15.refs_2_), channel_id=1, source_target_pairs={{0,2},{1,3},{2,0},{3,1},{4,6},{5,7},{6,4},{7,5},{8,10},{9,11},{10,... | collective-permute-start | bytes 301064 | tf_op jit(solution)/shard_map/ppermute | solution.py:77
  58.9 1.0 %collective-permute-start.20 = (bf16[8,6272]{1,0:T(8,128)(2,1)S(1)}, bf16[8,6272]{1,0:T(8,128)(2,1)S(1)}, u32[]{:S(2)}, u32[]{:S(2)}) collective-permute-start(bf16[8,6272]{1,0:T(8,128)(2,1)S(1)} %collective-permute-done.16.refs_3_), channel_id=1, source_target_pairs={{0,2},{1,3},{2,0},{3,1},{4,6},{5,7},{6,4},{7,5},{8,10},{9,11},{10,... | collective-permute-start | bytes 301064 | tf_op jit(solution)/shard_map/ppermute | solution.py:77
  59.9 2.9 %collective-permute-done.19.refs_6_ = bf16[8,6272]{1,0:T(8,128)(2,1)S(1)} collective-permute-done((bf16[8,6272]{1,0:T(8,128)(2,1)S(1)}, bf16[8,6272]{1,0:T(8,128)(2,1)S(1)}, u32[]{:S(2)}, u32[]{:S(2)}) %collective-permute-start.19) | collective-permute-done | bytes 100384 | tf_op jit(solution)/shard_map/ppermute | solution.py:77
  62.8 1.1 %collective-permute-done.20.refs_7_ = bf16[8,6272]{1,0:T(8,128)(2,1)S(1)} collective-permute-done((bf16[8,6272]{1,0:T(8,128)(2,1)S(1)}, bf16[8,6272]{1,0:T(8,128)(2,1)S(1)}, u32[]{:S(2)}, u32[]{:S(2)}) %collective-permute-start.20) | collective-permute-done | bytes 100384 | tf_op jit(solution)/shard_map/ppermute | solution.py:77
  63.8 0.3 unpack.3.left.own
  64.3 0.6 shrink_own.1.own_part
  64.9 2.2 %collective-permute-done.21.left.other = bf16[9,64,1024]{2,1,0:T(8,128)(2,1)S(1)} collective-permute-done((bf16[9,64,1024]{2,1,0:T(8,128)(2,1)S(1)}, bf16[9,64,1024]{2,1,0:T(8,128)(2,1)S(1)}, u32[]{:S(2)}, u32[]{:S(2)}) %collective-permute-start.21) | collective-permute-done | bytes 1179680 | tf_op jit(solution)/shard_map/ppermute | solution.py:157
  67.1 0.9 shrink.1.refs_0_
  68.1 1.1 %collective-permute-start.23 = (bf16[32,128]{1,0:T(8,128)(2,1)S(1)}, bf16[32,128]{1,0:T(8,128)(2,1)S(1)}, u32[]{:S(2)}, u32[]{:S(2)}) collective-permute-start(bf16[32,128]{1,0:T(8,128)(2,1)S(1)} %shrink.1.refs_0_), channel_id=1, source_target_pairs={{0,2},{1,3},{2,0},{3,1},{4,6},{5,7},{6,4},{7,5},{8,10},{9,11},{10,... | collective-permute-start | bytes 24584 | tf_op jit(solution)/shard_map/ppermute | solution.py:77
  69.1 0.7 collective-permute-start.24
  69.8 1.5 %base_own.1.own_ref = f32[64,512]{1,0:T(8,128)S(1)} custom-call(bf16[9,64,1024]{2,1,0:T(8,128)(2,1)S(1)} %unpack.3.left.own, bf16[8192,512]{1,0:T(8,128)(2,1)S(1)} %get-tuple-element.42.held), custom_call_target="tpu_custom_call" | custom-call | flops 536870912 | bytes 8388608 | tf_op jit(solution)/shard_map/base_own/pallas_call | solution.py:303
  71.4 0.4 collective-permute-done.23.refs_2_
  71.7 0.5 collective-permute-done.24.refs_3_
  72.2 0.8 collective-permute-start.25
  73.0 0.7 collective-permute-start.26
  73.7 2.9 %collective-permute-start.27 = (bf16[128,128]{1,0:T(8,128)(2,1)S(1)}, bf16[128,128]{1,0:T(8,128)(2,1)S(1)}, u32[]{:S(2)}, u32[]{:S(2)}) collective-permute-start(bf16[128,128]{1,0:T(8,128)(2,1)S(1)} %join_coords.1.refs_0_), channel_id=1, source_target_pairs={{0,12},{1,13},{2,14},{3,15},{4,8},{5,9},{6,10},{7,11},{8,4},{9,5},... | collective-permute-start | bytes 98312 | tf_op jit(solution)/shard_map/ppermute | solution.py:77
  76.6 1.5 %base_project.1.base_ref = f32[128,512]{1,0:T(8,128)S(1)} custom-call(s32[1]{0:T(128)} %bitcast.refs_1_.me_ref, f32[64,512]{1,0:T(8,128)S(1)} %base_own.1.own_ref, bf16[9,64,1024]{2,1,0:T(8,128)(2,1)S(1)} %collective-permute-done.21.left.other, bf16[8192,512]{1,0:T(8,128)(2,1)S(1)} %get-tuple-element.42.held), custom_call_target="tpu_custom_call" | custom-call | flops 536870912 | bytes 8388608 | tf_op jit(solution)/shard_map/base_project/pallas_call | solution.py:574
  78.2 0.3 collective-permute-done.26.refs_2_
  78.5 0.9 %collective-permute-done.27.refs_3_ = bf16[128,128]{1,0:T(8,128)(2,1)S(1)} collective-permute-done((bf16[128,128]{1,0:T(8,128)(2,1)S(1)}, bf16[128,128]{1,0:T(8,128)(2,1)S(1)}, u32[]{:S(2)}, u32[]{:S(2)}) %collective-permute-start.27) | collective-permute-done | bytes 32800 | tf_op jit(solution)/shard_map/ppermute | solution.py:77
  79.5 0.3 add_delta.1
  79.8 3.4 %collective-permute-start.29 = (bf16[4,6,512]{2,1,0:T(8,128)(2,1)S(1)}, bf16[4,6,512]{2,1,0:T(8,128)(2,1)S(1)}, u32[]{:S(2)}, u32[]{:S(2)}) collective-permute-start(bf16[4,6,512]{2,1,0:T(8,128)(2,1)S(1)} %get-tuple-element.45), channel_id=1, source_target_pairs={{0,8},{1,9},{2,10},{3,11},{4,12},{5,13},{6,14},{7,15},{8,0},{9,1},... | collective-permute-start | bytes 73736 | tf_op jit(solution)/shard_map/ppermute | solution.py:77
  83.3 0.9 %collective-permute-start.30 = (bf16[4,6,512]{2,1,0:T(8,128)(2,1)S(1)}, bf16[4,6,512]{2,1,0:T(8,128)(2,1)S(1)}, u32[]{:S(2)}, u32[]{:S(2)}) collective-permute-start(bf16[4,6,512]{2,1,0:T(8,128)(2,1)S(1)} %get-tuple-element.46), channel_id=1, source_target_pairs={{0,12},{1,13},{2,14},{3,15},{4,8},{5,9},{6,10},{7,11},{8,4},{9,5},... | collective-permute-start | bytes 73736 | tf_op jit(solution)/shard_map/ppermute | solution.py:77
  84.2 0.9 collective-permute-done.29.refs_2_
  85.2 3.8 %collective-permute-done.30.refs_3_ = bf16[4,6,512]{2,1,0:T(8,128)(2,1)S(1)} collective-permute-done((bf16[4,6,512]{2,1,0:T(8,128)(2,1)S(1)}, bf16[4,6,512]{2,1,0:T(8,128)(2,1)S(1)}, u32[]{:S(2)}, u32[]{:S(2)}) %collective-permute-start.30) | collective-permute-done | bytes 24608 | tf_op jit(solution)/shard_map/ppermute | solution.py:77
  89.1 1.0 %collective-permute-start.32 = (bf16[4,6,512]{2,1,0:T(8,128)(2,1)S(1)}, bf16[4,6,512]{2,1,0:T(8,128)(2,1)S(1)}, u32[]{:S(2)}, u32[]{:S(2)}) collective-permute-start(bf16[4,6,512]{2,1,0:T(8,128)(2,1)S(1)} %get-tuple-element.49), channel_id=1, source_target_pairs={{0,2},{1,3},{2,0},{3,1},{4,6},{5,7},{6,4},{7,5},{8,10},{9,11},{10,... | collective-permute-start | bytes 73736 | tf_op jit(solution)/shard_map/ppermute | solution.py:77
  90.1 0.8 collective-permute-start.33
  91.0 2.1 %collective-permute-done.32.refs_2_ = bf16[4,6,512]{2,1,0:T(8,128)(2,1)S(1)} collective-permute-done((bf16[4,6,512]{2,1,0:T(8,128)(2,1)S(1)}, bf16[4,6,512]{2,1,0:T(8,128)(2,1)S(1)}, u32[]{:S(2)}, u32[]{:S(2)}) %collective-permute-start.32) | collective-permute-done | bytes 24608 | tf_op jit(solution)/shard_map/ppermute | solution.py:77
  93.1 0.4 collective-permute-done.33.refs_3_
  93.5 0.7 collect.1
  (50 shorter events, 0.8 us)
Async XLA Ops:
  0.0 0.9 copy-start.2
  0.9 0.7 copy-start.3
  2.0 7.4 %collective-permute-start = (bf16[8,6144]{1,0:T(8,128)(2,1)S(1)}, bf16[8,6144]{1,0:T(8,128)(2,1)S(1)}, u32[]{:S(2)}, u32[]{:S(2)}) collective-permute-start(bf16[8,6144]{1,0:T(8,128)(2,1)S(1)} %norm_chunk.1.refs_0_), channel_id=1, source_target_pairs={{0,4},{1,5},{2,6},{3,7},{4,0},{5,1},{6,2},{7,3},{8,12},{9,13},{10,... | collective-permute-start | bytes 294920 | tf_op jit(solution)/shard_map/ppermute | solution.py:77
  5.1 10.4 %collective-permute-start.1 = (bf16[8,6144]{1,0:T(8,128)(2,1)S(1)}, bf16[8,6144]{1,0:T(8,128)(2,1)S(1)}, u32[]{:S(2)}, u32[]{:S(2)}) collective-permute-start(bf16[8,6144]{1,0:T(8,128)(2,1)S(1)} %norm_chunk.1.refs_0_), channel_id=1, source_target_pairs={{0,8},{1,9},{2,10},{3,11},{4,12},{5,13},{6,14},{7,15},{8,0},{9,1},... | collective-permute-start | bytes 294920 | tf_op jit(solution)/shard_map/ppermute | solution.py:77
  7.7 9.4 %collective-permute-start.2 = (bf16[8,6144]{1,0:T(8,128)(2,1)S(1)}, bf16[8,6144]{1,0:T(8,128)(2,1)S(1)}, u32[]{:S(2)}, u32[]{:S(2)}) collective-permute-start(bf16[8,6144]{1,0:T(8,128)(2,1)S(1)} %norm_chunk.1.refs_0_), channel_id=1, source_target_pairs={{0,12},{1,13},{2,14},{3,15},{4,8},{5,9},{6,10},{7,11},{8,4},{9,5},... | collective-permute-start | bytes 294920 | tf_op jit(solution)/shard_map/ppermute | solution.py:77
  7.7 9.9 %collective-permute-start.3 = (bf16[8,6144]{1,0:T(8,128)(2,1)S(1)}, bf16[8,6144]{1,0:T(8,128)(2,1)S(1)}, u32[]{:S(2)}, u32[]{:S(2)}) collective-permute-start(bf16[8,6144]{1,0:T(8,128)(2,1)S(1)} %norm_chunk.1.refs_0_), channel_id=1, source_target_pairs={{0,2},{1,3},{2,0},{3,1},{4,6},{5,7},{6,4},{7,5},{8,10},{9,11},{10,... | collective-permute-start | bytes 294920 | tf_op jit(solution)/shard_map/ppermute | solution.py:77
  9.4 12.7 %slice-start = ((s8[4718592]{0:T(1024)(128)(4,1)}), s8[4194304]{0:T(1024)(128)(4,1)S(1)}, s32[]{:S(2)}) async-start(s8[4718592]{0:T(1024)(128)(4,1)} %bitcast.4), calls=%async_computation | async-start | bytes 8388608
  9.4 12.6 %copy-start.6 = (bf16[640]{0:T(1024)(128)(2,1)S(1)}, bf16[640]{0:T(1024)(128)(2,1)}, u32[]{:S(2)}) copy-start(bf16[640]{0:T(1024)(128)(2,1)} %param.14) | copy-start | bytes 3844
  9.4 12.6 %copy-start.4 = (s32[6]{0:T(128)S(1)}, s32[6]{0:T(128)}, u32[]{:S(2)}) copy-start(s32[6]{0:T(128)} %len_ref.1) | copy-start | bytes 76
  9.4 12.7 %slice-start.1 = ((s8[4718592]{0:T(1024)(128)(4,1)}), s8[524288]{0:T(1024)(128)(4,1)S(1)}, s32[]{:S(2)}) async-start(s8[4718592]{0:T(1024)(128)(4,1)} %bitcast.4), calls=%async_computation.1 | async-start | bytes 1048576
  13.7 5.6 %collective-permute-start.4 = (bf16[8,6144]{1,0:T(8,128)(2,1)S(1)}, bf16[8,6144]{1,0:T(8,128)(2,1)S(1)}, u32[]{:S(2)}, u32[]{:S(2)}) collective-permute-start(bf16[8,6144]{1,0:T(8,128)(2,1)S(1)} %get-tuple-element.28.refs_1_), channel_id=1, source_target_pairs={{0,2},{1,3},{2,0},{3,1},{4,6},{5,7},{6,4},{7,5},{8,10},{9,11},{10,... | collective-permute-start | bytes 294920 | tf_op jit(solution)/shard_map/ppermute | solution.py:77
  15.5 4.9 %collective-permute-start.5 = (bf16[8,6144]{1,0:T(8,128)(2,1)S(1)}, bf16[8,6144]{1,0:T(8,128)(2,1)S(1)}, u32[]{:S(2)}, u32[]{:S(2)}) collective-permute-start(bf16[8,6144]{1,0:T(8,128)(2,1)S(1)} %collective-permute-done.1.refs_2_), channel_id=1, source_target_pairs={{0,2},{1,3},{2,0},{3,1},{4,6},{5,7},{6,4},{7,5},{8,10},{9,11},{10,... | collective-permute-start | bytes 294920 | tf_op jit(solution)/shard_map/ppermute | solution.py:77
  17.0 4.6 %collective-permute-start.6 = (bf16[8,6144]{1,0:T(8,128)(2,1)S(1)}, bf16[8,6144]{1,0:T(8,128)(2,1)S(1)}, u32[]{:S(2)}, u32[]{:S(2)}) collective-permute-start(bf16[8,6144]{1,0:T(8,128)(2,1)S(1)} %collective-permute-done.2.refs_3_), channel_id=1, source_target_pairs={{0,2},{1,3},{2,0},{3,1},{4,6},{5,7},{6,4},{7,5},{8,10},{9,11},{10,... | collective-permute-start | bytes 294920 | tf_op jit(solution)/shard_map/ppermute | solution.py:77
  21.7 3.0 %slice-start.2 = ((s8[4718592]{0:T(1024)(128)(4,1)}), s8[4194304]{0:T(1024)(128)(4,1)S(1)}, s32[]{:S(2)}) async-start(s8[4718592]{0:T(1024)(128)(4,1)} %bitcast.6), calls=%async_computation.2 | async-start | bytes 8388608
  22.0 2.7 %collective-permute-start.7 = (bf16[8,64,1024]{2,1,0:T(8,128)(2,1)S(1)}, bf16[8,64,1024]{2,1,0:T(8,128)(2,1)S(1)}, u32[]{:S(2)}, u32[]{:S(2)}) collective-permute-start(bf16[8,64,1024]{2,1,0:T(8,128)(2,1)S(1)} %unpack.2.left), channel_id=1, source_target_pairs={{0,1},{1,0},{2,3},{3,2},{4,5},{5,4},{6,7},{7,6},{8,9},{9,8},{10,11... | collective-permute-start | bytes 3145736 | tf_op jit(solution)/shard_map/ppermute | solution.py:157
  22.1 2.6 %slice-start.3 = ((s8[4718592]{0:T(1024)(128)(4,1)}), s8[524288]{0:T(1024)(128)(4,1)S(1)}, s32[]{:S(2)}) async-start(s8[4718592]{0:T(1024)(128)(4,1)} %bitcast.6), calls=%async_computation.3 | async-start | bytes 1048576
  24.7 16.0 %copy-start.5 = (s32[6]{0:T(128)S(1)}, s32[6]{0:T(128)}, u32[]{:S(2)}) copy-start(s32[6]{0:T(128)} %ids_ref.1) | copy-start | bytes 76
  27.2 6.1 %collective-permute-start.10 = (bf16[4,6,640]{2,1,0:T(8,128)(2,1)S(1)}, bf16[4,6,640]{2,1,0:T(8,128)(2,1)S(1)}, u32[]{:S(2)}, u32[]{:S(2)}) collective-permute-start(bf16[4,6,640]{2,1,0:T(8,128)(2,1)S(1)} %get-tuple-element.36), channel_id=1, source_target_pairs={{0,12},{1,13},{2,14},{3,15},{4,8},{5,9},{6,10},{7,11},{8,4},{9,5},... | collective-permute-start | bytes 92168 | tf_op jit(solution)/shard_map/ppermute | solution.py:77
  30.6 4.4 %collective-permute-start.8 = (bf16[4,6,640]{2,1,0:T(8,128)(2,1)S(1)}, bf16[4,6,640]{2,1,0:T(8,128)(2,1)S(1)}, u32[]{:S(2)}, u32[]{:S(2)}) collective-permute-start(bf16[4,6,640]{2,1,0:T(8,128)(2,1)S(1)} %get-tuple-element.34), channel_id=1, source_target_pairs={{0,4},{1,5},{2,6},{3,7},{4,0},{5,1},{6,2},{7,3},{8,12},{9,13},{10,... | collective-permute-start | bytes 92168 | tf_op jit(solution)/shard_map/ppermute | solution.py:77
  30.6 5.3 %collective-permute-start.9 = (bf16[4,6,640]{2,1,0:T(8,128)(2,1)S(1)}, bf16[4,6,640]{2,1,0:T(8,128)(2,1)S(1)}, u32[]{:S(2)}, u32[]{:S(2)}) collective-permute-start(bf16[4,6,640]{2,1,0:T(8,128)(2,1)S(1)} %get-tuple-element.35), channel_id=1, source_target_pairs={{0,8},{1,9},{2,10},{3,11},{4,12},{5,13},{6,14},{7,15},{8,0},{9,1},... | collective-permute-start | bytes 92168 | tf_op jit(solution)/shard_map/ppermute | solution.py:77
  36.0 2.0 %collective-permute-start.11 = (bf16[4,6,640]{2,1,0:T(8,128)(2,1)S(1)}, bf16[4,6,640]{2,1,0:T(8,128)(2,1)S(1)}, u32[]{:S(2)}, u32[]{:S(2)}) collective-permute-start(bf16[4,6,640]{2,1,0:T(8,128)(2,1)S(1)} %get-tuple-element.38), channel_id=1, source_target_pairs={{0,1},{1,0},{2,3},{3,2},{4,5},{5,4},{6,7},{7,6},{8,9},{9,8},{10,11... | collective-permute-start | bytes 92168 | tf_op jit(solution)/shard_map/ppermute | solution.py:77
  36.1 4.4 %collective-permute-start.12 = (bf16[4,6,640]{2,1,0:T(8,128)(2,1)S(1)}, bf16[4,6,640]{2,1,0:T(8,128)(2,1)S(1)}, u32[]{:S(2)}, u32[]{:S(2)}) collective-permute-start(bf16[4,6,640]{2,1,0:T(8,128)(2,1)S(1)} %get-tuple-element.39), channel_id=1, source_target_pairs={{0,2},{1,3},{2,0},{3,1},{4,6},{5,7},{6,4},{7,5},{8,10},{9,11},{10,... | collective-permute-start | bytes 92168 | tf_op jit(solution)/shard_map/ppermute | solution.py:77
  36.8 3.9 %collective-permute-start.13 = (bf16[4,6,640]{2,1,0:T(8,128)(2,1)S(1)}, bf16[4,6,640]{2,1,0:T(8,128)(2,1)S(1)}, u32[]{:S(2)}, u32[]{:S(2)}) collective-permute-start(bf16[4,6,640]{2,1,0:T(8,128)(2,1)S(1)} %get-tuple-element.40), channel_id=1, source_target_pairs={{0,3},{1,2},{2,1},{3,0},{4,7},{5,6},{6,5},{7,4},{8,11},{9,10},{10,... | collective-permute-start | bytes 92168 | tf_op jit(solution)/shard_map/ppermute | solution.py:77
  45.9 18.3 %copy-start = (bf16[2,8192,16]{1,2,0:T(8,128)(2,1)S(1)}, bf16[2,8192,16]{1,2,0:T(8,128)(2,1)}, u32[]{:S(2)}) copy-start(bf16[2,8192,16]{1,2,0:T(8,128)(2,1)} %param.20) | copy-start | bytes 1572868
  45.9 5.4 %collective-permute-start.14 = (bf16[8,6272]{1,0:T(8,128)(2,1)S(1)}, bf16[8,6272]{1,0:T(8,128)(2,1)S(1)}, u32[]{:S(2)}, u32[]{:S(2)}) collective-permute-start(bf16[8,6272]{1,0:T(8,128)(2,1)S(1)} %attend.1.refs_0_), channel_id=1, source_target_pairs={{0,4},{1,5},{2,6},{3,7},{4,0},{5,1},{6,2},{7,3},{8,12},{9,13},{10,... | collective-permute-start | bytes 301064 | tf_op jit(solution)/shard_map/ppermute | solution.py:77
  47.6 10.3 %collective-permute-start.15 = (bf16[8,6272]{1,0:T(8,128)(2,1)S(1)}, bf16[8,6272]{1,0:T(8,128)(2,1)S(1)}, u32[]{:S(2)}, u32[]{:S(2)}) collective-permute-start(bf16[8,6272]{1,0:T(8,128)(2,1)S(1)} %attend.1.refs_0_), channel_id=1, source_target_pairs={{0,8},{1,9},{2,10},{3,11},{4,12},{5,13},{6,14},{7,15},{8,0},{9,1},... | collective-permute-start | bytes 301064 | tf_op jit(solution)/shard_map/ppermute | solution.py:77
  48.2 10.6 %collective-permute-start.16 = (bf16[8,6272]{1,0:T(8,128)(2,1)S(1)}, bf16[8,6272]{1,0:T(8,128)(2,1)S(1)}, u32[]{:S(2)}, u32[]{:S(2)}) collective-permute-start(bf16[8,6272]{1,0:T(8,128)(2,1)S(1)} %attend.1.refs_0_), channel_id=1, source_target_pairs={{0,12},{1,13},{2,14},{3,15},{4,8},{5,9},{6,10},{7,11},{8,4},{9,5},... | collective-permute-start | bytes 301064 | tf_op jit(solution)/shard_map/ppermute | solution.py:77
  50.4 9.5 %collective-permute-start.17 = (bf16[8,6272]{1,0:T(8,128)(2,1)S(1)}, bf16[8,6272]{1,0:T(8,128)(2,1)S(1)}, u32[]{:S(2)}, u32[]{:S(2)}) collective-permute-start(bf16[8,6272]{1,0:T(8,128)(2,1)S(1)} %attend.1.refs_0_), channel_id=1, source_target_pairs={{0,2},{1,3},{2,0},{3,1},{4,6},{5,7},{6,4},{7,5},{8,10},{9,11},{10,... | collective-permute-start | bytes 301064 | tf_op jit(solution)/shard_map/ppermute | solution.py:77
  54.8 5.1 %collective-permute-start.18 = (bf16[8,6272]{1,0:T(8,128)(2,1)S(1)}, bf16[8,6272]{1,0:T(8,128)(2,1)S(1)}, u32[]{:S(2)}, u32[]{:S(2)}) collective-permute-start(bf16[8,6272]{1,0:T(8,128)(2,1)S(1)} %get-tuple-element.41.refs_1_), channel_id=1, source_target_pairs={{0,2},{1,3},{2,0},{3,1},{4,6},{5,7},{6,4},{7,5},{8,10},{9,11},{10,... | collective-permute-start | bytes 301064 | tf_op jit(solution)/shard_map/ppermute | solution.py:77
  57.9 4.9 %collective-permute-start.19 = (bf16[8,6272]{1,0:T(8,128)(2,1)S(1)}, bf16[8,6272]{1,0:T(8,128)(2,1)S(1)}, u32[]{:S(2)}, u32[]{:S(2)}) collective-permute-start(bf16[8,6272]{1,0:T(8,128)(2,1)S(1)} %collective-permute-done.15.refs_2_), channel_id=1, source_target_pairs={{0,2},{1,3},{2,0},{3,1},{4,6},{5,7},{6,4},{7,5},{8,10},{9,11},{10,... | collective-permute-start | bytes 301064 | tf_op jit(solution)/shard_map/ppermute | solution.py:77
  58.9 5.0 %collective-permute-start.20 = (bf16[8,6272]{1,0:T(8,128)(2,1)S(1)}, bf16[8,6272]{1,0:T(8,128)(2,1)S(1)}, u32[]{:S(2)}, u32[]{:S(2)}) collective-permute-start(bf16[8,6272]{1,0:T(8,128)(2,1)S(1)} %collective-permute-done.16.refs_3_), channel_id=1, source_target_pairs={{0,2},{1,3},{2,0},{3,1},{4,6},{5,7},{6,4},{7,5},{8,10},{9,11},{10,... | collective-permute-start | bytes 301064 | tf_op jit(solution)/shard_map/ppermute | solution.py:77
  64.2 2.9 %collective-permute-start.21 = (bf16[9,64,1024]{2,1,0:T(8,128)(2,1)S(1)}, bf16[9,64,1024]{2,1,0:T(8,128)(2,1)S(1)}, u32[]{:S(2)}, u32[]{:S(2)}) collective-permute-start(bf16[9,64,1024]{2,1,0:T(8,128)(2,1)S(1)} %unpack.3.left.own), channel_id=1, source_target_pairs={{0,1},{1,0},{2,3},{3,2},{4,5},{5,4},{6,7},{7,6},{8,9},{9,8},{10,11... | collective-permute-start | bytes 3538952 | tf_op jit(solution)/shard_map/ppermute | solution.py:157
  67.9 3.4 %collective-permute-start.22 = (bf16[32,128]{1,0:T(8,128)(2,1)S(1)}, bf16[32,128]{1,0:T(8,128)(2,1)S(1)}, u32[]{:S(2)}, u32[]{:S(2)}) collective-permute-start(bf16[32,128]{1,0:T(8,128)(2,1)S(1)} %shrink.1.refs_0_), channel_id=1, source_target_pairs={{0,1},{1,0},{2,3},{3,2},{4,5},{5,4},{6,7},{7,6},{8,9},{9,8},{10,11... | collective-permute-start | bytes 24584 | tf_op jit(solution)/shard_map/ppermute | solution.py:77
  68.1 3.7 %collective-permute-start.23 = (bf16[32,128]{1,0:T(8,128)(2,1)S(1)}, bf16[32,128]{1,0:T(8,128)(2,1)S(1)}, u32[]{:S(2)}, u32[]{:S(2)}) collective-permute-start(bf16[32,128]{1,0:T(8,128)(2,1)S(1)} %shrink.1.refs_0_), channel_id=1, source_target_pairs={{0,2},{1,3},{2,0},{3,1},{4,6},{5,7},{6,4},{7,5},{8,10},{9,11},{10,... | collective-permute-start | bytes 24584 | tf_op jit(solution)/shard_map/ppermute | solution.py:77
  69.1 3.1 %collective-permute-start.24 = (bf16[32,128]{1,0:T(8,128)(2,1)S(1)}, bf16[32,128]{1,0:T(8,128)(2,1)S(1)}, u32[]{:S(2)}, u32[]{:S(2)}) collective-permute-start(bf16[32,128]{1,0:T(8,128)(2,1)S(1)} %shrink.1.refs_0_), channel_id=1, source_target_pairs={{0,3},{1,2},{2,1},{3,0},{4,7},{5,6},{6,5},{7,4},{8,11},{9,10},{10,... | collective-permute-start | bytes 24584 | tf_op jit(solution)/shard_map/ppermute | solution.py:77
  72.2 7.2 %copy-start.1 = (bf16[32,16,512]{2,1,0:T(8,128)(2,1)S(1)}, bf16[32,16,512]{2,1,0:T(8,128)(2,1)}, u32[]{:S(2)}) copy-start(bf16[32,16,512]{2,1,0:T(8,128)(2,1)} %param.21) | copy-start | bytes 1572868
  72.2 5.9 %collective-permute-start.25 = (bf16[128,128]{1,0:T(8,128)(2,1)S(1)}, bf16[128,128]{1,0:T(8,128)(2,1)S(1)}, u32[]{:S(2)}, u32[]{:S(2)}) collective-permute-start(bf16[128,128]{1,0:T(8,128)(2,1)S(1)} %join_coords.1.refs_0_), channel_id=1, source_target_pairs={{0,4},{1,5},{2,6},{3,7},{4,0},{5,1},{6,2},{7,3},{8,12},{9,13},{10,... | collective-permute-start | bytes 98312 | tf_op jit(solution)/shard_map/ppermute | solution.py:77
  73.0 5.5 %collective-permute-start.26 = (bf16[128,128]{1,0:T(8,128)(2,1)S(1)}, bf16[128,128]{1,0:T(8,128)(2,1)S(1)}, u32[]{:S(2)}, u32[]{:S(2)}) collective-permute-start(bf16[128,128]{1,0:T(8,128)(2,1)S(1)} %join_coords.1.refs_0_), channel_id=1, source_target_pairs={{0,8},{1,9},{2,10},{3,11},{4,12},{5,13},{6,14},{7,15},{8,0},{9,1},... | collective-permute-start | bytes 98312 | tf_op jit(solution)/shard_map/ppermute | solution.py:77
  73.7 5.7 %collective-permute-start.27 = (bf16[128,128]{1,0:T(8,128)(2,1)S(1)}, bf16[128,128]{1,0:T(8,128)(2,1)S(1)}, u32[]{:S(2)}, u32[]{:S(2)}) collective-permute-start(bf16[128,128]{1,0:T(8,128)(2,1)S(1)} %join_coords.1.refs_0_), channel_id=1, source_target_pairs={{0,12},{1,13},{2,14},{3,15},{4,8},{5,9},{6,10},{7,11},{8,4},{9,5},... | collective-permute-start | bytes 98312 | tf_op jit(solution)/shard_map/ppermute | solution.py:77
  79.8 4.5 %collective-permute-start.28 = (bf16[4,6,512]{2,1,0:T(8,128)(2,1)S(1)}, bf16[4,6,512]{2,1,0:T(8,128)(2,1)S(1)}, u32[]{:S(2)}, u32[]{:S(2)}) collective-permute-start(bf16[4,6,512]{2,1,0:T(8,128)(2,1)S(1)} %get-tuple-element.44), channel_id=1, source_target_pairs={{0,4},{1,5},{2,6},{3,7},{4,0},{5,1},{6,2},{7,3},{8,12},{9,13},{10,... | collective-permute-start | bytes 73736 | tf_op jit(solution)/shard_map/ppermute | solution.py:77
  79.8 5.3 %collective-permute-start.29 = (bf16[4,6,512]{2,1,0:T(8,128)(2,1)S(1)}, bf16[4,6,512]{2,1,0:T(8,128)(2,1)S(1)}, u32[]{:S(2)}, u32[]{:S(2)}) collective-permute-start(bf16[4,6,512]{2,1,0:T(8,128)(2,1)S(1)} %get-tuple-element.45), channel_id=1, source_target_pairs={{0,8},{1,9},{2,10},{3,11},{4,12},{5,13},{6,14},{7,15},{8,0},{9,1},... | collective-permute-start | bytes 73736 | tf_op jit(solution)/shard_map/ppermute | solution.py:77
  83.3 5.7 %collective-permute-start.30 = (bf16[4,6,512]{2,1,0:T(8,128)(2,1)S(1)}, bf16[4,6,512]{2,1,0:T(8,128)(2,1)S(1)}, u32[]{:S(2)}, u32[]{:S(2)}) collective-permute-start(bf16[4,6,512]{2,1,0:T(8,128)(2,1)S(1)} %get-tuple-element.46), channel_id=1, source_target_pairs={{0,12},{1,13},{2,14},{3,15},{4,8},{5,9},{6,10},{7,11},{8,4},{9,5},... | collective-permute-start | bytes 73736 | tf_op jit(solution)/shard_map/ppermute | solution.py:77
  89.0 1.9 %collective-permute-start.31 = (bf16[4,6,512]{2,1,0:T(8,128)(2,1)S(1)}, bf16[4,6,512]{2,1,0:T(8,128)(2,1)S(1)}, u32[]{:S(2)}, u32[]{:S(2)}) collective-permute-start(bf16[4,6,512]{2,1,0:T(8,128)(2,1)S(1)} %get-tuple-element.48), channel_id=1, source_target_pairs={{0,1},{1,0},{2,3},{3,2},{4,5},{5,4},{6,7},{7,6},{8,9},{9,8},{10,11... | collective-permute-start | bytes 73736 | tf_op jit(solution)/shard_map/ppermute | solution.py:77
  89.1 4.0 %collective-permute-start.32 = (bf16[4,6,512]{2,1,0:T(8,128)(2,1)S(1)}, bf16[4,6,512]{2,1,0:T(8,128)(2,1)S(1)}, u32[]{:S(2)}, u32[]{:S(2)}) collective-permute-start(bf16[4,6,512]{2,1,0:T(8,128)(2,1)S(1)} %get-tuple-element.49), channel_id=1, source_target_pairs={{0,2},{1,3},{2,0},{3,1},{4,6},{5,7},{6,4},{7,5},{8,10},{9,11},{10,... | collective-permute-start | bytes 73736 | tf_op jit(solution)/shard_map/ppermute | solution.py:77
  90.1 3.3 %collective-permute-start.33 = (bf16[4,6,512]{2,1,0:T(8,128)(2,1)S(1)}, bf16[4,6,512]{2,1,0:T(8,128)(2,1)S(1)}, u32[]{:S(2)}, u32[]{:S(2)}) collective-permute-start(bf16[4,6,512]{2,1,0:T(8,128)(2,1)S(1)} %get-tuple-element.50), channel_id=1, source_target_pairs={{0,3},{1,2},{2,1},{3,0},{4,7},{5,6},{6,5},{7,4},{8,11},{9,10},{10,... | collective-permute-start | bytes 73736 | tf_op jit(solution)/shard_map/ppermute | solution.py:77

commit v7 on v6

--- a/solution.py
+++ b/solution.py
@@ -101,60 +101,40 @@
     return [joined] + [move(joined, devices, k, 0, 0) for k in range(1, outer)]
 
 
-def turn_kernel(devices, me_ref, *refs):
-    outer, _ = factors(devices // 2)
-    parts, outs = refs[:outer], refs[outer:]
-    in_plane = [lax.rem(place(devices, me_ref[0], 0, m, c), len(outs)) for m, c in neighbours(devices)]
-    for out_ref, at in zip(outs, in_plane):
+def turn_kernel(rows, *refs):
+    wide, stage = refs[-2:]
+    outer = wide.shape[0]
+    parts, outs = refs[:outer], refs[outer:-2]
+    for k, part in enumerate(parts):
+        wide[k] = part[...].astype(jnp.float32)
+    for at, out_ref in enumerate(outs):
         for k in range(outer):
-            out_ref[k] = parts[k][at]
-
-
-def exchange(parts, me, devices):
+            stage[k * rows : (k + 1) * rows, :] = wide[k, at * rows : (at + 1) * rows, :]
+        out_ref[...] = stage[...].astype(jnp.bfloat16)
+
+
+def exchange(parts, rows, devices):
     outer, _ = factors(devices // 2)
     around = neighbours(devices)
-    _, rows, cols = parts[0].shape
+    cols = parts[0].shape[1]
     arrived = [parts[0]] + [move(parts[k], devices, k, 0, 0) for k in range(1, outer)]
     turned = pl.pallas_call(
-        functools.partial(turn_kernel, devices),
-        out_shape=[jax.ShapeDtypeStruct((outer, rows, cols), parts[0].dtype) for _ in around],
-        in_specs=[SMEM] + [VMEM] * outer,
+        functools.partial(turn_kernel, rows),
+        out_shape=[jax.ShapeDtypeStruct((outer * rows, cols), parts[0].dtype) for _ in around],
+        in_specs=[VMEM] * outer,
         out_specs=[VMEM] * len(around),
+        scratch_shapes=[
+            pltpu.VMEM((outer, *parts[0].shape), jnp.float32),
+            pltpu.VMEM((outer * rows, cols), jnp.float32),
+        ],
         compiler_params=params(16),
         name="turn",
-    )(me, *arrived)
+    )(*arrived)
     return [x if mc == (0, 0) else move(x, devices, 0, *mc) for x, mc in zip(turned, around)]
 
 
-def in_order(devices, me, parts, ordered):
-    for part, (m, c) in zip(parts, neighbours(devices)):
-        for k in range(part.shape[0]):
-            ordered[place(devices, me, k, m, c)] = part[k]
-
-
-def collect_kernel(devices, me_ref, *refs):
-    parts, (out_ref, ordered) = refs[:-2], refs[-2:]
-    in_order(devices, me_ref[0], parts, ordered)
-    cols = ordered.shape[2]
-    for d in range(devices):
-        out_ref[:, d * cols : (d + 1) * cols] = ordered[d]
-
-
-def collect(me, parts, devices):
-    _, rows, cols = parts[0].shape
-    return pl.pallas_call(
-        functools.partial(collect_kernel, devices),
-        out_shape=jax.ShapeDtypeStruct((rows, devices * cols), parts[0].dtype),
-        in_specs=[SMEM] + [VMEM] * len(parts),
-        out_specs=VMEM,
-        scratch_shapes=[pltpu.VMEM((devices, rows, cols), parts[0].dtype)],
-        compiler_params=params(16),
-        name="collect",
-    )(me, *parts)
-
-
 def across(x, devices):
-    return lax.ppermute(x, "tensor", [(d, d ^ 1) for d in range(devices)])
+    return move(x, devices, 0, 0, 1)
 
 
 def write_chunk(stage, rows, out_ref):
@@ -347,42 +327,42 @@
     )(left, held, cache)
 
 
-def qkv_kernel(devices, rows, me_ref, bias_ref, own_ref, left, held, cache, *refs):
+def qkv_kernel(devices, rows, bias_ref, own_ref, left, held, cache, *refs):
     outer, inner = factors(devices // 2)
-    outs, (kept, acc, sems) = refs[:outer], refs[outer:]
+    outs, (kept, acc, stage, sems) = refs[:outer], refs[outer:]
     copies = cache_copies(cache, kept, sems)
     for copy in copies:
         copy.start()
     multiply(left, held, acc)
     bias = bias_ref[...].astype(jnp.float32)
-    me = me_ref[0]
-    for c, product in enumerate((own_ref, acc)):
-        for m in range(inner):
-            at = lax.rem(place(devices, me, 0, m, c), 2 * inner)
-            for k in range(outer):
-                slot = m * outer + k
-                mine = product[8 * slot : 8 * slot + rows, :]
-                outs[k][at] = (mine + bias).astype(jnp.bfloat16)
+    products = own_ref, acc
+    for k in range(outer):
+        for at, (m, c) in enumerate(neighbours(devices)):
+            slot = m * outer + k
+            mine = products[c][8 * slot : 8 * slot + rows, :]
+            stage[at * rows : (at + 1) * rows, :] = mine + bias
+        outs[k][...] = stage[...].astype(jnp.bfloat16)
     for copy in copies:
         copy.wait()
 
 
-def qkv_project(me, own, left, held, bias, cache, devices, rows):
+def qkv_project(own, left, held, bias, cache, devices, rows):
     outer, inner = factors(devices // 2)
     cols = own.shape[1]
-    part = jax.ShapeDtypeStruct((2 * inner, rows, cols), jnp.bfloat16)
+    part = jax.ShapeDtypeStruct((2 * inner * rows, cols), jnp.bfloat16)
     *parts, kept = pl.pallas_call(
         functools.partial(qkv_kernel, devices, rows),
         out_shape=[part] * outer + [jax.ShapeDtypeStruct(cache.shape, cache.dtype)],
-        in_specs=[SMEM, VMEM, VMEM, VMEM, VMEM, HBM],
+        in_specs=[VMEM, VMEM, VMEM, VMEM, HBM],
         out_specs=[VMEM] * (outer + 1),
         scratch_shapes=[
             pltpu.VMEM(own.shape, jnp.float32),
+            pltpu.VMEM((2 * inner * rows, cols), jnp.float32),
             pltpu.SemaphoreType.DMA((cache.shape[0],)),
         ],
         compiler_params=params(28),
         name="qkv_project",
-    )(me, bias, own, left, held, cache)
+    )(bias, own, left, held, cache)
     return parts, kept
 
 
@@ -393,20 +373,28 @@
     while at < end:
         d, lane = at // cols, at % cols
         width = min(end - at, cols - lane)
-        pieces.append(ordered[d, :, lane : lane + width].astype(jnp.float32))
+        pieces.append(ordered[d, :, lane : lane + width])
         at += width
     return pieces[0] if len(pieces) == 1 else jnp.concatenate(pieces, axis=1)
 
 
+def in_order(devices, me, parts, wide, ordered):
+    rows = ordered.shape[1]
+    for at, (m, c) in enumerate(neighbours(devices)):
+        wide[at] = parts[at][...].astype(jnp.float32)
+        for k in range(wide.shape[1] // rows):
+            ordered[place(devices, me, k, m, c)] = wide[at, k * rows : (k + 1) * rows, :]
+
+
 def attend_kernel(devices, rows, me_ref, len_ref, ids_ref, cos_ref, sin_ref, keys, values, *refs):
-    parts, (out_ref, ordered, heads, mixed, stage) = refs[:-5], refs[-5:]
+    parts, (out_ref, wide, ordered, heads, mixed, stage) = refs[:-6], refs[-6:]
     total_heads = QUERY_HEADS + 2 * KVH
     half = HEAD_SIZE // 2
-    in_order(devices, me_ref[0], parts, ordered)
+    in_order(devices, me_ref[0], parts, wide, ordered)
     for h in range(total_heads):
         heads[pl.ds(h, rows, stride=total_heads), :] = head_of(ordered, h)
     scale = 1.0 / HEAD_SIZE**0.5
-
+    upper = lax.broadcasted_iota(jnp.int32, (2 * GROUPS, HEAD_SIZE), 0) < GROUPS
     for r in range(rows):
         base = r * total_heads
         turned = heads[base : base + QUERY_HEADS + KVH, :]
@@ -419,14 +407,22 @@
         new_value = heads[base + QUERY_HEADS + KVH : base + total_heads, :]
         scores = []
         own = []
+        for k in range(0, KVH, 2):
+            mine = slice(k * GROUPS, (k + 2) * GROUPS)
+            both = query_f[mine]
+            wide_query = jnp.concatenate(
+                [jnp.where(upper, both, 0.0), jnp.where(upper, 0.0, both)], axis=1
+            ).astype(jnp.bfloat16)
+            scores.append(
+                lax.dot_general(
+                    wide_query,
+                    keys[r, :, k * HEAD_SIZE : (k + 2) * HEAD_SIZE],
+                    (((1,), (1,)), ((), ())),
+                    preferred_element_type=jnp.float32,
+                )
+            )
         for k in range(KVH):
             mine = slice(k * GROUPS, (k + 1) * GROUPS)
-            key = keys[r, :, k * HEAD_SIZE : (k + 1) * HEAD_SIZE]
-            scores.append(
-                lax.dot_general(
-                    query[mine], key, (((1,), (1,)), ((), ())), preferred_element_type=jnp.float32
-                )
-            )
             own.append(jnp.sum(query_f[mine] * new_key[k : k + 1], axis=-1, keepdims=True))
         score = jnp.concatenate(scores, axis=0) * scale
         own = jnp.concatenate(own, axis=0) * scale
@@ -437,13 +433,18 @@
         total = jnp.sum(expo, axis=-1, keepdims=True) + expo_own
         weight = (expo / total).astype(jnp.bfloat16)
         weight_own = (expo_own / total).astype(jnp.bfloat16).astype(jnp.float32)
-        for k in range(KVH):
-            mine = slice(k * GROUPS, (k + 1) * GROUPS)
-            value = values[r, :, k * HEAD_SIZE : (k + 1) * HEAD_SIZE]
-            part = jnp.dot(weight[mine], value, preferred_element_type=jnp.float32)
-            part = part + weight_own[mine] * new_value[k : k + 1]
-            at = r * QUERY_HEADS + k * GROUPS
-            mixed[at : at + GROUPS, :] = part
+        for k in range(0, KVH, 2):
+            both = jnp.dot(
+                weight[k * GROUPS : (k + 2) * GROUPS],
+                values[r, :, k * HEAD_SIZE : (k + 2) * HEAD_SIZE],
+                preferred_element_type=jnp.float32,
+            )
+            for i in range(2):
+                mine = slice((k + i) * GROUPS, (k + i + 1) * GROUPS)
+                part = both[i * GROUPS : (i + 1) * GROUPS, i * HEAD_SIZE : (i + 1) * HEAD_SIZE]
+                part = part + weight_own[mine] * new_value[k + i : k + i + 1]
+                at = r * QUERY_HEADS + (k + i) * GROUPS
+                mixed[at : at + GROUPS, :] = part
     per_block = QUERY_HEADS // BLOCKS
     for h in range(QUERY_HEADS):
         j, lane = h // per_block, h % per_block
@@ -464,7 +465,8 @@
         in_specs=[SMEM] * 3 + [VMEM] * (4 + len(parts)),
         out_specs=VMEM,
         scratch_shapes=[
-            pltpu.VMEM((devices, rows, parts[0].shape[2]), jnp.bfloat16),
+            pltpu.VMEM((len(parts), *parts[0].shape), jnp.float32),
+            pltpu.VMEM((devices, rows, parts[0].shape[1]), jnp.float32),
             pltpu.VMEM((rows * total_heads, HEAD_SIZE), jnp.float32),
             pltpu.VMEM((rows * QUERY_HEADS, HEAD_SIZE), jnp.float32),
             pltpu.VMEM((BLOCKS * rows, features // BLOCKS), jnp.float32),
@@ -512,7 +514,7 @@
 
 
 def shrink_kernel(
-    devices, me_ref, down_ref, own_part, own, other, coords_ref, ids, place_of, total
+    devices, me_ref, down_ref, own_part, own, other, after, coords_ref, ids, place_of, total
 ):
     me = me_ref[0]
     stored, rank, _ = down_ref.shape
@@ -540,13 +542,13 @@
     coords_ref[...] = coords
 
 
-def shrink(me, own_part, own, other, down, devices):
+def shrink(me, own_part, own, other, down, after, devices):
     stored, rank, features = down.shape
     rows = devices * 8
     return pl.pallas_call(
         functools.partial(shrink_kernel, devices),
         out_shape=jax.ShapeDtypeStruct((stored * rank, rows), jnp.bfloat16),
-        in_specs=[SMEM, VMEM, VMEM, VMEM, VMEM],
+        in_specs=[SMEM, VMEM, VMEM, VMEM, VMEM, ANY],
         out_specs=VMEM,
         scratch_shapes=[
             pltpu.VMEM((rows, LANES), jnp.float32),
@@ -555,7 +557,7 @@
         ],
         compiler_params=params(48),
         name="shrink",
-    )(me, down, own_part, own, other)
+    )(me, down, own_part, own, other, after)
 
 
 def base_kernel(devices, me_ref, own_ref, left, held, out_ref, acc):
@@ -586,40 +588,30 @@
 
 
 def add_kernel(devices, rows, me_ref, base_ref, up_ref, *refs):
-    outer, inner = factors(devices // 2)
-    lines, outs, (coords, projected) = refs[:outer], refs[outer : 2 * outer], refs[2 * outer :]
+    lines, (out_ref, coords) = refs[:-2], refs[-2:]
     part = coords.shape[1]
-    me = me_ref[0]
     for k, line in enumerate(lines):
         for at, (m, c) in enumerate(neighbours(devices)):
-            coords[place(devices, me, k, m, c)] = line[at * part : (at + 1) * part, :]
+            coords[place(devices, me_ref[0], k, m, c)] = line[at * part : (at + 1) * part, :]
     delta = lax.dot_general(
         coords[...].reshape(devices * part, coords.shape[2]),
         up_ref[...],
         (((0,), (0,)), ((), ())),
         preferred_element_type=jnp.float32,
     )
-    projected[...] = base_ref[...] + delta
-    for k, out_ref in enumerate(outs):
-        for m, c in neighbours(devices):
-            d = place(devices, me, k, m, c)
-            row = projected[pl.ds(pl.multiple_of(8 * d, 8), 8), :]
-            out_ref[lax.rem(d, 2 * inner)] = row[:rows].astype(jnp.bfloat16)
+    projected = base_ref[...] + delta
+    for d in range(devices):
+        out_ref[d] = projected[8 * d : 8 * d + rows, :].astype(jnp.bfloat16)
 
 
 def add_delta(me, base, lines, up, devices, rows):
-    outer, inner = factors(devices // 2)
     part = up.shape[0] // devices
-    out = jax.ShapeDtypeStruct((2 * inner, rows, base.shape[1]), jnp.bfloat16)
     return pl.pallas_call(
         functools.partial(add_kernel, devices, rows),
-        out_shape=[out] * outer,
-        in_specs=[SMEM, VMEM, VMEM] + [VMEM] * outer,
-        out_specs=[VMEM] * outer,
-        scratch_shapes=[
-            pltpu.VMEM((devices, part, lines[0].shape[1]), jnp.bfloat16),
-            pltpu.VMEM(base.shape, jnp.float32),
-        ],
+        out_shape=jax.ShapeDtypeStruct((devices, rows, base.shape[1]), jnp.bfloat16),
+        in_specs=[SMEM, VMEM, VMEM] + [VMEM] * len(lines),
+        out_specs=VMEM,
+        scratch_shapes=[pltpu.VMEM((devices, part, lines[0].shape[1]), jnp.bfloat16)],
         compiler_params=params(48),
         name="add_delta",
     )(me, base, up, *lines)
@@ -659,8 +651,8 @@
     mine = unpack(chunks, rows, hidden.shape[1], False)
     theirs = across(mine, devices)
     own, keys = qkv_own(mine, held, rotated_key_cache)
-    parts, values = qkv_project(me, own, theirs, held, bias, past_value_cache, devices, rows)
-    parts = exchange(parts, me, devices)
+    parts, values = qkv_project(own, theirs, held, bias, past_value_cache, devices, rows)
+    parts = exchange(parts, rows, devices)
     chunk = attend(
         me, lengths, row_adapter_index, parts, cosine, sine, keys, values, devices
     )
@@ -671,10 +663,12 @@
     theirs = across(mine, devices)
     own_part = shrink_own(mine, down)
     own = own_rows(mine, held, "base_own")
-    lines = gather_coords(shrink(me, own_part, mine, theirs, down, devices), devices)
+    coords = shrink(me, own_part, mine, theirs, down, own, devices)
+    lines = gather_coords(coords, devices)
     base = base_project(me, own, theirs, held, devices)
-    parts = exchange(add_delta(me, base, lines, up, devices, rows), me, devices)
-    return collect(me, parts, devices)
+    projected = add_delta(me, base, lines, up, devices, rows)
+    projected = lax.all_to_all(projected, "tensor", split_axis=0, concat_axis=0, tiled=True)
+    return jnp.transpose(projected, (1, 0, 2)).reshape(rows, -1)
 
 
 def solution(mesh):

time: 94.4 us -> 94.2 us (level)
  blocking collectives: 0 us -> 12.5 us
  waiting for transfers between devices: 30.1 us -> 22.2 us
  starting transfers between devices: 37.5 us -> 31.2 us
  local copies, waits for them, and re-layouts: 1.67 us -> 4.47 us
  Pallas kernels: 24.3 us -> 23 us
    all_to_all x0 -> x1, blocking collectives: none -> 12.5 us  [per_device(): lax.all_to_all(projected, 'tensor', split_axis=0, concat_axis=0, tiled=True)]
    ppermute x32 -> x28, starting transfers between devices: 37.4 us -> 31.2 us  [move(): lax.ppermute(x, 'tensor', [(d, place(devices, d, k, m, c)) for d in range...]
    ppermute x32 -> x28, waiting for transfers between devices: 27.7 us -> 22.2 us  [move(): lax.ppermute(x, 'tensor', [(d, place(devices, d, k, m, c)) for d in range...]
    unnamed x22 -> x27, local copies, waits for them, and re-layouts: 1.66 us -> 4.46 us
    ppermute x2 -> x0, waiting for transfers between devices: 2.41 us -> none  [across(): return lax.ppermute(x, 'tensor', [(d, d ^ 1) for d in range(devices)])]
  transfers between devices with their start and end apart: 34 -> 28, of which waited for: 22 -> 16; matrix products, arithmetic and copies ran while one was open for 0% -> 0% of each run, Pallas kernels for 15% -> 15%
where the time goes in v7:
time: 94.2 us; the launch traced here: 93.9 us
  starting transfers between devices  31.2 us (33%)
  Pallas kernels  23 us (24%)
  waiting for transfers between devices  22.2 us (24%)
  blocking collectives  12.5 us (13%)
  local copies, waits for them, and re-layouts  4.47 us (5%)
    ppermute x28, starting transfers between devices, move(): lax.ppermute(x, 'tensor', [(d, place(devices, d, k, m, c)) for d in range...  31.2 us
    ppermute x28, waiting for transfers between devices, move(): lax.ppermute(x, 'tensor', [(d, place(devices, d, k, m, c)) for d in range...  22.2 us
    all_to_all x1, blocking collectives, per_device(): lax.all_to_all(projected, 'tensor', split_axis=0, concat_axis=0, tiled=True)  12.5 us
    pallas_call x2, Pallas kernels, hold(): pl.pallas_call(functools.partial(hold_kernel, len(arrays)), out_shape=(ja...  7.7 us
    pallas_call x1, Pallas kernels, attend(): pl.pallas_call(functools.partial(attend_kernel, devices, rows), out_shape...  4.66 us
    unnamed x27, local copies, waits for them, and re-layouts  4.46 us
    pallas_call x1, Pallas kernels, qkv_project(): pl.pallas_call(functools.partial(qkv_kernel, devices, rows), out_shape=[p...  2.35 us
    pallas_call x1, Pallas kernels, qkv_own(): pl.pallas_call(qkv_own_kernel, out_shape=(jax.ShapeDtypeStruct((rows, col...  2.31 us
  transfers between devices with their start and end apart: 28, of which 16 were waited for; matrix products, arithmetic and copies ran while one was open for 0% of the time, Pallas kernels for 15%

profile of v7, /device:TPU:0, one launch (start us, length us, event | category | flops | bytes accessed | tf_op | source)
XLA Modules:
  0.0 93.9 jit_solution(15619868258567517849)
XLA Ops:
  0.0 0.9 copy-done.4
  0.9 0.7 copy-done.5
  1.6 0.4 norm_chunk.1.refs_0_
  2.0 3.1 %collective-permute-start = (bf16[8,6144]{1,0:T(8,128)(2,1)S(1)}, bf16[8,6144]{1,0:T(8,128)(2,1)S(1)}, u32[]{:S(2)}, u32[]{:S(2)}) collective-permute-start(bf16[8,6144]{1,0:T(8,128)(2,1)S(1)} %norm_chunk.1.refs_0_), channel_id=1, source_target_pairs={{0,4},{1,5},{2,6},{3,7},{4,0},{5,1},{6,2},{7,3},{8,12},{9,13},{10,... | collective-permute-start | bytes 294920 | tf_op jit(solution)/shard_map/ppermute | solution.py:77
  5.1 2.6 %collective-permute-start.1 = (bf16[8,6144]{1,0:T(8,128)(2,1)S(1)}, bf16[8,6144]{1,0:T(8,128)(2,1)S(1)}, u32[]{:S(2)}, u32[]{:S(2)}) collective-permute-start(bf16[8,6144]{1,0:T(8,128)(2,1)S(1)} %norm_chunk.1.refs_0_), channel_id=1, source_target_pairs={{0,8},{1,9},{2,10},{3,11},{4,12},{5,13},{6,14},{7,15},{8,0},{9,1},... | collective-permute-start | bytes 294920 | tf_op jit(solution)/shard_map/ppermute | solution.py:77
  7.7 1.7 %collective-permute-start.3 = (bf16[8,6144]{1,0:T(8,128)(2,1)S(1)}, bf16[8,6144]{1,0:T(8,128)(2,1)S(1)}, u32[]{:S(2)}, u32[]{:S(2)}) collective-permute-start(bf16[8,6144]{1,0:T(8,128)(2,1)S(1)} %norm_chunk.1.refs_0_), channel_id=1, source_target_pairs={{0,2},{1,3},{2,0},{3,1},{4,6},{5,7},{6,4},{7,5},{8,10},{9,11},{10,... | collective-permute-start | bytes 294920 | tf_op jit(solution)/shard_map/ppermute | solution.py:77
  9.5 4.2 %hold_qkv.1 = (bf16[8192,640]{1,0:T(8,128)(2,1)S(1)}, bf16[8,6144]{1,0:T(8,128)(2,1)S(1)}) custom-call(bf16[8,6144]{1,0:T(8,128)(2,1)S(1)} %collective-permute-done.refs_0_, s32[1]{0:T(128)} %bitcast.refs_1_.me_ref, bf16[8192,640]{1,0:T(8,128)(2,1)} %refs_2_.1), custom_call_target="tpu_custom_call", output_to_operand_aliasing={{1}: (0, {})} | custom-call | bytes 20971520 | tf_op jit(solution)/shard_map/hold_qkv/pallas_call | solution.py:256
  13.7 0.4 collective-permute-start.4
  14.0 1.5 %collective-permute-done.1.refs_2_ = bf16[8,6144]{1,0:T(8,128)(2,1)S(1)} collective-permute-done((bf16[8,6144]{1,0:T(8,128)(2,1)S(1)}, bf16[8,6144]{1,0:T(8,128)(2,1)S(1)}, u32[]{:S(2)}, u32[]{:S(2)}) %collective-permute-start.1) | collective-permute-done | bytes 98336 | tf_op jit(solution)/shard_map/ppermute | solution.py:77
  15.5 1.5 %collective-permute-start.5 = (bf16[8,6144]{1,0:T(8,128)(2,1)S(1)}, bf16[8,6144]{1,0:T(8,128)(2,1)S(1)}, u32[]{:S(2)}, u32[]{:S(2)}) collective-permute-start(bf16[8,6144]{1,0:T(8,128)(2,1)S(1)} %collective-permute-done.1.refs_2_), channel_id=1, source_target_pairs={{0,2},{1,3},{2,0},{3,1},{4,6},{5,7},{6,4},{7,5},{8,10},{9,11},{10,... | collective-permute-start | bytes 294920 | tf_op jit(solution)/shard_map/ppermute | solution.py:77
  17.0 0.5 collective-permute-start.6
  17.6 1.8 %collective-permute-done.4.refs_5_ = bf16[8,6144]{1,0:T(8,128)(2,1)S(1)} collective-permute-done((bf16[8,6144]{1,0:T(8,128)(2,1)S(1)}, bf16[8,6144]{1,0:T(8,128)(2,1)S(1)}, u32[]{:S(2)}, u32[]{:S(2)}) %collective-permute-start.4) | collective-permute-done | bytes 98336 | tf_op jit(solution)/shard_map/ppermute | solution.py:77
  19.3 1.1 %collective-permute-done.5.refs_6_ = bf16[8,6144]{1,0:T(8,128)(2,1)S(1)} collective-permute-done((bf16[8,6144]{1,0:T(8,128)(2,1)S(1)}, bf16[8,6144]{1,0:T(8,128)(2,1)S(1)}, u32[]{:S(2)}, u32[]{:S(2)}) %collective-permute-start.5) | collective-permute-done | bytes 98336 | tf_op jit(solution)/shard_map/ppermute | solution.py:77
  20.4 1.3 %collective-permute-done.6.refs_7_ = bf16[8,6144]{1,0:T(8,128)(2,1)S(1)} collective-permute-done((bf16[8,6144]{1,0:T(8,128)(2,1)S(1)}, bf16[8,6144]{1,0:T(8,128)(2,1)S(1)}, u32[]{:S(2)}, u32[]{:S(2)}) %collective-permute-start.6) | collective-permute-done | bytes 98336 | tf_op jit(solution)/shard_map/ppermute | solution.py:77
  21.7 0.3 unpack.2.left
  22.0 0.1 collective-permute-start.7
  22.1 0.0 slice-start.1
  22.1 2.3 %qkv_own.1 = (f32[64,640]{1,0:T(8,128)S(1)}, bf16[6,384,1024]{2,1,0:T(8,128)(2,1)S(1)}) custom-call(bf16[8,64,1024]{2,1,0:T(8,128)(2,1)S(1)} %unpack.2.left, bf16[8192,640]{1,0:T(8,128)(2,1)S(1)} %get-tuple-element.21.held, bf16[6,384,1024]{2,1,0:T(8,128)(2,1)S(1)} %bitcast.10), custom_call_target="tpu_custom_call" | custom-call | flops 671088640 | bytes 10485760 | tf_op jit(solution)/shard_map/qkv_own/pallas_call | solution.py:313
  24.5 2.1 %copy-done = bf16[6,384,1024]{2,1,0:T(8,128)(2,1)} copy-done((bf16[6,384,1024]{2,1,0:T(8,128)(2,1)}, bf16[6,384,1024]{2,1,0:T(8,128)(2,1)S(1)}, u32[]{:S(2)}) %copy-start) | copy-done | bytes 4718616
  26.7 2.3 %qkv_project.1 = (bf16[24,640]{1,0:T(8,128)(2,1)S(1)}, bf16[24,640]{1,0:T(8,128)(2,1)S(1)}, bf16[24,640]{1,0:T(8,128)(2,1)S(1)}, bf16[24,640]{1,0:T(8,128)(2,1)S(1)}, bf16[6,384,1024]{2,1,0:T(8,128)(2,1)S(1)}) custom-call(bf16[1,640]{1,0:T(2,128)(2,1)S(1)} %reshape.24.bias_ref, f32[64,640]{1,0:T(8,128)S(1)} %get-tuple-element.23.own_ref, ...), custom_call_target="tpu_custom_call" | custom-call | tf_op jit(solution)/shard_map/qkv_project/pallas_call | solution.py:353
  29.0 3.4 %collective-permute-start.10 = (bf16[24,640]{1,0:T(8,128)(2,1)S(1)}, bf16[24,640]{1,0:T(8,128)(2,1)S(1)}, u32[]{:S(2)}, u32[]{:S(2)}) collective-permute-start(bf16[24,640]{1,0:T(8,128)(2,1)S(1)} %get-tuple-element.28), channel_id=1, source_target_pairs={{0,12},{1,13},{2,14},{3,15},{4,8},{5,9},{6,10},{7,11},{8,4},{9,5},... | collective-permute-start | bytes 92168 | tf_op jit(solution)/shard_map/ppermute | solution.py:77
  32.4 1.1 %collective-permute-start.9 = (bf16[24,640]{1,0:T(8,128)(2,1)S(1)}, bf16[24,640]{1,0:T(8,128)(2,1)S(1)}, u32[]{:S(2)}, u32[]{:S(2)}) collective-permute-start(bf16[24,640]{1,0:T(8,128)(2,1)S(1)} %get-tuple-element.27), channel_id=1, source_target_pairs={{0,8},{1,9},{2,10},{3,11},{4,12},{5,13},{6,14},{7,15},{8,0},{9,1},... | collective-permute-start | bytes 92168 | tf_op jit(solution)/shard_map/ppermute | solution.py:77
  33.5 0.1 fusion
  33.6 1.4 %collective-permute-done.10.refs_3_ = bf16[24,640]{1,0:T(8,128)(2,1)S(1)} collective-permute-done((bf16[24,640]{1,0:T(8,128)(2,1)S(1)}, bf16[24,640]{1,0:T(8,128)(2,1)S(1)}, u32[]{:S(2)}, u32[]{:S(2)}) %collective-permute-start.10) | collective-permute-done | bytes 30752 | tf_op jit(solution)/shard_map/ppermute | solution.py:77
  34.9 1.7 %collective-permute-done.8.refs_1_ = bf16[24,640]{1,0:T(8,128)(2,1)S(1)} collective-permute-done((bf16[24,640]{1,0:T(8,128)(2,1)S(1)}, bf16[24,640]{1,0:T(8,128)(2,1)S(1)}, u32[]{:S(2)}, u32[]{:S(2)}) %collective-permute-start.8) | collective-permute-done | bytes 30752 | tf_op jit(solution)/shard_map/ppermute | solution.py:77
  36.6 0.6 collective-permute-done.9.refs_2_
  37.2 0.1 turn.1
  37.3 0.1 collective-permute-start.11
  37.4 0.8 collective-permute-start.12
  38.1 1.1 %collective-permute-start.13 = (bf16[24,640]{1,0:T(8,128)(2,1)S(1)}, bf16[24,640]{1,0:T(8,128)(2,1)S(1)}, u32[]{:S(2)}, u32[]{:S(2)}) collective-permute-start(bf16[24,640]{1,0:T(8,128)(2,1)S(1)} %get-tuple-element.32), channel_id=1, source_target_pairs={{0,3},{1,2},{2,1},{3,0},{4,7},{5,6},{6,5},{7,4},{8,11},{9,10},{10,... | collective-permute-start | bytes 92168 | tf_op jit(solution)/shard_map/ppermute | solution.py:77
  39.2 0.1 pad_maximum_fusion
  39.3 2.2 %collective-permute-done.12.refs_2_ = bf16[24,640]{1,0:T(8,128)(2,1)S(1)} collective-permute-done((bf16[24,640]{1,0:T(8,128)(2,1)S(1)}, bf16[24,640]{1,0:T(8,128)(2,1)S(1)}, u32[]{:S(2)}, u32[]{:S(2)}) %collective-permute-start.12) | collective-permute-done | bytes 30752 | tf_op jit(solution)/shard_map/ppermute | solution.py:77
  41.5 0.2 collective-permute-done.13.refs_3_
  41.8 4.7 %attend.1.refs_0_ = bf16[8,6272]{1,0:T(8,128)(2,1)S(1)} custom-call(s32[1]{0:T(128)} %bitcast.refs_1_.me_ref, s32[6]{0:T(128)S(1)} %copy-done.6, s32[6]{0:T(128)S(1)} %copy-done.7, f32[6,128]{1,0:T(8,128)S(1)} %get-tuple-element.38.cos_ref, f32[6,128]{1,0:T(8,128)S(1)} %get-tuple-element.39.sin_ref, bf16[6,384,1024]{2,1,0:T(8,128)(2,1)S(1)} %copy-done.1, ...), custom_call_target="tpu_custom_call" | custom-call | tf_op jit(solution)/shard_map/attend/pallas_call | solution.py:462
  46.5 2.1 %collective-permute-start.14 = (bf16[8,6272]{1,0:T(8,128)(2,1)S(1)}, bf16[8,6272]{1,0:T(8,128)(2,1)S(1)}, u32[]{:S(2)}, u32[]{:S(2)}) collective-permute-start(bf16[8,6272]{1,0:T(8,128)(2,1)S(1)} %attend.1.refs_0_), channel_id=1, source_target_pairs={{0,4},{1,5},{2,6},{3,7},{4,0},{5,1},{6,2},{7,3},{8,12},{9,13},{10,... | collective-permute-start | bytes 301064 | tf_op jit(solution)/shard_map/ppermute | solution.py:77
  48.5 0.3 collective-permute-start.15
  48.8 2.2 %collective-permute-start.16 = (bf16[8,6272]{1,0:T(8,128)(2,1)S(1)}, bf16[8,6272]{1,0:T(8,128)(2,1)S(1)}, u32[]{:S(2)}, u32[]{:S(2)}) collective-permute-start(bf16[8,6272]{1,0:T(8,128)(2,1)S(1)} %attend.1.refs_0_), channel_id=1, source_target_pairs={{0,12},{1,13},{2,14},{3,15},{4,8},{5,9},{6,10},{7,11},{8,4},{9,5},... | collective-permute-start | bytes 301064 | tf_op jit(solution)/shard_map/ppermute | solution.py:77
  51.0 1.0 %collective-permute-start.17 = (bf16[8,6272]{1,0:T(8,128)(2,1)S(1)}, bf16[8,6272]{1,0:T(8,128)(2,1)S(1)}, u32[]{:S(2)}, u32[]{:S(2)}) collective-permute-start(bf16[8,6272]{1,0:T(8,128)(2,1)S(1)} %attend.1.refs_0_), channel_id=1, source_target_pairs={{0,2},{1,3},{2,0},{3,1},{4,6},{5,7},{6,4},{7,5},{8,10},{9,11},{10,... | collective-permute-start | bytes 301064 | tf_op jit(solution)/shard_map/ppermute | solution.py:77
  52.0 3.5 %hold_output.1 = (bf16[8192,512]{1,0:T(8,128)(2,1)S(1)}, bf16[8,6272]{1,0:T(8,128)(2,1)S(1)}) custom-call(bf16[8,6272]{1,0:T(8,128)(2,1)S(1)} %collective-permute-done.14.refs_0_, bf16[8192,512]{1,0:T(8,128)(2,1)} %refs_1_.1), custom_call_target="tpu_custom_call", output_to_operand_aliasing={{1}: (0, {})} | custom-call | bytes 16777216 | tf_op jit(solution)/shard_map/hold_output/pallas_call | solution.py:256
  55.5 1.1 %collective-permute-start.18 = (bf16[8,6272]{1,0:T(8,128)(2,1)S(1)}, bf16[8,6272]{1,0:T(8,128)(2,1)S(1)}, u32[]{:S(2)}, u32[]{:S(2)}) collective-permute-start(bf16[8,6272]{1,0:T(8,128)(2,1)S(1)} %get-tuple-element.33.refs_1_), channel_id=1, source_target_pairs={{0,2},{1,3},{2,0},{3,1},{4,6},{5,7},{6,4},{7,5},{8,10},{9,11},{10,... | collective-permute-start | bytes 301064 | tf_op jit(solution)/shard_map/ppermute | solution.py:77
  56.6 1.9 %collective-permute-done.15.refs_2_ = bf16[8,6272]{1,0:T(8,128)(2,1)S(1)} collective-permute-done((bf16[8,6272]{1,0:T(8,128)(2,1)S(1)}, bf16[8,6272]{1,0:T(8,128)(2,1)S(1)}, u32[]{:S(2)}, u32[]{:S(2)}) %collective-permute-start.15) | collective-permute-done | bytes 100384 | tf_op jit(solution)/shard_map/ppermute | solution.py:77
  58.5 1.1 %collective-permute-start.19 = (bf16[8,6272]{1,0:T(8,128)(2,1)S(1)}, bf16[8,6272]{1,0:T(8,128)(2,1)S(1)}, u32[]{:S(2)}, u32[]{:S(2)}) collective-permute-start(bf16[8,6272]{1,0:T(8,128)(2,1)S(1)} %collective-permute-done.15.refs_2_), channel_id=1, source_target_pairs={{0,2},{1,3},{2,0},{3,1},{4,6},{5,7},{6,4},{7,5},{8,10},{9,11},{10,... | collective-permute-start | bytes 301064 | tf_op jit(solution)/shard_map/ppermute | solution.py:77
  59.6 1.0 %collective-permute-start.20 = (bf16[8,6272]{1,0:T(8,128)(2,1)S(1)}, bf16[8,6272]{1,0:T(8,128)(2,1)S(1)}, u32[]{:S(2)}, u32[]{:S(2)}) collective-permute-start(bf16[8,6272]{1,0:T(8,128)(2,1)S(1)} %collective-permute-done.16.refs_3_), channel_id=1, source_target_pairs={{0,2},{1,3},{2,0},{3,1},{4,6},{5,7},{6,4},{7,5},{8,10},{9,11},{10,... | collective-permute-start | bytes 301064 | tf_op jit(solution)/shard_map/ppermute | solution.py:77
  60.5 3.4 %collective-permute-done.19.refs_6_ = bf16[8,6272]{1,0:T(8,128)(2,1)S(1)} collective-permute-done((bf16[8,6272]{1,0:T(8,128)(2,1)S(1)}, bf16[8,6272]{1,0:T(8,128)(2,1)S(1)}, u32[]{:S(2)}, u32[]{:S(2)}) %collective-permute-start.19) | collective-permute-done | bytes 100384 | tf_op jit(solution)/shard_map/ppermute | solution.py:77
  63.9 1.1 %collective-permute-done.20.refs_7_ = bf16[8,6272]{1,0:T(8,128)(2,1)S(1)} collective-permute-done((bf16[8,6272]{1,0:T(8,128)(2,1)S(1)}, bf16[8,6272]{1,0:T(8,128)(2,1)S(1)}, u32[]{:S(2)}, u32[]{:S(2)}) %collective-permute-start.20) | collective-permute-done | bytes 100384 | tf_op jit(solution)/shard_map/ppermute | solution.py:77
  65.0 0.3 unpack.3.left.own
  65.3 0.1 collective-permute-start.21
  65.4 0.6 shrink_own.1.own_part
  66.0 1.6 %base_own.1.own_ref.after = f32[64,512]{1,0:T(8,128)S(1)} custom-call(bf16[9,64,1024]{2,1,0:T(8,128)(2,1)S(1)} %unpack.3.left.own, bf16[8192,512]{1,0:T(8,128)(2,1)S(1)} %get-tuple-element.34.held), custom_call_target="tpu_custom_call" | custom-call | flops 536870912 | bytes 8388608 | tf_op jit(solution)/shard_map/base_own/pallas_call | solution.py:283
  67.6 0.6 collective-permute-done.21.left.other
  68.2 0.9 shrink.1.refs_0_
  69.1 0.2 collective-permute-start.22
  69.2 1.0 %collective-permute-start.23 = (bf16[32,128]{1,0:T(8,128)(2,1)S(1)}, bf16[32,128]{1,0:T(8,128)(2,1)S(1)}, u32[]{:S(2)}, u32[]{:S(2)}) collective-permute-start(bf16[32,128]{1,0:T(8,128)(2,1)S(1)} %shrink.1.refs_0_), channel_id=1, source_target_pairs={{0,2},{1,3},{2,0},{3,1},{4,6},{5,7},{6,4},{7,5},{8,10},{9,11},{10,... | collective-permute-start | bytes 24584 | tf_op jit(solution)/shard_map/ppermute | solution.py:77
  70.3 0.7 collective-permute-start.24
  70.9 1.9 %collective-permute-done.23.refs_2_ = bf16[32,128]{1,0:T(8,128)(2,1)S(1)} collective-permute-done((bf16[32,128]{1,0:T(8,128)(2,1)S(1)}, bf16[32,128]{1,0:T(8,128)(2,1)S(1)}, u32[]{:S(2)}, u32[]{:S(2)}) %collective-permute-start.23) | collective-permute-done | bytes 8224 | tf_op jit(solution)/shard_map/ppermute | solution.py:77
  72.9 0.5 collective-permute-done.24.refs_3_
  73.3 0.6 collective-permute-start.25
  74.0 0.8 collective-permute-start.26
  74.7 3.0 %collective-permute-start.27 = (bf16[128,128]{1,0:T(8,128)(2,1)S(1)}, bf16[128,128]{1,0:T(8,128)(2,1)S(1)}, u32[]{:S(2)}, u32[]{:S(2)}) collective-permute-start(bf16[128,128]{1,0:T(8,128)(2,1)S(1)} %join_coords.1.refs_0_), channel_id=1, source_target_pairs={{0,12},{1,13},{2,14},{3,15},{4,8},{5,9},{6,10},{7,11},{8,4},{9,5},... | collective-permute-start | bytes 98312 | tf_op jit(solution)/shard_map/ppermute | solution.py:77
  77.7 1.5 %base_project.1.base_ref = f32[128,512]{1,0:T(8,128)S(1)} custom-call(s32[1]{0:T(128)} %bitcast.refs_1_.me_ref, f32[64,512]{1,0:T(8,128)S(1)} %base_own.1.own_ref.after, bf16[9,64,1024]{2,1,0:T(8,128)(2,1)S(1)} %collective-permute-done.21.left.other, bf16[8192,512]{1,0:T(8,128)(2,1)S(1)} %get-tuple-element.34.held), custom_call_target="tpu_custom_call" | custom-call | flops 536870912 | bytes 8388608 | tf_op jit(solution)/shard_map/base_project/pallas_call | solution.py:576
  79.3 1.2 %collective-permute-done.27.refs_3_ = bf16[128,128]{1,0:T(8,128)(2,1)S(1)} collective-permute-done((bf16[128,128]{1,0:T(8,128)(2,1)S(1)}, bf16[128,128]{1,0:T(8,128)(2,1)S(1)}, u32[]{:S(2)}, u32[]{:S(2)}) %collective-permute-start.27) | collective-permute-done | bytes 32800 | tf_op jit(solution)/shard_map/ppermute | solution.py:77
  80.5 0.3 add_delta.1
  80.7 12.5 %all_to_all.5 = bf16[16,6,512]{2,1,0:T(8,128)(2,1)S(1)} all-to-all(bf16[16,6,512]{2,1,0:T(8,128)(2,1)S(1)} %add_delta.1), channel_id=1, replica_groups=mesh['group'=2,'tensor'=16] {'tensor'}, dimensions={0} | all-to-all | bytes 196608 | tf_op jit(solution)/shard_map/all_to_all | solution.py:670
  93.3 0.7 copy.17
  (42 shorter events, 0.1 us)
Async XLA Ops:
  0.0 0.9 copy-start.4
  0.9 0.7 copy-start.5
  2.0 7.4 %collective-permute-start = (bf16[8,6144]{1,0:T(8,128)(2,1)S(1)}, bf16[8,6144]{1,0:T(8,128)(2,1)S(1)}, u32[]{:S(2)}, u32[]{:S(2)}) collective-permute-start(bf16[8,6144]{1,0:T(8,128)(2,1)S(1)} %norm_chunk.1.refs_0_), channel_id=1, source_target_pairs={{0,4},{1,5},{2,6},{3,7},{4,0},{5,1},{6,2},{7,3},{8,12},{9,13},{10,... | collective-permute-start | bytes 294920 | tf_op jit(solution)/shard_map/ppermute | solution.py:77
  5.1 10.4 %collective-permute-start.1 = (bf16[8,6144]{1,0:T(8,128)(2,1)S(1)}, bf16[8,6144]{1,0:T(8,128)(2,1)S(1)}, u32[]{:S(2)}, u32[]{:S(2)}) collective-permute-start(bf16[8,6144]{1,0:T(8,128)(2,1)S(1)} %norm_chunk.1.refs_0_), channel_id=1, source_target_pairs={{0,8},{1,9},{2,10},{3,11},{4,12},{5,13},{6,14},{7,15},{8,0},{9,1},... | collective-permute-start | bytes 294920 | tf_op jit(solution)/shard_map/ppermute | solution.py:77
  7.7 9.4 %collective-permute-start.2 = (bf16[8,6144]{1,0:T(8,128)(2,1)S(1)}, bf16[8,6144]{1,0:T(8,128)(2,1)S(1)}, u32[]{:S(2)}, u32[]{:S(2)}) collective-permute-start(bf16[8,6144]{1,0:T(8,128)(2,1)S(1)} %norm_chunk.1.refs_0_), channel_id=1, source_target_pairs={{0,12},{1,13},{2,14},{3,15},{4,8},{5,9},{6,10},{7,11},{8,4},{9,5},... | collective-permute-start | bytes 294920 | tf_op jit(solution)/shard_map/ppermute | solution.py:77
  7.7 9.9 %collective-permute-start.3 = (bf16[8,6144]{1,0:T(8,128)(2,1)S(1)}, bf16[8,6144]{1,0:T(8,128)(2,1)S(1)}, u32[]{:S(2)}, u32[]{:S(2)}) collective-permute-start(bf16[8,6144]{1,0:T(8,128)(2,1)S(1)} %norm_chunk.1.refs_0_), channel_id=1, source_target_pairs={{0,2},{1,3},{2,0},{3,1},{4,6},{5,7},{6,4},{7,5},{8,10},{9,11},{10,... | collective-permute-start | bytes 294920 | tf_op jit(solution)/shard_map/ppermute | solution.py:77
  9.4 12.7 %slice-start.2 = ((s8[4718592]{0:T(1024)(128)(4,1)}), s8[4194304]{0:T(1024)(128)(4,1)S(1)}, s32[]{:S(2)}) async-start(s8[4718592]{0:T(1024)(128)(4,1)} %bitcast.9), calls=%async_computation.3 | async-start | bytes 8388608
  9.4 12.6 %copy-start.8 = (bf16[640]{0:T(1024)(128)(2,1)S(1)}, bf16[640]{0:T(1024)(128)(2,1)}, u32[]{:S(2)}) copy-start(bf16[640]{0:T(1024)(128)(2,1)} %param.14) | copy-start | bytes 3844
  9.4 12.6 %copy-start.6 = (s32[6]{0:T(128)S(1)}, s32[6]{0:T(128)}, u32[]{:S(2)}) copy-start(s32[6]{0:T(128)} %len_ref.1) | copy-start | bytes 76
  9.4 12.7 %slice-start.3 = ((s8[4718592]{0:T(1024)(128)(4,1)}), s8[524288]{0:T(1024)(128)(4,1)S(1)}, s32[]{:S(2)}) async-start(s8[4718592]{0:T(1024)(128)(4,1)} %bitcast.9), calls=%async_computation.4 | async-start | bytes 1048576
  13.7 5.6 %collective-permute-start.4 = (bf16[8,6144]{1,0:T(8,128)(2,1)S(1)}, bf16[8,6144]{1,0:T(8,128)(2,1)S(1)}, u32[]{:S(2)}, u32[]{:S(2)}) collective-permute-start(bf16[8,6144]{1,0:T(8,128)(2,1)S(1)} %get-tuple-element.20.refs_1_), channel_id=1, source_target_pairs={{0,2},{1,3},{2,0},{3,1},{4,6},{5,7},{6,4},{7,5},{8,10},{9,11},{10,... | collective-permute-start | bytes 294920 | tf_op jit(solution)/shard_map/ppermute | solution.py:77
  15.5 4.9 %collective-permute-start.5 = (bf16[8,6144]{1,0:T(8,128)(2,1)S(1)}, bf16[8,6144]{1,0:T(8,128)(2,1)S(1)}, u32[]{:S(2)}, u32[]{:S(2)}) collective-permute-start(bf16[8,6144]{1,0:T(8,128)(2,1)S(1)} %collective-permute-done.1.refs_2_), channel_id=1, source_target_pairs={{0,2},{1,3},{2,0},{3,1},{4,6},{5,7},{6,4},{7,5},{8,10},{9,11},{10,... | collective-permute-start | bytes 294920 | tf_op jit(solution)/shard_map/ppermute | solution.py:77
  17.0 4.6 %collective-permute-start.6 = (bf16[8,6144]{1,0:T(8,128)(2,1)S(1)}, bf16[8,6144]{1,0:T(8,128)(2,1)S(1)}, u32[]{:S(2)}, u32[]{:S(2)}) collective-permute-start(bf16[8,6144]{1,0:T(8,128)(2,1)S(1)} %collective-permute-done.2.refs_3_), channel_id=1, source_target_pairs={{0,2},{1,3},{2,0},{3,1},{4,6},{5,7},{6,4},{7,5},{8,10},{9,11},{10,... | collective-permute-start | bytes 294920 | tf_op jit(solution)/shard_map/ppermute | solution.py:77
  21.7 5.0 %slice-start = ((s8[4718592]{0:T(1024)(128)(4,1)}), s8[524288]{0:T(1024)(128)(4,1)S(1)}, s32[]{:S(2)}) async-start(s8[4718592]{0:T(1024)(128)(4,1)} %bitcast.7), calls=%async_computation.1 | async-start | bytes 1048576
  22.0 4.6 %collective-permute-start.7 = (bf16[8,64,1024]{2,1,0:T(8,128)(2,1)S(1)}, bf16[8,64,1024]{2,1,0:T(8,128)(2,1)S(1)}, u32[]{:S(2)}, u32[]{:S(2)}) collective-permute-start(bf16[8,64,1024]{2,1,0:T(8,128)(2,1)S(1)} %unpack.2.left), channel_id=1, source_target_pairs={{0,1},{1,0},{2,3},{3,2},{4,5},{5,4},{6,7},{7,6},{8,9},{9,8},{10,11... | collective-permute-start | bytes 3145736 | tf_op jit(solution)/shard_map/ppermute | solution.py:77
  22.1 4.5 %slice-start.1 = ((s8[4718592]{0:T(1024)(128)(4,1)}), s8[4194304]{0:T(1024)(128)(4,1)S(1)}, s32[]{:S(2)}) async-start(s8[4718592]{0:T(1024)(128)(4,1)} %bitcast.7), calls=%async_computation.2 | async-start | bytes 8388608
  24.5 2.1 %copy-start = (bf16[6,384,1024]{2,1,0:T(8,128)(2,1)}, bf16[6,384,1024]{2,1,0:T(8,128)(2,1)S(1)}, u32[]{:S(2)}) copy-start(bf16[6,384,1024]{2,1,0:T(8,128)(2,1)S(1)} %get-tuple-element.22.keys) | copy-start | bytes 14155780
  26.6 15.1 %copy-start.1 = (bf16[6,384,1024]{2,1,0:T(8,128)(2,1)S(1)}, bf16[6,384,1024]{2,1,0:T(8,128)(2,1)}, u32[]{:S(2)}) copy-start(bf16[6,384,1024]{2,1,0:T(8,128)(2,1)} %copy-done) | copy-start | bytes 14155780
  26.6 15.1 %copy-start.7 = (s32[6]{0:T(128)S(1)}, s32[6]{0:T(128)}, u32[]{:S(2)}) copy-start(s32[6]{0:T(128)} %ids_ref.1) | copy-start | bytes 76
  29.0 5.9 %collective-permute-start.10 = (bf16[24,640]{1,0:T(8,128)(2,1)S(1)}, bf16[24,640]{1,0:T(8,128)(2,1)S(1)}, u32[]{:S(2)}, u32[]{:S(2)}) collective-permute-start(bf16[24,640]{1,0:T(8,128)(2,1)S(1)} %get-tuple-element.28), channel_id=1, source_target_pairs={{0,12},{1,13},{2,14},{3,15},{4,8},{5,9},{6,10},{7,11},{8,4},{9,5},... | collective-permute-start | bytes 92168 | tf_op jit(solution)/shard_map/ppermute | solution.py:77
  32.4 4.2 %collective-permute-start.8 = (bf16[24,640]{1,0:T(8,128)(2,1)S(1)}, bf16[24,640]{1,0:T(8,128)(2,1)S(1)}, u32[]{:S(2)}, u32[]{:S(2)}) collective-permute-start(bf16[24,640]{1,0:T(8,128)(2,1)S(1)} %get-tuple-element.26), channel_id=1, source_target_pairs={{0,4},{1,5},{2,6},{3,7},{4,0},{5,1},{6,2},{7,3},{8,12},{9,13},{10,... | collective-permute-start | bytes 92168 | tf_op jit(solution)/shard_map/ppermute | solution.py:77
  32.4 4.8 %collective-permute-start.9 = (bf16[24,640]{1,0:T(8,128)(2,1)S(1)}, bf16[24,640]{1,0:T(8,128)(2,1)S(1)}, u32[]{:S(2)}, u32[]{:S(2)}) collective-permute-start(bf16[24,640]{1,0:T(8,128)(2,1)S(1)} %get-tuple-element.27), channel_id=1, source_target_pairs={{0,8},{1,9},{2,10},{3,11},{4,12},{5,13},{6,14},{7,15},{8,0},{9,1},... | collective-permute-start | bytes 92168 | tf_op jit(solution)/shard_map/ppermute | solution.py:77
  37.3 2.0 %collective-permute-start.11 = (bf16[24,640]{1,0:T(8,128)(2,1)S(1)}, bf16[24,640]{1,0:T(8,128)(2,1)S(1)}, u32[]{:S(2)}, u32[]{:S(2)}) collective-permute-start(bf16[24,640]{1,0:T(8,128)(2,1)S(1)} %get-tuple-element.30), channel_id=1, source_target_pairs={{0,1},{1,0},{2,3},{3,2},{4,5},{5,4},{6,7},{7,6},{8,9},{9,8},{10,11... | collective-permute-start | bytes 92168 | tf_op jit(solution)/shard_map/ppermute | solution.py:77
  37.4 4.2 %collective-permute-start.12 = (bf16[24,640]{1,0:T(8,128)(2,1)S(1)}, bf16[24,640]{1,0:T(8,128)(2,1)S(1)}, u32[]{:S(2)}, u32[]{:S(2)}) collective-permute-start(bf16[24,640]{1,0:T(8,128)(2,1)S(1)} %get-tuple-element.31), channel_id=1, source_target_pairs={{0,2},{1,3},{2,0},{3,1},{4,6},{5,7},{6,4},{7,5},{8,10},{9,11},{10,... | collective-permute-start | bytes 92168 | tf_op jit(solution)/shard_map/ppermute | solution.py:77
  38.1 3.6 %collective-permute-start.13 = (bf16[24,640]{1,0:T(8,128)(2,1)S(1)}, bf16[24,640]{1,0:T(8,128)(2,1)S(1)}, u32[]{:S(2)}, u32[]{:S(2)}) collective-permute-start(bf16[24,640]{1,0:T(8,128)(2,1)S(1)} %get-tuple-element.32), channel_id=1, source_target_pairs={{0,3},{1,2},{2,1},{3,0},{4,7},{5,6},{6,5},{7,4},{8,11},{9,10},{10,... | collective-permute-start | bytes 92168 | tf_op jit(solution)/shard_map/ppermute | solution.py:77
  46.4 18.9 %copy-start.2 = (bf16[2,8192,16]{1,2,0:T(8,128)(2,1)S(1)}, bf16[2,8192,16]{1,2,0:T(8,128)(2,1)}, u32[]{:S(2)}) copy-start(bf16[2,8192,16]{1,2,0:T(8,128)(2,1)} %param.20) | copy-start | bytes 1572868
  46.5 5.5 %collective-permute-start.14 = (bf16[8,6272]{1,0:T(8,128)(2,1)S(1)}, bf16[8,6272]{1,0:T(8,128)(2,1)S(1)}, u32[]{:S(2)}, u32[]{:S(2)}) collective-permute-start(bf16[8,6272]{1,0:T(8,128)(2,1)S(1)} %attend.1.refs_0_), channel_id=1, source_target_pairs={{0,4},{1,5},{2,6},{3,7},{4,0},{5,1},{6,2},{7,3},{8,12},{9,13},{10,... | collective-permute-start | bytes 301064 | tf_op jit(solution)/shard_map/ppermute | solution.py:77
  48.5 9.9 %collective-permute-start.15 = (bf16[8,6272]{1,0:T(8,128)(2,1)S(1)}, bf16[8,6272]{1,0:T(8,128)(2,1)S(1)}, u32[]{:S(2)}, u32[]{:S(2)}) collective-permute-start(bf16[8,6272]{1,0:T(8,128)(2,1)S(1)} %attend.1.refs_0_), channel_id=1, source_target_pairs={{0,8},{1,9},{2,10},{3,11},{4,12},{5,13},{6,14},{7,15},{8,0},{9,1},... | collective-permute-start | bytes 301064 | tf_op jit(solution)/shard_map/ppermute | solution.py:77
  48.8 10.8 %collective-permute-start.16 = (bf16[8,6272]{1,0:T(8,128)(2,1)S(1)}, bf16[8,6272]{1,0:T(8,128)(2,1)S(1)}, u32[]{:S(2)}, u32[]{:S(2)}) collective-permute-start(bf16[8,6272]{1,0:T(8,128)(2,1)S(1)} %attend.1.refs_0_), channel_id=1, source_target_pairs={{0,12},{1,13},{2,14},{3,15},{4,8},{5,9},{6,10},{7,11},{8,4},{9,5},... | collective-permute-start | bytes 301064 | tf_op jit(solution)/shard_map/ppermute | solution.py:77
  51.0 9.5 %collective-permute-start.17 = (bf16[8,6272]{1,0:T(8,128)(2,1)S(1)}, bf16[8,6272]{1,0:T(8,128)(2,1)S(1)}, u32[]{:S(2)}, u32[]{:S(2)}) collective-permute-start(bf16[8,6272]{1,0:T(8,128)(2,1)S(1)} %attend.1.refs_0_), channel_id=1, source_target_pairs={{0,2},{1,3},{2,0},{3,1},{4,6},{5,7},{6,4},{7,5},{8,10},{9,11},{10,... | collective-permute-start | bytes 301064 | tf_op jit(solution)/shard_map/ppermute | solution.py:77
  55.5 5.1 %collective-permute-start.18 = (bf16[8,6272]{1,0:T(8,128)(2,1)S(1)}, bf16[8,6272]{1,0:T(8,128)(2,1)S(1)}, u32[]{:S(2)}, u32[]{:S(2)}) collective-permute-start(bf16[8,6272]{1,0:T(8,128)(2,1)S(1)} %get-tuple-element.33.refs_1_), channel_id=1, source_target_pairs={{0,2},{1,3},{2,0},{3,1},{4,6},{5,7},{6,4},{7,5},{8,10},{9,11},{10,... | collective-permute-start | bytes 301064 | tf_op jit(solution)/shard_map/ppermute | solution.py:77
  58.5 5.4 %collective-permute-start.19 = (bf16[8,6272]{1,0:T(8,128)(2,1)S(1)}, bf16[8,6272]{1,0:T(8,128)(2,1)S(1)}, u32[]{:S(2)}, u32[]{:S(2)}) collective-permute-start(bf16[8,6272]{1,0:T(8,128)(2,1)S(1)} %collective-permute-done.15.refs_2_), channel_id=1, source_target_pairs={{0,2},{1,3},{2,0},{3,1},{4,6},{5,7},{6,4},{7,5},{8,10},{9,11},{10,... | collective-permute-start | bytes 301064 | tf_op jit(solution)/shard_map/ppermute | solution.py:77
  59.6 5.4 %collective-permute-start.20 = (bf16[8,6272]{1,0:T(8,128)(2,1)S(1)}, bf16[8,6272]{1,0:T(8,128)(2,1)S(1)}, u32[]{:S(2)}, u32[]{:S(2)}) collective-permute-start(bf16[8,6272]{1,0:T(8,128)(2,1)S(1)} %collective-permute-done.16.refs_3_), channel_id=1, source_target_pairs={{0,2},{1,3},{2,0},{3,1},{4,6},{5,7},{6,4},{7,5},{8,10},{9,11},{10,... | collective-permute-start | bytes 301064 | tf_op jit(solution)/shard_map/ppermute | solution.py:77
  65.3 2.9 %collective-permute-start.21 = (bf16[9,64,1024]{2,1,0:T(8,128)(2,1)S(1)}, bf16[9,64,1024]{2,1,0:T(8,128)(2,1)S(1)}, u32[]{:S(2)}, u32[]{:S(2)}) collective-permute-start(bf16[9,64,1024]{2,1,0:T(8,128)(2,1)S(1)} %unpack.3.left.own), channel_id=1, source_target_pairs={{0,1},{1,0},{2,3},{3,2},{4,5},{5,4},{6,7},{7,6},{8,9},{9,8},{10,11... | collective-permute-start | bytes 3538952 | tf_op jit(solution)/shard_map/ppermute | solution.py:77
  69.1 1.9 %collective-permute-start.22 = (bf16[32,128]{1,0:T(8,128)(2,1)S(1)}, bf16[32,128]{1,0:T(8,128)(2,1)S(1)}, u32[]{:S(2)}, u32[]{:S(2)}) collective-permute-start(bf16[32,128]{1,0:T(8,128)(2,1)S(1)} %shrink.1.refs_0_), channel_id=1, source_target_pairs={{0,1},{1,0},{2,3},{3,2},{4,5},{5,4},{6,7},{7,6},{8,9},{9,8},{10,11... | collective-permute-start | bytes 24584 | tf_op jit(solution)/shard_map/ppermute | solution.py:77
  69.2 3.7 %collective-permute-start.23 = (bf16[32,128]{1,0:T(8,128)(2,1)S(1)}, bf16[32,128]{1,0:T(8,128)(2,1)S(1)}, u32[]{:S(2)}, u32[]{:S(2)}) collective-permute-start(bf16[32,128]{1,0:T(8,128)(2,1)S(1)} %shrink.1.refs_0_), channel_id=1, source_target_pairs={{0,2},{1,3},{2,0},{3,1},{4,6},{5,7},{6,4},{7,5},{8,10},{9,11},{10,... | collective-permute-start | bytes 24584 | tf_op jit(solution)/shard_map/ppermute | solution.py:77
  70.3 3.1 %collective-permute-start.24 = (bf16[32,128]{1,0:T(8,128)(2,1)S(1)}, bf16[32,128]{1,0:T(8,128)(2,1)S(1)}, u32[]{:S(2)}, u32[]{:S(2)}) collective-permute-start(bf16[32,128]{1,0:T(8,128)(2,1)S(1)} %shrink.1.refs_0_), channel_id=1, source_target_pairs={{0,3},{1,2},{2,1},{3,0},{4,7},{5,6},{6,5},{7,4},{8,11},{9,10},{10,... | collective-permute-start | bytes 24584 | tf_op jit(solution)/shard_map/ppermute | solution.py:77
  73.3 7.1 %copy-start.3 = (bf16[32,16,512]{2,1,0:T(8,128)(2,1)S(1)}, bf16[32,16,512]{2,1,0:T(8,128)(2,1)}, u32[]{:S(2)}) copy-start(bf16[32,16,512]{2,1,0:T(8,128)(2,1)} %param.21) | copy-start | bytes 1572868
  73.3 5.9 %collective-permute-start.25 = (bf16[128,128]{1,0:T(8,128)(2,1)S(1)}, bf16[128,128]{1,0:T(8,128)(2,1)S(1)}, u32[]{:S(2)}, u32[]{:S(2)}) collective-permute-start(bf16[128,128]{1,0:T(8,128)(2,1)S(1)} %join_coords.1.refs_0_), channel_id=1, source_target_pairs={{0,4},{1,5},{2,6},{3,7},{4,0},{5,1},{6,2},{7,3},{8,12},{9,13},{10,... | collective-permute-start | bytes 98312 | tf_op jit(solution)/shard_map/ppermute | solution.py:77
  74.0 5.3 %collective-permute-start.26 = (bf16[128,128]{1,0:T(8,128)(2,1)S(1)}, bf16[128,128]{1,0:T(8,128)(2,1)S(1)}, u32[]{:S(2)}, u32[]{:S(2)}) collective-permute-start(bf16[128,128]{1,0:T(8,128)(2,1)S(1)} %join_coords.1.refs_0_), channel_id=1, source_target_pairs={{0,8},{1,9},{2,10},{3,11},{4,12},{5,13},{6,14},{7,15},{8,0},{9,1},... | collective-permute-start | bytes 98312 | tf_op jit(solution)/shard_map/ppermute | solution.py:77
  74.7 5.7 %collective-permute-start.27 = (bf16[128,128]{1,0:T(8,128)(2,1)S(1)}, bf16[128,128]{1,0:T(8,128)(2,1)S(1)}, u32[]{:S(2)}, u32[]{:S(2)}) collective-permute-start(bf16[128,128]{1,0:T(8,128)(2,1)S(1)} %join_coords.1.refs_0_), channel_id=1, source_target_pairs={{0,12},{1,13},{2,14},{3,15},{4,8},{5,9},{6,10},{7,11},{8,4},{9,5},... | collective-permute-start | bytes 98312 | tf_op jit(solution)/shard_map/ppermute | solution.py:77

commit v8 on v7

--- a/solution.py
+++ b/solution.py
@@ -360,7 +360,7 @@
             pltpu.VMEM((2 * inner * rows, cols), jnp.float32),
             pltpu.SemaphoreType.DMA((cache.shape[0],)),
         ],
-        compiler_params=params(28),
+        compiler_params=params(24),
         name="qkv_project",
     )(bias, own, left, held, cache)
     return parts, kept

time: 94.2 us -> 92.2 us (0.979)
  local copies, waits for them, and re-layouts: 4.47 us -> 2.32 us
    unnamed x27 -> x23, local copies, waits for them, and re-layouts: 4.46 us -> 2.32 us
  transfers between devices with their start and end apart: 28 -> 28, of which waited for: 16 -> 17; matrix products, arithmetic and copies ran while one was open for 0% -> 0% of each run, Pallas kernels for 15% -> 15%
where the time goes in v8:
time: 92.2 us; the launch traced here: 92 us
  starting transfers between devices  31.2 us (34%)
  Pallas kernels  23 us (25%)
  waiting for transfers between devices  22.4 us (24%)
  blocking collectives  12.5 us (14%)
  local copies, waits for them, and re-layouts  2.32 us (3%)
    ppermute x28, starting transfers between devices, move(): lax.ppermute(x, 'tensor', [(d, place(devices, d, k, m, c)) for d in range...  31.2 us
    ppermute x28, waiting for transfers between devices, move(): lax.ppermute(x, 'tensor', [(d, place(devices, d, k, m, c)) for d in range...  22.4 us
    all_to_all x1, blocking collectives, per_device(): lax.all_to_all(projected, 'tensor', split_axis=0, concat_axis=0, tiled=True)  12.5 us
    pallas_call x2, Pallas kernels, hold(): pl.pallas_call(functools.partial(hold_kernel, len(arrays)), out_shape=(ja...  7.7 us
    pallas_call x1, Pallas kernels, attend(): pl.pallas_call(functools.partial(attend_kernel, devices, rows), out_shape...  4.66 us
    pallas_call x1, Pallas kernels, qkv_own(): pl.pallas_call(qkv_own_kernel, out_shape=(jax.ShapeDtypeStruct((rows, col...  2.34 us
    pallas_call x1, Pallas kernels, qkv_project(): pl.pallas_call(functools.partial(qkv_kernel, devices, rows), out_shape=[p...  2.34 us
    unnamed x23, local copies, waits for them, and re-layouts  2.32 us
  transfers between devices with their start and end apart: 28, of which 17 were waited for; matrix products, arithmetic and copies ran while one was open for 0% of the time, Pallas kernels for 15%

profile of v8, /device:TPU:0, one launch (start us, length us, event | category | flops | bytes accessed | tf_op | source)
XLA Modules:
  0.0 92.0 jit_solution(8806823074621737043)
XLA Ops:
  0.0 0.9 copy-done.2
  0.9 0.7 copy-done.3
  1.6 0.4 norm_chunk.1.refs_0_
  2.0 3.1 %collective-permute-start = (bf16[8,6144]{1,0:T(8,128)(2,1)S(1)}, bf16[8,6144]{1,0:T(8,128)(2,1)S(1)}, u32[]{:S(2)}, u32[]{:S(2)}) collective-permute-start(bf16[8,6144]{1,0:T(8,128)(2,1)S(1)} %norm_chunk.1.refs_0_), channel_id=1, source_target_pairs={{0,4},{1,5},{2,6},{3,7},{4,0},{5,1},{6,2},{7,3},{8,12},{9,13},{10,... | collective-permute-start | bytes 294920 | tf_op jit(solution)/shard_map/ppermute | solution.py:77
  5.1 2.6 %collective-permute-start.1 = (bf16[8,6144]{1,0:T(8,128)(2,1)S(1)}, bf16[8,6144]{1,0:T(8,128)(2,1)S(1)}, u32[]{:S(2)}, u32[]{:S(2)}) collective-permute-start(bf16[8,6144]{1,0:T(8,128)(2,1)S(1)} %norm_chunk.1.refs_0_), channel_id=1, source_target_pairs={{0,8},{1,9},{2,10},{3,11},{4,12},{5,13},{6,14},{7,15},{8,0},{9,1},... | collective-permute-start | bytes 294920 | tf_op jit(solution)/shard_map/ppermute | solution.py:77
  7.7 1.7 %collective-permute-start.3 = (bf16[8,6144]{1,0:T(8,128)(2,1)S(1)}, bf16[8,6144]{1,0:T(8,128)(2,1)S(1)}, u32[]{:S(2)}, u32[]{:S(2)}) collective-permute-start(bf16[8,6144]{1,0:T(8,128)(2,1)S(1)} %norm_chunk.1.refs_0_), channel_id=1, source_target_pairs={{0,2},{1,3},{2,0},{3,1},{4,6},{5,7},{6,4},{7,5},{8,10},{9,11},{10,... | collective-permute-start | bytes 294920 | tf_op jit(solution)/shard_map/ppermute | solution.py:77
  9.5 4.2 %hold_qkv.1 = (bf16[8192,640]{1,0:T(8,128)(2,1)S(1)}, bf16[8,6144]{1,0:T(8,128)(2,1)S(1)}) custom-call(bf16[8,6144]{1,0:T(8,128)(2,1)S(1)} %collective-permute-done.refs_0_, s32[1]{0:T(128)} %bitcast.refs_1_.me_ref, bf16[8192,640]{1,0:T(8,128)(2,1)} %refs_2_.1), custom_call_target="tpu_custom_call", output_to_operand_aliasing={{1}: (0, {})} | custom-call | bytes 20971520 | tf_op jit(solution)/shard_map/hold_qkv/pallas_call | solution.py:256
  13.7 0.4 collective-permute-start.4
  14.0 1.5 %collective-permute-done.1.refs_2_ = bf16[8,6144]{1,0:T(8,128)(2,1)S(1)} collective-permute-done((bf16[8,6144]{1,0:T(8,128)(2,1)S(1)}, bf16[8,6144]{1,0:T(8,128)(2,1)S(1)}, u32[]{:S(2)}, u32[]{:S(2)}) %collective-permute-start.1) | collective-permute-done | bytes 98336 | tf_op jit(solution)/shard_map/ppermute | solution.py:77
  15.5 1.5 %collective-permute-start.5 = (bf16[8,6144]{1,0:T(8,128)(2,1)S(1)}, bf16[8,6144]{1,0:T(8,128)(2,1)S(1)}, u32[]{:S(2)}, u32[]{:S(2)}) collective-permute-start(bf16[8,6144]{1,0:T(8,128)(2,1)S(1)} %collective-permute-done.1.refs_2_), channel_id=1, source_target_pairs={{0,2},{1,3},{2,0},{3,1},{4,6},{5,7},{6,4},{7,5},{8,10},{9,11},{10,... | collective-permute-start | bytes 294920 | tf_op jit(solution)/shard_map/ppermute | solution.py:77
  17.0 0.5 collective-permute-start.6
  17.6 1.8 %collective-permute-done.4.refs_5_ = bf16[8,6144]{1,0:T(8,128)(2,1)S(1)} collective-permute-done((bf16[8,6144]{1,0:T(8,128)(2,1)S(1)}, bf16[8,6144]{1,0:T(8,128)(2,1)S(1)}, u32[]{:S(2)}, u32[]{:S(2)}) %collective-permute-start.4) | collective-permute-done | bytes 98336 | tf_op jit(solution)/shard_map/ppermute | solution.py:77
  19.3 1.1 %collective-permute-done.5.refs_6_ = bf16[8,6144]{1,0:T(8,128)(2,1)S(1)} collective-permute-done((bf16[8,6144]{1,0:T(8,128)(2,1)S(1)}, bf16[8,6144]{1,0:T(8,128)(2,1)S(1)}, u32[]{:S(2)}, u32[]{:S(2)}) %collective-permute-start.5) | collective-permute-done | bytes 98336 | tf_op jit(solution)/shard_map/ppermute | solution.py:77
  20.4 1.3 %collective-permute-done.6.refs_7_ = bf16[8,6144]{1,0:T(8,128)(2,1)S(1)} collective-permute-done((bf16[8,6144]{1,0:T(8,128)(2,1)S(1)}, bf16[8,6144]{1,0:T(8,128)(2,1)S(1)}, u32[]{:S(2)}, u32[]{:S(2)}) %collective-permute-start.6) | collective-permute-done | bytes 98336 | tf_op jit(solution)/shard_map/ppermute | solution.py:77
  21.7 0.3 unpack.2.left
  22.0 0.1 collective-permute-start.7
  22.1 0.0 slice-start.1
  22.1 2.3 %qkv_own.1 = (f32[64,640]{1,0:T(8,128)S(1)}, bf16[6,384,1024]{2,1,0:T(8,128)(2,1)S(1)}) custom-call(bf16[8,64,1024]{2,1,0:T(8,128)(2,1)S(1)} %unpack.2.left, bf16[8192,640]{1,0:T(8,128)(2,1)S(1)} %get-tuple-element.21.held, bf16[6,384,1024]{2,1,0:T(8,128)(2,1)S(1)} %bitcast.10), custom_call_target="tpu_custom_call" | custom-call | flops 671088640 | bytes 10485760 | tf_op jit(solution)/shard_map/qkv_own/pallas_call | solution.py:313
  24.5 0.2 collective-permute-done.7.left
  24.7 2.3 %qkv_project.1 = (bf16[24,640]{1,0:T(8,128)(2,1)S(1)}, bf16[24,640]{1,0:T(8,128)(2,1)S(1)}, bf16[24,640]{1,0:T(8,128)(2,1)S(1)}, bf16[24,640]{1,0:T(8,128)(2,1)S(1)}, bf16[6,384,1024]{2,1,0:T(8,128)(2,1)S(1)}) custom-call(bf16[1,640]{1,0:T(2,128)(2,1)S(1)} %reshape.24.bias_ref, f32[64,640]{1,0:T(8,128)S(1)} %get-tuple-element.23.own_ref, ...), custom_call_target="tpu_custom_call" | custom-call | tf_op jit(solution)/shard_map/qkv_project/pallas_call | solution.py:353
  27.1 3.4 %collective-permute-start.10 = (bf16[24,640]{1,0:T(8,128)(2,1)S(1)}, bf16[24,640]{1,0:T(8,128)(2,1)S(1)}, u32[]{:S(2)}, u32[]{:S(2)}) collective-permute-start(bf16[24,640]{1,0:T(8,128)(2,1)S(1)} %get-tuple-element.28), channel_id=1, source_target_pairs={{0,12},{1,13},{2,14},{3,15},{4,8},{5,9},{6,10},{7,11},{8,4},{9,5},... | collective-permute-start | bytes 92168 | tf_op jit(solution)/shard_map/ppermute | solution.py:77
  30.5 1.1 %collective-permute-start.9 = (bf16[24,640]{1,0:T(8,128)(2,1)S(1)}, bf16[24,640]{1,0:T(8,128)(2,1)S(1)}, u32[]{:S(2)}, u32[]{:S(2)}) collective-permute-start(bf16[24,640]{1,0:T(8,128)(2,1)S(1)} %get-tuple-element.27), channel_id=1, source_target_pairs={{0,8},{1,9},{2,10},{3,11},{4,12},{5,13},{6,14},{7,15},{8,0},{9,1},... | collective-permute-start | bytes 92168 | tf_op jit(solution)/shard_map/ppermute | solution.py:77
  31.5 0.1 fusion
  31.6 1.2 %collective-permute-done.10.refs_3_ = bf16[24,640]{1,0:T(8,128)(2,1)S(1)} collective-permute-done((bf16[24,640]{1,0:T(8,128)(2,1)S(1)}, bf16[24,640]{1,0:T(8,128)(2,1)S(1)}, u32[]{:S(2)}, u32[]{:S(2)}) %collective-permute-start.10) | collective-permute-done | bytes 30752 | tf_op jit(solution)/shard_map/ppermute | solution.py:77
  32.8 1.8 %collective-permute-done.8.refs_1_ = bf16[24,640]{1,0:T(8,128)(2,1)S(1)} collective-permute-done((bf16[24,640]{1,0:T(8,128)(2,1)S(1)}, bf16[24,640]{1,0:T(8,128)(2,1)S(1)}, u32[]{:S(2)}, u32[]{:S(2)}) %collective-permute-start.8) | collective-permute-done | bytes 30752 | tf_op jit(solution)/shard_map/ppermute | solution.py:77
  34.6 0.6 collective-permute-done.9.refs_2_
  35.3 0.1 turn.1
  35.3 0.1 collective-permute-start.11
  35.4 0.8 collective-permute-start.12
  36.2 1.1 %collective-permute-start.13 = (bf16[24,640]{1,0:T(8,128)(2,1)S(1)}, bf16[24,640]{1,0:T(8,128)(2,1)S(1)}, u32[]{:S(2)}, u32[]{:S(2)}) collective-permute-start(bf16[24,640]{1,0:T(8,128)(2,1)S(1)} %get-tuple-element.32), channel_id=1, source_target_pairs={{0,3},{1,2},{2,1},{3,0},{4,7},{5,6},{6,5},{7,4},{8,11},{9,10},{10,... | collective-permute-start | bytes 92168 | tf_op jit(solution)/shard_map/ppermute | solution.py:77
  37.3 0.1 pad_maximum_fusion
  37.4 2.2 %collective-permute-done.12.refs_2_ = bf16[24,640]{1,0:T(8,128)(2,1)S(1)} collective-permute-done((bf16[24,640]{1,0:T(8,128)(2,1)S(1)}, bf16[24,640]{1,0:T(8,128)(2,1)S(1)}, u32[]{:S(2)}, u32[]{:S(2)}) %collective-permute-start.12) | collective-permute-done | bytes 30752 | tf_op jit(solution)/shard_map/ppermute | solution.py:77
  39.6 0.2 collective-permute-done.13.refs_3_
  39.8 4.7 %attend.1.refs_0_ = bf16[8,6272]{1,0:T(8,128)(2,1)S(1)} custom-call(s32[1]{0:T(128)} %bitcast.refs_1_.me_ref, s32[6]{0:T(128)S(1)} %copy-done.4, s32[6]{0:T(128)S(1)} %copy-done.5, f32[6,128]{1,0:T(8,128)S(1)} %get-tuple-element.38.cos_ref, f32[6,128]{1,0:T(8,128)S(1)} %get-tuple-element.39.sin_ref, bf16[6,384,1024]{2,1,0:T(8,128)(2,1)S(1)} %get-tuple-element.22.keys, ...), custom_call_target="tpu_custom_call" | custom-call | tf_op jit(solution)/shard_map/attend/pallas_call | solution.py:462
  44.5 2.1 %collective-permute-start.14 = (bf16[8,6272]{1,0:T(8,128)(2,1)S(1)}, bf16[8,6272]{1,0:T(8,128)(2,1)S(1)}, u32[]{:S(2)}, u32[]{:S(2)}) collective-permute-start(bf16[8,6272]{1,0:T(8,128)(2,1)S(1)} %attend.1.refs_0_), channel_id=1, source_target_pairs={{0,4},{1,5},{2,6},{3,7},{4,0},{5,1},{6,2},{7,3},{8,12},{9,13},{10,... | collective-permute-start | bytes 301064 | tf_op jit(solution)/shard_map/ppermute | solution.py:77
  46.6 0.1 collective-permute-start.15
  46.7 2.3 %collective-permute-start.16 = (bf16[8,6272]{1,0:T(8,128)(2,1)S(1)}, bf16[8,6272]{1,0:T(8,128)(2,1)S(1)}, u32[]{:S(2)}, u32[]{:S(2)}) collective-permute-start(bf16[8,6272]{1,0:T(8,128)(2,1)S(1)} %attend.1.refs_0_), channel_id=1, source_target_pairs={{0,12},{1,13},{2,14},{3,15},{4,8},{5,9},{6,10},{7,11},{8,4},{9,5},... | collective-permute-start | bytes 301064 | tf_op jit(solution)/shard_map/ppermute | solution.py:77
  49.0 1.0 %collective-permute-start.17 = (bf16[8,6272]{1,0:T(8,128)(2,1)S(1)}, bf16[8,6272]{1,0:T(8,128)(2,1)S(1)}, u32[]{:S(2)}, u32[]{:S(2)}) collective-permute-start(bf16[8,6272]{1,0:T(8,128)(2,1)S(1)} %attend.1.refs_0_), channel_id=1, source_target_pairs={{0,2},{1,3},{2,0},{3,1},{4,6},{5,7},{6,4},{7,5},{8,10},{9,11},{10,... | collective-permute-start | bytes 301064 | tf_op jit(solution)/shard_map/ppermute | solution.py:77
  50.0 3.5 %hold_output.1 = (bf16[8192,512]{1,0:T(8,128)(2,1)S(1)}, bf16[8,6272]{1,0:T(8,128)(2,1)S(1)}) custom-call(bf16[8,6272]{1,0:T(8,128)(2,1)S(1)} %collective-permute-done.14.refs_0_, bf16[8192,512]{1,0:T(8,128)(2,1)} %refs_1_.1), custom_call_target="tpu_custom_call", output_to_operand_aliasing={{1}: (0, {})} | custom-call | bytes 16777216 | tf_op jit(solution)/shard_map/hold_output/pallas_call | solution.py:256
  53.5 1.1 %collective-permute-start.18 = (bf16[8,6272]{1,0:T(8,128)(2,1)S(1)}, bf16[8,6272]{1,0:T(8,128)(2,1)S(1)}, u32[]{:S(2)}, u32[]{:S(2)}) collective-permute-start(bf16[8,6272]{1,0:T(8,128)(2,1)S(1)} %get-tuple-element.33.refs_1_), channel_id=1, source_target_pairs={{0,2},{1,3},{2,0},{3,1},{4,6},{5,7},{6,4},{7,5},{8,10},{9,11},{10,... | collective-permute-start | bytes 301064 | tf_op jit(solution)/shard_map/ppermute | solution.py:77
  54.6 1.9 %collective-permute-done.15.refs_2_ = bf16[8,6272]{1,0:T(8,128)(2,1)S(1)} collective-permute-done((bf16[8,6272]{1,0:T(8,128)(2,1)S(1)}, bf16[8,6272]{1,0:T(8,128)(2,1)S(1)}, u32[]{:S(2)}, u32[]{:S(2)}) %collective-permute-start.15) | collective-permute-done | bytes 100384 | tf_op jit(solution)/shard_map/ppermute | solution.py:77
  56.5 1.0 %collective-permute-start.19 = (bf16[8,6272]{1,0:T(8,128)(2,1)S(1)}, bf16[8,6272]{1,0:T(8,128)(2,1)S(1)}, u32[]{:S(2)}, u32[]{:S(2)}) collective-permute-start(bf16[8,6272]{1,0:T(8,128)(2,1)S(1)} %collective-permute-done.15.refs_2_), channel_id=1, source_target_pairs={{0,2},{1,3},{2,0},{3,1},{4,6},{5,7},{6,4},{7,5},{8,10},{9,11},{10,... | collective-permute-start | bytes 301064 | tf_op jit(solution)/shard_map/ppermute | solution.py:77
  57.5 1.0 %collective-permute-start.20 = (bf16[8,6272]{1,0:T(8,128)(2,1)S(1)}, bf16[8,6272]{1,0:T(8,128)(2,1)S(1)}, u32[]{:S(2)}, u32[]{:S(2)}) collective-permute-start(bf16[8,6272]{1,0:T(8,128)(2,1)S(1)} %collective-permute-done.16.refs_3_), channel_id=1, source_target_pairs={{0,2},{1,3},{2,0},{3,1},{4,6},{5,7},{6,4},{7,5},{8,10},{9,11},{10,... | collective-permute-start | bytes 301064 | tf_op jit(solution)/shard_map/ppermute | solution.py:77
  58.6 3.3 %collective-permute-done.19.refs_6_ = bf16[8,6272]{1,0:T(8,128)(2,1)S(1)} collective-permute-done((bf16[8,6272]{1,0:T(8,128)(2,1)S(1)}, bf16[8,6272]{1,0:T(8,128)(2,1)S(1)}, u32[]{:S(2)}, u32[]{:S(2)}) %collective-permute-start.19) | collective-permute-done | bytes 100384 | tf_op jit(solution)/shard_map/ppermute | solution.py:77
  61.9 1.1 %collective-permute-done.20.refs_7_ = bf16[8,6272]{1,0:T(8,128)(2,1)S(1)} collective-permute-done((bf16[8,6272]{1,0:T(8,128)(2,1)S(1)}, bf16[8,6272]{1,0:T(8,128)(2,1)S(1)}, u32[]{:S(2)}, u32[]{:S(2)}) %collective-permute-start.20) | collective-permute-done | bytes 100384 | tf_op jit(solution)/shard_map/ppermute | solution.py:77
  63.0 0.3 unpack.3.left.own
  63.3 0.1 collective-permute-start.21
  63.4 0.6 shrink_own.1.own_part
  64.0 1.6 %base_own.1.own_ref.after = f32[64,512]{1,0:T(8,128)S(1)} custom-call(bf16[9,64,1024]{2,1,0:T(8,128)(2,1)S(1)} %unpack.3.left.own, bf16[8192,512]{1,0:T(8,128)(2,1)S(1)} %get-tuple-element.34.held), custom_call_target="tpu_custom_call" | custom-call | flops 536870912 | bytes 8388608 | tf_op jit(solution)/shard_map/base_own/pallas_call | solution.py:283
  65.6 0.6 collective-permute-done.21.left.other
  66.2 0.9 shrink.1.refs_0_
  67.1 0.2 collective-permute-start.22
  67.2 1.2 %collective-permute-start.23 = (bf16[32,128]{1,0:T(8,128)(2,1)S(1)}, bf16[32,128]{1,0:T(8,128)(2,1)S(1)}, u32[]{:S(2)}, u32[]{:S(2)}) collective-permute-start(bf16[32,128]{1,0:T(8,128)(2,1)S(1)} %shrink.1.refs_0_), channel_id=1, source_target_pairs={{0,2},{1,3},{2,0},{3,1},{4,6},{5,7},{6,4},{7,5},{8,10},{9,11},{10,... | collective-permute-start | bytes 24584 | tf_op jit(solution)/shard_map/ppermute | solution.py:77
  68.4 0.6 collective-permute-start.24
  69.0 1.9 %collective-permute-done.23.refs_2_ = bf16[32,128]{1,0:T(8,128)(2,1)S(1)} collective-permute-done((bf16[32,128]{1,0:T(8,128)(2,1)S(1)}, bf16[32,128]{1,0:T(8,128)(2,1)S(1)}, u32[]{:S(2)}, u32[]{:S(2)}) %collective-permute-start.23) | collective-permute-done | bytes 8224 | tf_op jit(solution)/shard_map/ppermute | solution.py:77
  70.9 0.6 collective-permute-done.24.refs_3_
  71.5 0.6 collective-permute-start.25
  72.1 0.7 collective-permute-start.26
  72.8 3.1 %collective-permute-start.27 = (bf16[128,128]{1,0:T(8,128)(2,1)S(1)}, bf16[128,128]{1,0:T(8,128)(2,1)S(1)}, u32[]{:S(2)}, u32[]{:S(2)}) collective-permute-start(bf16[128,128]{1,0:T(8,128)(2,1)S(1)} %join_coords.1.refs_0_), channel_id=1, source_target_pairs={{0,12},{1,13},{2,14},{3,15},{4,8},{5,9},{6,10},{7,11},{8,4},{9,5},... | collective-permute-start | bytes 98312 | tf_op jit(solution)/shard_map/ppermute | solution.py:77
  75.9 1.5 %base_project.1.base_ref = f32[128,512]{1,0:T(8,128)S(1)} custom-call(s32[1]{0:T(128)} %bitcast.refs_1_.me_ref, f32[64,512]{1,0:T(8,128)S(1)} %base_own.1.own_ref.after, bf16[9,64,1024]{2,1,0:T(8,128)(2,1)S(1)} %collective-permute-done.21.left.other, bf16[8192,512]{1,0:T(8,128)(2,1)S(1)} %get-tuple-element.34.held), custom_call_target="tpu_custom_call" | custom-call | flops 536870912 | bytes 8388608 | tf_op jit(solution)/shard_map/base_project/pallas_call | solution.py:576
  77.5 1.0 %collective-permute-done.27.refs_3_ = bf16[128,128]{1,0:T(8,128)(2,1)S(1)} collective-permute-done((bf16[128,128]{1,0:T(8,128)(2,1)S(1)}, bf16[128,128]{1,0:T(8,128)(2,1)S(1)}, u32[]{:S(2)}, u32[]{:S(2)}) %collective-permute-start.27) | collective-permute-done | bytes 32800 | tf_op jit(solution)/shard_map/ppermute | solution.py:77
  78.5 0.3 add_delta.1
  78.8 12.5 %all_to_all.5 = bf16[16,6,512]{2,1,0:T(8,128)(2,1)S(1)} all-to-all(bf16[16,6,512]{2,1,0:T(8,128)(2,1)S(1)} %add_delta.1), channel_id=1, replica_groups=mesh['group'=2,'tensor'=16] {'tensor'}, dimensions={0} | all-to-all | bytes 196608 | tf_op jit(solution)/shard_map/all_to_all | solution.py:670
  91.3 0.7 copy.17
  (38 shorter events, 0.1 us)
Async XLA Ops:
  0.0 0.9 copy-start.2
  0.9 0.7 copy-start.3
  2.0 7.4 %collective-permute-start = (bf16[8,6144]{1,0:T(8,128)(2,1)S(1)}, bf16[8,6144]{1,0:T(8,128)(2,1)S(1)}, u32[]{:S(2)}, u32[]{:S(2)}) collective-permute-start(bf16[8,6144]{1,0:T(8,128)(2,1)S(1)} %norm_chunk.1.refs_0_), channel_id=1, source_target_pairs={{0,4},{1,5},{2,6},{3,7},{4,0},{5,1},{6,2},{7,3},{8,12},{9,13},{10,... | collective-permute-start | bytes 294920 | tf_op jit(solution)/shard_map/ppermute | solution.py:77
  5.1 10.4 %collective-permute-start.1 = (bf16[8,6144]{1,0:T(8,128)(2,1)S(1)}, bf16[8,6144]{1,0:T(8,128)(2,1)S(1)}, u32[]{:S(2)}, u32[]{:S(2)}) collective-permute-start(bf16[8,6144]{1,0:T(8,128)(2,1)S(1)} %norm_chunk.1.refs_0_), channel_id=1, source_target_pairs={{0,8},{1,9},{2,10},{3,11},{4,12},{5,13},{6,14},{7,15},{8,0},{9,1},... | collective-permute-start | bytes 294920 | tf_op jit(solution)/shard_map/ppermute | solution.py:77
  7.7 9.4 %collective-permute-start.2 = (bf16[8,6144]{1,0:T(8,128)(2,1)S(1)}, bf16[8,6144]{1,0:T(8,128)(2,1)S(1)}, u32[]{:S(2)}, u32[]{:S(2)}) collective-permute-start(bf16[8,6144]{1,0:T(8,128)(2,1)S(1)} %norm_chunk.1.refs_0_), channel_id=1, source_target_pairs={{0,12},{1,13},{2,14},{3,15},{4,8},{5,9},{6,10},{7,11},{8,4},{9,5},... | collective-permute-start | bytes 294920 | tf_op jit(solution)/shard_map/ppermute | solution.py:77
  7.7 9.9 %collective-permute-start.3 = (bf16[8,6144]{1,0:T(8,128)(2,1)S(1)}, bf16[8,6144]{1,0:T(8,128)(2,1)S(1)}, u32[]{:S(2)}, u32[]{:S(2)}) collective-permute-start(bf16[8,6144]{1,0:T(8,128)(2,1)S(1)} %norm_chunk.1.refs_0_), channel_id=1, source_target_pairs={{0,2},{1,3},{2,0},{3,1},{4,6},{5,7},{6,4},{7,5},{8,10},{9,11},{10,... | collective-permute-start | bytes 294920 | tf_op jit(solution)/shard_map/ppermute | solution.py:77
  9.4 12.7 %slice-start.2 = ((s8[4718592]{0:T(1024)(128)(4,1)}), s8[4194304]{0:T(1024)(128)(4,1)S(1)}, s32[]{:S(2)}) async-start(s8[4718592]{0:T(1024)(128)(4,1)} %bitcast.9), calls=%async_computation.3 | async-start | bytes 8388608
  9.4 12.6 %copy-start.6 = (bf16[640]{0:T(1024)(128)(2,1)S(1)}, bf16[640]{0:T(1024)(128)(2,1)}, u32[]{:S(2)}) copy-start(bf16[640]{0:T(1024)(128)(2,1)} %param.14) | copy-start | bytes 3844
  9.4 12.6 %copy-start.4 = (s32[6]{0:T(128)S(1)}, s32[6]{0:T(128)}, u32[]{:S(2)}) copy-start(s32[6]{0:T(128)} %len_ref.1) | copy-start | bytes 76
  9.4 12.7 %slice-start.3 = ((s8[4718592]{0:T(1024)(128)(4,1)}), s8[524288]{0:T(1024)(128)(4,1)S(1)}, s32[]{:S(2)}) async-start(s8[4718592]{0:T(1024)(128)(4,1)} %bitcast.9), calls=%async_computation.4 | async-start | bytes 1048576
  13.7 5.6 %collective-permute-start.4 = (bf16[8,6144]{1,0:T(8,128)(2,1)S(1)}, bf16[8,6144]{1,0:T(8,128)(2,1)S(1)}, u32[]{:S(2)}, u32[]{:S(2)}) collective-permute-start(bf16[8,6144]{1,0:T(8,128)(2,1)S(1)} %get-tuple-element.20.refs_1_), channel_id=1, source_target_pairs={{0,2},{1,3},{2,0},{3,1},{4,6},{5,7},{6,4},{7,5},{8,10},{9,11},{10,... | collective-permute-start | bytes 294920 | tf_op jit(solution)/shard_map/ppermute | solution.py:77
  15.5 4.9 %collective-permute-start.5 = (bf16[8,6144]{1,0:T(8,128)(2,1)S(1)}, bf16[8,6144]{1,0:T(8,128)(2,1)S(1)}, u32[]{:S(2)}, u32[]{:S(2)}) collective-permute-start(bf16[8,6144]{1,0:T(8,128)(2,1)S(1)} %collective-permute-done.1.refs_2_), channel_id=1, source_target_pairs={{0,2},{1,3},{2,0},{3,1},{4,6},{5,7},{6,4},{7,5},{8,10},{9,11},{10,... | collective-permute-start | bytes 294920 | tf_op jit(solution)/shard_map/ppermute | solution.py:77
  17.0 4.6 %collective-permute-start.6 = (bf16[8,6144]{1,0:T(8,128)(2,1)S(1)}, bf16[8,6144]{1,0:T(8,128)(2,1)S(1)}, u32[]{:S(2)}, u32[]{:S(2)}) collective-permute-start(bf16[8,6144]{1,0:T(8,128)(2,1)S(1)} %collective-permute-done.2.refs_3_), channel_id=1, source_target_pairs={{0,2},{1,3},{2,0},{3,1},{4,6},{5,7},{6,4},{7,5},{8,10},{9,11},{10,... | collective-permute-start | bytes 294920 | tf_op jit(solution)/shard_map/ppermute | solution.py:77
  21.7 3.0 %slice-start = ((s8[4718592]{0:T(1024)(128)(4,1)}), s8[4194304]{0:T(1024)(128)(4,1)S(1)}, s32[]{:S(2)}) async-start(s8[4718592]{0:T(1024)(128)(4,1)} %bitcast.7), calls=%async_computation.1 | async-start | bytes 8388608
  22.0 2.7 %collective-permute-start.7 = (bf16[8,64,1024]{2,1,0:T(8,128)(2,1)S(1)}, bf16[8,64,1024]{2,1,0:T(8,128)(2,1)S(1)}, u32[]{:S(2)}, u32[]{:S(2)}) collective-permute-start(bf16[8,64,1024]{2,1,0:T(8,128)(2,1)S(1)} %unpack.2.left), channel_id=1, source_target_pairs={{0,1},{1,0},{2,3},{3,2},{4,5},{5,4},{6,7},{7,6},{8,9},{9,8},{10,11... | collective-permute-start | bytes 3145736 | tf_op jit(solution)/shard_map/ppermute | solution.py:77
  22.1 2.6 %slice-start.1 = ((s8[4718592]{0:T(1024)(128)(4,1)}), s8[524288]{0:T(1024)(128)(4,1)S(1)}, s32[]{:S(2)}) async-start(s8[4718592]{0:T(1024)(128)(4,1)} %bitcast.7), calls=%async_computation.2 | async-start | bytes 1048576
  24.7 15.1 %copy-start.5 = (s32[6]{0:T(128)S(1)}, s32[6]{0:T(128)}, u32[]{:S(2)}) copy-start(s32[6]{0:T(128)} %ids_ref.1) | copy-start | bytes 76
  27.1 5.8 %collective-permute-start.10 = (bf16[24,640]{1,0:T(8,128)(2,1)S(1)}, bf16[24,640]{1,0:T(8,128)(2,1)S(1)}, u32[]{:S(2)}, u32[]{:S(2)}) collective-permute-start(bf16[24,640]{1,0:T(8,128)(2,1)S(1)} %get-tuple-element.28), channel_id=1, source_target_pairs={{0,12},{1,13},{2,14},{3,15},{4,8},{5,9},{6,10},{7,11},{8,4},{9,5},... | collective-permute-start | bytes 92168 | tf_op jit(solution)/shard_map/ppermute | solution.py:77
  30.5 4.2 %collective-permute-start.8 = (bf16[24,640]{1,0:T(8,128)(2,1)S(1)}, bf16[24,640]{1,0:T(8,128)(2,1)S(1)}, u32[]{:S(2)}, u32[]{:S(2)}) collective-permute-start(bf16[24,640]{1,0:T(8,128)(2,1)S(1)} %get-tuple-element.26), channel_id=1, source_target_pairs={{0,4},{1,5},{2,6},{3,7},{4,0},{5,1},{6,2},{7,3},{8,12},{9,13},{10,... | collective-permute-start | bytes 92168 | tf_op jit(solution)/shard_map/ppermute | solution.py:77
  30.5 4.8 %collective-permute-start.9 = (bf16[24,640]{1,0:T(8,128)(2,1)S(1)}, bf16[24,640]{1,0:T(8,128)(2,1)S(1)}, u32[]{:S(2)}, u32[]{:S(2)}) collective-permute-start(bf16[24,640]{1,0:T(8,128)(2,1)S(1)} %get-tuple-element.27), channel_id=1, source_target_pairs={{0,8},{1,9},{2,10},{3,11},{4,12},{5,13},{6,14},{7,15},{8,0},{9,1},... | collective-permute-start | bytes 92168 | tf_op jit(solution)/shard_map/ppermute | solution.py:77
  35.3 2.0 %collective-permute-start.11 = (bf16[24,640]{1,0:T(8,128)(2,1)S(1)}, bf16[24,640]{1,0:T(8,128)(2,1)S(1)}, u32[]{:S(2)}, u32[]{:S(2)}) collective-permute-start(bf16[24,640]{1,0:T(8,128)(2,1)S(1)} %get-tuple-element.30), channel_id=1, source_target_pairs={{0,1},{1,0},{2,3},{3,2},{4,5},{5,4},{6,7},{7,6},{8,9},{9,8},{10,11... | collective-permute-start | bytes 92168 | tf_op jit(solution)/shard_map/ppermute | solution.py:77
  35.4 4.2 %collective-permute-start.12 = (bf16[24,640]{1,0:T(8,128)(2,1)S(1)}, bf16[24,640]{1,0:T(8,128)(2,1)S(1)}, u32[]{:S(2)}, u32[]{:S(2)}) collective-permute-start(bf16[24,640]{1,0:T(8,128)(2,1)S(1)} %get-tuple-element.31), channel_id=1, source_target_pairs={{0,2},{1,3},{2,0},{3,1},{4,6},{5,7},{6,4},{7,5},{8,10},{9,11},{10,... | collective-permute-start | bytes 92168 | tf_op jit(solution)/shard_map/ppermute | solution.py:77
  36.2 3.6 %collective-permute-start.13 = (bf16[24,640]{1,0:T(8,128)(2,1)S(1)}, bf16[24,640]{1,0:T(8,128)(2,1)S(1)}, u32[]{:S(2)}, u32[]{:S(2)}) collective-permute-start(bf16[24,640]{1,0:T(8,128)(2,1)S(1)} %get-tuple-element.32), channel_id=1, source_target_pairs={{0,3},{1,2},{2,1},{3,0},{4,7},{5,6},{6,5},{7,4},{8,11},{9,10},{10,... | collective-permute-start | bytes 92168 | tf_op jit(solution)/shard_map/ppermute | solution.py:77
  44.5 18.9 %copy-start = (bf16[2,8192,16]{1,2,0:T(8,128)(2,1)S(1)}, bf16[2,8192,16]{1,2,0:T(8,128)(2,1)}, u32[]{:S(2)}) copy-start(bf16[2,8192,16]{1,2,0:T(8,128)(2,1)} %param.20) | copy-start | bytes 1572868
  44.5 5.5 %collective-permute-start.14 = (bf16[8,6272]{1,0:T(8,128)(2,1)S(1)}, bf16[8,6272]{1,0:T(8,128)(2,1)S(1)}, u32[]{:S(2)}, u32[]{:S(2)}) collective-permute-start(bf16[8,6272]{1,0:T(8,128)(2,1)S(1)} %attend.1.refs_0_), channel_id=1, source_target_pairs={{0,4},{1,5},{2,6},{3,7},{4,0},{5,1},{6,2},{7,3},{8,12},{9,13},{10,... | collective-permute-start | bytes 301064 | tf_op jit(solution)/shard_map/ppermute | solution.py:77
  46.6 10.0 %collective-permute-start.15 = (bf16[8,6272]{1,0:T(8,128)(2,1)S(1)}, bf16[8,6272]{1,0:T(8,128)(2,1)S(1)}, u32[]{:S(2)}, u32[]{:S(2)}) collective-permute-start(bf16[8,6272]{1,0:T(8,128)(2,1)S(1)} %attend.1.refs_0_), channel_id=1, source_target_pairs={{0,8},{1,9},{2,10},{3,11},{4,12},{5,13},{6,14},{7,15},{8,0},{9,1},... | collective-permute-start | bytes 301064 | tf_op jit(solution)/shard_map/ppermute | solution.py:77
  46.7 10.8 %collective-permute-start.16 = (bf16[8,6272]{1,0:T(8,128)(2,1)S(1)}, bf16[8,6272]{1,0:T(8,128)(2,1)S(1)}, u32[]{:S(2)}, u32[]{:S(2)}) collective-permute-start(bf16[8,6272]{1,0:T(8,128)(2,1)S(1)} %attend.1.refs_0_), channel_id=1, source_target_pairs={{0,12},{1,13},{2,14},{3,15},{4,8},{5,9},{6,10},{7,11},{8,4},{9,5},... | collective-permute-start | bytes 301064 | tf_op jit(solution)/shard_map/ppermute | solution.py:77
  49.0 9.5 %collective-permute-start.17 = (bf16[8,6272]{1,0:T(8,128)(2,1)S(1)}, bf16[8,6272]{1,0:T(8,128)(2,1)S(1)}, u32[]{:S(2)}, u32[]{:S(2)}) collective-permute-start(bf16[8,6272]{1,0:T(8,128)(2,1)S(1)} %attend.1.refs_0_), channel_id=1, source_target_pairs={{0,2},{1,3},{2,0},{3,1},{4,6},{5,7},{6,4},{7,5},{8,10},{9,11},{10,... | collective-permute-start | bytes 301064 | tf_op jit(solution)/shard_map/ppermute | solution.py:77
  53.5 5.1 %collective-permute-start.18 = (bf16[8,6272]{1,0:T(8,128)(2,1)S(1)}, bf16[8,6272]{1,0:T(8,128)(2,1)S(1)}, u32[]{:S(2)}, u32[]{:S(2)}) collective-permute-start(bf16[8,6272]{1,0:T(8,128)(2,1)S(1)} %get-tuple-element.33.refs_1_), channel_id=1, source_target_pairs={{0,2},{1,3},{2,0},{3,1},{4,6},{5,7},{6,4},{7,5},{8,10},{9,11},{10,... | collective-permute-start | bytes 301064 | tf_op jit(solution)/shard_map/ppermute | solution.py:77
  56.5 5.4 %collective-permute-start.19 = (bf16[8,6272]{1,0:T(8,128)(2,1)S(1)}, bf16[8,6272]{1,0:T(8,128)(2,1)S(1)}, u32[]{:S(2)}, u32[]{:S(2)}) collective-permute-start(bf16[8,6272]{1,0:T(8,128)(2,1)S(1)} %collective-permute-done.15.refs_2_), channel_id=1, source_target_pairs={{0,2},{1,3},{2,0},{3,1},{4,6},{5,7},{6,4},{7,5},{8,10},{9,11},{10,... | collective-permute-start | bytes 301064 | tf_op jit(solution)/shard_map/ppermute | solution.py:77
  57.5 5.5 %collective-permute-start.20 = (bf16[8,6272]{1,0:T(8,128)(2,1)S(1)}, bf16[8,6272]{1,0:T(8,128)(2,1)S(1)}, u32[]{:S(2)}, u32[]{:S(2)}) collective-permute-start(bf16[8,6272]{1,0:T(8,128)(2,1)S(1)} %collective-permute-done.16.refs_3_), channel_id=1, source_target_pairs={{0,2},{1,3},{2,0},{3,1},{4,6},{5,7},{6,4},{7,5},{8,10},{9,11},{10,... | collective-permute-start | bytes 301064 | tf_op jit(solution)/shard_map/ppermute | solution.py:77
  63.3 2.9 %collective-permute-start.21 = (bf16[9,64,1024]{2,1,0:T(8,128)(2,1)S(1)}, bf16[9,64,1024]{2,1,0:T(8,128)(2,1)S(1)}, u32[]{:S(2)}, u32[]{:S(2)}) collective-permute-start(bf16[9,64,1024]{2,1,0:T(8,128)(2,1)S(1)} %unpack.3.left.own), channel_id=1, source_target_pairs={{0,1},{1,0},{2,3},{3,2},{4,5},{5,4},{6,7},{7,6},{8,9},{9,8},{10,11... | collective-permute-start | bytes 3538952 | tf_op jit(solution)/shard_map/ppermute | solution.py:77
  67.1 1.9 %collective-permute-start.22 = (bf16[32,128]{1,0:T(8,128)(2,1)S(1)}, bf16[32,128]{1,0:T(8,128)(2,1)S(1)}, u32[]{:S(2)}, u32[]{:S(2)}) collective-permute-start(bf16[32,128]{1,0:T(8,128)(2,1)S(1)} %shrink.1.refs_0_), channel_id=1, source_target_pairs={{0,1},{1,0},{2,3},{3,2},{4,5},{5,4},{6,7},{7,6},{8,9},{9,8},{10,11... | collective-permute-start | bytes 24584 | tf_op jit(solution)/shard_map/ppermute | solution.py:77
  67.2 3.7 %collective-permute-start.23 = (bf16[32,128]{1,0:T(8,128)(2,1)S(1)}, bf16[32,128]{1,0:T(8,128)(2,1)S(1)}, u32[]{:S(2)}, u32[]{:S(2)}) collective-permute-start(bf16[32,128]{1,0:T(8,128)(2,1)S(1)} %shrink.1.refs_0_), channel_id=1, source_target_pairs={{0,2},{1,3},{2,0},{3,1},{4,6},{5,7},{6,4},{7,5},{8,10},{9,11},{10,... | collective-permute-start | bytes 24584 | tf_op jit(solution)/shard_map/ppermute | solution.py:77
  68.4 3.1 %collective-permute-start.24 = (bf16[32,128]{1,0:T(8,128)(2,1)S(1)}, bf16[32,128]{1,0:T(8,128)(2,1)S(1)}, u32[]{:S(2)}, u32[]{:S(2)}) collective-permute-start(bf16[32,128]{1,0:T(8,128)(2,1)S(1)} %shrink.1.refs_0_), channel_id=1, source_target_pairs={{0,3},{1,2},{2,1},{3,0},{4,7},{5,6},{6,5},{7,4},{8,11},{9,10},{10,... | collective-permute-start | bytes 24584 | tf_op jit(solution)/shard_map/ppermute | solution.py:77
  71.5 7.0 %copy-start.1 = (bf16[32,16,512]{2,1,0:T(8,128)(2,1)S(1)}, bf16[32,16,512]{2,1,0:T(8,128)(2,1)}, u32[]{:S(2)}) copy-start(bf16[32,16,512]{2,1,0:T(8,128)(2,1)} %param.21) | copy-start | bytes 1572868
  71.5 5.9 %collective-permute-start.25 = (bf16[128,128]{1,0:T(8,128)(2,1)S(1)}, bf16[128,128]{1,0:T(8,128)(2,1)S(1)}, u32[]{:S(2)}, u32[]{:S(2)}) collective-permute-start(bf16[128,128]{1,0:T(8,128)(2,1)S(1)} %join_coords.1.refs_0_), channel_id=1, source_target_pairs={{0,4},{1,5},{2,6},{3,7},{4,0},{5,1},{6,2},{7,3},{8,12},{9,13},{10,... | collective-permute-start | bytes 98312 | tf_op jit(solution)/shard_map/ppermute | solution.py:77
  72.1 5.4 %collective-permute-start.26 = (bf16[128,128]{1,0:T(8,128)(2,1)S(1)}, bf16[128,128]{1,0:T(8,128)(2,1)S(1)}, u32[]{:S(2)}, u32[]{:S(2)}) collective-permute-start(bf16[128,128]{1,0:T(8,128)(2,1)S(1)} %join_coords.1.refs_0_), channel_id=1, source_target_pairs={{0,8},{1,9},{2,10},{3,11},{4,12},{5,13},{6,14},{7,15},{8,0},{9,1},... | collective-permute-start | bytes 98312 | tf_op jit(solution)/shard_map/ppermute | solution.py:77
  72.8 5.7 %collective-permute-start.27 = (bf16[128,128]{1,0:T(8,128)(2,1)S(1)}, bf16[128,128]{1,0:T(8,128)(2,1)S(1)}, u32[]{:S(2)}, u32[]{:S(2)}) collective-permute-start(bf16[128,128]{1,0:T(8,128)(2,1)S(1)} %join_coords.1.refs_0_), channel_id=1, source_target_pairs={{0,12},{1,13},{2,14},{3,15},{4,8},{5,9},{6,10},{7,11},{8,4},{9,5},... | collective-permute-start | bytes 98312 | tf_op jit(solution)/shard_map/ppermute | solution.py:77

commit v9 on v8

--- a/solution.py
+++ b/solution.py
@@ -427,11 +427,12 @@
         score = jnp.concatenate(scores, axis=0) * scale
         own = jnp.concatenate(own, axis=0) * scale
         valid = lax.broadcasted_iota(jnp.int32, score.shape, 1) < len_ref[r]
-        top = jnp.maximum(jnp.max(jnp.where(valid, score, -1e30), axis=-1, keepdims=True), own)
-        expo = jnp.where(valid, jnp.exp(score - top), 0.0)
+        score = jnp.where(valid, score, -1e30)
+        top = jnp.maximum(jnp.max(score, axis=-1, keepdims=True), own)
+        expo = jnp.exp(score - top)
         expo_own = jnp.exp(own - top)
         total = jnp.sum(expo, axis=-1, keepdims=True) + expo_own
-        weight = (expo / total).astype(jnp.bfloat16)
+        weight = (expo * (1.0 / total)).astype(jnp.bfloat16)
         weight_own = (expo_own / total).astype(jnp.bfloat16).astype(jnp.float32)
         for k in range(0, KVH, 2):
             both = jnp.dot(

time: 92.2 us -> 92.3 us (level)
  no operation moved by 1% of the time
where the time goes in v9:
time: 92.3 us; the launch traced here: 92 us
  starting transfers between devices  31.2 us (34%)
  Pallas kernels  23.1 us (25%)
  waiting for transfers between devices  22.4 us (24%)
  blocking collectives  12.5 us (14%)
  local copies, waits for them, and re-layouts  2.32 us (3%)
    ppermute x28, starting transfers between devices, move(): lax.ppermute(x, 'tensor', [(d, place(devices, d, k, m, c)) for d in range...  31.2 us
    ppermute x28, waiting for transfers between devices, move(): lax.ppermute(x, 'tensor', [(d, place(devices, d, k, m, c)) for d in range...  22.4 us
    all_to_all x1, blocking collectives, per_device(): lax.all_to_all(projected, 'tensor', split_axis=0, concat_axis=0, tiled=True)  12.5 us
    pallas_call x2, Pallas kernels, hold(): pl.pallas_call(functools.partial(hold_kernel, len(arrays)), out_shape=(ja...  7.7 us
    pallas_call x1, Pallas kernels, attend(): pl.pallas_call(functools.partial(attend_kernel, devices, rows), out_shape...  4.7 us
    pallas_call x1, Pallas kernels, qkv_own(): pl.pallas_call(qkv_own_kernel, out_shape=(jax.ShapeDtypeStruct((rows, col...  2.34 us
    pallas_call x1, Pallas kernels, qkv_project(): pl.pallas_call(functools.partial(qkv_kernel, devices, rows), out_shape=[p...  2.34 us
    unnamed x23, local copies, waits for them, and re-layouts  2.32 us
  transfers between devices with their start and end apart: 28, of which 17 were waited for; matrix products, arithmetic and copies ran while one was open for 0% of the time, Pallas kernels for 15%

profile of v9, /device:TPU:0, one launch (start us, length us, event | category | flops | bytes accessed | tf_op | source)
XLA Modules:
  0.0 92.0 jit_solution(3402235892947637121)
XLA Ops:
  0.0 0.9 copy-done.2
  0.9 0.7 copy-done.3
  1.6 0.4 norm_chunk.1.refs_0_
  2.0 3.1 %collective-permute-start = (bf16[8,6144]{1,0:T(8,128)(2,1)S(1)}, bf16[8,6144]{1,0:T(8,128)(2,1)S(1)}, u32[]{:S(2)}, u32[]{:S(2)}) collective-permute-start(bf16[8,6144]{1,0:T(8,128)(2,1)S(1)} %norm_chunk.1.refs_0_), channel_id=1, source_target_pairs={{0,4},{1,5},{2,6},{3,7},{4,0},{5,1},{6,2},{7,3},{8,12},{9,13},{10,... | collective-permute-start | bytes 294920 | tf_op jit(solution)/shard_map/ppermute | solution.py:77
  5.1 2.6 %collective-permute-start.1 = (bf16[8,6144]{1,0:T(8,128)(2,1)S(1)}, bf16[8,6144]{1,0:T(8,128)(2,1)S(1)}, u32[]{:S(2)}, u32[]{:S(2)}) collective-permute-start(bf16[8,6144]{1,0:T(8,128)(2,1)S(1)} %norm_chunk.1.refs_0_), channel_id=1, source_target_pairs={{0,8},{1,9},{2,10},{3,11},{4,12},{5,13},{6,14},{7,15},{8,0},{9,1},... | collective-permute-start | bytes 294920 | tf_op jit(solution)/shard_map/ppermute | solution.py:77
  7.7 1.7 %collective-permute-start.3 = (bf16[8,6144]{1,0:T(8,128)(2,1)S(1)}, bf16[8,6144]{1,0:T(8,128)(2,1)S(1)}, u32[]{:S(2)}, u32[]{:S(2)}) collective-permute-start(bf16[8,6144]{1,0:T(8,128)(2,1)S(1)} %norm_chunk.1.refs_0_), channel_id=1, source_target_pairs={{0,2},{1,3},{2,0},{3,1},{4,6},{5,7},{6,4},{7,5},{8,10},{9,11},{10,... | collective-permute-start | bytes 294920 | tf_op jit(solution)/shard_map/ppermute | solution.py:77
  9.5 4.2 %hold_qkv.1 = (bf16[8192,640]{1,0:T(8,128)(2,1)S(1)}, bf16[8,6144]{1,0:T(8,128)(2,1)S(1)}) custom-call(bf16[8,6144]{1,0:T(8,128)(2,1)S(1)} %collective-permute-done.refs_0_, s32[1]{0:T(128)} %bitcast.refs_1_.me_ref, bf16[8192,640]{1,0:T(8,128)(2,1)} %refs_2_.1), custom_call_target="tpu_custom_call", output_to_operand_aliasing={{1}: (0, {})} | custom-call | bytes 20971520 | tf_op jit(solution)/shard_map/hold_qkv/pallas_call | solution.py:256
  13.7 0.4 collective-permute-start.4
  14.0 1.5 %collective-permute-done.1.refs_2_ = bf16[8,6144]{1,0:T(8,128)(2,1)S(1)} collective-permute-done((bf16[8,6144]{1,0:T(8,128)(2,1)S(1)}, bf16[8,6144]{1,0:T(8,128)(2,1)S(1)}, u32[]{:S(2)}, u32[]{:S(2)}) %collective-permute-start.1) | collective-permute-done | bytes 98336 | tf_op jit(solution)/shard_map/ppermute | solution.py:77
  15.5 1.5 %collective-permute-start.5 = (bf16[8,6144]{1,0:T(8,128)(2,1)S(1)}, bf16[8,6144]{1,0:T(8,128)(2,1)S(1)}, u32[]{:S(2)}, u32[]{:S(2)}) collective-permute-start(bf16[8,6144]{1,0:T(8,128)(2,1)S(1)} %collective-permute-done.1.refs_2_), channel_id=1, source_target_pairs={{0,2},{1,3},{2,0},{3,1},{4,6},{5,7},{6,4},{7,5},{8,10},{9,11},{10,... | collective-permute-start | bytes 294920 | tf_op jit(solution)/shard_map/ppermute | solution.py:77
  17.0 0.5 collective-permute-start.6
  17.6 1.8 %collective-permute-done.4.refs_5_ = bf16[8,6144]{1,0:T(8,128)(2,1)S(1)} collective-permute-done((bf16[8,6144]{1,0:T(8,128)(2,1)S(1)}, bf16[8,6144]{1,0:T(8,128)(2,1)S(1)}, u32[]{:S(2)}, u32[]{:S(2)}) %collective-permute-start.4) | collective-permute-done | bytes 98336 | tf_op jit(solution)/shard_map/ppermute | solution.py:77
  19.3 1.1 %collective-permute-done.5.refs_6_ = bf16[8,6144]{1,0:T(8,128)(2,1)S(1)} collective-permute-done((bf16[8,6144]{1,0:T(8,128)(2,1)S(1)}, bf16[8,6144]{1,0:T(8,128)(2,1)S(1)}, u32[]{:S(2)}, u32[]{:S(2)}) %collective-permute-start.5) | collective-permute-done | bytes 98336 | tf_op jit(solution)/shard_map/ppermute | solution.py:77
  20.4 1.3 %collective-permute-done.6.refs_7_ = bf16[8,6144]{1,0:T(8,128)(2,1)S(1)} collective-permute-done((bf16[8,6144]{1,0:T(8,128)(2,1)S(1)}, bf16[8,6144]{1,0:T(8,128)(2,1)S(1)}, u32[]{:S(2)}, u32[]{:S(2)}) %collective-permute-start.6) | collective-permute-done | bytes 98336 | tf_op jit(solution)/shard_map/ppermute | solution.py:77
  21.7 0.3 unpack.2.left
  22.0 0.1 collective-permute-start.7
  22.1 0.0 slice-start.1
  22.1 2.3 %qkv_own.1 = (f32[64,640]{1,0:T(8,128)S(1)}, bf16[6,384,1024]{2,1,0:T(8,128)(2,1)S(1)}) custom-call(bf16[8,64,1024]{2,1,0:T(8,128)(2,1)S(1)} %unpack.2.left, bf16[8192,640]{1,0:T(8,128)(2,1)S(1)} %get-tuple-element.21.held, bf16[6,384,1024]{2,1,0:T(8,128)(2,1)S(1)} %bitcast.10), custom_call_target="tpu_custom_call" | custom-call | flops 671088640 | bytes 10485760 | tf_op jit(solution)/shard_map/qkv_own/pallas_call | solution.py:313
  24.5 0.2 collective-permute-done.7.left
  24.7 2.3 %qkv_project.1 = (bf16[24,640]{1,0:T(8,128)(2,1)S(1)}, bf16[24,640]{1,0:T(8,128)(2,1)S(1)}, bf16[24,640]{1,0:T(8,128)(2,1)S(1)}, bf16[24,640]{1,0:T(8,128)(2,1)S(1)}, bf16[6,384,1024]{2,1,0:T(8,128)(2,1)S(1)}) custom-call(bf16[1,640]{1,0:T(2,128)(2,1)S(1)} %reshape.24.bias_ref, f32[64,640]{1,0:T(8,128)S(1)} %get-tuple-element.23.own_ref, ...), custom_call_target="tpu_custom_call" | custom-call | tf_op jit(solution)/shard_map/qkv_project/pallas_call | solution.py:353
  27.1 3.4 %collective-permute-start.10 = (bf16[24,640]{1,0:T(8,128)(2,1)S(1)}, bf16[24,640]{1,0:T(8,128)(2,1)S(1)}, u32[]{:S(2)}, u32[]{:S(2)}) collective-permute-start(bf16[24,640]{1,0:T(8,128)(2,1)S(1)} %get-tuple-element.28), channel_id=1, source_target_pairs={{0,12},{1,13},{2,14},{3,15},{4,8},{5,9},{6,10},{7,11},{8,4},{9,5},... | collective-permute-start | bytes 92168 | tf_op jit(solution)/shard_map/ppermute | solution.py:77
  30.5 1.1 %collective-permute-start.9 = (bf16[24,640]{1,0:T(8,128)(2,1)S(1)}, bf16[24,640]{1,0:T(8,128)(2,1)S(1)}, u32[]{:S(2)}, u32[]{:S(2)}) collective-permute-start(bf16[24,640]{1,0:T(8,128)(2,1)S(1)} %get-tuple-element.27), channel_id=1, source_target_pairs={{0,8},{1,9},{2,10},{3,11},{4,12},{5,13},{6,14},{7,15},{8,0},{9,1},... | collective-permute-start | bytes 92168 | tf_op jit(solution)/shard_map/ppermute | solution.py:77
  31.5 0.1 fusion
  31.6 1.2 %collective-permute-done.10.refs_3_ = bf16[24,640]{1,0:T(8,128)(2,1)S(1)} collective-permute-done((bf16[24,640]{1,0:T(8,128)(2,1)S(1)}, bf16[24,640]{1,0:T(8,128)(2,1)S(1)}, u32[]{:S(2)}, u32[]{:S(2)}) %collective-permute-start.10) | collective-permute-done | bytes 30752 | tf_op jit(solution)/shard_map/ppermute | solution.py:77
  32.8 1.8 %collective-permute-done.8.refs_1_ = bf16[24,640]{1,0:T(8,128)(2,1)S(1)} collective-permute-done((bf16[24,640]{1,0:T(8,128)(2,1)S(1)}, bf16[24,640]{1,0:T(8,128)(2,1)S(1)}, u32[]{:S(2)}, u32[]{:S(2)}) %collective-permute-start.8) | collective-permute-done | bytes 30752 | tf_op jit(solution)/shard_map/ppermute | solution.py:77
  34.6 0.6 collective-permute-done.9.refs_2_
  35.3 0.1 turn.1
  35.3 0.1 collective-permute-start.11
  35.4 0.8 collective-permute-start.12
  36.2 1.1 %collective-permute-start.13 = (bf16[24,640]{1,0:T(8,128)(2,1)S(1)}, bf16[24,640]{1,0:T(8,128)(2,1)S(1)}, u32[]{:S(2)}, u32[]{:S(2)}) collective-permute-start(bf16[24,640]{1,0:T(8,128)(2,1)S(1)} %get-tuple-element.32), channel_id=1, source_target_pairs={{0,3},{1,2},{2,1},{3,0},{4,7},{5,6},{6,5},{7,4},{8,11},{9,10},{10,... | collective-permute-start | bytes 92168 | tf_op jit(solution)/shard_map/ppermute | solution.py:77
  37.3 0.1 pad_maximum_fusion
  37.4 2.2 %collective-permute-done.12.refs_2_ = bf16[24,640]{1,0:T(8,128)(2,1)S(1)} collective-permute-done((bf16[24,640]{1,0:T(8,128)(2,1)S(1)}, bf16[24,640]{1,0:T(8,128)(2,1)S(1)}, u32[]{:S(2)}, u32[]{:S(2)}) %collective-permute-start.12) | collective-permute-done | bytes 30752 | tf_op jit(solution)/shard_map/ppermute | solution.py:77
  39.6 0.2 collective-permute-done.13.refs_3_
  39.8 4.7 %attend.1.refs_0_ = bf16[8,6272]{1,0:T(8,128)(2,1)S(1)} custom-call(s32[1]{0:T(128)} %bitcast.refs_1_.me_ref, s32[6]{0:T(128)S(1)} %copy-done.4, s32[6]{0:T(128)S(1)} %copy-done.5, f32[6,128]{1,0:T(8,128)S(1)} %get-tuple-element.38.cos_ref, f32[6,128]{1,0:T(8,128)S(1)} %get-tuple-element.39.sin_ref, bf16[6,384,1024]{2,1,0:T(8,128)(2,1)S(1)} %get-tuple-element.22.keys, ...), custom_call_target="tpu_custom_call" | custom-call | tf_op jit(solution)/shard_map/attend/pallas_call | solution.py:463
  44.5 2.1 %collective-permute-start.14 = (bf16[8,6272]{1,0:T(8,128)(2,1)S(1)}, bf16[8,6272]{1,0:T(8,128)(2,1)S(1)}, u32[]{:S(2)}, u32[]{:S(2)}) collective-permute-start(bf16[8,6272]{1,0:T(8,128)(2,1)S(1)} %attend.1.refs_0_), channel_id=1, source_target_pairs={{0,4},{1,5},{2,6},{3,7},{4,0},{5,1},{6,2},{7,3},{8,12},{9,13},{10,... | collective-permute-start | bytes 301064 | tf_op jit(solution)/shard_map/ppermute | solution.py:77
  46.6 0.1 collective-permute-start.15
  46.7 2.3 %collective-permute-start.16 = (bf16[8,6272]{1,0:T(8,128)(2,1)S(1)}, bf16[8,6272]{1,0:T(8,128)(2,1)S(1)}, u32[]{:S(2)}, u32[]{:S(2)}) collective-permute-start(bf16[8,6272]{1,0:T(8,128)(2,1)S(1)} %attend.1.refs_0_), channel_id=1, source_target_pairs={{0,12},{1,13},{2,14},{3,15},{4,8},{5,9},{6,10},{7,11},{8,4},{9,5},... | collective-permute-start | bytes 301064 | tf_op jit(solution)/shard_map/ppermute | solution.py:77
  49.1 1.0 %collective-permute-start.17 = (bf16[8,6272]{1,0:T(8,128)(2,1)S(1)}, bf16[8,6272]{1,0:T(8,128)(2,1)S(1)}, u32[]{:S(2)}, u32[]{:S(2)}) collective-permute-start(bf16[8,6272]{1,0:T(8,128)(2,1)S(1)} %attend.1.refs_0_), channel_id=1, source_target_pairs={{0,2},{1,3},{2,0},{3,1},{4,6},{5,7},{6,4},{7,5},{8,10},{9,11},{10,... | collective-permute-start | bytes 301064 | tf_op jit(solution)/shard_map/ppermute | solution.py:77
  50.1 3.5 %hold_output.1 = (bf16[8192,512]{1,0:T(8,128)(2,1)S(1)}, bf16[8,6272]{1,0:T(8,128)(2,1)S(1)}) custom-call(bf16[8,6272]{1,0:T(8,128)(2,1)S(1)} %collective-permute-done.14.refs_0_, bf16[8192,512]{1,0:T(8,128)(2,1)} %refs_1_.1), custom_call_target="tpu_custom_call", output_to_operand_aliasing={{1}: (0, {})} | custom-call | bytes 16777216 | tf_op jit(solution)/shard_map/hold_output/pallas_call | solution.py:256
  53.6 1.1 %collective-permute-start.18 = (bf16[8,6272]{1,0:T(8,128)(2,1)S(1)}, bf16[8,6272]{1,0:T(8,128)(2,1)S(1)}, u32[]{:S(2)}, u32[]{:S(2)}) collective-permute-start(bf16[8,6272]{1,0:T(8,128)(2,1)S(1)} %get-tuple-element.33.refs_1_), channel_id=1, source_target_pairs={{0,2},{1,3},{2,0},{3,1},{4,6},{5,7},{6,4},{7,5},{8,10},{9,11},{10,... | collective-permute-start | bytes 301064 | tf_op jit(solution)/shard_map/ppermute | solution.py:77
  54.6 1.9 %collective-permute-done.15.refs_2_ = bf16[8,6272]{1,0:T(8,128)(2,1)S(1)} collective-permute-done((bf16[8,6272]{1,0:T(8,128)(2,1)S(1)}, bf16[8,6272]{1,0:T(8,128)(2,1)S(1)}, u32[]{:S(2)}, u32[]{:S(2)}) %collective-permute-start.15) | collective-permute-done | bytes 100384 | tf_op jit(solution)/shard_map/ppermute | solution.py:77
  56.6 1.0 %collective-permute-start.19 = (bf16[8,6272]{1,0:T(8,128)(2,1)S(1)}, bf16[8,6272]{1,0:T(8,128)(2,1)S(1)}, u32[]{:S(2)}, u32[]{:S(2)}) collective-permute-start(bf16[8,6272]{1,0:T(8,128)(2,1)S(1)} %collective-permute-done.15.refs_2_), channel_id=1, source_target_pairs={{0,2},{1,3},{2,0},{3,1},{4,6},{5,7},{6,4},{7,5},{8,10},{9,11},{10,... | collective-permute-start | bytes 301064 | tf_op jit(solution)/shard_map/ppermute | solution.py:77
  57.6 1.0 %collective-permute-start.20 = (bf16[8,6272]{1,0:T(8,128)(2,1)S(1)}, bf16[8,6272]{1,0:T(8,128)(2,1)S(1)}, u32[]{:S(2)}, u32[]{:S(2)}) collective-permute-start(bf16[8,6272]{1,0:T(8,128)(2,1)S(1)} %collective-permute-done.16.refs_3_), channel_id=1, source_target_pairs={{0,2},{1,3},{2,0},{3,1},{4,6},{5,7},{6,4},{7,5},{8,10},{9,11},{10,... | collective-permute-start | bytes 301064 | tf_op jit(solution)/shard_map/ppermute | solution.py:77
  58.6 3.3 %collective-permute-done.19.refs_6_ = bf16[8,6272]{1,0:T(8,128)(2,1)S(1)} collective-permute-done((bf16[8,6272]{1,0:T(8,128)(2,1)S(1)}, bf16[8,6272]{1,0:T(8,128)(2,1)S(1)}, u32[]{:S(2)}, u32[]{:S(2)}) %collective-permute-start.19) | collective-permute-done | bytes 100384 | tf_op jit(solution)/shard_map/ppermute | solution.py:77
  62.0 1.1 %collective-permute-done.20.refs_7_ = bf16[8,6272]{1,0:T(8,128)(2,1)S(1)} collective-permute-done((bf16[8,6272]{1,0:T(8,128)(2,1)S(1)}, bf16[8,6272]{1,0:T(8,128)(2,1)S(1)}, u32[]{:S(2)}, u32[]{:S(2)}) %collective-permute-start.20) | collective-permute-done | bytes 100384 | tf_op jit(solution)/shard_map/ppermute | solution.py:77
  63.0 0.3 unpack.3.left.own
  63.4 0.1 collective-permute-start.21
  63.4 0.6 shrink_own.1.own_part
  64.1 1.6 %base_own.1.own_ref.after = f32[64,512]{1,0:T(8,128)S(1)} custom-call(bf16[9,64,1024]{2,1,0:T(8,128)(2,1)S(1)} %unpack.3.left.own, bf16[8192,512]{1,0:T(8,128)(2,1)S(1)} %get-tuple-element.34.held), custom_call_target="tpu_custom_call" | custom-call | flops 536870912 | bytes 8388608 | tf_op jit(solution)/shard_map/base_own/pallas_call | solution.py:283
  65.7 0.6 collective-permute-done.21.left.other
  66.3 0.9 shrink.1.refs_0_
  67.1 0.2 collective-permute-start.22
  67.3 1.2 %collective-permute-start.23 = (bf16[32,128]{1,0:T(8,128)(2,1)S(1)}, bf16[32,128]{1,0:T(8,128)(2,1)S(1)}, u32[]{:S(2)}, u32[]{:S(2)}) collective-permute-start(bf16[32,128]{1,0:T(8,128)(2,1)S(1)} %shrink.1.refs_0_), channel_id=1, source_target_pairs={{0,2},{1,3},{2,0},{3,1},{4,6},{5,7},{6,4},{7,5},{8,10},{9,11},{10,... | collective-permute-start | bytes 24584 | tf_op jit(solution)/shard_map/ppermute | solution.py:77
  68.4 0.6 collective-permute-start.24
  69.0 1.9 %collective-permute-done.23.refs_2_ = bf16[32,128]{1,0:T(8,128)(2,1)S(1)} collective-permute-done((bf16[32,128]{1,0:T(8,128)(2,1)S(1)}, bf16[32,128]{1,0:T(8,128)(2,1)S(1)}, u32[]{:S(2)}, u32[]{:S(2)}) %collective-permute-start.23) | collective-permute-done | bytes 8224 | tf_op jit(solution)/shard_map/ppermute | solution.py:77
  70.9 0.6 collective-permute-done.24.refs_3_
  71.5 0.6 collective-permute-start.25
  72.1 0.7 collective-permute-start.26
  72.8 3.1 %collective-permute-start.27 = (bf16[128,128]{1,0:T(8,128)(2,1)S(1)}, bf16[128,128]{1,0:T(8,128)(2,1)S(1)}, u32[]{:S(2)}, u32[]{:S(2)}) collective-permute-start(bf16[128,128]{1,0:T(8,128)(2,1)S(1)} %join_coords.1.refs_0_), channel_id=1, source_target_pairs={{0,12},{1,13},{2,14},{3,15},{4,8},{5,9},{6,10},{7,11},{8,4},{9,5},... | collective-permute-start | bytes 98312 | tf_op jit(solution)/shard_map/ppermute | solution.py:77
  75.9 1.5 %base_project.1.base_ref = f32[128,512]{1,0:T(8,128)S(1)} custom-call(s32[1]{0:T(128)} %bitcast.refs_1_.me_ref, f32[64,512]{1,0:T(8,128)S(1)} %base_own.1.own_ref.after, bf16[9,64,1024]{2,1,0:T(8,128)(2,1)S(1)} %collective-permute-done.21.left.other, bf16[8192,512]{1,0:T(8,128)(2,1)S(1)} %get-tuple-element.34.held), custom_call_target="tpu_custom_call" | custom-call | flops 536870912 | bytes 8388608 | tf_op jit(solution)/shard_map/base_project/pallas_call | solution.py:577
  77.5 1.0 %collective-permute-done.27.refs_3_ = bf16[128,128]{1,0:T(8,128)(2,1)S(1)} collective-permute-done((bf16[128,128]{1,0:T(8,128)(2,1)S(1)}, bf16[128,128]{1,0:T(8,128)(2,1)S(1)}, u32[]{:S(2)}, u32[]{:S(2)}) %collective-permute-start.27) | collective-permute-done | bytes 32800 | tf_op jit(solution)/shard_map/ppermute | solution.py:77
  78.5 0.3 add_delta.1
  78.8 12.5 %all_to_all.5 = bf16[16,6,512]{2,1,0:T(8,128)(2,1)S(1)} all-to-all(bf16[16,6,512]{2,1,0:T(8,128)(2,1)S(1)} %add_delta.1), channel_id=1, replica_groups=mesh['group'=2,'tensor'=16] {'tensor'}, dimensions={0} | all-to-all | bytes 196608 | tf_op jit(solution)/shard_map/all_to_all | solution.py:671
  91.3 0.7 copy.17
  (38 shorter events, 0.1 us)
Async XLA Ops:
  0.0 0.9 copy-start.2
  0.9 0.7 copy-start.3
  2.0 7.4 %collective-permute-start = (bf16[8,6144]{1,0:T(8,128)(2,1)S(1)}, bf16[8,6144]{1,0:T(8,128)(2,1)S(1)}, u32[]{:S(2)}, u32[]{:S(2)}) collective-permute-start(bf16[8,6144]{1,0:T(8,128)(2,1)S(1)} %norm_chunk.1.refs_0_), channel_id=1, source_target_pairs={{0,4},{1,5},{2,6},{3,7},{4,0},{5,1},{6,2},{7,3},{8,12},{9,13},{10,... | collective-permute-start | bytes 294920 | tf_op jit(solution)/shard_map/ppermute | solution.py:77
  5.1 10.4 %collective-permute-start.1 = (bf16[8,6144]{1,0:T(8,128)(2,1)S(1)}, bf16[8,6144]{1,0:T(8,128)(2,1)S(1)}, u32[]{:S(2)}, u32[]{:S(2)}) collective-permute-start(bf16[8,6144]{1,0:T(8,128)(2,1)S(1)} %norm_chunk.1.refs_0_), channel_id=1, source_target_pairs={{0,8},{1,9},{2,10},{3,11},{4,12},{5,13},{6,14},{7,15},{8,0},{9,1},... | collective-permute-start | bytes 294920 | tf_op jit(solution)/shard_map/ppermute | solution.py:77
  7.7 9.4 %collective-permute-start.2 = (bf16[8,6144]{1,0:T(8,128)(2,1)S(1)}, bf16[8,6144]{1,0:T(8,128)(2,1)S(1)}, u32[]{:S(2)}, u32[]{:S(2)}) collective-permute-start(bf16[8,6144]{1,0:T(8,128)(2,1)S(1)} %norm_chunk.1.refs_0_), channel_id=1, source_target_pairs={{0,12},{1,13},{2,14},{3,15},{4,8},{5,9},{6,10},{7,11},{8,4},{9,5},... | collective-permute-start | bytes 294920 | tf_op jit(solution)/shard_map/ppermute | solution.py:77
  7.7 9.9 %collective-permute-start.3 = (bf16[8,6144]{1,0:T(8,128)(2,1)S(1)}, bf16[8,6144]{1,0:T(8,128)(2,1)S(1)}, u32[]{:S(2)}, u32[]{:S(2)}) collective-permute-start(bf16[8,6144]{1,0:T(8,128)(2,1)S(1)} %norm_chunk.1.refs_0_), channel_id=1, source_target_pairs={{0,2},{1,3},{2,0},{3,1},{4,6},{5,7},{6,4},{7,5},{8,10},{9,11},{10,... | collective-permute-start | bytes 294920 | tf_op jit(solution)/shard_map/ppermute | solution.py:77
  9.4 12.7 %slice-start.2 = ((s8[4718592]{0:T(1024)(128)(4,1)}), s8[4194304]{0:T(1024)(128)(4,1)S(1)}, s32[]{:S(2)}) async-start(s8[4718592]{0:T(1024)(128)(4,1)} %bitcast.9), calls=%async_computation.3 | async-start | bytes 8388608
  9.4 12.6 %copy-start.6 = (bf16[640]{0:T(1024)(128)(2,1)S(1)}, bf16[640]{0:T(1024)(128)(2,1)}, u32[]{:S(2)}) copy-start(bf16[640]{0:T(1024)(128)(2,1)} %param.14) | copy-start | bytes 3844
  9.4 12.6 %copy-start.4 = (s32[6]{0:T(128)S(1)}, s32[6]{0:T(128)}, u32[]{:S(2)}) copy-start(s32[6]{0:T(128)} %len_ref.1) | copy-start | bytes 76
  9.4 12.7 %slice-start.3 = ((s8[4718592]{0:T(1024)(128)(4,1)}), s8[524288]{0:T(1024)(128)(4,1)S(1)}, s32[]{:S(2)}) async-start(s8[4718592]{0:T(1024)(128)(4,1)} %bitcast.9), calls=%async_computation.4 | async-start | bytes 1048576
  13.7 5.6 %collective-permute-start.4 = (bf16[8,6144]{1,0:T(8,128)(2,1)S(1)}, bf16[8,6144]{1,0:T(8,128)(2,1)S(1)}, u32[]{:S(2)}, u32[]{:S(2)}) collective-permute-start(bf16[8,6144]{1,0:T(8,128)(2,1)S(1)} %get-tuple-element.20.refs_1_), channel_id=1, source_target_pairs={{0,2},{1,3},{2,0},{3,1},{4,6},{5,7},{6,4},{7,5},{8,10},{9,11},{10,... | collective-permute-start | bytes 294920 | tf_op jit(solution)/shard_map/ppermute | solution.py:77
  15.5 4.9 %collective-permute-start.5 = (bf16[8,6144]{1,0:T(8,128)(2,1)S(1)}, bf16[8,6144]{1,0:T(8,128)(2,1)S(1)}, u32[]{:S(2)}, u32[]{:S(2)}) collective-permute-start(bf16[8,6144]{1,0:T(8,128)(2,1)S(1)} %collective-permute-done.1.refs_2_), channel_id=1, source_target_pairs={{0,2},{1,3},{2,0},{3,1},{4,6},{5,7},{6,4},{7,5},{8,10},{9,11},{10,... | collective-permute-start | bytes 294920 | tf_op jit(solution)/shard_map/ppermute | solution.py:77
  17.0 4.6 %collective-permute-start.6 = (bf16[8,6144]{1,0:T(8,128)(2,1)S(1)}, bf16[8,6144]{1,0:T(8,128)(2,1)S(1)}, u32[]{:S(2)}, u32[]{:S(2)}) collective-permute-start(bf16[8,6144]{1,0:T(8,128)(2,1)S(1)} %collective-permute-done.2.refs_3_), channel_id=1, source_target_pairs={{0,2},{1,3},{2,0},{3,1},{4,6},{5,7},{6,4},{7,5},{8,10},{9,11},{10,... | collective-permute-start | bytes 294920 | tf_op jit(solution)/shard_map/ppermute | solution.py:77
  21.7 3.0 %slice-start = ((s8[4718592]{0:T(1024)(128)(4,1)}), s8[4194304]{0:T(1024)(128)(4,1)S(1)}, s32[]{:S(2)}) async-start(s8[4718592]{0:T(1024)(128)(4,1)} %bitcast.7), calls=%async_computation.1 | async-start | bytes 8388608
  22.0 2.7 %collective-permute-start.7 = (bf16[8,64,1024]{2,1,0:T(8,128)(2,1)S(1)}, bf16[8,64,1024]{2,1,0:T(8,128)(2,1)S(1)}, u32[]{:S(2)}, u32[]{:S(2)}) collective-permute-start(bf16[8,64,1024]{2,1,0:T(8,128)(2,1)S(1)} %unpack.2.left), channel_id=1, source_target_pairs={{0,1},{1,0},{2,3},{3,2},{4,5},{5,4},{6,7},{7,6},{8,9},{9,8},{10,11... | collective-permute-start | bytes 3145736 | tf_op jit(solution)/shard_map/ppermute | solution.py:77
  22.1 2.6 %slice-start.1 = ((s8[4718592]{0:T(1024)(128)(4,1)}), s8[524288]{0:T(1024)(128)(4,1)S(1)}, s32[]{:S(2)}) async-start(s8[4718592]{0:T(1024)(128)(4,1)} %bitcast.7), calls=%async_computation.2 | async-start | bytes 1048576
  24.7 15.1 %copy-start.5 = (s32[6]{0:T(128)S(1)}, s32[6]{0:T(128)}, u32[]{:S(2)}) copy-start(s32[6]{0:T(128)} %ids_ref.1) | copy-start | bytes 76
  27.1 5.8 %collective-permute-start.10 = (bf16[24,640]{1,0:T(8,128)(2,1)S(1)}, bf16[24,640]{1,0:T(8,128)(2,1)S(1)}, u32[]{:S(2)}, u32[]{:S(2)}) collective-permute-start(bf16[24,640]{1,0:T(8,128)(2,1)S(1)} %get-tuple-element.28), channel_id=1, source_target_pairs={{0,12},{1,13},{2,14},{3,15},{4,8},{5,9},{6,10},{7,11},{8,4},{9,5},... | collective-permute-start | bytes 92168 | tf_op jit(solution)/shard_map/ppermute | solution.py:77
  30.5 4.2 %collective-permute-start.8 = (bf16[24,640]{1,0:T(8,128)(2,1)S(1)}, bf16[24,640]{1,0:T(8,128)(2,1)S(1)}, u32[]{:S(2)}, u32[]{:S(2)}) collective-permute-start(bf16[24,640]{1,0:T(8,128)(2,1)S(1)} %get-tuple-element.26), channel_id=1, source_target_pairs={{0,4},{1,5},{2,6},{3,7},{4,0},{5,1},{6,2},{7,3},{8,12},{9,13},{10,... | collective-permute-start | bytes 92168 | tf_op jit(solution)/shard_map/ppermute | solution.py:77
  30.5 4.8 %collective-permute-start.9 = (bf16[24,640]{1,0:T(8,128)(2,1)S(1)}, bf16[24,640]{1,0:T(8,128)(2,1)S(1)}, u32[]{:S(2)}, u32[]{:S(2)}) collective-permute-start(bf16[24,640]{1,0:T(8,128)(2,1)S(1)} %get-tuple-element.27), channel_id=1, source_target_pairs={{0,8},{1,9},{2,10},{3,11},{4,12},{5,13},{6,14},{7,15},{8,0},{9,1},... | collective-permute-start | bytes 92168 | tf_op jit(solution)/shard_map/ppermute | solution.py:77
  35.3 2.0 %collective-permute-start.11 = (bf16[24,640]{1,0:T(8,128)(2,1)S(1)}, bf16[24,640]{1,0:T(8,128)(2,1)S(1)}, u32[]{:S(2)}, u32[]{:S(2)}) collective-permute-start(bf16[24,640]{1,0:T(8,128)(2,1)S(1)} %get-tuple-element.30), channel_id=1, source_target_pairs={{0,1},{1,0},{2,3},{3,2},{4,5},{5,4},{6,7},{7,6},{8,9},{9,8},{10,11... | collective-permute-start | bytes 92168 | tf_op jit(solution)/shard_map/ppermute | solution.py:77
  35.4 4.2 %collective-permute-start.12 = (bf16[24,640]{1,0:T(8,128)(2,1)S(1)}, bf16[24,640]{1,0:T(8,128)(2,1)S(1)}, u32[]{:S(2)}, u32[]{:S(2)}) collective-permute-start(bf16[24,640]{1,0:T(8,128)(2,1)S(1)} %get-tuple-element.31), channel_id=1, source_target_pairs={{0,2},{1,3},{2,0},{3,1},{4,6},{5,7},{6,4},{7,5},{8,10},{9,11},{10,... | collective-permute-start | bytes 92168 | tf_op jit(solution)/shard_map/ppermute | solution.py:77
  36.2 3.6 %collective-permute-start.13 = (bf16[24,640]{1,0:T(8,128)(2,1)S(1)}, bf16[24,640]{1,0:T(8,128)(2,1)S(1)}, u32[]{:S(2)}, u32[]{:S(2)}) collective-permute-start(bf16[24,640]{1,0:T(8,128)(2,1)S(1)} %get-tuple-element.32), channel_id=1, source_target_pairs={{0,3},{1,2},{2,1},{3,0},{4,7},{5,6},{6,5},{7,4},{8,11},{9,10},{10,... | collective-permute-start | bytes 92168 | tf_op jit(solution)/shard_map/ppermute | solution.py:77
  44.5 18.9 %copy-start = (bf16[2,8192,16]{1,2,0:T(8,128)(2,1)S(1)}, bf16[2,8192,16]{1,2,0:T(8,128)(2,1)}, u32[]{:S(2)}) copy-start(bf16[2,8192,16]{1,2,0:T(8,128)(2,1)} %param.20) | copy-start | bytes 1572868
  44.5 5.5 %collective-permute-start.14 = (bf16[8,6272]{1,0:T(8,128)(2,1)S(1)}, bf16[8,6272]{1,0:T(8,128)(2,1)S(1)}, u32[]{:S(2)}, u32[]{:S(2)}) collective-permute-start(bf16[8,6272]{1,0:T(8,128)(2,1)S(1)} %attend.1.refs_0_), channel_id=1, source_target_pairs={{0,4},{1,5},{2,6},{3,7},{4,0},{5,1},{6,2},{7,3},{8,12},{9,13},{10,... | collective-permute-start | bytes 301064 | tf_op jit(solution)/shard_map/ppermute | solution.py:77
  46.6 10.0 %collective-permute-start.15 = (bf16[8,6272]{1,0:T(8,128)(2,1)S(1)}, bf16[8,6272]{1,0:T(8,128)(2,1)S(1)}, u32[]{:S(2)}, u32[]{:S(2)}) collective-permute-start(bf16[8,6272]{1,0:T(8,128)(2,1)S(1)} %attend.1.refs_0_), channel_id=1, source_target_pairs={{0,8},{1,9},{2,10},{3,11},{4,12},{5,13},{6,14},{7,15},{8,0},{9,1},... | collective-permute-start | bytes 301064 | tf_op jit(solution)/shard_map/ppermute | solution.py:77
  46.7 10.8 %collective-permute-start.16 = (bf16[8,6272]{1,0:T(8,128)(2,1)S(1)}, bf16[8,6272]{1,0:T(8,128)(2,1)S(1)}, u32[]{:S(2)}, u32[]{:S(2)}) collective-permute-start(bf16[8,6272]{1,0:T(8,128)(2,1)S(1)} %attend.1.refs_0_), channel_id=1, source_target_pairs={{0,12},{1,13},{2,14},{3,15},{4,8},{5,9},{6,10},{7,11},{8,4},{9,5},... | collective-permute-start | bytes 301064 | tf_op jit(solution)/shard_map/ppermute | solution.py:77
  49.1 9.5 %collective-permute-start.17 = (bf16[8,6272]{1,0:T(8,128)(2,1)S(1)}, bf16[8,6272]{1,0:T(8,128)(2,1)S(1)}, u32[]{:S(2)}, u32[]{:S(2)}) collective-permute-start(bf16[8,6272]{1,0:T(8,128)(2,1)S(1)} %attend.1.refs_0_), channel_id=1, source_target_pairs={{0,2},{1,3},{2,0},{3,1},{4,6},{5,7},{6,4},{7,5},{8,10},{9,11},{10,... | collective-permute-start | bytes 301064 | tf_op jit(solution)/shard_map/ppermute | solution.py:77
  53.6 5.1 %collective-permute-start.18 = (bf16[8,6272]{1,0:T(8,128)(2,1)S(1)}, bf16[8,6272]{1,0:T(8,128)(2,1)S(1)}, u32[]{:S(2)}, u32[]{:S(2)}) collective-permute-start(bf16[8,6272]{1,0:T(8,128)(2,1)S(1)} %get-tuple-element.33.refs_1_), channel_id=1, source_target_pairs={{0,2},{1,3},{2,0},{3,1},{4,6},{5,7},{6,4},{7,5},{8,10},{9,11},{10,... | collective-permute-start | bytes 301064 | tf_op jit(solution)/shard_map/ppermute | solution.py:77
  56.6 5.4 %collective-permute-start.19 = (bf16[8,6272]{1,0:T(8,128)(2,1)S(1)}, bf16[8,6272]{1,0:T(8,128)(2,1)S(1)}, u32[]{:S(2)}, u32[]{:S(2)}) collective-permute-start(bf16[8,6272]{1,0:T(8,128)(2,1)S(1)} %collective-permute-done.15.refs_2_), channel_id=1, source_target_pairs={{0,2},{1,3},{2,0},{3,1},{4,6},{5,7},{6,4},{7,5},{8,10},{9,11},{10,... | collective-permute-start | bytes 301064 | tf_op jit(solution)/shard_map/ppermute | solution.py:77
  57.6 5.5 %collective-permute-start.20 = (bf16[8,6272]{1,0:T(8,128)(2,1)S(1)}, bf16[8,6272]{1,0:T(8,128)(2,1)S(1)}, u32[]{:S(2)}, u32[]{:S(2)}) collective-permute-start(bf16[8,6272]{1,0:T(8,128)(2,1)S(1)} %collective-permute-done.16.refs_3_), channel_id=1, source_target_pairs={{0,2},{1,3},{2,0},{3,1},{4,6},{5,7},{6,4},{7,5},{8,10},{9,11},{10,... | collective-permute-start | bytes 301064 | tf_op jit(solution)/shard_map/ppermute | solution.py:77
  63.4 2.9 %collective-permute-start.21 = (bf16[9,64,1024]{2,1,0:T(8,128)(2,1)S(1)}, bf16[9,64,1024]{2,1,0:T(8,128)(2,1)S(1)}, u32[]{:S(2)}, u32[]{:S(2)}) collective-permute-start(bf16[9,64,1024]{2,1,0:T(8,128)(2,1)S(1)} %unpack.3.left.own), channel_id=1, source_target_pairs={{0,1},{1,0},{2,3},{3,2},{4,5},{5,4},{6,7},{7,6},{8,9},{9,8},{10,11... | collective-permute-start | bytes 3538952 | tf_op jit(solution)/shard_map/ppermute | solution.py:77
  67.1 1.9 %collective-permute-start.22 = (bf16[32,128]{1,0:T(8,128)(2,1)S(1)}, bf16[32,128]{1,0:T(8,128)(2,1)S(1)}, u32[]{:S(2)}, u32[]{:S(2)}) collective-permute-start(bf16[32,128]{1,0:T(8,128)(2,1)S(1)} %shrink.1.refs_0_), channel_id=1, source_target_pairs={{0,1},{1,0},{2,3},{3,2},{4,5},{5,4},{6,7},{7,6},{8,9},{9,8},{10,11... | collective-permute-start | bytes 24584 | tf_op jit(solution)/shard_map/ppermute | solution.py:77
  67.3 3.7 %collective-permute-start.23 = (bf16[32,128]{1,0:T(8,128)(2,1)S(1)}, bf16[32,128]{1,0:T(8,128)(2,1)S(1)}, u32[]{:S(2)}, u32[]{:S(2)}) collective-permute-start(bf16[32,128]{1,0:T(8,128)(2,1)S(1)} %shrink.1.refs_0_), channel_id=1, source_target_pairs={{0,2},{1,3},{2,0},{3,1},{4,6},{5,7},{6,4},{7,5},{8,10},{9,11},{10,... | collective-permute-start | bytes 24584 | tf_op jit(solution)/shard_map/ppermute | solution.py:77
  68.4 3.1 %collective-permute-start.24 = (bf16[32,128]{1,0:T(8,128)(2,1)S(1)}, bf16[32,128]{1,0:T(8,128)(2,1)S(1)}, u32[]{:S(2)}, u32[]{:S(2)}) collective-permute-start(bf16[32,128]{1,0:T(8,128)(2,1)S(1)} %shrink.1.refs_0_), channel_id=1, source_target_pairs={{0,3},{1,2},{2,1},{3,0},{4,7},{5,6},{6,5},{7,4},{8,11},{9,10},{10,... | collective-permute-start | bytes 24584 | tf_op jit(solution)/shard_map/ppermute | solution.py:77
  71.5 7.0 %copy-start.1 = (bf16[32,16,512]{2,1,0:T(8,128)(2,1)S(1)}, bf16[32,16,512]{2,1,0:T(8,128)(2,1)}, u32[]{:S(2)}) copy-start(bf16[32,16,512]{2,1,0:T(8,128)(2,1)} %param.21) | copy-start | bytes 1572868
  71.5 5.9 %collective-permute-start.25 = (bf16[128,128]{1,0:T(8,128)(2,1)S(1)}, bf16[128,128]{1,0:T(8,128)(2,1)S(1)}, u32[]{:S(2)}, u32[]{:S(2)}) collective-permute-start(bf16[128,128]{1,0:T(8,128)(2,1)S(1)} %join_coords.1.refs_0_), channel_id=1, source_target_pairs={{0,4},{1,5},{2,6},{3,7},{4,0},{5,1},{6,2},{7,3},{8,12},{9,13},{10,... | collective-permute-start | bytes 98312 | tf_op jit(solution)/shard_map/ppermute | solution.py:77
  72.1 5.4 %collective-permute-start.26 = (bf16[128,128]{1,0:T(8,128)(2,1)S(1)}, bf16[128,128]{1,0:T(8,128)(2,1)S(1)}, u32[]{:S(2)}, u32[]{:S(2)}) collective-permute-start(bf16[128,128]{1,0:T(8,128)(2,1)S(1)} %join_coords.1.refs_0_), channel_id=1, source_target_pairs={{0,8},{1,9},{2,10},{3,11},{4,12},{5,13},{6,14},{7,15},{8,0},{9,1},... | collective-permute-start | bytes 98312 | tf_op jit(solution)/shard_map/ppermute | solution.py:77
  72.8 5.7 %collective-permute-start.27 = (bf16[128,128]{1,0:T(8,128)(2,1)S(1)}, bf16[128,128]{1,0:T(8,128)(2,1)S(1)}, u32[]{:S(2)}, u32[]{:S(2)}) collective-permute-start(bf16[128,128]{1,0:T(8,128)(2,1)S(1)} %join_coords.1.refs_0_), channel_id=1, source_target_pairs={{0,12},{1,13},{2,14},{3,15},{4,8},{5,9},{6,10},{7,11},{8,4},{9,5},... | collective-permute-start | bytes 98312 | tf_op jit(solution)/shard_map/ppermute | solution.py:77
